TPU v7x, 32 devices: a whole 2x2x4 slice. The times are simulated.
32 devices in a mesh: row: 8 (over z, x), feat: 4 (over y, core).
Axes of the slice: x: 2, y: 2, z: 4, core: 2. Of those that a mesh axis runs over, the one named last changes fastest.
Arguments:
- candidates: bfloat16 [512, 16384], P('row', 'feat'), may hold values from -48 to 48, as said below
- inv_factor: bfloat16 [16384, 16384], P('row', 'feat'), may hold values from -1.5 to 1.5, as said below
- weights: float32 [512], P('row'), may hold values from 0.01 to 0.1
- strata: int32 [512], P('row'), may hold values from 0 to 15, never falling along the last dimension, each value on 1 to 256 neighbouring positions
Outputs:
- new_weight: float32 [512], P('row')
- leverage: float32 [512], P('row')
- information: float32 [16384, 16384], P('row', 'feat')
Inputs may be any that keep to these rules, and one draw needn't show every extreme that they name: `candidates`: row scales and column scales differ. `inv_factor`: zero above the diagonal, positive on the diagonal.
All inputs are finite; a program needn't handle non-finite values.
Results may differ from a plain program's by a relative error of at most 0.0029.
Values may be sent and summed in bfloat16 or wider, within the bound.
No kernel may reach another device: no remote copies, remote signals or barrier semaphores. Data moves between devices by JAX's collectives and lax.ppermute only.
A program may use at most 128 MiB of HBM per device.

v0:
```python
import jax
import jax.numpy as jnp
from jax import lax
from jax.sharding import PartitionSpec as P


def broadcast(shard, axis, root):
    mine = lax.axis_index(axis) == root
    return lax.psum(jnp.where(mine, shard, jnp.zeros_like(shard)), axis)


def per_device(candidates, inv_factor, weights, strata):
    rows_dev = candidates.shape[0]
    feat_block = candidates.shape[1]
    row_block = inv_factor.shape[0]
    row_count = lax.axis_size("row")
    feat_count = lax.axis_size("feat")
    features = feat_block * feat_count
    gathered = lax.all_gather(candidates, "row", axis=0, tiled=True)
    partial_value = lax.dot_general(
        gathered, inv_factor, (((1,), (1,)), ((), ())), preferred_element_type=jnp.float32
    )
    shaped = partial_value.reshape(row_count, rows_dev, row_block)
    summed = lax.psum_scatter(shaped, "feat", scatter_dimension=1, tiled=True)
    squares = jnp.sum(summed * summed, axis=2)
    reduced = lax.psum_scatter(squares, "row", scatter_dimension=0, tiled=True)
    raw_leverage = lax.all_gather(reduced, "feat", axis=1, tiled=True).reshape(rows_dev)
    leverage = raw_leverage / features
    strata_count = 2 * row_count
    membership = (strata[:, None] == jnp.arange(strata_count, dtype=jnp.int32)[None, :]).astype(
        jnp.float32
    )
    products = weights * raw_leverage
    local_product = lax.dot_general(
        membership, products, (((0,), (0,)), ((), ())), precision=lax.Precision.HIGHEST
    )
    local_mass = lax.dot_general(
        membership, weights, (((0,), (0,)), ((), ())), precision=lax.Precision.HIGHEST
    )
    stratum_product, stratum_mass = lax.psum((local_product, local_mass), "row")
    stratum_ratio = stratum_mass / stratum_product
    row_ratio = jnp.dot(membership, stratum_ratio, precision=lax.Precision.HIGHEST)
    new_weight = products * row_ratio
    weight_step = new_weight - weights
    step_all = lax.all_gather(weight_step, "row", axis=0, tiled=True)
    scaled_all = (step_all[:, None] * gathered.astype(jnp.float32)).astype(jnp.bfloat16)
    blocks_per_feat = row_count // feat_count
    row_index = lax.axis_index("row")
    offset = row_index % blocks_per_feat * row_block
    mine = lax.dynamic_slice_in_dim(gathered, offset, row_block, 1)
    root_index = row_index // blocks_per_feat
    column_block = broadcast(mine, "feat", root_index)
    information = lax.dot_general(
        column_block, scaled_all, (((0,), (0,)), ((), ())), preferred_element_type=jnp.float32
    )
    return (new_weight, leverage, information)


def solution(mesh):
    in_specs = (P("row", "feat"), P("row", "feat"), P("row"), P("row"))
    out_specs = (P("row"), P("row"), P("row", "feat"))
    return jax.shard_map(
        per_device, mesh=mesh, in_specs=in_specs, out_specs=out_specs, check_vma=False
    )
```

profile of v0, /device:TPU:0, one launch (start us, length us, event | category | flops | bytes accessed | tf_op | source)
XLA Modules:
  0.0 236.7 jit_solution(13465466392613539596)
XLA Ops:
  7.2 0.0 all-gather.2.cloned.1.call-start
  7.2 0.7 all-gather.2.cloned.1.call-update
  7.9 0.0 reduce-scatter.2.cloned.1.call-start
  7.9 78.3 %all-gather.2.cloned.1.call-done = bf16[512,4096]{1,0:T(8,128)(2,1)} async-done(((bf16[64,4096]{1,0:T(8,128)(2,1)}), bf16[512,4096]{1,0:T(8,128)(2,1)}) %all-gather.2.cloned.1.call-update) | async-done | bytes 4194320 | tf_op jit(solution)/shard_map/all_gather | solution.py:19
  86.3 15.0 %fusion.12 = f32[512,2048]{1,0:T(8,128)} fusion(bf16[512,4096]{1,0:T(8,128)(2,1)} %all-gather.2.cloned.1.call-done, bf16[2048,4096]{1,0:T(8,128)(2,1)} %param.5), kind=kOutput, calls=%fused_computation.22 | convolution fusion | flops 8589934592 | bytes 25165824 | tf_op jit(solution)/shard_map/dot_general | solution.py:20
  101.2 0.0 copy-start.4
  101.2 0.0 copy-start
  101.2 0.0 copy-start.1
  101.2 0.0 copy-start.3
  101.2 0.0 reduce-scatter.2.cloned.1.call-update
  101.3 0.0 all-reduce.6.cloned.1.call-start
  101.3 0.5 copy-done.4
  101.9 0.6 dynamic-slice
  103.1 0.0 copy-done
  103.1 0.6 fusion.11
  103.8 0.0 copy-done.1
  103.8 0.0 copy-done.3
  103.8 0.2 convolution_bitcast_fusion.2
  104.0 4.0 %dynamic-slice_select_fusion = bf16[512,2048]{1,0:T(8,128)(2,1)} fusion(bf16[512,4096]{1,0:T(8,128)(2,1)} %all-gather.2.cloned.1.call-done, s32[]{:T(128)S(6)} %select_n.25, pred[]{:T(512)S(6)} %eq.21), kind=kLoop, calls=%fused_computation.3 | loop fusion | flops 1048576 | bytes 4194309 | tf_op jit(solution)/shard_map/jit(_where)/select_n | solution.py:9
  107.9 0.0 all-reduce.6.cloned.1.call-update
  108.0 36.2 %reduce-scatter.2.cloned.1.call-done = f32[8,16,2048]{2,1,0:T(8,128)} async-done(((f32[8,64,2048]{2,1,0:T(8,128)}), f32[8,16,2048]{2,1,0:T(8,128)}) %reduce-scatter.2.cloned.1.call-update) | async-done | bytes 1048592 | tf_op jit(solution)/shard_map/reduce_scatter | solution.py:24
  144.2 1.4 multiply_reduce_fusion
  145.6 21.4 %all-reduce.2 = f32[8,16]{1,0:T(8,128)S(1)} all-reduce(f32[8,16]{1,0:T(8,128)S(1)} %multiply_reduce_fusion), channel_id=3, replica_groups=mesh['row'=8,'feat'=4] {'row'}, use_global_device_ids=true, to_apply=%region_2.0.clone | all-reduce | flops 128 | bytes 1024
  166.9 0.7 fusion.6
  167.7 5.9 %all-reduce = f32[64]{0:T(128)S(1)} all-reduce(f32[64]{0:T(128)S(1)} %fusion.6), channel_id=1, replica_groups=mesh['row'=8,'feat'=4] {'feat'}, use_global_device_ids=true, to_apply=%add | all-reduce | flops 64 | bytes 512 | tf_op jit(solution)/shard_map/reshape | solution.py:27
  173.6 0.5 broadcast_multiply_fusion
  174.1 0.2 convolution_bitcast_fusion.1
  175.0 17.5 %all-reduce.3 = (f32[16]{0:T(128)S(1)}, f32[16]{0:T(128)S(1)}) all-reduce(f32[16]{0:T(128)S(1)} %convolution_bitcast_fusion.2, f32[16]{0:T(128)S(1)} %convolution_bitcast_fusion.1), channel_id=1, replica_groups=mesh['row'=8,'feat'=4] {'row'}, use_global_device_ids=true, to_apply=%region_3.0 | all-reduce | flops 32 | bytes 256 | tf_op jit(solution)/shard_map/psum | solution.py:40
  192.5 0.2 fusion.2
  192.7 0.0 copy-start.2
  192.7 0.1 subtract_dynamic-update-slice_fusion
  192.8 18.8 %all-reduce.1 = f32[512]{0:T(512)S(1)} all-reduce(f32[512]{0:T(512)S(1)} %subtract_dynamic-update-slice_fusion), channel_id=1, replica_groups=mesh['row'=8,'feat'=4] {'row'}, use_global_device_ids=true, to_apply=%add.1 | all-reduce | flops 512 | bytes 4096
  211.5 0.0 all-reduce.6.cloned.1.call-done
  211.5 18.6 %fusion = f32[2048,4096]{1,0:T(8,128)} fusion(bf16[512,2048]{1,0:T(8,128)(2,1)} %all-reduce.6.cloned.1.call-done, bf16[512,4096]{1,0:T(8,128)(2,1)} %all-gather.2.cloned.1.call-done, f32[512]{0:T(512)S(1)} %all-reduce.1), kind=kOutput, calls=%fused_computation.1 | convolution fusion | flops 8596226048 | bytes 39847936 | tf_op jit(solution)/shard_map/dot_general | solution.py:53
  230.1 0.0 copy-done.2
  (2 shorter events, 0.0 us)
Async XLA Ops:
  7.2 79.1 %all-gather.2.cloned.1.call-start = ((), (), s32[]{:S(2)}) async-start(), calls=%async_computation.1 | async-start | bytes 4718592 | tf_op jit(solution)/shard_map/all_gather | solution.py:19
  7.9 136.3 %reduce-scatter.2.cloned.1.call-start = ((), (), s32[]{:S(2)}) async-start(), calls=%async_computation.2 | async-start | bytes 5242880 | tf_op jit(solution)/shard_map/reduce_scatter | solution.py:24
  101.2 0.7 copy-start.4
  101.2 1.9 copy-start
  101.2 2.5 %copy-start.1 = (f32[64]{0:T(128)S(1)}, f32[64]{0:T(128)}, u32[]{:S(2)}) copy-start(f32[64]{0:T(128)} %param.6) | copy-start | bytes 772
  101.2 2.5 %copy-start.3 = (s32[64]{0:T(128)S(1)}, s32[64]{0:T(128)}, u32[]{:S(2)}) copy-start(s32[64]{0:T(128)} %param.7) | copy-start | bytes 772
  101.3 110.3 %all-reduce.6.cloned.1.call-start = ((), (), s32[]{:S(2)}) async-start(), calls=%async_computation.3 | async-start | bytes 4194304 | tf_op jit(solution)/shard_map/psum | solution.py:9
  192.7 37.5 %copy-start.2 = (f32[64]{0:T(128)}, f32[64]{0:T(128)S(1)}, u32[]{:S(2)}) copy-start(f32[64]{0:T(128)S(1)} %fusion.2) | copy-start | bytes 772
Sparse Core Ops, SparseCore 0:
  10.1 76.0 all-gather.1
  101.4 42.7 reduce-scatter.1
  146.7 51.5 all-reduce.5
where the time goes:
time: 237 us
  waiting for transfers between devices  115 us (49%)
  blocking collectives  63.5 us (27%)
  matrix products  34.1 us (14%)
  between operations  15.1 us (6%)
  other arithmetic  6 us (3%)
  local copies, waits for them, and re-layouts  2.52 us (1%)
    all_gather x1, waiting for transfers between devices, per_device(): gathered = lax.all_gather(candidates, 'row', axis=0, tiled=True)  78.3 us
    unnamed x2, blocking collectives  40.1 us
    reduce_scatter x1, waiting for transfers between devices, per_device(): summed = lax.psum_scatter(shaped, 'feat', scatter_dimension=1, tiled=True)  36.2 us
    dot_general x1, matrix products, per_device(): lax.dot_general(column_block, scaled_all, (((0,), (0,)), ((), ())), prefe...  18.6 us
    psum x1, blocking collectives, per_device(): stratum_product, stratum_mass = lax.psum((local_product, local_mass), 'row')  17.5 us
    dot_general x1, matrix products, per_device(): lax.dot_general(gathered, inv_factor, (((1,), (1,)), ((), ())), preferred...  15 us
    reshape x1, blocking collectives, per_device(): lax.all_gather(reduced, 'feat', axis=1, tiled=True).reshape(rows_dev)  5.91 us
  transfers between devices with their start and end apart: 3, of which 2 were waited for; matrix products, arithmetic and copies ran while one was open for 4% of the time, Pallas kernels for 0%

commit v1 on v0

v1 whole, which is shorter than its diff:
```python
import jax
import jax.numpy as jnp
from jax import lax
from jax.sharding import PartitionSpec as P

BOTH = ("row", "feat")
HI = 4


def ring_order(count):
    return list(range(0, count, 2)) + list(range(1, count, 2))[::-1]


def ring_next(count):
    order = ring_order(count)
    return {order[i]: order[(i + 1) % count] for i in range(count)}


def tree_sum(values):
    values = list(values)
    while len(values) > 1:
        values = [values[i] + values[i + 1] for i in range(0, len(values), 2)]
    return values[0]


def make(mesh):
    rows_n, feats_n = mesh.shape["row"], mesh.shape["feat"]
    hi_n = HI
    lo_n = rows_n // hi_n
    pairs_row = [(r, f) for r in range(rows_n) for f in range(feats_n)]

    def perm(fn, keep=lambda r, f: True):
        out = []
        for r, f in pairs_row:
            if keep(r, f):
                r2, f2 = fn(r, f)
                out.append((r * feats_n + f, r2 * feats_n + f2))
        return out

    def send(x, pairs):
        return lax.ppermute(x, BOTH, pairs)

    hi_next, lo_next = ring_next(hi_n), ring_next(lo_n)
    hi_pairs = perm(lambda r, f: (hi_next[r // lo_n] * lo_n + r % lo_n, f))
    lo_pairs = perm(lambda r, f: (r // lo_n * lo_n + lo_next[r % lo_n], f))
    per_feat = rows_n // feats_n

    def root(r):
        return r // per_feat

    hi_order, lo_order = ring_order(hi_n), ring_order(lo_n)

    def source(r, k, s):
        h, l = r // lo_n, r % lo_n
        h2 = hi_order[(hi_order.index(h) - k) % hi_n]
        l2 = lo_order[(lo_order.index(l) - s) % lo_n]
        return h2 * lo_n + l2

    slots = [(k, s) for k in range(hi_n) for s in range(lo_n)]
    source_table = [[source(r, k, s) for k, s in slots] for r in range(rows_n)]

    def per_device(candidates, inv_factor, weights, strata):
        rows_dev, feat_block = candidates.shape
        row_block = inv_factor.shape[0]
        features = feat_block * feats_n
        row, feat = lax.axis_index("row"), lax.axis_index("feat")
        rows = rows_dev * rows_n

        small = jnp.stack([weights, strata.astype(jnp.float32)])
        small_all = lax.all_gather(small, "row", axis=1, tiled=True)
        weights_all, strata_all = small_all[0], small_all[1].astype(jnp.int32)

        chunks = {}
        held = candidates
        for k in range(hi_n):
            if k:
                held = send(held, hi_pairs)
            chunks[k, 0] = held
            other = held
            for s in range(1, lo_n):
                other = send(other, lo_pairs)
                chunks[k, s] = other

        groups = [[(0, s) for s in range(lo_n)] + [(1, 0)]]
        for k in range(1, hi_n):
            groups.append([(k, s) for s in range(1, lo_n)] + ([(k + 1, 0)] if k + 1 < hi_n else []))

        offset = row % per_feat * row_block
        root_row = row // per_feat
        sums, columns = {}, []
        for group in groups:
            block = jnp.concatenate([chunks[slot] for slot in group], axis=0)
            part = lax.dot_general(
                block, inv_factor, (((1,), (1,)), ((), ())), preferred_element_type=jnp.float32
            )
            width = row_block
            bit = 1
            while bit < feats_n:
                width //= 2
                mine_high = (feat // bit) % 2
                keep = lax.dynamic_slice_in_dim(part, mine_high * width, width, 1)
                away = lax.dynamic_slice_in_dim(part, (1 - mine_high) * width, width, 1)
                got = send(away.astype(jnp.bfloat16), perm(lambda r, f: (r, f ^ bit)))
                part = keep + got.astype(jnp.float32)
                bit *= 2
            square = jnp.sum(part * part, axis=1).reshape(len(group), rows_dev)
            for i, slot in enumerate(group):
                sums[slot] = square[i]

            mine = lax.dynamic_slice_in_dim(block, offset, row_block, 1)
            value = jnp.where(feat == root_row, mine, jnp.zeros_like(mine))
            half = mine.shape[0] // 2
            low, high = value[:half], value[half:]
            beside = send(value, perm(lambda r, f: (r, f ^ 1), lambda r, f: f == root(r)))
            bit = 2
            while bit < feats_n:
                def held_by(r, f, core):
                    d = f ^ root(r)
                    return d == 0 or (1 < d < bit and (d & 1) == core)
                low = low + send(low, [
                    (r * feats_n + f, r * feats_n + (f ^ bit))
                    for r, f in pairs_row if held_by(r, f, 0)
                ])
                high = high + send(high, [
                    (r * feats_n + f, r * feats_n + (f ^ bit ^ (1 if f == root(r) else 0)))
                    for r, f in pairs_row if held_by(r, f, 1)
                ])
                bit *= 2
            far = ((feat ^ root_row) // 2) != 0
            swap = perm(lambda r, f: (r, f ^ 1), lambda r, f: (f ^ root(r)) > 1)
            is_low = ((feat ^ root_row) & 1) == 0
            other = send(jnp.where(is_low, low, high), swap)
            far_value = jnp.concatenate(
                [jnp.where(is_low, low, other), jnp.where(is_low, other, high)], axis=0
            )
            columns.append(jnp.where(far, far_value, value + beside))

        order = [slot for group in groups for slot in group]
        table = jnp.asarray(
            [[source_table[r][slots.index(slot)] for slot in order] for r in range(rows_n)], jnp.int32
        )
        places = table[row]
        one_hot = (places[None, :] == jnp.arange(rows_n, dtype=jnp.int32)[:, None]).astype(jnp.float32)
        local = jnp.stack([sums[slot] for slot in order])
        total = jnp.sum(one_hot[:, :, None] * local[None, :, :], axis=1)

        def exchange(x, axis_n, first, count, on_row):
            got = [x]
            for d in range(1, count):
                if on_row:
                    pairs = perm(lambda r, f: (r ^ (d * first), f))
                else:
                    pairs = perm(lambda r, f: (r, f ^ (d * first)))
                got.append(send(x, pairs))
            return tree_sum(got)

        total = exchange(total, feats_n, 1, feats_n, False)
        first = 1
        while first < rows_n:
            count = min(8, rows_n // first)
            total = exchange(total, rows_n, first, count, True)
            first *= count

        raw_all = total.reshape(rows)
        strata_count = 2 * rows_n
        membership = (
            strata_all[:, None] == jnp.arange(strata_count, dtype=jnp.int32)[None, :]
        ).astype(jnp.float32)
        products = weights_all * raw_all
        stratum_product = jnp.sum(membership * products[:, None], axis=0)
        stratum_mass = jnp.sum(membership * weights_all[:, None], axis=0)
        stratum_ratio = stratum_mass / stratum_product
        row_ratio = jnp.sum(
            jnp.where(membership > 0, stratum_ratio[None, :], 0.0), axis=1
        )
        new_all = products * row_ratio
        step = (new_all - weights_all).reshape(rows_n, rows_dev)
        step_local = jnp.sum(one_hot[:, :, None] * step[:, None, :], axis=0).reshape(rows)

        gathered = jnp.concatenate([chunks[slot] for slot in order], axis=0)
        column_block = jnp.concatenate(columns, axis=0)
        scaled = (step_local[:, None] * gathered.astype(jnp.float32)).astype(jnp.bfloat16)
        information = lax.dot_general(
            column_block, scaled, (((0,), (0,)), ((), ())), preferred_element_type=jnp.float32
        )
        new_weight = lax.dynamic_slice_in_dim(new_all, row * rows_dev, rows_dev)
        leverage = lax.dynamic_slice_in_dim(raw_all, row * rows_dev, rows_dev) / features
        return (new_weight, leverage, information)

    return per_device


def solution(mesh):
    in_specs = (P("row", "feat"), P("row", "feat"), P("row"), P("row"))
    out_specs = (P("row"), P("row"), P("row", "feat"))
    return jax.shard_map(
        make(mesh), mesh=mesh, in_specs=in_specs, out_specs=out_specs, check_vma=False
    )
```

time: 237 us -> 203 us (0.86)
  waiting for transfers between devices: 115 us -> 31.6 us
  starting transfers between devices: 0.12 us -> 52.4 us
  blocking collectives: 63.5 us -> 22.4 us
  matrix products: 34.1 us -> 63.4 us
  between operations: 15.1 us -> 1.37 us
  local copies, waits for them, and re-layouts: 2.52 us -> 14.8 us
  other arithmetic: 6 us -> 16.6 us
    all_gather x1 -> x0, waiting for transfers between devices: 78.3 us -> none  [per_device(): gathered = lax.all_gather(candidates, 'row', axis=0, tiled=True)]
    ppermute x0 -> x41, starting transfers between devices: none -> 52.4 us  [send(): return lax.ppermute(x, BOTH, pairs)]
    unnamed x2 -> x0, blocking collectives: 40.1 us -> none
    reduce_scatter x1 -> x0, waiting for transfers between devices: 36.2 us -> none  [per_device(): summed = lax.psum_scatter(shaped, 'feat', scatter_dimension=1, tiled=True)]
    ppermute x0 -> x41, waiting for transfers between devices: none -> 31.6 us  [send(): return lax.ppermute(x, BOTH, pairs)]
    dot_general x5, matrix products: 34.1 us -> 63.4 us  [the longest x4 45.1 us: per_device(): lax.dot_general(block, inv_factor, (((1,), (1,)), ((), ())), preferred_el...]
    all_gather x0 -> x1, blocking collectives: none -> 22.4 us  [per_device(): small_all = lax.all_gather(small, 'row', axis=1, tiled=True)]
    psum x1 -> x0, blocking collectives: 17.5 us -> none  [per_device(): stratum_product, stratum_mass = lax.psum((local_product, local_mass), 'row')]
  transfers between devices with their start and end apart: 3 -> 41, of which waited for: 2 -> 9; matrix products, arithmetic and copies ran while one was open for 4% -> 37% of each run, Pallas kernels for 0% -> 0%
where the time goes in v1:
time: 203 us
  matrix products  63.4 us (31%)
  starting transfers between devices  52.4 us (26%)
  waiting for transfers between devices  31.6 us (16%)
  blocking collectives  22.4 us (11%)
  other arithmetic  16.6 us (8%)
  local copies, waits for them, and re-layouts  14.8 us (7%)
    ppermute x41, starting transfers between devices, send(): return lax.ppermute(x, BOTH, pairs)  52.4 us
    dot_general x4, matrix products, per_device(): lax.dot_general(block, inv_factor, (((1,), (1,)), ((), ())), preferred_el...  45.1 us
    ppermute x41, waiting for transfers between devices, send(): return lax.ppermute(x, BOTH, pairs)  31.6 us
    all_gather x1, blocking collectives, per_device(): small_all = lax.all_gather(small, 'row', axis=1, tiled=True)  22.4 us
    dot_general x1, matrix products, per_device(): lax.dot_general(column_block, scaled, (((0,), (0,)), ((), ())), preferred...  18.3 us
    unnamed x38, local copies, waits for them, and re-layouts  7.83 us
    select_n x4, other arithmetic, per_device(): columns.append(jnp.where(far, far_value, value + beside))  6.77 us
  transfers between devices with their start and end apart: 41, of which 9 were waited for; matrix products, arithmetic and copies ran while one was open for 37% of the time, Pallas kernels for 0%

profile of v1, /device:TPU:0, one launch (start us, length us, event | category | flops | bytes accessed | tf_op | source)
XLA Modules:
  0.0 202.6 jit_solution(11165990571154402793)
XLA Ops:
  0.6 3.0 %collective-permute-start = (bf16[64,4096]{1,0:T(8,128)(2,1)}, bf16[64,4096]{1,0:T(8,128)(2,1)S(1)}, u32[]{:S(2)}, u32[]{:S(2)}) collective-permute-start(bf16[64,4096]{1,0:T(8,128)(2,1)} %param.5), channel_id=1, source_target_pairs={{0,4},{1,5},{2,6},{3,7},{4,0},{5,1},{6,2},{7,3},{8,12},{9,13},{10,... | collective-permute-start | bytes 1572872 | tf_op jit(solution)/shard_map/ppermute | solution.py:41
  3.6 2.6 %collective-permute-start.1 = (bf16[64,4096]{1,0:T(8,128)(2,1)}, bf16[64,4096]{1,0:T(8,128)(2,1)S(1)}, u32[]{:S(2)}, u32[]{:S(2)}) collective-permute-start(bf16[64,4096]{1,0:T(8,128)(2,1)} %param.5), channel_id=1, source_target_pairs={{0,16},{1,17},{2,18},{3,19},{4,20},{5,21},{6,22},{7,23},{8,0},{9,1... | collective-permute-start | bytes 1572872 | tf_op jit(solution)/shard_map/ppermute | solution.py:41
  6.2 2.0 constant_dynamic-update-slice_fusion.14
  9.5 22.4 %all-gather = f32[8,64,2]{1,2,0:T(2,128)S(1)} all-gather(f32[1,64,2]{1,2,0:T(2,128)S(1)} %maximum_bitcast_fusion), channel_id=1, replica_groups=mesh['row'=8,'feat'=4] {'row'}, dimensions={0}, use_global_device_ids=true | all-gather | bytes 4608 | tf_op jit(solution)/shard_map/all_gather | solution.py:70
  34.9 1.0 fusion.12
  36.0 2.2 %collective-permute-start.28 = (bf16[192,2048]{1,0:T(8,128)(2,1)S(1)}, bf16[192,2048]{1,0:T(8,128)(2,1)}, u32[]{:S(2)}, u32[]{:S(2)}) collective-permute-start(bf16[192,2048]{1,0:T(8,128)(2,1)S(1)} %dynamic-slice_select_fusion), channel_id=1, source_target_pairs={{0,1},{4,5},{9,8},{13,12},{18,19},{22,23},{27,26},{31,30}} | collective-permute-start | bytes 2359304 | tf_op jit(solution)/shard_map/ppermute | solution.py:41
  38.2 2.8 %collective-permute-start.25 = (bf16[96,2048]{1,0:T(8,128)(2,1)}, bf16[96,2048]{1,0:T(8,128)(2,1)S(1)}, u32[]{:S(2)}, u32[]{:S(2)}) collective-permute-start(bf16[96,2048]{1,0:T(8,128)(2,1)} %get-tuple-element.7), channel_id=1, source_target_pairs={{0,2},{4,6},{9,11},{13,15},{18,16},{22,20},{27,25},{31,29}} | collective-permute-start | bytes 1179656 | tf_op jit(solution)/shard_map/ppermute | solution.py:41
  41.0 1.3 collective-permute-start.26
  42.3 10.4 %fusion.16 = f32[192,2048]{1,0:T(8,128)} fusion(bf16[192,4096]{1,0:T(8,128)(2,1)S(1)} %get-tuple-element.26, bf16[2048,4096]{1,0:T(8,128)(2,1)} %param.6), kind=kOutput, calls=%fused_computation.100 | convolution fusion | flops 3221225472 | bytes 19922944 | tf_op jit(solution)/shard_map/dot_general | solution.py:93
  52.6 1.2 dynamic-slice_convert_fusion
  55.1 1.4 collective-permute-start.27
  56.5 1.2 convert_add_fusion
  58.6 10.0 %collective-permute-done.4 = bf16[64,4096]{1,0:T(8,128)(2,1)S(1)} collective-permute-done((bf16[64,4096]{1,0:T(8,128)(2,1)}, bf16[64,4096]{1,0:T(8,128)(2,1)S(1)}, u32[]{:S(2)}, u32[]{:S(2)}) %collective-permute-start.4) | collective-permute-done | bytes 524320 | tf_op jit(solution)/shard_map/ppermute | solution.py:41
  69.5 1.0 constant_dynamic-update-slice_fusion.10
  70.6 11.4 %fusion.17 = f32[128,2048]{1,0:T(8,128)S(1)} fusion(bf16[128,4096]{1,0:T(8,128)(2,1)S(1)} %get-tuple-element.22, bf16[2048,4096]{1,0:T(8,128)(2,1)} %param.6), kind=kOutput, calls=%fused_computation.101 | convolution fusion | flops 2147483648 | bytes 18874368 | tf_op jit(solution)/shard_map/dot_general | solution.py:93
  82.0 2.5 %collective-permute-start.32 = (bf16[128,2048]{1,0:T(8,128)(2,1)S(1)}, bf16[128,2048]{1,0:T(8,128)(2,1)}, u32[]{:S(2)}, u32[]{:S(2)}) collective-permute-start(bf16[128,2048]{1,0:T(8,128)(2,1)S(1)} %dynamic-slice_select_fusion.2), channel_id=1, source_target_pairs={{0,1},{4,5},{9,8},{13,12},{18,19},{22,23},{27,26},{31,30}} | collective-permute-start | bytes 1572872 | tf_op jit(solution)/shard_map/ppermute | solution.py:41
  84.5 1.3 collective-permute-start.29
  85.9 1.3 collective-permute-start.30
  87.2 1.2 multiply_reduce_fusion
  88.5 1.2 collective-permute-done.29
  89.7 2.8 %collective-permute-done.30 = bf16[64,2048]{1,0:T(8,128)(2,1)S(1)} collective-permute-done((bf16[64,2048]{1,0:T(8,128)(2,1)S(1)}, bf16[64,2048]{1,0:T(8,128)(2,1)S(1)}, u32[]{:S(2)}, u32[]{:S(2)}) %collective-permute-start.30) | collective-permute-done | bytes 262176 | tf_op jit(solution)/shard_map/ppermute | solution.py:41
  93.9 1.4 collective-permute-start.31
  95.3 1.1 broadcast_select_fusion.1
  96.4 2.8 %collective-permute-start.7 = (bf16[128,512]{1,0:T(8,128)(2,1)S(1)}, bf16[128,512]{1,0:T(8,128)(2,1)S(1)}, u32[]{:S(2)}, u32[]{:S(2)}) collective-permute-start(bf16[128,512]{1,0:T(8,128)(2,1)S(1)} %dynamic-slice_convert_fusion.6), channel_id=1, source_target_pairs={{0,2},{1,3},{2,0},{3,1},{4,6},{5,7},{6,4},{7,5},{8,10},{9,11},{10,... | collective-permute-start | bytes 393224 | tf_op jit(solution)/shard_map/ppermute | solution.py:41
  99.2 2.4 %maximum_select_fusion = bf16[192,2048]{1,0:T(8,128)(2,1)} fusion(bf16[96,2048]{1,0:T(8,128)(2,1)S(1)} %get-tuple-element.6, bf16[96,2048]{1,0:T(8,128)(2,1)S(1)} %get-tuple-element.5, bf16[192,2048]{1,0:T(8,128)(2,1)} %collective-permute-done.28, pred[]{:T(512)S(6)} %ne.75, bf16[192,4096]{1,0:T(8,128)(2,1)S(1)} %copy-done.2, s32[]{:T(128)S(6)} %select_n.212, ...), kind=kLoop, calls=%fused_computation.10 | loop fusion | flops 3932160 | bytes 3145734 | tf_op jit(solution)/shard_map/jit(_where)/select_n | solution.py:136
  101.7 1.6 collective-permute-done.7
  103.5 3.9 %collective-permute-done.8 = bf16[64,4096]{1,0:T(8,128)(2,1)S(1)} collective-permute-done((bf16[64,4096]{1,0:T(8,128)(2,1)}, bf16[64,4096]{1,0:T(8,128)(2,1)S(1)}, u32[]{:S(2)}, u32[]{:S(2)}) %collective-permute-start.8) | collective-permute-done | bytes 524320 | tf_op jit(solution)/shard_map/ppermute | solution.py:41
  109.4 12.4 %fusion.18 = f32[128,2048]{1,0:T(8,128)} fusion(bf16[128,4096]{1,0:T(8,128)(2,1)S(1)} %get-tuple-element.18, bf16[2048,4096]{1,0:T(8,128)(2,1)} %param.6), kind=kOutput, calls=%fused_computation.102 | convolution fusion | flops 2147483648 | bytes 18874368 | tf_op jit(solution)/shard_map/dot_general | solution.py:93
  121.8 3.6 %collective-permute-start.36 = (bf16[128,2048]{1,0:T(8,128)(2,1)S(1)}, bf16[128,2048]{1,0:T(8,128)(2,1)}, u32[]{:S(2)}, u32[]{:S(2)}) collective-permute-start(bf16[128,2048]{1,0:T(8,128)(2,1)S(1)} %dynamic-slice_select_fusion.1), channel_id=1, source_target_pairs={{0,1},{4,5},{9,8},{13,12},{18,19},{22,23},{27,26},{31,30}} | collective-permute-start | bytes 1572872 | tf_op jit(solution)/shard_map/ppermute | solution.py:41
  125.5 2.2 %collective-permute-start.33 = (bf16[64,2048]{1,0:T(8,128)(2,1)S(1)}, bf16[64,2048]{1,0:T(8,128)(2,1)S(1)}, u32[]{:S(2)}, u32[]{:S(2)}) collective-permute-start(bf16[64,2048]{1,0:T(8,128)(2,1)S(1)} %get-tuple-element.15), channel_id=1, source_target_pairs={{0,2},{4,6},{9,11},{13,15},{18,16},{22,20},{27,25},{31,29}} | collective-permute-start | bytes 786440 | tf_op jit(solution)/shard_map/ppermute | solution.py:41
  127.7 1.3 collective-permute-start.34
  129.0 1.1 dynamic-slice_convert_fusion.1
  130.2 1.1 broadcast_select_fusion.7
  131.8 2.1 %maximum_select_fusion.1 = bf16[128,2048]{1,0:T(8,128)(2,1)} fusion(bf16[64,2048]{1,0:T(8,128)(2,1)S(1)} %get-tuple-element.10, bf16[64,2048]{1,0:T(8,128)(2,1)S(1)} %get-tuple-element.9, bf16[128,2048]{1,0:T(8,128)(2,1)} %collective-permute-done.32, pred[]{:T(512)S(6)} %ne.75, bf16[128,4096]{1,0:T(8,128)(2,1)S(1)} %get-tuple-element.22, s32[]{:T(128)S(6)} %select_n.212, ...), kind=kLoop, calls=%fused_computation.14 | loop fusion | flops 2621440 | bytes 2097158 | tf_op jit(solution)/shard_map/jit(_where)/select_n | solution.py:136
  135.1 4.6 %collective-permute-done.11 = bf16[128,512]{1,0:T(8,128)(2,1)S(1)} collective-permute-done((bf16[128,512]{1,0:T(8,128)(2,1)S(1)}, bf16[128,512]{1,0:T(8,128)(2,1)S(1)}, u32[]{:S(2)}, u32[]{:S(2)}) %collective-permute-start.11) | collective-permute-done | bytes 131104 | tf_op jit(solution)/shard_map/ppermute | solution.py:41
  140.0 5.9 %collective-permute-done.12 = bf16[64,4096]{1,0:T(8,128)(2,1)S(1)} collective-permute-done((bf16[64,4096]{1,0:T(8,128)(2,1)}, bf16[64,4096]{1,0:T(8,128)(2,1)S(1)}, u32[]{:S(2)}, u32[]{:S(2)}) %collective-permute-start.12) | collective-permute-done | bytes 524320 | tf_op jit(solution)/shard_map/ppermute | solution.py:41
  145.9 10.9 %fusion.19 = f32[64,2048]{1,0:T(8,128)S(1)} fusion(bf16[64,4096]{1,0:T(8,128)(2,1)S(1)} %collective-permute-done.12, bf16[2048,4096]{1,0:T(8,128)(2,1)} %param.6), kind=kOutput, calls=%fused_computation.103 | convolution fusion | flops 1073741824 | bytes 17825792 | tf_op jit(solution)/shard_map/dot_general | solution.py:93
  157.0 1.3 collective-permute-done.13
  158.5 3.9 %collective-permute-start.37 = (bf16[32,2048]{1,0:T(8,128)(2,1)S(1)}, bf16[32,2048]{1,0:T(8,128)(2,1)S(1)}, u32[]{:S(2)}, u32[]{:S(2)}) collective-permute-start(bf16[32,2048]{1,0:T(8,128)(2,1)S(1)} %get-tuple-element.33), channel_id=1, source_target_pairs={{0,2},{4,6},{9,11},{13,15},{18,16},{22,20},{27,25},{31,29}} | collective-permute-start | bytes 393224 | tf_op jit(solution)/shard_map/ppermute | solution.py:41
  162.4 1.3 collective-permute-start.38
  164.1 1.8 collective-permute-start.15
  165.9 2.1 %maximum_select_fusion.2 = bf16[128,2048]{1,0:T(8,128)(2,1)} fusion(bf16[64,2048]{1,0:T(8,128)(2,1)S(1)} %get-tuple-element.12, bf16[64,2048]{1,0:T(8,128)(2,1)S(1)} %get-tuple-element.11, bf16[128,2048]{1,0:T(8,128)(2,1)} %collective-permute-done.36, pred[]{:T(512)S(6)} %ne.75, bf16[128,4096]{1,0:T(8,128)(2,1)S(1)} %get-tuple-element.18, s32[]{:T(128)S(6)} %select_n.212, ...), kind=kLoop, calls=%fused_computation.15 | loop fusion | flops 2621440 | bytes 2097158 | tf_op jit(solution)/shard_map/jit(_where)/select_n | solution.py:136
  168.4 3.4 %collective-permute-start.23 = (f32[8,64]{1,0:T(8,128)S(1)}, f32[8,64]{1,0:T(8,128)S(1)}, u32[]{:S(2)}, u32[]{:S(2)}) collective-permute-start(f32[8,64]{1,0:T(8,128)S(1)} %add_add_fusion.1), channel_id=1, source_target_pairs={{0,24},{1,25},{2,26},{3,27},{4,28},{5,29},{6,30},{7,31},{8,16},{9,... | collective-permute-start | bytes 6152 | tf_op jit(solution)/shard_map/ppermute | solution.py:41
  172.6 3.9 %collective-permute-start.21 = (f32[8,64]{1,0:T(8,128)S(1)}, f32[8,64]{1,0:T(8,128)S(1)}, u32[]{:S(2)}, u32[]{:S(2)}) collective-permute-start(f32[8,64]{1,0:T(8,128)S(1)} %add_add_fusion.1), channel_id=1, source_target_pairs={{0,16},{1,17},{2,18},{3,19},{4,20},{5,21},{6,22},{7,23},{8,24},{9,... | collective-permute-start | bytes 6152 | tf_op jit(solution)/shard_map/ppermute | solution.py:41
  176.6 1.9 collective-permute-start.19
  178.5 1.6 collective-permute-start.18
  180.1 1.3 collective-permute-start.40
  184.3 18.3 %fusion = f32[2048,4096]{1,0:T(8,128)} fusion(bf16[512,4096]{1,0:T(8,128)(2,1)} %constant_dynamic-update-slice_fusion.7, f32[512]{0:T(512)S(1)} %mul.134, bf16[64,2048]{1,0:T(8,128)(2,1)S(1)} %maximum_select_fusion.3, bf16[128,2048]{1,0:T(8,128)(2,1)} %maximum_select_fusion.2, bf16[128,2048]{1,0:T(8,128)(2,1)S(1)} %copy-done.14, ...), kind=kOutput, calls=%fused_computation.1 | convolution fusion | flops 8604614656 | bytes 39847936 | tf_op jit(solution)/shard_map/dot_general | solution.py:183
  (141 shorter events, 17.8 us)
Async XLA Ops:
  0.6 32.2 %collective-permute-start = (bf16[64,4096]{1,0:T(8,128)(2,1)}, bf16[64,4096]{1,0:T(8,128)(2,1)S(1)}, u32[]{:S(2)}, u32[]{:S(2)}) collective-permute-start(bf16[64,4096]{1,0:T(8,128)(2,1)} %param.5), channel_id=1, source_target_pairs={{0,4},{1,5},{2,6},{3,7},{4,0},{5,1},{6,2},{7,3},{8,12},{9,13},{10,... | collective-permute-start | bytes 1572872 | tf_op jit(solution)/shard_map/ppermute | solution.py:41
  3.6 30.2 %collective-permute-start.1 = (bf16[64,4096]{1,0:T(8,128)(2,1)}, bf16[64,4096]{1,0:T(8,128)(2,1)S(1)}, u32[]{:S(2)}, u32[]{:S(2)}) collective-permute-start(bf16[64,4096]{1,0:T(8,128)(2,1)} %param.5), channel_id=1, source_target_pairs={{0,16},{1,17},{2,18},{3,19},{4,20},{5,21},{6,22},{7,23},{8,0},{9,1... | collective-permute-start | bytes 1572872 | tf_op jit(solution)/shard_map/ppermute | solution.py:41
  34.8 17.9 %copy-start.1 = (bf16[192,4096]{1,0:T(8,128)(2,1)}, bf16[192,4096]{1,0:T(8,128)(2,1)S(1)}, u32[]{:S(2)}) copy-start(bf16[192,4096]{1,0:T(8,128)(2,1)S(1)} %get-tuple-element.26) | copy-start | bytes 4718596
  36.0 60.4 %collective-permute-start.28 = (bf16[192,2048]{1,0:T(8,128)(2,1)S(1)}, bf16[192,2048]{1,0:T(8,128)(2,1)}, u32[]{:S(2)}, u32[]{:S(2)}) collective-permute-start(bf16[192,2048]{1,0:T(8,128)(2,1)S(1)} %dynamic-slice_select_fusion), channel_id=1, source_target_pairs={{0,1},{4,5},{9,8},{13,12},{18,19},{22,23},{27,26},{31,30}} | collective-permute-start | bytes 2359304 | tf_op jit(solution)/shard_map/ppermute | solution.py:41
  38.2 15.8 %collective-permute-start.25 = (bf16[96,2048]{1,0:T(8,128)(2,1)}, bf16[96,2048]{1,0:T(8,128)(2,1)S(1)}, u32[]{:S(2)}, u32[]{:S(2)}) collective-permute-start(bf16[96,2048]{1,0:T(8,128)(2,1)} %get-tuple-element.7), channel_id=1, source_target_pairs={{0,2},{4,6},{9,11},{13,15},{18,16},{22,20},{27,25},{31,29}} | collective-permute-start | bytes 1179656 | tf_op jit(solution)/shard_map/ppermute | solution.py:41
  41.0 13.1 %collective-permute-start.26 = (bf16[96,2048]{1,0:T(8,128)(2,1)S(1)}, bf16[96,2048]{1,0:T(8,128)(2,1)S(1)}, u32[]{:S(2)}, u32[]{:S(2)}) collective-permute-start(bf16[96,2048]{1,0:T(8,128)(2,1)S(1)} %get-tuple-element.8), channel_id=1, source_target_pairs={{0,3},{4,7},{9,10},{13,14},{18,17},{22,21},{27,24},{31,28}} | collective-permute-start | bytes 1179656 | tf_op jit(solution)/shard_map/ppermute | solution.py:41
  53.8 2.7 %collective-permute-start.2 = (bf16[192,1024]{1,0:T(8,128)(2,1)S(1)}, bf16[192,1024]{1,0:T(8,128)(2,1)S(1)}, u32[]{:S(2)}, u32[]{:S(2)}) collective-permute-start(bf16[192,1024]{1,0:T(8,128)(2,1)S(1)} %dynamic-slice_convert_fusion), channel_id=1, source_target_pairs={{0,1},{1,0},{2,3},{3,2},{4,5},{5,4},{6,7},{7,6},{8,9},{9,8},{10,11... | collective-permute-start | bytes 1179656 | tf_op jit(solution)/shard_map/ppermute | solution.py:41
  53.9 15.5 %collective-permute-start.5 = (bf16[64,4096]{1,0:T(8,128)(2,1)}, bf16[64,4096]{1,0:T(8,128)(2,1)S(1)}, u32[]{:S(2)}, u32[]{:S(2)}) collective-permute-start(bf16[64,4096]{1,0:T(8,128)(2,1)} %copy-done.11), channel_id=1, source_target_pairs={{0,16},{1,17},{2,18},{3,19},{4,20},{5,21},{6,22},{7,23},{8,0},{9,1... | collective-permute-start | bytes 1572872 | tf_op jit(solution)/shard_map/ppermute | solution.py:41
  54.0 16.5 %copy-start.4 = (bf16[96,2048]{1,0:T(8,128)(2,1)}, bf16[96,2048]{1,0:T(8,128)(2,1)S(1)}, u32[]{:S(2)}) copy-start(bf16[96,2048]{1,0:T(8,128)(2,1)S(1)} %collective-permute-done.25) | copy-start | bytes 1179652
  54.0 14.5 %collective-permute-start.4 = (bf16[64,4096]{1,0:T(8,128)(2,1)}, bf16[64,4096]{1,0:T(8,128)(2,1)S(1)}, u32[]{:S(2)}, u32[]{:S(2)}) collective-permute-start(bf16[64,4096]{1,0:T(8,128)(2,1)} %copy-done.11), channel_id=1, source_target_pairs={{0,4},{1,5},{2,6},{3,7},{4,0},{5,1},{6,2},{7,3},{8,12},{9,13},{10,... | collective-permute-start | bytes 1572872 | tf_op jit(solution)/shard_map/ppermute | solution.py:41
  54.1 16.4 %copy-start.6 = (bf16[96,2048]{1,0:T(8,128)(2,1)}, bf16[96,2048]{1,0:T(8,128)(2,1)S(1)}, u32[]{:S(2)}) copy-start(bf16[96,2048]{1,0:T(8,128)(2,1)S(1)} %collective-permute-done.26) | copy-start | bytes 1179652
  55.1 38.8 %collective-permute-start.27 = (bf16[96,2048]{1,0:T(8,128)(2,1)}, bf16[96,2048]{1,0:T(8,128)(2,1)}, u32[]{:S(2)}, u32[]{:S(2)}) collective-permute-start(bf16[96,2048]{1,0:T(8,128)(2,1)} %broadcast_select_fusion.2), channel_id=1, source_target_pairs={{2,3},{3,2},{6,7},{7,6},{10,11},{11,10},{14,15},{15,14},{16,17},{1... | collective-permute-start | bytes 1179656 | tf_op jit(solution)/shard_map/ppermute | solution.py:41
  58.6 27.3 %collective-permute-start.3 = (bf16[192,512]{1,0:T(8,128)(2,1)}, bf16[192,512]{1,0:T(8,128)(2,1)}, u32[]{:S(2)}, u32[]{:S(2)}) collective-permute-start(bf16[192,512]{1,0:T(8,128)(2,1)} %dynamic-slice_convert_fusion.3), channel_id=1, source_target_pairs={{0,2},{1,3},{2,0},{3,1},{4,6},{5,7},{6,4},{7,5},{8,10},{9,11},{10,... | collective-permute-start | bytes 589832 | tf_op jit(solution)/shard_map/ppermute | solution.py:41
  82.0 13.3 %copy-start.5 = (bf16[96,2048]{1,0:T(8,128)(2,1)S(1)}, bf16[96,2048]{1,0:T(8,128)(2,1)}, u32[]{:S(2)}) copy-start(bf16[96,2048]{1,0:T(8,128)(2,1)} %copy-done.4) | copy-start | bytes 1179652
  82.0 17.2 %copy-start.2 = (bf16[192,4096]{1,0:T(8,128)(2,1)S(1)}, bf16[192,4096]{1,0:T(8,128)(2,1)}, u32[]{:S(2)}) copy-start(bf16[192,4096]{1,0:T(8,128)(2,1)} %copy-done.1) | copy-start | bytes 4718596
  82.0 49.3 %collective-permute-start.32 = (bf16[128,2048]{1,0:T(8,128)(2,1)S(1)}, bf16[128,2048]{1,0:T(8,128)(2,1)}, u32[]{:S(2)}, u32[]{:S(2)}) collective-permute-start(bf16[128,2048]{1,0:T(8,128)(2,1)S(1)} %dynamic-slice_select_fusion.2), channel_id=1, source_target_pairs={{0,1},{4,5},{9,8},{13,12},{18,19},{22,23},{27,26},{31,30}} | collective-permute-start | bytes 1572872 | tf_op jit(solution)/shard_map/ppermute | solution.py:41
  84.5 5.2 %collective-permute-start.29 = (bf16[64,2048]{1,0:T(8,128)(2,1)S(1)}, bf16[64,2048]{1,0:T(8,128)(2,1)S(1)}, u32[]{:S(2)}, u32[]{:S(2)}) collective-permute-start(bf16[64,2048]{1,0:T(8,128)(2,1)S(1)} %get-tuple-element.13), channel_id=1, source_target_pairs={{0,2},{4,6},{9,11},{13,15},{18,16},{22,20},{27,25},{31,29}} | collective-permute-start | bytes 786440 | tf_op jit(solution)/shard_map/ppermute | solution.py:41
  85.9 6.6 %collective-permute-start.30 = (bf16[64,2048]{1,0:T(8,128)(2,1)S(1)}, bf16[64,2048]{1,0:T(8,128)(2,1)S(1)}, u32[]{:S(2)}, u32[]{:S(2)}) collective-permute-start(bf16[64,2048]{1,0:T(8,128)(2,1)S(1)} %get-tuple-element.14), channel_id=1, source_target_pairs={{0,3},{4,7},{9,10},{13,14},{18,17},{22,21},{27,24},{31,28}} | collective-permute-start | bytes 786440 | tf_op jit(solution)/shard_map/ppermute | solution.py:41
  89.7 3.6 %collective-permute-start.6 = (bf16[128,1024]{1,0:T(8,128)(2,1)S(1)}, bf16[128,1024]{1,0:T(8,128)(2,1)S(1)}, u32[]{:S(2)}, u32[]{:S(2)}) collective-permute-start(bf16[128,1024]{1,0:T(8,128)(2,1)S(1)} %dynamic-slice_convert_fusion.2), channel_id=1, source_target_pairs={{0,1},{1,0},{2,3},{3,2},{4,5},{5,4},{6,7},{7,6},{8,9},{9,8},{10,11... | collective-permute-start | bytes 786440 | tf_op jit(solution)/shard_map/ppermute | solution.py:41
  92.5 15.8 %collective-permute-start.9 = (bf16[64,4096]{1,0:T(8,128)(2,1)}, bf16[64,4096]{1,0:T(8,128)(2,1)S(1)}, u32[]{:S(2)}, u32[]{:S(2)}) collective-permute-start(bf16[64,4096]{1,0:T(8,128)(2,1)} %copy-done.13), channel_id=1, source_target_pairs={{0,16},{1,17},{2,18},{3,19},{4,20},{5,21},{6,22},{7,23},{8,0},{9,1... | collective-permute-start | bytes 1572872 | tf_op jit(solution)/shard_map/ppermute | solution.py:41
  93.3 14.1 %collective-permute-start.8 = (bf16[64,4096]{1,0:T(8,128)(2,1)}, bf16[64,4096]{1,0:T(8,128)(2,1)S(1)}, u32[]{:S(2)}, u32[]{:S(2)}) collective-permute-start(bf16[64,4096]{1,0:T(8,128)(2,1)} %copy-done.13), channel_id=1, source_target_pairs={{0,4},{1,5},{2,6},{3,7},{4,0},{5,1},{6,2},{7,3},{8,12},{9,13},{10,... | collective-permute-start | bytes 1572872 | tf_op jit(solution)/shard_map/ppermute | solution.py:41
  93.9 36.2 %collective-permute-start.31 = (bf16[64,2048]{1,0:T(8,128)(2,1)}, bf16[64,2048]{1,0:T(8,128)(2,1)}, u32[]{:S(2)}, u32[]{:S(2)}) collective-permute-start(bf16[64,2048]{1,0:T(8,128)(2,1)} %broadcast_select_fusion.8), channel_id=1, source_target_pairs={{2,3},{3,2},{6,7},{7,6},{10,11},{11,10},{14,15},{15,14},{16,17},{1... | collective-permute-start | bytes 786440 | tf_op jit(solution)/shard_map/ppermute | solution.py:41
  96.4 6.9 %collective-permute-start.7 = (bf16[128,512]{1,0:T(8,128)(2,1)S(1)}, bf16[128,512]{1,0:T(8,128)(2,1)S(1)}, u32[]{:S(2)}, u32[]{:S(2)}) collective-permute-start(bf16[128,512]{1,0:T(8,128)(2,1)S(1)} %dynamic-slice_convert_fusion.6), channel_id=1, source_target_pairs={{0,2},{1,3},{2,0},{3,1},{4,6},{5,7},{6,4},{7,5},{8,10},{9,11},{10,... | collective-permute-start | bytes 393224 | tf_op jit(solution)/shard_map/ppermute | solution.py:41
  109.4 20.8 %copy-start.9 = (bf16[64,2048]{1,0:T(8,128)(2,1)S(1)}, bf16[64,2048]{1,0:T(8,128)(2,1)}, u32[]{:S(2)}) copy-start(bf16[64,2048]{1,0:T(8,128)(2,1)} %copy-done.8) | copy-start | bytes 786436
  121.8 42.3 %collective-permute-start.36 = (bf16[128,2048]{1,0:T(8,128)(2,1)S(1)}, bf16[128,2048]{1,0:T(8,128)(2,1)}, u32[]{:S(2)}, u32[]{:S(2)}) collective-permute-start(bf16[128,2048]{1,0:T(8,128)(2,1)S(1)} %dynamic-slice_select_fusion.1), channel_id=1, source_target_pairs={{0,1},{4,5},{9,8},{13,12},{18,19},{22,23},{27,26},{31,30}} | collective-permute-start | bytes 1572872 | tf_op jit(solution)/shard_map/ppermute | solution.py:41
  125.5 8.6 %collective-permute-start.33 = (bf16[64,2048]{1,0:T(8,128)(2,1)S(1)}, bf16[64,2048]{1,0:T(8,128)(2,1)S(1)}, u32[]{:S(2)}, u32[]{:S(2)}) collective-permute-start(bf16[64,2048]{1,0:T(8,128)(2,1)S(1)} %get-tuple-element.15), channel_id=1, source_target_pairs={{0,2},{4,6},{9,11},{13,15},{18,16},{22,20},{27,25},{31,29}} | collective-permute-start | bytes 786440 | tf_op jit(solution)/shard_map/ppermute | solution.py:41
  127.7 6.7 %collective-permute-start.34 = (bf16[64,2048]{1,0:T(8,128)(2,1)S(1)}, bf16[64,2048]{1,0:T(8,128)(2,1)S(1)}, u32[]{:S(2)}, u32[]{:S(2)}) collective-permute-start(bf16[64,2048]{1,0:T(8,128)(2,1)S(1)} %get-tuple-element.16), channel_id=1, source_target_pairs={{0,3},{4,7},{9,10},{13,14},{18,17},{22,21},{27,24},{31,28}} | collective-permute-start | bytes 786440 | tf_op jit(solution)/shard_map/ppermute | solution.py:41
  130.1 3.8 %collective-permute-start.10 = (bf16[128,1024]{1,0:T(8,128)(2,1)S(1)}, bf16[128,1024]{1,0:T(8,128)(2,1)S(1)}, u32[]{:S(2)}, u32[]{:S(2)}) collective-permute-start(bf16[128,1024]{1,0:T(8,128)(2,1)S(1)} %dynamic-slice_convert_fusion.1), channel_id=1, source_target_pairs={{0,1},{1,0},{2,3},{3,2},{4,5},{5,4},{6,7},{7,6},{8,9},{9,8},{10,11... | collective-permute-start | bytes 786440 | tf_op jit(solution)/shard_map/ppermute | solution.py:41
  131.3 14.6 %collective-permute-start.12 = (bf16[64,4096]{1,0:T(8,128)(2,1)}, bf16[64,4096]{1,0:T(8,128)(2,1)S(1)}, u32[]{:S(2)}, u32[]{:S(2)}) collective-permute-start(bf16[64,4096]{1,0:T(8,128)(2,1)} %copy-done.12), channel_id=1, source_target_pairs={{0,4},{1,5},{2,6},{3,7},{4,0},{5,1},{6,2},{7,3},{8,12},{9,13},{10,... | collective-permute-start | bytes 1572872 | tf_op jit(solution)/shard_map/ppermute | solution.py:41
  134.0 5.7 %collective-permute-start.11 = (bf16[128,512]{1,0:T(8,128)(2,1)S(1)}, bf16[128,512]{1,0:T(8,128)(2,1)S(1)}, u32[]{:S(2)}, u32[]{:S(2)}) collective-permute-start(bf16[128,512]{1,0:T(8,128)(2,1)S(1)} %dynamic-slice_convert_fusion.5), channel_id=1, source_target_pairs={{0,2},{1,3},{2,0},{3,1},{4,6},{5,7},{6,4},{7,5},{8,10},{9,11},{10,... | collective-permute-start | bytes 393224 | tf_op jit(solution)/shard_map/ppermute | solution.py:41
  134.4 5.5 %collective-permute-start.35 = (bf16[64,2048]{1,0:T(8,128)(2,1)S(1)}, bf16[64,2048]{1,0:T(8,128)(2,1)S(1)}, u32[]{:S(2)}, u32[]{:S(2)}) collective-permute-start(bf16[64,2048]{1,0:T(8,128)(2,1)S(1)} %broadcast_select_fusion.5), channel_id=1, source_target_pairs={{2,3},{3,2},{6,7},{7,6},{10,11},{11,10},{14,15},{15,14},{16,17},{1... | collective-permute-start | bytes 786440 | tf_op jit(solution)/shard_map/ppermute | solution.py:41
  156.9 1.4 collective-permute-start.13
  158.3 5.3 %collective-permute-start.14 = (bf16[64,512]{1,0:T(8,128)(2,1)S(1)}, bf16[64,512]{1,0:T(8,128)(2,1)S(1)}, u32[]{:S(2)}, u32[]{:S(2)}) collective-permute-start(bf16[64,512]{1,0:T(8,128)(2,1)S(1)} %dynamic-slice_convert_fusion.7), channel_id=1, source_target_pairs={{0,2},{1,3},{2,0},{3,1},{4,6},{5,7},{6,4},{7,5},{8,10},{9,11},{10,... | collective-permute-start | bytes 196616 | tf_op jit(solution)/shard_map/ppermute | solution.py:41
  158.5 14.2 %collective-permute-start.37 = (bf16[32,2048]{1,0:T(8,128)(2,1)S(1)}, bf16[32,2048]{1,0:T(8,128)(2,1)S(1)}, u32[]{:S(2)}, u32[]{:S(2)}) collective-permute-start(bf16[32,2048]{1,0:T(8,128)(2,1)S(1)} %get-tuple-element.33), channel_id=1, source_target_pairs={{0,2},{4,6},{9,11},{13,15},{18,16},{22,20},{27,25},{31,29}} | collective-permute-start | bytes 393224 | tf_op jit(solution)/shard_map/ppermute | solution.py:41
  162.4 14.2 %collective-permute-start.38 = (bf16[32,2048]{1,0:T(8,128)(2,1)S(1)}, bf16[32,2048]{1,0:T(8,128)(2,1)S(1)}, u32[]{:S(2)}, u32[]{:S(2)}) collective-permute-start(bf16[32,2048]{1,0:T(8,128)(2,1)S(1)} %get-tuple-element.34), channel_id=1, source_target_pairs={{0,3},{4,7},{9,10},{13,14},{18,17},{22,21},{27,24},{31,28}} | collective-permute-start | bytes 393224 | tf_op jit(solution)/shard_map/ppermute | solution.py:41
  163.9 4.0 %collective-permute-start.17 = (f32[8,64]{1,0:T(8,128)S(1)}, f32[8,64]{1,0:T(8,128)S(1)}, u32[]{:S(2)}, u32[]{:S(2)}) collective-permute-start(f32[8,64]{1,0:T(8,128)S(1)} %multiply_reduce_fusion.5), channel_id=1, source_target_pairs={{0,3},{1,2},{2,1},{3,0},{4,7},{5,6},{6,5},{7,4},{8,11},{9,10},{10,... | collective-permute-start | bytes 6152 | tf_op jit(solution)/shard_map/ppermute | solution.py:41
  164.0 4.0 %collective-permute-start.16 = (f32[8,64]{1,0:T(8,128)S(1)}, f32[8,64]{1,0:T(8,128)S(1)}, u32[]{:S(2)}, u32[]{:S(2)}) collective-permute-start(f32[8,64]{1,0:T(8,128)S(1)} %multiply_reduce_fusion.5), channel_id=1, source_target_pairs={{0,2},{1,3},{2,0},{3,1},{4,6},{5,7},{6,4},{7,5},{8,10},{9,11},{10,... | collective-permute-start | bytes 6152 | tf_op jit(solution)/shard_map/ppermute | solution.py:41
  164.1 20.2 %copy-start.14 = (bf16[128,2048]{1,0:T(8,128)(2,1)S(1)}, bf16[128,2048]{1,0:T(8,128)(2,1)}, u32[]{:S(2)}) copy-start(bf16[128,2048]{1,0:T(8,128)(2,1)} %maximum_select_fusion.1) | copy-start | bytes 1572868
  164.1 3.9 %collective-permute-start.15 = (f32[8,64]{1,0:T(8,128)S(1)}, f32[8,64]{1,0:T(8,128)S(1)}, u32[]{:S(2)}, u32[]{:S(2)}) collective-permute-start(f32[8,64]{1,0:T(8,128)S(1)} %multiply_reduce_fusion.5), channel_id=1, source_target_pairs={{0,1},{1,0},{2,3},{3,2},{4,5},{5,4},{6,7},{7,6},{8,9},{9,8},{10,11... | collective-permute-start | bytes 6152 | tf_op jit(solution)/shard_map/ppermute | solution.py:41
  168.0 8.6 %collective-permute-start.24 = (f32[8,64]{1,0:T(8,128)S(1)}, f32[8,64]{1,0:T(8,128)S(1)}, u32[]{:S(2)}, u32[]{:S(2)}) collective-permute-start(f32[8,64]{1,0:T(8,128)S(1)} %add_add_fusion.1), channel_id=1, source_target_pairs={{0,28},{1,29},{2,30},{3,31},{4,24},{5,25},{6,26},{7,27},{8,20},{9,... | collective-permute-start | bytes 6152 | tf_op jit(solution)/shard_map/ppermute | solution.py:41
  168.4 10.1 %collective-permute-start.23 = (f32[8,64]{1,0:T(8,128)S(1)}, f32[8,64]{1,0:T(8,128)S(1)}, u32[]{:S(2)}, u32[]{:S(2)}) collective-permute-start(f32[8,64]{1,0:T(8,128)S(1)} %add_add_fusion.1), channel_id=1, source_target_pairs={{0,24},{1,25},{2,26},{3,27},{4,28},{5,29},{6,30},{7,31},{8,16},{9,... | collective-permute-start | bytes 6152 | tf_op jit(solution)/shard_map/ppermute | solution.py:41
  172.6 7.5 %collective-permute-start.22 = (f32[8,64]{1,0:T(8,128)S(1)}, f32[8,64]{1,0:T(8,128)S(1)}, u32[]{:S(2)}, u32[]{:S(2)}) collective-permute-start(f32[8,64]{1,0:T(8,128)S(1)} %add_add_fusion.1), channel_id=1, source_target_pairs={{0,20},{1,21},{2,22},{3,23},{4,16},{5,17},{6,18},{7,19},{8,28},{9,... | collective-permute-start | bytes 6152 | tf_op jit(solution)/shard_map/ppermute | solution.py:41
  172.6 8.8 %collective-permute-start.21 = (f32[8,64]{1,0:T(8,128)S(1)}, f32[8,64]{1,0:T(8,128)S(1)}, u32[]{:S(2)}, u32[]{:S(2)}) collective-permute-start(f32[8,64]{1,0:T(8,128)S(1)} %add_add_fusion.1), channel_id=1, source_target_pairs={{0,16},{1,17},{2,18},{3,19},{4,20},{5,21},{6,22},{7,23},{8,24},{9,... | collective-permute-start | bytes 6152 | tf_op jit(solution)/shard_map/ppermute | solution.py:41
  176.6 5.8 %collective-permute-start.20 = (f32[8,64]{1,0:T(8,128)S(1)}, f32[8,64]{1,0:T(8,128)S(1)}, u32[]{:S(2)}, u32[]{:S(2)}) collective-permute-start(f32[8,64]{1,0:T(8,128)S(1)} %add_add_fusion.1), channel_id=1, source_target_pairs={{0,12},{1,13},{2,14},{3,15},{4,8},{5,9},{6,10},{7,11},{8,4},{9,5},... | collective-permute-start | bytes 6152 | tf_op jit(solution)/shard_map/ppermute | solution.py:41
  176.6 5.8 %collective-permute-start.19 = (f32[8,64]{1,0:T(8,128)S(1)}, f32[8,64]{1,0:T(8,128)S(1)}, u32[]{:S(2)}, u32[]{:S(2)}) collective-permute-start(f32[8,64]{1,0:T(8,128)S(1)} %add_add_fusion.1), channel_id=1, source_target_pairs={{0,8},{1,9},{2,10},{3,11},{4,12},{5,13},{6,14},{7,15},{8,0},{9,1},... | collective-permute-start | bytes 6152 | tf_op jit(solution)/shard_map/ppermute | solution.py:41
  178.5 3.9 %collective-permute-start.18 = (f32[8,64]{1,0:T(8,128)S(1)}, f32[8,64]{1,0:T(8,128)S(1)}, u32[]{:S(2)}, u32[]{:S(2)}) collective-permute-start(f32[8,64]{1,0:T(8,128)S(1)} %add_add_fusion.1), channel_id=1, source_target_pairs={{0,4},{1,5},{2,6},{3,7},{4,0},{5,1},{6,2},{7,3},{8,12},{9,13},{10,... | collective-permute-start | bytes 6152 | tf_op jit(solution)/shard_map/ppermute | solution.py:41
  180.1 4.0 %collective-permute-start.40 = (bf16[64,2048]{1,0:T(8,128)(2,1)S(1)}, bf16[64,2048]{1,0:T(8,128)(2,1)S(1)}, u32[]{:S(2)}, u32[]{:S(2)}) collective-permute-start(bf16[64,2048]{1,0:T(8,128)(2,1)S(1)} %dynamic-slice_select_fusion.3), channel_id=1, source_target_pairs={{0,1},{4,5},{9,8},{13,12},{18,19},{22,23},{27,26},{31,30}} | collective-permute-start | bytes 786440 | tf_op jit(solution)/shard_map/ppermute | solution.py:41
  181.4 2.7 %collective-permute-start.39 = (bf16[32,2048]{1,0:T(8,128)(2,1)S(1)}, bf16[32,2048]{1,0:T(8,128)(2,1)S(1)}, u32[]{:S(2)}, u32[]{:S(2)}) collective-permute-start(bf16[32,2048]{1,0:T(8,128)(2,1)S(1)} %broadcast_select_fusion.11), channel_id=1, source_target_pairs={{2,3},{3,2},{6,7},{7,6},{10,11},{11,10},{14,15},{15,14},{16,17},{1... | collective-permute-start | bytes 393224 | tf_op jit(solution)/shard_map/ppermute | solution.py:41
  (8 other events, 54.4 us)

commit v2 on v0

v2 whole, which is shorter than its diff:
```python
import functools

import jax
import jax.numpy as jnp
from jax import lax
from jax.experimental import pallas as pl
from jax.experimental.pallas import tpu as pltpu
from jax.sharding import PartitionSpec as P

BOTH = ("row", "feat")
HI = 4
MIB = 1 << 20
LANES = 128


def ring_order(count):
    return list(range(0, count, 2)) + list(range(1, count, 2))[::-1]


def ring_next(count):
    order = ring_order(count)
    return {order[i]: order[(i + 1) % count] for i in range(count)}


def call(kernel, name, grid, in_specs, out_specs, out_shape, scratch, vmem=24):
    return pl.pallas_call(
        kernel,
        grid_spec=pltpu.PrefetchScalarGridSpec(
            num_scalar_prefetch=1,
            grid=grid,
            in_specs=in_specs,
            out_specs=out_specs,
            scratch_shapes=scratch,
        ),
        out_shape=out_shape,
        compiler_params=pltpu.CompilerParams(
            dimension_semantics=("arbitrary",) * len(grid), vmem_limit_bytes=vmem * MIB
        ),
        cost_estimate=pl.CostEstimate(flops=1000, bytes_accessed=1000, transcendentals=0),
        name=name,
    )


def whole(shape):
    return pl.BlockSpec(shape, lambda i, s: (0,) * len(shape))


def whiten_kernel(steps, fold, starts_ref, f_ref, *refs):
    pieces, (keep_ref, away_ref, x_ref, sum_ref) = refs[:-4], refs[-4:]
    step = pl.program_id(0)
    place = 0
    for piece in pieces:
        x_ref[pl.ds(place, piece.shape[0]), :] = piece[...]
        place += piece.shape[0]
    part = jnp.dot(f_ref[...], x_ref[...].T, preferred_element_type=jnp.float32)

    @pl.when(step == 0)
    def _():
        sum_ref[...] = part

    @pl.when(step > 0)
    def _():
        sum_ref[...] += part

    @pl.when(step == steps - 1)
    def _():
        blocks = starts_ref.shape[0]
        size = sum_ref.shape[0] // blocks
        short = size // fold
        for i in range(blocks):
            start = pl.multiple_of(starts_ref[i], size)
            block = jnp.concatenate(
                [sum_ref[pl.ds(start + j * short, short), :] for j in range(fold)], axis=1
            )
            if i < blocks // 2:
                keep_ref[pl.ds(i * short, short), :] = block
            else:
                away_ref[pl.ds((i - blocks // 2) * short, short), :] = block.astype(jnp.bfloat16)


def whiten(starts, inv_factor, pieces):
    row_block, feat_block = inv_factor.shape
    rows = sum(p.shape[0] for p in pieces)
    fold = max(1, LANES // rows)
    width = min(512, feat_block)
    steps = feat_block // width
    out = (row_block // 2 // fold, rows * fold)
    return call(
        functools.partial(whiten_kernel, steps, fold),
        "whiten",
        (steps,),
        [pl.BlockSpec((row_block, width), lambda i, s: (0, i))]
        + [pl.BlockSpec((p.shape[0], width), lambda i, s: (0, i)) for p in pieces],
        [whole(out)] * 2,
        [jax.ShapeDtypeStruct(out, jnp.float32), jax.ShapeDtypeStruct(out, jnp.bfloat16)],
        [pltpu.VMEM((rows, width), jnp.bfloat16), pltpu.VMEM((row_block, rows), jnp.float32)],
        vmem=50,
    )(starts, inv_factor, *pieces)


def pick_kernel(_, *refs):
    place = 0
    for piece in refs[:-1]:
        refs[-1][pl.ds(place, piece.shape[0]), :] = piece[...]
        place += piece.shape[0]


def pick(block, pieces, width):
    rows = sum(p.shape[0] for p in pieces)
    return call(
        pick_kernel,
        "pick",
        (1,),
        [pl.BlockSpec((p.shape[0], width), lambda i, s: (0, s[0])) for p in pieces],
        whole((rows, width)),
        jax.ShapeDtypeStruct((rows, width), jnp.bfloat16),
        [],
    )(block, *pieces)


def pack_kernel(count, flags_ref, *refs):
    out_ref = refs[-1]

    def copy(sources):
        place = 0
        for source in sources:
            out_ref[pl.ds(place, source.shape[0]), :] = source[...]
            place += source.shape[0]

    @pl.when(flags_ref[0] == 1)
    def _():
        copy(refs[:count])

    @pl.when(flags_ref[0] == 0)
    def _():
        copy(refs[count:-1])


def pack(flag, own, got):
    rows, width = sum(x.shape[0] for x in own), own[0].shape[1]
    return call(
        functools.partial(pack_kernel, len(own)),
        "pack",
        (1,),
        [whole(x.shape) for x in own + got],
        whole((rows, width)),
        jax.ShapeDtypeStruct((rows, width), jnp.bfloat16),
        [],
    )(flag, *own, *got)


def join_kernel(flags_ref, own_ref, other_ref, out_ref):
    wide = min(256, own_ref.shape[1])

    def turn(source):
        for c in range(source.shape[1] // wide):
            out_ref[pl.ds(c * wide, wide), :] = source[:, c * wide:(c + 1) * wide].T

    @pl.when(flags_ref[0] == 1)
    def _():
        turn(own_ref)

    @pl.when(flags_ref[0] == 0)
    def _():
        turn(other_ref)


def join(flag, own, other):
    rows, width = own.shape
    return call(
        join_kernel,
        "join",
        (1,),
        [whole(own.shape)] * 2,
        whole((width, rows)),
        jax.ShapeDtypeStruct((width, rows), jnp.bfloat16),
        [],
    )(flag, own, other)


def square_kernel(sizes, places_ref, *refs):
    out_ref = refs[-1]
    count = out_ref.shape[1]
    slot = 0
    for g, size in enumerate(sizes):
        value = refs[2 * g][...] + refs[2 * g + 1][...].astype(jnp.float32)
        line = jnp.sum(value * value, axis=0, keepdims=True)
        for i in range(size):
            total = line[:, i * count:(i + 1) * count]
            for j in range(1, line.shape[1] // (size * count)):
                total += line[:, (j * size + i) * count:(j * size + i + 1) * count]
            out_ref[pl.ds(places_ref[slot], 1), :] = total
            slot += 1


def squares(places, pairs, sizes, count):
    shapes = [x.shape for pair in pairs for x in pair]
    out = (sum(sizes), count)
    return call(
        functools.partial(square_kernel, sizes),
        "squares",
        (1,),
        [whole(shape) for shape in shapes],
        whole(out),
        jax.ShapeDtypeStruct(out, jnp.float32),
        [],
    )(places, *[x for pair in pairs for x in pair])


def weight_kernel(strata_n, features, row_ref, raw_ref, w_ref, strata_ref, wide_ref, new_ref, lev_ref, all_ref):
    raw, weights, strata = raw_ref[...], w_ref[...], strata_ref[...]
    products = weights * raw
    ratio = jnp.zeros_like(raw)
    for s in range(strata_n):
        inside = strata == float(s)
        mass = jnp.sum(jnp.where(inside, weights, 0.0), keepdims=True)
        product = jnp.sum(jnp.where(inside, products, 0.0), keepdims=True)
        ratio = jnp.where(inside, mass / product, ratio)
    new = products * ratio
    all_ref[...] = new
    new_ref[...] = all_ref[pl.ds(row_ref[0], 1), :]
    lev_ref[...] = raw_ref[pl.ds(row_ref[0], 1), :] / features
    step = new - weights
    groups, count = step.shape
    for g in range(groups):
        wide_ref[pl.ds(g * count, count), :] = jnp.broadcast_to(step[g:g + 1, :], (LANES, count)).T


def weight_step(row, raw, weights, strata, features):
    groups, count = raw.shape
    return call(
        functools.partial(weight_kernel, 2 * groups, features),
        "weight_step",
        (1,),
        [whole(raw.shape)] * 3,
        [whole((groups * count, LANES)), whole((1, count)), whole((1, count))],
        [
            jax.ShapeDtypeStruct((groups * count, LANES), jnp.float32),
            jax.ShapeDtypeStruct((1, count), jnp.float32),
            jax.ShapeDtypeStruct((1, count), jnp.float32),
        ],
        [pltpu.VMEM((groups, count), jnp.float32)],
    )(row, raw, weights, strata)


def information_kernel(starts_ref, d_ref, col_ref, *refs):
    pieces, (out_ref, s_ref) = refs[:-2], refs[-2:]
    place = 0
    for i, piece in enumerate(pieces):
        size = piece.shape[0]
        scale = d_ref[pl.ds(pl.multiple_of(starts_ref[i], size), size), :]
        for c in range(piece.shape[1] // LANES):
            value = piece[:, c * LANES:(c + 1) * LANES].astype(jnp.float32)
            s_ref[pl.ds(place, size), c * LANES:(c + 1) * LANES] = (scale * value).astype(jnp.bfloat16)
        place += size
    out_ref[...] = jnp.dot(col_ref[...], s_ref[...], preferred_element_type=jnp.float32)


def increment(starts, step_wide, column_t, pieces):
    row_block, rows = column_t.shape
    feat_block = pieces[0].shape[1]
    width = min(512, feat_block)
    return call(
        information_kernel,
        "increment",
        (feat_block // width,),
        [whole(step_wide.shape), whole(column_t.shape)]
        + [pl.BlockSpec((p.shape[0], width), lambda i, s: (0, i)) for p in pieces],
        pl.BlockSpec((row_block, width), lambda i, s: (0, i)),
        jax.ShapeDtypeStruct((row_block, feat_block), jnp.float32),
        [pltpu.VMEM((rows, width), jnp.bfloat16)],
        vmem=44,
    )(starts, step_wide, column_t, *pieces)


def make(mesh):
    rows_n, feats_n = mesh.shape["row"], mesh.shape["feat"]
    hi_n = HI
    lo_n = rows_n // hi_n
    per_feat = rows_n // feats_n
    everyone = [(r, f) for r in range(rows_n) for f in range(feats_n)]

    def perm(target, keep=lambda r, f: True):
        out = []
        for r, f in everyone:
            if keep(r, f):
                r2, f2 = target(r, f)
                out.append((r * feats_n + f, r2 * feats_n + f2))
        return out

    def send(x, pairs):
        return lax.ppermute(x, BOTH, pairs)

    def swap(x, r_bit, f_bit):
        return send(x, perm(lambda r, f: (r ^ r_bit, f ^ f_bit)))

    fence = lax.optimization_barrier
    hi_next, lo_next = ring_next(hi_n), ring_next(lo_n)
    hi_pairs = perm(lambda r, f: (hi_next[r // lo_n] * lo_n + r % lo_n, f))
    lo_pairs = perm(lambda r, f: (r // lo_n * lo_n + lo_next[r % lo_n], f))
    hi_order, lo_order = ring_order(hi_n), ring_order(lo_n)

    def source(r, k, s):
        h, l = r // lo_n, r % lo_n
        h2 = hi_order[(hi_order.index(h) - k) % hi_n]
        l2 = lo_order[(lo_order.index(l) - s) % lo_n]
        return h2 * lo_n + l2

    feat_bits = [1 << b for b in range(feats_n.bit_length() - 1)]
    far_bits = feat_bits[1:]
    row_bits = [1 << b for b in range(rows_n.bit_length() - 1)]
    relative = [0]
    for bit in reversed(feat_bits):
        relative = relative + [j + bit for j in relative]

    groups = [[(0, s) for s in range(lo_n)] + [(1, 0)]]
    for k in range(1, hi_n):
        groups.append([(k, s) for s in range(1, lo_n)] + ([(k + 1, 0)] if k + 1 < hi_n else []))
    slots = [slot for group in groups for slot in group]

    def per_device(candidates, inv_factor, weights, strata):
        rows_dev, feat_block = candidates.shape
        row_block = inv_factor.shape[0]
        features = feat_block * feats_n
        half = rows_dev // 2
        row, feat = lax.axis_index("row"), lax.axis_index("feat")
        starts = (jnp.asarray(relative, jnp.int32) ^ feat) * (row_block // feats_n)
        table = jnp.asarray([[source(r, *slot) for slot in slots] for r in range(rows_n)], jnp.int32)
        places = table[row]
        block = (row % per_feat)[None]
        apart = feat ^ (row // per_feat)

        def pieces_of(chosen):
            return [p for slot in chosen for p in chunks[slot]]

        def column_far(mine):
            for bit in reversed(far_bits):
                got = send(mine, perm(
                    lambda r, f: (r, f ^ bit),
                    lambda r, f: (f ^ (r // per_feat)) % (2 * bit) == 0,
                ))
                if len(far_bits) > 1:
                    mine = got = jnp.where(apart % (2 * bit) == 0, mine, got)
            return got

        def halve(part, got):
            part = part + got.astype(jnp.float32)
            left = part.shape[0] // 2
            return part[:left], part[left:].astype(jnp.bfloat16)

        chunks = {(0, 0): [candidates]}
        small = jnp.stack([weights, strata.astype(jnp.float32)])
        small_all = jnp.where((jnp.arange(rows_n) == row)[:, None, None], small[None], 0.0)
        small_bits = list(row_bits)

        columns, far_columns, near, far = [], [], {}, {}
        for k in range(hi_n + 1):
            fresh, out = [], {}
            if k < hi_n - 1:
                fresh.append((k + 1, 0))
                chunks[k + 1, 0] = [send(chunks[k, 0][0], hi_pairs)]
            if k < hi_n:
                held = chunks[k, 0][0]
                for s in range(1, lo_n):
                    fresh.append((k, s))
                    if k < hi_n - 1:
                        held = send(held, lo_pairs)
                        chunks[k, s] = [held]
                    else:
                        held = send(held[:half], lo_pairs)
                        chunks[k, s] = [held, send(chunks[k - 1, s][0][half:], hi_pairs)]
            out["fresh"] = [chunks[slot] for slot in fresh]
            if small_bits:
                bit = small_bits.pop(0)
                out["small"] = small_all + swap(small_all, bit, 0)
            if k > 0:
                group = pieces_of(groups[k - 1])
                mine = pick(block, group, row_block)
                columns.append(mine)
                out["far_column"] = column_far(mine)
                out["white"] = whiten(starts, inv_factor, group)
            if k > 1:
                keep, away = near[k - 2]
                out["near"] = halve(keep, swap(away, 0, 1))
            if k > 2:
                keep, away = far[k - 3]
                for bit in far_bits[:-1]:
                    keep, away = halve(keep, swap(away, 0, bit))
                out["far"] = (keep, swap(away, 0, far_bits[-1]))
            out = fence(out)
            for slot, value in zip(fresh, out["fresh"]):
                chunks[slot] = value
            small_all = out.get("small", small_all)
            if k > 0:
                far_columns.append(out["far_column"])
                near[k - 1] = out["white"]
            if k > 1:
                far[k - 2] = out["near"]
            if k > 2:
                far[k - 3] = out["far"]
        while small_bits:
            small_all = small_all + swap(small_all, small_bits.pop(0), 0)

        def last_far(g):
            keep, away = far[g]
            for bit in far_bits[:-1]:
                keep, away = halve(keep, swap(away, 0, bit))
            return keep, swap(away, 0, far_bits[-1])

        keep, away = near[hi_n - 1]
        far[hi_n - 1] = fence(halve(keep, swap(away, 0, 1)))
        packed = pack((apart == 0).astype(jnp.int32)[None], columns, far_columns)
        far[hi_n - 2], far[hi_n - 1], packed = fence((last_far(hi_n - 2), last_far(hi_n - 1), packed))
        total = squares(places, [far[g] for g in range(hi_n)], [len(g) for g in groups], rows_dev)

        total = total + swap(total, 0, 1)
        bits = [(0, bit) for bit in far_bits] + [(bit, 0) for bit in row_bits]
        beside = swap(packed, 0, 1)
        column_t = None
        while bits:
            first, rest = bits[0], bits[1:2]
            bits = bits[2:]
            if rest:
                second = rest[0]
                both = (first[0] ^ second[0], first[1] ^ second[1])
                total = (total + swap(total, *first)) + (swap(total, *second) + swap(total, *both))
            else:
                total = total + swap(total, *first)
            if beside is not None:
                total, beside = fence((total, beside))
                column_t = join((apart % 2 == 0).astype(jnp.int32)[None], packed, beside)
                beside = None
            elif column_t is not None and bits:
                total, column_t = fence((total, column_t))
        total, column_t = fence((total, column_t))

        step_wide, new_weight, leverage = weight_step(
            row[None], total, small_all[:, 0], small_all[:, 1], features
        )
        piece_starts = []
        for i, slot in enumerate(slots):
            place = places[i] * rows_dev
            for piece in chunks[slot]:
                piece_starts.append(place)
                place = place + piece.shape[0]
        information = increment(jnp.stack(piece_starts), step_wide, column_t, pieces_of(slots))
        return (new_weight.reshape(rows_dev), leverage.reshape(rows_dev), information)

    return per_device


def solution(mesh):
    in_specs = (P("row", "feat"), P("row", "feat"), P("row"), P("row"))
    out_specs = (P("row"), P("row"), P("row", "feat"))
    return jax.shard_map(
        make(mesh), mesh=mesh, in_specs=in_specs, out_specs=out_specs, check_vma=False
    )
```

time: 237 us -> 157 us (0.66)
  waiting for transfers between devices: 115 us -> 20.5 us
  Pallas kernels: 0 us -> 68.3 us
  blocking collectives: 63.5 us -> 0 us
  starting transfers between devices: 0.12 us -> 38.7 us
  matrix products: 34.1 us -> 0 us
  local copies, waits for them, and re-layouts: 2.52 us -> 19.9 us
  between operations: 15.1 us -> 6.31 us
  other arithmetic: 6 us -> 1.72 us
    all_gather x1 -> x0, waiting for transfers between devices: 78.3 us -> none  [per_device(): gathered = lax.all_gather(candidates, 'row', axis=0, tiled=True)]
    pallas_call x0 -> x13, Pallas kernels: none -> 68.3 us  [the longest x4 46.6 us: whiten(): call(functools.partial(whiten_kernel, steps, fold), 'whiten', (steps,), [...]
    unnamed x2 -> x0, blocking collectives: 40.1 us -> none
    ppermute x0 -> x31, starting transfers between devices: none -> 38.7 us  [send(): return lax.ppermute(x, BOTH, pairs)]
    reduce_scatter x1 -> x0, waiting for transfers between devices: 36.2 us -> none  [per_device(): summed = lax.psum_scatter(shaped, 'feat', scatter_dimension=1, tiled=True)]
    dot_general x5 -> x0, matrix products: 34.1 us -> none  [the longest x1 18.6 us: per_device(): lax.dot_general(column_block, scaled_all, (((0,), (0,)), ((), ())), prefe...]
    ppermute x0 -> x31, waiting for transfers between devices: none -> 20.5 us  [send(): return lax.ppermute(x, BOTH, pairs)]
    psum x1 -> x0, blocking collectives: 17.5 us -> none  [per_device(): stratum_product, stratum_mass = lax.psum((local_product, local_mass), 'row')]
  transfers between devices with their start and end apart: 3 -> 31, of which waited for: 2 -> 7; matrix products, arithmetic and copies ran while one was open for 4% -> 4% of each run, Pallas kernels for 0% -> 33%
where the time goes in v2:
time: 157 us; the launch traced here: 155 us
  Pallas kernels  68.3 us (44%)
  starting transfers between devices  38.7 us (25%)
  waiting for transfers between devices  20.5 us (13%)
  local copies, waits for them, and re-layouts  19.9 us (13%)
  between operations  6.31 us (4%)
  other arithmetic  1.72 us (1%)
    pallas_call x4, Pallas kernels, whiten(): call(functools.partial(whiten_kernel, steps, fold), 'whiten', (steps,), [...  46.6 us
    ppermute x31, starting transfers between devices, send(): return lax.ppermute(x, BOTH, pairs)  38.7 us
    ppermute x31, waiting for transfers between devices, send(): return lax.ppermute(x, BOTH, pairs)  20.5 us
    pallas_call x1, Pallas kernels, increment(): call(information_kernel, 'increment', (feat_block // width,), [whole(step...  15.5 us
    unnamed x70, local copies, waits for them, and re-layouts  14.8 us
    slice x8, local copies, waits for them, and re-layouts, halve(): return (part[:left], part[left:].astype(jnp.bfloat16))  3.64 us
  transfers between devices with their start and end apart: 31, of which 7 were waited for; matrix products, arithmetic and copies ran while one was open for 4% of the time, Pallas kernels for 33%

profile of v2, /device:TPU:0, one launch (start us, length us, event | category | flops | bytes accessed | tf_op | source)
XLA Modules:
  0.0 155.5 jit_solution(10070980773342953981)
XLA Ops:
  0.6 3.0 %collective-permute-start.1 = (bf16[64,4096]{1,0:T(8,128)(2,1)}, bf16[64,4096]{1,0:T(8,128)(2,1)S(1)}, u32[]{:S(2)}, u32[]{:S(2)}) collective-permute-start(bf16[64,4096]{1,0:T(8,128)(2,1)} %refs_0_.5), channel_id=1, source_target_pairs={{0,4},{1,5},{2,6},{3,7},{4,0},{5,1},{6,2},{7,3},{8,12},{9,13},{10,... | collective-permute-start | bytes 1572872 | tf_op jit(solution)/shard_map/ppermute | solution.py:292
  3.6 2.6 %collective-permute-start = (bf16[64,4096]{1,0:T(8,128)(2,1)}, bf16[64,4096]{1,0:T(8,128)(2,1)S(1)}, u32[]{:S(2)}, u32[]{:S(2)}) collective-permute-start(bf16[64,4096]{1,0:T(8,128)(2,1)} %refs_0_.5), channel_id=1, source_target_pairs={{0,16},{1,17},{2,18},{3,19},{4,20},{5,21},{6,22},{7,23},{8,0},{9,1... | collective-permute-start | bytes 1572872 | tf_op jit(solution)/shard_map/ppermute | solution.py:292
  8.2 7.8 %collective-permute-done.2 = f32[8,2,64]{2,0,1:T(8,128)S(1)} collective-permute-done((f32[8,2,64]{2,0,1:T(8,128)S(1)}, f32[8,2,64]{2,0,1:T(8,128)S(1)}, u32[]{:S(2)}, u32[]{:S(2)}) %collective-permute-start.2) | collective-permute-done | bytes 4128 | tf_op jit(solution)/shard_map/ppermute | solution.py:292
  16.0 1.4 collective-permute-done.refs_2_
  17.5 1.2 copy-done.4
  18.8 4.5 %collective-permute-start.3 = (bf16[192,2048]{1,0:T(8,128)(2,1)S(1)}, bf16[192,2048]{1,0:T(8,128)(2,1)}, u32[]{:S(2)}, u32[]{:S(2)}) collective-permute-start(bf16[192,2048]{1,0:T(8,128)(2,1)S(1)} %pick.4.refs_0_), channel_id=1, source_target_pairs={{0,2},{4,6},{9,11},{13,15},{18,16},{22,20},{27,25},{31,29}} | collective-permute-start | bytes 2359304 | tf_op jit(solution)/shard_map/ppermute | solution.py:292
  24.1 1.7 %collective-permute-start.6 = (f32[8,2,64]{2,0,1:T(8,128)S(1)}, f32[8,2,64]{2,0,1:T(8,128)S(1)}, u32[]{:S(2)}, u32[]{:S(2)}) collective-permute-start(f32[8,2,64]{2,0,1:T(8,128)S(1)} %fusion), channel_id=1, source_target_pairs={{0,8},{1,9},{2,10},{3,11},{4,12},{5,13},{6,14},{7,15},{8,0},{9,1},... | collective-permute-start | bytes 12296 | tf_op jit(solution)/shard_map/ppermute | solution.py:292
  25.8 12.1 %whiten.4 = (f32[1024,192]{1,0:T(8,128)S(1)}, bf16[1024,192]{1,0:T(8,128)(2,1)S(1)}) custom-call(s32[4]{0:T(128)S(1)} %xor_multiply_fusion.starts_ref, bf16[2048,4096]{1,0:T(8,128)(2,1)} %f_ref.7, bf16[64,4096]{1,0:T(8,128)(2,1)S(1)} %copy-done.5, bf16[64,4096]{1,0:T(8,128)(2,1)S(1)} %collective-permute-done.1.refs_1_, ...), custom_call_target="tpu_custom_call" | custom-call | flops 1000 | bytes 1000 | tf_op jit(solution)/shard_map/whiten/pallas_call | solution.py:88
  38.1 3.7 %collective-permute-start.7 = (bf16[128,2048]{1,0:T(8,128)(2,1)S(1)}, bf16[128,2048]{1,0:T(8,128)(2,1)S(1)}, u32[]{:S(2)}, u32[]{:S(2)}) collective-permute-start(bf16[128,2048]{1,0:T(8,128)(2,1)S(1)} %pick.5.refs_1_), channel_id=1, source_target_pairs={{0,2},{4,6},{9,11},{13,15},{18,16},{22,20},{27,25},{31,29}} | collective-permute-start | bytes 1572872 | tf_op jit(solution)/shard_map/ppermute | solution.py:292
  41.9 1.6 %collective-permute-start.9 = (bf16[64,4096]{1,0:T(8,128)(2,1)S(1)}, bf16[64,4096]{1,0:T(8,128)(2,1)S(1)}, u32[]{:S(2)}, u32[]{:S(2)}) collective-permute-start(bf16[64,4096]{1,0:T(8,128)(2,1)S(1)} %collective-permute-done.4.refs_1_.refs_4_), channel_id=1, source_target_pairs={{0,4},{1,5},{2,6},{3,7},{4,0},{5,1},{6,2},{7,3},{8,12},{9,13},{10,... | collective-permute-start | bytes 1572872 | tf_op jit(solution)/shard_map/ppermute | solution.py:292
  43.4 11.5 %whiten.5 = (f32[1024,128]{1,0:T(8,128)S(1)}, bf16[1024,128]{1,0:T(8,128)(2,1)S(1)}) custom-call(s32[4]{0:T(128)S(1)} %xor_multiply_fusion.starts_ref, bf16[2048,4096]{1,0:T(8,128)(2,1)} %f_ref.7, bf16[64,4096]{1,0:T(8,128)(2,1)S(1)} %collective-permute-done.5.refs_0_.refs_3_, bf16[64,4096]{1,0:T(8,128)(2,1)S(1)} %collective-permute-done.4.refs_1_.refs_4_), custom_call_target="tpu_custom_call" | custom-call | flops 1000 | bytes 1000 | tf_op jit(solution)/shard_map/whiten/pallas_call | solution.py:88
  55.1 0.9 slice.92.refs_0_
  56.0 0.8 copy-done.24
  56.8 0.7 collective-permute-done.8.refs_1_.refs_6_
  57.6 2.6 %collective-permute-start.13 = (bf16[128,2048]{1,0:T(8,128)(2,1)S(1)}, bf16[128,2048]{1,0:T(8,128)(2,1)S(1)}, u32[]{:S(2)}, u32[]{:S(2)}) collective-permute-start(bf16[128,2048]{1,0:T(8,128)(2,1)S(1)} %pick.6.refs_2_), channel_id=1, source_target_pairs={{0,2},{4,6},{9,11},{13,15},{18,16},{22,20},{27,25},{31,29}} | collective-permute-start | bytes 1572872 | tf_op jit(solution)/shard_map/ppermute | solution.py:292
  60.9 0.9 collective-permute-start.15
  61.8 11.5 %whiten.6 = (f32[1024,128]{1,0:T(8,128)S(1)}, bf16[1024,128]{1,0:T(8,128)(2,1)S(1)}) custom-call(s32[4]{0:T(128)S(1)} %xor_multiply_fusion.starts_ref, bf16[2048,4096]{1,0:T(8,128)(2,1)} %f_ref.7, bf16[64,4096]{1,0:T(8,128)(2,1)S(1)} %collective-permute-done.9.refs_0_.refs_5_, bf16[64,4096]{1,0:T(8,128)(2,1)S(1)} %collective-permute-done.8.refs_1_.refs_6_), custom_call_target="tpu_custom_call" | custom-call | flops 1000 | bytes 1000 | tf_op jit(solution)/shard_map/whiten/pallas_call | solution.py:88
  73.3 2.7 %collective-permute-start.12 = (bf16[512,192]{1,0:T(8,128)(2,1)S(1)}, bf16[512,192]{1,0:T(8,128)(2,1)S(1)}, u32[]{:S(2)}, u32[]{:S(2)}) collective-permute-start(bf16[512,192]{1,0:T(8,128)(2,1)S(1)} %slice.106), channel_id=1, source_target_pairs={{0,2},{1,3},{2,0},{3,1},{4,6},{5,7},{6,4},{7,5},{8,10},{9,11},{10,... | collective-permute-start | bytes 589832 | tf_op jit(solution)/shard_map/ppermute | solution.py:292
  76.1 0.7 slice.94.refs_2_
  76.8 5.6 %collective-permute-done.12.refs_1_ = bf16[512,192]{1,0:T(8,128)(2,1)S(1)} collective-permute-done((bf16[512,192]{1,0:T(8,128)(2,1)S(1)}, bf16[512,192]{1,0:T(8,128)(2,1)S(1)}, u32[]{:S(2)}, u32[]{:S(2)}) %collective-permute-start.12) | collective-permute-done | bytes 196640 | tf_op jit(solution)/shard_map/ppermute | solution.py:292
  82.5 0.7 copy-done.30
  83.3 3.7 %collective-permute-start.18 = (bf16[64,2048]{1,0:T(8,128)(2,1)S(1)}, bf16[64,2048]{1,0:T(8,128)(2,1)S(1)}, u32[]{:S(2)}, u32[]{:S(2)}) collective-permute-start(bf16[64,2048]{1,0:T(8,128)(2,1)S(1)} %pick.7.refs_3_), channel_id=1, source_target_pairs={{0,2},{4,6},{9,11},{13,15},{18,16},{22,20},{27,25},{31,29}} | collective-permute-start | bytes 786440 | tf_op jit(solution)/shard_map/ppermute | solution.py:292
  87.0 11.5 %whiten.7 = (f32[512,128]{1,0:T(8,128)S(1)}, bf16[512,128]{1,0:T(8,128)(2,1)S(1)}) custom-call(s32[4]{0:T(128)S(1)} %xor_multiply_fusion.starts_ref, bf16[2048,4096]{1,0:T(8,128)(2,1)} %f_ref.7, bf16[32,4096]{1,0:T(8,128)(2,1)S(1)} %collective-permute-done.14.refs_0_.refs_7_, bf16[32,4096]{1,0:T(8,128)(2,1)S(1)} %collective-permute-done.15.refs_1_.refs_8_), custom_call_target="tpu_custom_call" | custom-call | flops 1000 | bytes 1000 | tf_op jit(solution)/shard_map/whiten/pallas_call | solution.py:88
  99.4 0.7 slice.96.refs_4_
  100.1 3.5 %collective-permute-done.17.refs_3_ = bf16[512,128]{1,0:T(8,128)(2,1)S(1)} collective-permute-done((bf16[512,128]{1,0:T(8,128)(2,1)S(1)}, bf16[512,128]{1,0:T(8,128)(2,1)S(1)}, u32[]{:S(2)}, u32[]{:S(2)}) %collective-permute-start.17) | collective-permute-done | bytes 131104 | tf_op jit(solution)/shard_map/ppermute | solution.py:292
  103.7 1.3 collective-permute-done.21
  105.7 0.8 collective-permute-start.22
  106.5 1.1 copy-done.12
  107.6 1.0 copy-done.16
  108.7 1.0 copy-done.18
  109.7 0.9 copy-done.21
  110.7 1.0 copy-done.25
  111.7 1.0 copy-done.27
  112.8 0.9 copy-done.29
  113.7 1.3 pack.1.own_ref
  115.1 0.7 constant_dynamic-slice_fusion
  115.8 1.0 copy-done.19
  116.8 0.9 copy-done.22
  117.8 0.9 copy-done.23
  118.7 0.9 copy-done.31
  119.7 0.9 copy-done.33
  120.6 1.7 %squares.1 = f32[8,64]{1,0:T(8,128)S(1)} custom-call(s32[8]{0:T(128)S(1)} %get-tuple-element.116.places_ref, f32[512,192]{1,0:T(8,128)S(1)} %copy-done.19, bf16[512,192]{1,0:T(8,128)(2,1)S(1)} %copy-done.31, f32[512,128]{1,0:T(8,128)S(1)} %copy-done.22, bf16[512,128]{1,0:T(8,128)(2,1)S(1)} %copy-done.33, f32[512,128]{1,0:T(8,128)S(1)} %copy-done.23, ...), custom_call_target="tpu_custom_call" | custom-call | flops 1000 | bytes 1000 | tf_op jit(solution)/shard_map/squares/pallas_call | solution.py:199
  123.6 2.2 %collective-permute-start.26 = (f32[8,64]{1,0:T(8,128)S(1)}, f32[8,64]{1,0:T(8,128)S(1)}, u32[]{:S(2)}, u32[]{:S(2)}) collective-permute-start(f32[8,64]{1,0:T(8,128)S(1)} %add.66), channel_id=1, source_target_pairs={{0,6},{1,7},{2,4},{3,5},{4,2},{5,3},{6,0},{7,1},{8,14},{9,15},{10,... | collective-permute-start | bytes 6152 | tf_op jit(solution)/shard_map/ppermute | solution.py:292
  126.3 0.8 collective-permute-start.24
  132.3 1.6 %collective-permute-start.30 = (f32[8,64]{1,0:T(8,128)S(1)}, f32[8,64]{1,0:T(8,128)S(1)}, u32[]{:S(2)}, u32[]{:S(2)}) collective-permute-start(f32[8,64]{1,0:T(8,128)S(1)} %add_add_fusion.1), channel_id=1, source_target_pairs={{0,24},{1,25},{2,26},{3,27},{4,28},{5,29},{6,30},{7,31},{8,16},{9,... | collective-permute-start | bytes 6152 | tf_op jit(solution)/shard_map/ppermute | solution.py:292
  133.9 2.9 %collective-permute-start.28 = (f32[8,64]{1,0:T(8,128)S(1)}, f32[8,64]{1,0:T(8,128)S(1)}, u32[]{:S(2)}, u32[]{:S(2)}) collective-permute-start(f32[8,64]{1,0:T(8,128)S(1)} %add_add_fusion.1), channel_id=1, source_target_pairs={{0,8},{1,9},{2,10},{3,11},{4,12},{5,13},{6,14},{7,15},{8,0},{9,1},... | collective-permute-start | bytes 6152 | tf_op jit(solution)/shard_map/ppermute | solution.py:292
  136.8 2.4 %join.1.col_ref = bf16[2048,512]{1,0:T(8,128)(2,1)S(1)} custom-call(s32[1]{0:T(128)} %bitcast.6.flags_ref, bf16[512,2048]{1,0:T(8,128)(2,1)S(1)} %pack.1.own_ref, bf16[512,2048]{1,0:T(8,128)(2,1)} %collective-permute-done.27.other_ref), custom_call_target="tpu_custom_call" | custom-call | flops 1000 | bytes 1000 | tf_op jit(solution)/shard_map/join/pallas_call | solution.py:170
  139.9 15.5 %increment.1 = f32[2048,4096]{1,0:T(8,128)} custom-call(s32[9]{0:T(128)S(1)} %stack.51.starts_ref, f32[512,128]{1,0:T(8,128)S(1)} %get-tuple-element.111.d_ref, bf16[2048,512]{1,0:T(8,128)(2,1)S(1)} %join.1.col_ref, bf16[64,4096]{1,0:T(8,128)(2,1)S(1)} %copy-done.6, bf16[64,4096]{1,0:T(8,128)(2,1)S(1)} %copy-done.8, bf16[64,4096]{1,0:T(8,128)(2,1)S(1)} %copy-done.10, ...), custom_call_target="tpu_custom_call" | custom-call | flops 1000 | bytes 1000 | tf_op jit(solution)/shard_map/increment/pallas_call | solution.py:263
  (126 shorter events, 8.5 us)
Async XLA Ops:
  0.6 25.2 %copy-start.34 = (s32[4]{0:T(128)S(1)}, s32[4]{0:T(128)}, u32[]{:S(2)}) copy-start(s32[4]{0:T(128)} %constant.61.clone) | copy-start | bytes 52
  0.6 15.4 %collective-permute-start.1 = (bf16[64,4096]{1,0:T(8,128)(2,1)}, bf16[64,4096]{1,0:T(8,128)(2,1)S(1)}, u32[]{:S(2)}, u32[]{:S(2)}) collective-permute-start(bf16[64,4096]{1,0:T(8,128)(2,1)} %refs_0_.5), channel_id=1, source_target_pairs={{0,4},{1,5},{2,6},{3,7},{4,0},{5,1},{6,2},{7,3},{8,12},{9,13},{10,... | collective-permute-start | bytes 1572872 | tf_op jit(solution)/shard_map/ppermute | solution.py:292
  3.6 13.8 %collective-permute-start = (bf16[64,4096]{1,0:T(8,128)(2,1)}, bf16[64,4096]{1,0:T(8,128)(2,1)S(1)}, u32[]{:S(2)}, u32[]{:S(2)}) collective-permute-start(bf16[64,4096]{1,0:T(8,128)(2,1)} %refs_0_.5), channel_id=1, source_target_pairs={{0,16},{1,17},{2,18},{3,19},{4,20},{5,21},{6,22},{7,23},{8,0},{9,1... | collective-permute-start | bytes 1572872 | tf_op jit(solution)/shard_map/ppermute | solution.py:292
  7.6 8.3 %collective-permute-start.2 = (f32[8,2,64]{2,0,1:T(8,128)S(1)}, f32[8,2,64]{2,0,1:T(8,128)S(1)}, u32[]{:S(2)}, u32[]{:S(2)}) collective-permute-start(f32[8,2,64]{2,0,1:T(8,128)S(1)} %broadcast_select_fusion), channel_id=1, source_target_pairs={{0,4},{1,5},{2,6},{3,7},{4,0},{5,1},{6,2},{7,3},{8,12},{9,13},{10,... | collective-permute-start | bytes 12296 | tf_op jit(solution)/shard_map/ppermute | solution.py:292
  16.0 21.9 %copy-start.7 = (bf16[64,4096]{1,0:T(8,128)(2,1)}, bf16[64,4096]{1,0:T(8,128)(2,1)S(1)}, u32[]{:S(2)}) copy-start(bf16[64,4096]{1,0:T(8,128)(2,1)S(1)} %collective-permute-done.1.refs_1_) | copy-start | bytes 1572868
  17.5 20.5 %copy-start.9 = (bf16[64,4096]{1,0:T(8,128)(2,1)}, bf16[64,4096]{1,0:T(8,128)(2,1)S(1)}, u32[]{:S(2)}) copy-start(bf16[64,4096]{1,0:T(8,128)(2,1)S(1)} %collective-permute-done.refs_2_) | copy-start | bytes 1572868
  18.7 7.1 %copy-start.5 = (bf16[64,4096]{1,0:T(8,128)(2,1)S(1)}, bf16[64,4096]{1,0:T(8,128)(2,1)}, u32[]{:S(2)}) copy-start(bf16[64,4096]{1,0:T(8,128)(2,1)} %refs_0_.5) | copy-start | bytes 1572868
  18.7 19.2 %copy-start.11 = (bf16[192,2048]{1,0:T(8,128)(2,1)}, bf16[192,2048]{1,0:T(8,128)(2,1)S(1)}, u32[]{:S(2)}) copy-start(bf16[192,2048]{1,0:T(8,128)(2,1)S(1)} %pick.4.refs_0_) | copy-start | bytes 2359300
  18.8 19.2 %collective-permute-start.3 = (bf16[192,2048]{1,0:T(8,128)(2,1)S(1)}, bf16[192,2048]{1,0:T(8,128)(2,1)}, u32[]{:S(2)}, u32[]{:S(2)}) collective-permute-start(bf16[192,2048]{1,0:T(8,128)(2,1)S(1)} %pick.4.refs_0_), channel_id=1, source_target_pairs={{0,2},{4,6},{9,11},{13,15},{18,16},{22,20},{27,25},{31,29}} | collective-permute-start | bytes 2359304 | tf_op jit(solution)/shard_map/ppermute | solution.py:292
  23.3 14.7 %collective-permute-start.5 = (bf16[64,4096]{1,0:T(8,128)(2,1)S(1)}, bf16[64,4096]{1,0:T(8,128)(2,1)S(1)}, u32[]{:S(2)}, u32[]{:S(2)}) collective-permute-start(bf16[64,4096]{1,0:T(8,128)(2,1)S(1)} %collective-permute-done.refs_2_), channel_id=1, source_target_pairs={{0,4},{1,5},{2,6},{3,7},{4,0},{5,1},{6,2},{7,3},{8,12},{9,13},{10,... | collective-permute-start | bytes 1572872 | tf_op jit(solution)/shard_map/ppermute | solution.py:292
  23.8 14.2 %collective-permute-start.4 = (bf16[64,4096]{1,0:T(8,128)(2,1)S(1)}, bf16[64,4096]{1,0:T(8,128)(2,1)S(1)}, u32[]{:S(2)}, u32[]{:S(2)}) collective-permute-start(bf16[64,4096]{1,0:T(8,128)(2,1)S(1)} %collective-permute-done.refs_2_), channel_id=1, source_target_pairs={{0,16},{1,17},{2,18},{3,19},{4,20},{5,21},{6,22},{7,23},{8,0},{9,1... | collective-permute-start | bytes 1572872 | tf_op jit(solution)/shard_map/ppermute | solution.py:292
  24.1 13.9 %collective-permute-start.6 = (f32[8,2,64]{2,0,1:T(8,128)S(1)}, f32[8,2,64]{2,0,1:T(8,128)S(1)}, u32[]{:S(2)}, u32[]{:S(2)}) collective-permute-start(f32[8,2,64]{2,0,1:T(8,128)S(1)} %fusion), channel_id=1, source_target_pairs={{0,8},{1,9},{2,10},{3,11},{4,12},{5,13},{6,14},{7,15},{8,0},{9,1},... | collective-permute-start | bytes 12296 | tf_op jit(solution)/shard_map/ppermute | solution.py:292
  38.0 17.0 %copy-start = (bf16[64,4096]{1,0:T(8,128)(2,1)}, bf16[64,4096]{1,0:T(8,128)(2,1)S(1)}, u32[]{:S(2)}) copy-start(bf16[64,4096]{1,0:T(8,128)(2,1)S(1)} %collective-permute-done.5.refs_0_.refs_3_) | copy-start | bytes 1572868
  38.0 17.0 %copy-start.2 = (bf16[64,4096]{1,0:T(8,128)(2,1)}, bf16[64,4096]{1,0:T(8,128)(2,1)S(1)}, u32[]{:S(2)}) copy-start(bf16[64,4096]{1,0:T(8,128)(2,1)S(1)} %collective-permute-done.4.refs_1_.refs_4_) | copy-start | bytes 1572868
  38.0 17.0 %collective-permute-start.10 = (bf16[1024,192]{1,0:T(8,128)(2,1)S(1)}, bf16[1024,192]{1,0:T(8,128)(2,1)S(1)}, u32[]{:S(2)}, u32[]{:S(2)}) collective-permute-start(bf16[1024,192]{1,0:T(8,128)(2,1)S(1)} %get-tuple-element.66), channel_id=1, source_target_pairs={{0,1},{1,0},{2,3},{3,2},{4,5},{5,4},{6,7},{7,6},{8,9},{9,8},{10,11... | collective-permute-start | bytes 1179656 | tf_op jit(solution)/shard_map/ppermute | solution.py:292
  38.1 16.8 %copy-start.15 = (bf16[128,2048]{1,0:T(8,128)(2,1)}, bf16[128,2048]{1,0:T(8,128)(2,1)S(1)}, u32[]{:S(2)}) copy-start(bf16[128,2048]{1,0:T(8,128)(2,1)S(1)} %pick.5.refs_1_) | copy-start | bytes 1572868
  38.1 17.9 %collective-permute-start.7 = (bf16[128,2048]{1,0:T(8,128)(2,1)S(1)}, bf16[128,2048]{1,0:T(8,128)(2,1)S(1)}, u32[]{:S(2)}, u32[]{:S(2)}) collective-permute-start(bf16[128,2048]{1,0:T(8,128)(2,1)S(1)} %pick.5.refs_1_), channel_id=1, source_target_pairs={{0,2},{4,6},{9,11},{13,15},{18,16},{22,20},{27,25},{31,29}} | collective-permute-start | bytes 1572872 | tf_op jit(solution)/shard_map/ppermute | solution.py:292
  41.9 14.9 %collective-permute-start.9 = (bf16[64,4096]{1,0:T(8,128)(2,1)S(1)}, bf16[64,4096]{1,0:T(8,128)(2,1)S(1)}, u32[]{:S(2)}, u32[]{:S(2)}) collective-permute-start(bf16[64,4096]{1,0:T(8,128)(2,1)S(1)} %collective-permute-done.4.refs_1_.refs_4_), channel_id=1, source_target_pairs={{0,4},{1,5},{2,6},{3,7},{4,0},{5,1},{6,2},{7,3},{8,12},{9,13},{10,... | collective-permute-start | bytes 1572872 | tf_op jit(solution)/shard_map/ppermute | solution.py:292
  43.4 14.1 %collective-permute-start.8 = (bf16[64,4096]{1,0:T(8,128)(2,1)S(1)}, bf16[64,4096]{1,0:T(8,128)(2,1)S(1)}, u32[]{:S(2)}, u32[]{:S(2)}) collective-permute-start(bf16[64,4096]{1,0:T(8,128)(2,1)S(1)} %collective-permute-done.4.refs_1_.refs_4_), channel_id=1, source_target_pairs={{0,16},{1,17},{2,18},{3,19},{4,20},{5,21},{6,22},{7,23},{8,0},{9,1... | collective-permute-start | bytes 1572872 | tf_op jit(solution)/shard_map/ppermute | solution.py:292
  43.4 11.5 %collective-permute-start.11 = (f32[8,2,64]{2,0,1:T(8,128)S(1)}, f32[8,2,64]{2,0,1:T(8,128)S(1)}, u32[]{:S(2)}, u32[]{:S(2)}) collective-permute-start(f32[8,2,64]{2,0,1:T(8,128)S(1)} %add.60), channel_id=1, source_target_pairs={{0,16},{1,17},{2,18},{3,19},{4,20},{5,21},{6,22},{7,23},{8,24},{9,... | collective-permute-start | bytes 12296 | tf_op jit(solution)/shard_map/ppermute | solution.py:292
  57.6 15.7 %copy-start.17 = (bf16[128,2048]{1,0:T(8,128)(2,1)}, bf16[128,2048]{1,0:T(8,128)(2,1)S(1)}, u32[]{:S(2)}) copy-start(bf16[128,2048]{1,0:T(8,128)(2,1)S(1)} %pick.6.refs_2_) | copy-start | bytes 1572868
  57.6 25.6 %collective-permute-start.13 = (bf16[128,2048]{1,0:T(8,128)(2,1)S(1)}, bf16[128,2048]{1,0:T(8,128)(2,1)S(1)}, u32[]{:S(2)}, u32[]{:S(2)}) collective-permute-start(bf16[128,2048]{1,0:T(8,128)(2,1)S(1)} %pick.6.refs_2_), channel_id=1, source_target_pairs={{0,2},{4,6},{9,11},{13,15},{18,16},{22,20},{27,25},{31,29}} | collective-permute-start | bytes 1572872 | tf_op jit(solution)/shard_map/ppermute | solution.py:292
  60.2 15.9 %collective-permute-start.16 = (bf16[1024,128]{1,0:T(8,128)(2,1)S(1)}, bf16[1024,128]{1,0:T(8,128)(2,1)S(1)}, u32[]{:S(2)}, u32[]{:S(2)}) collective-permute-start(bf16[1024,128]{1,0:T(8,128)(2,1)S(1)} %get-tuple-element.75), channel_id=1, source_target_pairs={{0,1},{1,0},{2,3},{3,2},{4,5},{5,4},{6,7},{7,6},{8,9},{9,8},{10,11... | collective-permute-start | bytes 786440 | tf_op jit(solution)/shard_map/ppermute | solution.py:292
  60.3 22.9 %collective-permute-start.14 = (bf16[32,4096]{1,0:T(8,128)(2,1)S(1)}, bf16[32,4096]{1,0:T(8,128)(2,1)S(1)}, u32[]{:S(2)}, u32[]{:S(2)}) collective-permute-start(bf16[32,4096]{1,0:T(8,128)(2,1)S(1)} %slice.74), channel_id=1, source_target_pairs={{0,4},{1,5},{2,6},{3,7},{4,0},{5,1},{6,2},{7,3},{8,12},{9,13},{10,... | collective-permute-start | bytes 786440 | tf_op jit(solution)/shard_map/ppermute | solution.py:292
  60.9 22.3 %collective-permute-start.15 = (bf16[32,4096]{1,0:T(8,128)(2,1)S(1)}, bf16[32,4096]{1,0:T(8,128)(2,1)S(1)}, u32[]{:S(2)}, u32[]{:S(2)}) collective-permute-start(bf16[32,4096]{1,0:T(8,128)(2,1)S(1)} %slice.75), channel_id=1, source_target_pairs={{0,16},{1,17},{2,18},{3,19},{4,20},{5,21},{6,22},{7,23},{8,0},{9,1... | collective-permute-start | bytes 786440 | tf_op jit(solution)/shard_map/ppermute | solution.py:292
  73.3 9.1 %collective-permute-start.12 = (bf16[512,192]{1,0:T(8,128)(2,1)S(1)}, bf16[512,192]{1,0:T(8,128)(2,1)S(1)}, u32[]{:S(2)}, u32[]{:S(2)}) collective-permute-start(bf16[512,192]{1,0:T(8,128)(2,1)S(1)} %slice.106), channel_id=1, source_target_pairs={{0,2},{1,3},{2,0},{3,1},{4,6},{5,7},{6,4},{7,5},{8,10},{9,11},{10,... | collective-permute-start | bytes 589832 | tf_op jit(solution)/shard_map/ppermute | solution.py:292
  83.2 15.3 %copy-start.13 = (bf16[32,4096]{1,0:T(8,128)(2,1)}, bf16[32,4096]{1,0:T(8,128)(2,1)S(1)}, u32[]{:S(2)}) copy-start(bf16[32,4096]{1,0:T(8,128)(2,1)S(1)} %collective-permute-done.15.refs_1_.refs_8_) | copy-start | bytes 786436
  83.2 15.3 %copy-start.26 = (bf16[128,2048]{1,0:T(8,128)(2,1)}, bf16[128,2048]{1,0:T(8,128)(2,1)S(1)}, u32[]{:S(2)}) copy-start(bf16[128,2048]{1,0:T(8,128)(2,1)S(1)} %collective-permute-done.13.refs_6_) | copy-start | bytes 1572868
  83.2 15.4 %collective-permute-start.19 = (bf16[1024,128]{1,0:T(8,128)(2,1)S(1)}, bf16[1024,128]{1,0:T(8,128)(2,1)S(1)}, u32[]{:S(2)}, u32[]{:S(2)}) collective-permute-start(bf16[1024,128]{1,0:T(8,128)(2,1)S(1)} %get-tuple-element.85), channel_id=1, source_target_pairs={{0,1},{1,0},{2,3},{3,2},{4,5},{5,4},{6,7},{7,6},{8,9},{9,8},{10,11... | collective-permute-start | bytes 786440 | tf_op jit(solution)/shard_map/ppermute | solution.py:292
  83.3 15.2 %copy-start.20 = (bf16[64,2048]{1,0:T(8,128)(2,1)}, bf16[64,2048]{1,0:T(8,128)(2,1)S(1)}, u32[]{:S(2)}) copy-start(bf16[64,2048]{1,0:T(8,128)(2,1)S(1)} %pick.7.refs_3_) | copy-start | bytes 786436
  83.3 20.2 %collective-permute-start.18 = (bf16[64,2048]{1,0:T(8,128)(2,1)S(1)}, bf16[64,2048]{1,0:T(8,128)(2,1)S(1)}, u32[]{:S(2)}, u32[]{:S(2)}) collective-permute-start(bf16[64,2048]{1,0:T(8,128)(2,1)S(1)} %pick.7.refs_3_), channel_id=1, source_target_pairs={{0,2},{4,6},{9,11},{13,15},{18,16},{22,20},{27,25},{31,29}} | collective-permute-start | bytes 786440 | tf_op jit(solution)/shard_map/ppermute | solution.py:292
  98.5 5.0 %collective-permute-start.17 = (bf16[512,128]{1,0:T(8,128)(2,1)S(1)}, bf16[512,128]{1,0:T(8,128)(2,1)S(1)}, u32[]{:S(2)}, u32[]{:S(2)}) collective-permute-start(bf16[512,128]{1,0:T(8,128)(2,1)S(1)} %slice.108), channel_id=1, source_target_pairs={{0,2},{1,3},{2,0},{3,1},{4,6},{5,7},{6,4},{7,5},{8,10},{9,11},{10,... | collective-permute-start | bytes 393224 | tf_op jit(solution)/shard_map/ppermute | solution.py:292
  103.6 1.4 collective-permute-start.21
  103.7 11.3 %collective-permute-start.20 = (bf16[512,128]{1,0:T(8,128)(2,1)}, bf16[512,128]{1,0:T(8,128)(2,1)}, u32[]{:S(2)}, u32[]{:S(2)}) collective-permute-start(bf16[512,128]{1,0:T(8,128)(2,1)} %slice.107), channel_id=1, source_target_pairs={{0,2},{1,3},{2,0},{3,1},{4,6},{5,7},{6,4},{7,5},{8,10},{9,11},{10,... | collective-permute-start | bytes 393224 | tf_op jit(solution)/shard_map/ppermute | solution.py:292
  105.7 9.3 %collective-permute-start.22 = (bf16[256,128]{1,0:T(8,128)(2,1)}, bf16[256,128]{1,0:T(8,128)(2,1)}, u32[]{:S(2)}, u32[]{:S(2)}) collective-permute-start(bf16[256,128]{1,0:T(8,128)(2,1)} %slice.109), channel_id=1, source_target_pairs={{0,2},{1,3},{2,0},{3,1},{4,6},{5,7},{6,4},{7,5},{8,10},{9,11},{10,... | collective-permute-start | bytes 196616 | tf_op jit(solution)/shard_map/ppermute | solution.py:292
  115.0 17.3 %collective-permute-start.27 = (bf16[512,2048]{1,0:T(8,128)(2,1)S(1)}, bf16[512,2048]{1,0:T(8,128)(2,1)}, u32[]{:S(2)}, u32[]{:S(2)}) collective-permute-start(bf16[512,2048]{1,0:T(8,128)(2,1)S(1)} %pack.1.own_ref), channel_id=1, source_target_pairs={{0,1},{1,0},{2,3},{3,2},{4,5},{5,4},{6,7},{7,6},{8,9},{9,8},{10,11... | collective-permute-start | bytes 6291464 | tf_op jit(solution)/shard_map/ppermute | solution.py:292
  122.3 1.3 collective-permute-start.23
  123.6 8.6 %collective-permute-start.26 = (f32[8,64]{1,0:T(8,128)S(1)}, f32[8,64]{1,0:T(8,128)S(1)}, u32[]{:S(2)}, u32[]{:S(2)}) collective-permute-start(f32[8,64]{1,0:T(8,128)S(1)} %add.66), channel_id=1, source_target_pairs={{0,6},{1,7},{2,4},{3,5},{4,2},{5,3},{6,0},{7,1},{8,14},{9,15},{10,... | collective-permute-start | bytes 6152 | tf_op jit(solution)/shard_map/ppermute | solution.py:292
  125.8 6.5 %collective-permute-start.25 = (f32[8,64]{1,0:T(8,128)S(1)}, f32[8,64]{1,0:T(8,128)S(1)}, u32[]{:S(2)}, u32[]{:S(2)}) collective-permute-start(f32[8,64]{1,0:T(8,128)S(1)} %add.66), channel_id=1, source_target_pairs={{0,4},{1,5},{2,6},{3,7},{4,0},{5,1},{6,2},{7,3},{8,12},{9,13},{10,... | collective-permute-start | bytes 6152 | tf_op jit(solution)/shard_map/ppermute | solution.py:292
  126.3 5.9 %collective-permute-start.24 = (f32[8,64]{1,0:T(8,128)S(1)}, f32[8,64]{1,0:T(8,128)S(1)}, u32[]{:S(2)}, u32[]{:S(2)}) collective-permute-start(f32[8,64]{1,0:T(8,128)S(1)} %add.66), channel_id=1, source_target_pairs={{0,2},{1,3},{2,0},{3,1},{4,6},{5,7},{6,4},{7,5},{8,10},{9,11},{10,... | collective-permute-start | bytes 6152 | tf_op jit(solution)/shard_map/ppermute | solution.py:292
  132.3 6.9 %collective-permute-start.30 = (f32[8,64]{1,0:T(8,128)S(1)}, f32[8,64]{1,0:T(8,128)S(1)}, u32[]{:S(2)}, u32[]{:S(2)}) collective-permute-start(f32[8,64]{1,0:T(8,128)S(1)} %add_add_fusion.1), channel_id=1, source_target_pairs={{0,24},{1,25},{2,26},{3,27},{4,28},{5,29},{6,30},{7,31},{8,16},{9,... | collective-permute-start | bytes 6152 | tf_op jit(solution)/shard_map/ppermute | solution.py:292
  133.9 5.3 %collective-permute-start.29 = (f32[8,64]{1,0:T(8,128)S(1)}, f32[8,64]{1,0:T(8,128)S(1)}, u32[]{:S(2)}, u32[]{:S(2)}) collective-permute-start(f32[8,64]{1,0:T(8,128)S(1)} %add_add_fusion.1), channel_id=1, source_target_pairs={{0,16},{1,17},{2,18},{3,19},{4,20},{5,21},{6,22},{7,23},{8,24},{9,... | collective-permute-start | bytes 6152 | tf_op jit(solution)/shard_map/ppermute | solution.py:292
  133.9 5.3 %collective-permute-start.28 = (f32[8,64]{1,0:T(8,128)S(1)}, f32[8,64]{1,0:T(8,128)S(1)}, u32[]{:S(2)}, u32[]{:S(2)}) collective-permute-start(f32[8,64]{1,0:T(8,128)S(1)} %add_add_fusion.1), channel_id=1, source_target_pairs={{0,8},{1,9},{2,10},{3,11},{4,12},{5,13},{6,14},{7,15},{8,0},{9,1},... | collective-permute-start | bytes 6152 | tf_op jit(solution)/shard_map/ppermute | solution.py:292
  136.8 3.1 %copy-start.3 = (bf16[64,4096]{1,0:T(8,128)(2,1)S(1)}, bf16[64,4096]{1,0:T(8,128)(2,1)}, u32[]{:S(2)}) copy-start(bf16[64,4096]{1,0:T(8,128)(2,1)} %copy-done.2) | copy-start | bytes 1572868
  136.8 3.1 %copy-start.6 = (bf16[64,4096]{1,0:T(8,128)(2,1)S(1)}, bf16[64,4096]{1,0:T(8,128)(2,1)}, u32[]{:S(2)}) copy-start(bf16[64,4096]{1,0:T(8,128)(2,1)} %refs_0_.5) | copy-start | bytes 1572868
  136.8 3.1 %copy-start.8 = (bf16[64,4096]{1,0:T(8,128)(2,1)S(1)}, bf16[64,4096]{1,0:T(8,128)(2,1)}, u32[]{:S(2)}) copy-start(bf16[64,4096]{1,0:T(8,128)(2,1)} %copy-done.7) | copy-start | bytes 1572868
  136.8 3.1 %copy-start.10 = (bf16[64,4096]{1,0:T(8,128)(2,1)S(1)}, bf16[64,4096]{1,0:T(8,128)(2,1)}, u32[]{:S(2)}) copy-start(bf16[64,4096]{1,0:T(8,128)(2,1)} %copy-done.9) | copy-start | bytes 1572868
  136.8 3.1 %copy-start.14 = (bf16[32,4096]{1,0:T(8,128)(2,1)S(1)}, bf16[32,4096]{1,0:T(8,128)(2,1)}, u32[]{:S(2)}) copy-start(bf16[32,4096]{1,0:T(8,128)(2,1)} %copy-done.13) | copy-start | bytes 786436
  (18 other events, 21.4 us)

commit v3 on v2

v3 whole, which is shorter than its diff:
```python
import functools

import jax
import jax.numpy as jnp
from jax import lax
from jax.experimental import pallas as pl
from jax.experimental.pallas import tpu as pltpu
from jax.sharding import PartitionSpec as P

BOTH = ("row", "feat")
HI = 4
MIB = 1 << 20
LANES = 128


def ring_order(count):
    return list(range(0, count, 2)) + list(range(1, count, 2))[::-1]


def ring_next(count):
    order = ring_order(count)
    return {order[i]: order[(i + 1) % count] for i in range(count)}


def call(kernel, name, out_shape, scratch, args, fixed=(), vmem=16, flops=1000):
    on_vmem = pl.BlockSpec(memory_space=pltpu.VMEM)
    on_hbm = pl.BlockSpec(memory_space=pltpu.HBM)
    scalars, rest = args
    out_hbm = "out" in fixed
    held = [x for x in fixed if not isinstance(x, str)]
    return pl.pallas_call(
        kernel,
        in_specs=[pl.BlockSpec(memory_space=pltpu.SMEM)] + [on_hbm] * len(held) + [on_vmem] * len(rest),
        out_specs=jax.tree.map(lambda _: on_hbm if out_hbm else on_vmem, out_shape),
        out_shape=out_shape,
        scratch_shapes=scratch,
        compiler_params=pltpu.CompilerParams(vmem_limit_bytes=vmem * MIB),
        cost_estimate=pl.CostEstimate(flops=flops, bytes_accessed=1000, transcendentals=0),
        name=name,
    )(scalars, *held, *rest)


def whiten_kernel(tile, starts_ref, f_ref, *refs):
    pieces, (keep_ref, away_ref, x_ref, xt_ref, buf_ref, sems) = refs[:-6], refs[-6:]
    slots = buf_ref.shape[0]
    tiles = f_ref.shape[0] // tile
    per_block = tiles // starts_ref.shape[0]
    half = tiles // 2

    def copy(t):
        order = lax.rem(t + half, tiles)
        start = starts_ref[order // per_block] + lax.rem(order, per_block) * tile
        slot = lax.rem(t, slots)
        return pltpu.make_async_copy(
            f_ref.at[pl.ds(pl.multiple_of(start, tile), tile)], buf_ref.at[slot], sems.at[slot]
        )

    for t in range(min(slots, tiles)):
        copy(jnp.int32(t)).start()
    place = 0
    for piece in pieces:
        x_ref[pl.ds(place, piece.shape[0]), :] = piece[...]
        place += piece.shape[0]
    wide = min(512, x_ref.shape[1])
    for c in range(x_ref.shape[1] // wide):
        xt_ref[pl.ds(c * wide, wide), :] = x_ref[:, c * wide:(c + 1) * wide].T

    def product(t):
        copy(t).wait()
        part = jnp.dot(buf_ref[lax.rem(t, slots)], xt_ref[...], preferred_element_type=jnp.float32)

        @pl.when(t + slots < tiles)
        def _():
            copy(t + slots).start()

        return part

    def away(t, carry):
        away_ref[pl.ds(pl.multiple_of(t * tile, tile), tile), :] = product(t).astype(jnp.bfloat16)
        return carry

    def keep(t, carry):
        keep_ref[pl.ds(pl.multiple_of((t - half) * tile, tile), tile), :] = product(t)
        return carry

    lax.fori_loop(0, half, away, 0)
    lax.fori_loop(half, tiles, keep, 0)


def whiten(starts, inv_factor, pieces):
    row_block, feat_block = inv_factor.shape
    rows = sum(p.shape[0] for p in pieces)
    tile = min(256, row_block // starts.shape[0])
    slots = 3
    out = (row_block // 2, rows)
    return call(
        functools.partial(whiten_kernel, tile),
        "whiten",
        [jax.ShapeDtypeStruct(out, jnp.float32), jax.ShapeDtypeStruct(out, jnp.bfloat16)],
        [
            pltpu.VMEM((rows, feat_block), jnp.bfloat16),
            pltpu.VMEM((feat_block, rows), jnp.bfloat16),
            pltpu.VMEM((slots, tile, feat_block), jnp.bfloat16),
            pltpu.SemaphoreType.DMA((slots,)),
        ],
        (starts, pieces),
        (inv_factor,),
        vmem=46,
        flops=8 * row_block * feat_block * rows,
    )


def halve_kernel(_, part_ref, got_ref, keep_ref, away_ref):
    left = keep_ref.shape[0]
    keep_ref[...] = part_ref[:left, :] + got_ref[:left, :].astype(jnp.float32)
    away_ref[...] = (part_ref[left:, :] + got_ref[left:, :].astype(jnp.float32)).astype(jnp.bfloat16)


def halve(starts, part, got):
    out = (part.shape[0] // 2, part.shape[1])
    return call(
        halve_kernel,
        "halve",
        [jax.ShapeDtypeStruct(out, jnp.float32), jax.ShapeDtypeStruct(out, jnp.bfloat16)],
        [],
        (starts, [part, got]),
    )


def pick_kernel(count, half, block_ref, *refs):
    pieces, outs = refs[:count], refs[count:]
    width = outs[0].shape[1]
    start = pl.multiple_of(block_ref[0] * width, width)
    place = 0
    for piece in pieces:
        outs[0][pl.ds(place, piece.shape[0]), :] = piece[:, pl.ds(start, width)]
        place += piece.shape[0]
    if half:
        outs[1][...] = pieces[-1][:half, :]
        for out, piece in zip(outs[2:], pieces):
            out[...] = piece[half:, :]


def pick(block, pieces, width, half=0):
    rows = sum(p.shape[0] for p in pieces)
    out = [jax.ShapeDtypeStruct((rows, width), jnp.bfloat16)]
    if half:
        out += [jax.ShapeDtypeStruct((half, pieces[0].shape[1]), jnp.bfloat16)] * len(pieces)
    return call(
        functools.partial(pick_kernel, len(pieces), half), "pick", out, [], (block, pieces)
    )


def pack_kernel(count, flag_ref, *refs):
    out_ref = refs[-1]

    def copy(sources):
        place = 0
        for source in sources:
            out_ref[pl.ds(place, source.shape[0]), :] = source[...]
            place += source.shape[0]

    @pl.when(flag_ref[0] == 1)
    def _():
        copy(refs[:count])

    @pl.when(flag_ref[0] == 0)
    def _():
        copy(refs[count:-1])


def pack(flag, own, got):
    out = (sum(x.shape[0] for x in own), own[0].shape[1])
    return call(
        functools.partial(pack_kernel, len(own)),
        "pack",
        jax.ShapeDtypeStruct(out, jnp.bfloat16),
        [],
        (flag, own + got),
    )


def join_kernel(flag_ref, own_ref, other_ref, out_ref):
    wide = min(256, own_ref.shape[1])

    def turn(source):
        for c in range(source.shape[1] // wide):
            out_ref[pl.ds(c * wide, wide), :] = source[:, c * wide:(c + 1) * wide].T

    @pl.when(flag_ref[0] == 1)
    def _():
        turn(own_ref)

    @pl.when(flag_ref[0] == 0)
    def _():
        turn(other_ref)


def join(flag, own, other):
    rows, width = own.shape
    return call(
        join_kernel, "join", jax.ShapeDtypeStruct((width, rows), jnp.bfloat16), [], (flag, [own, other])
    )


def square_kernel(sizes, places_ref, *refs):
    out_ref = refs[-1]
    count = out_ref.shape[1]
    slot = 0
    for g, size in enumerate(sizes):
        value = refs[2 * g][...] + refs[2 * g + 1][...].astype(jnp.float32)
        line = jnp.sum(value * value, axis=0, keepdims=True)
        for i in range(size):
            out_ref[pl.ds(places_ref[slot], 1), :] = line[:, i * count:(i + 1) * count]
            slot += 1


def squares(places, pairs, sizes, count):
    return call(
        functools.partial(square_kernel, sizes),
        "squares",
        jax.ShapeDtypeStruct((sum(sizes), count), jnp.float32),
        [],
        (places, [x for pair in pairs for x in pair]),
    )


def weight_kernel(strata_n, features, row_ref, raw_ref, w_ref, strata_ref, wide_ref, new_ref, lev_ref, all_ref):
    raw, weights, strata = raw_ref[...], w_ref[...], strata_ref[...]
    products = weights * raw
    ratio = jnp.zeros_like(raw)
    for s in range(strata_n):
        inside = strata == float(s)
        mass = jnp.sum(jnp.where(inside, weights, 0.0), keepdims=True)
        product = jnp.sum(jnp.where(inside, products, 0.0), keepdims=True)
        ratio = jnp.where(inside, mass / product, ratio)
    new = products * ratio
    all_ref[...] = new
    new_ref[...] = all_ref[pl.ds(row_ref[0], 1), :]
    lev_ref[...] = raw_ref[pl.ds(row_ref[0], 1), :] / features
    step = new - weights
    groups, count = step.shape
    for g in range(groups):
        wide_ref[pl.ds(g * count, count), :] = jnp.broadcast_to(step[g:g + 1, :], (LANES, count)).T


def weight_step(row, raw, weights, strata, features):
    groups, count = raw.shape
    return call(
        functools.partial(weight_kernel, 2 * groups, features),
        "weight_step",
        [
            jax.ShapeDtypeStruct((groups * count, LANES), jnp.float32),
            jax.ShapeDtypeStruct((1, count), jnp.float32),
            jax.ShapeDtypeStruct((1, count), jnp.float32),
        ],
        [pltpu.VMEM((groups, count), jnp.float32)],
        (row, [raw, weights, strata]),
    )


def information_kernel(starts_ref, d_ref, col_ref, *refs):
    pieces, (out_ref, s_ref, buf_ref, sems) = refs[:-4], refs[-4:]
    width = s_ref.shape[1]
    steps = out_ref.shape[1] // width

    def copy(j):
        slot = lax.rem(j, 2)
        return pltpu.make_async_copy(
            buf_ref.at[slot], out_ref.at[:, pl.ds(pl.multiple_of(j * width, width), width)], sems.at[slot]
        )

    def step(j, carry):
        place = 0
        for i, piece in enumerate(pieces):
            size = piece.shape[0]
            scale = d_ref[pl.ds(pl.multiple_of(starts_ref[i], size), size), :]
            for c in range(width // LANES):
                start = pl.multiple_of(j * width + c * LANES, LANES)
                value = piece[:, pl.ds(start, LANES)].astype(jnp.float32)
                s_ref[pl.ds(place, size), c * LANES:(c + 1) * LANES] = (scale * value).astype(jnp.bfloat16)
            place += size

        @pl.when(j > 1)
        def _():
            copy(j - 2).wait()

        buf_ref[lax.rem(j, 2)] = jnp.dot(col_ref[...], s_ref[...], preferred_element_type=jnp.float32)
        copy(j).start()
        return carry

    lax.fori_loop(0, steps, step, 0)
    for j in range(max(0, steps - 2), steps):
        copy(jnp.int32(j)).wait()


def increment(starts, step_wide, column_t, pieces):
    row_block, rows = column_t.shape
    feat_block = pieces[0].shape[1]
    width = min(512, feat_block)
    return call(
        information_kernel,
        "increment",
        jax.ShapeDtypeStruct((row_block, feat_block), jnp.float32),
        [
            pltpu.VMEM((rows, width), jnp.bfloat16),
            pltpu.VMEM((2, row_block, width), jnp.float32),
            pltpu.SemaphoreType.DMA((2,)),
        ],
        (starts, [step_wide, column_t] + pieces),
        ("out",),
        24,
    )


def make(mesh):
    rows_n, feats_n = mesh.shape["row"], mesh.shape["feat"]
    hi_n = HI
    lo_n = rows_n // hi_n
    per_feat = rows_n // feats_n
    everyone = [(r, f) for r in range(rows_n) for f in range(feats_n)]

    def perm(target, keep=lambda r, f: True):
        out = []
        for r, f in everyone:
            if keep(r, f):
                r2, f2 = target(r, f)
                out.append((r * feats_n + f, r2 * feats_n + f2))
        return out

    def send(x, pairs):
        return lax.ppermute(x, BOTH, pairs)

    def swap(x, r_bit, f_bit):
        return send(x, perm(lambda r, f: (r ^ r_bit, f ^ f_bit)))

    fence = lax.optimization_barrier
    hi_next, lo_next = ring_next(hi_n), ring_next(lo_n)
    hi_pairs = perm(lambda r, f: (hi_next[r // lo_n] * lo_n + r % lo_n, f))
    lo_pairs = perm(lambda r, f: (r // lo_n * lo_n + lo_next[r % lo_n], f))
    hi_order, lo_order = ring_order(hi_n), ring_order(lo_n)

    def source(r, k, s):
        h, l = r // lo_n, r % lo_n
        h2 = hi_order[(hi_order.index(h) - k) % hi_n]
        l2 = lo_order[(lo_order.index(l) - s) % lo_n]
        return h2 * lo_n + l2

    feat_bits = [1 << b for b in range(feats_n.bit_length() - 1)]
    far_bits = feat_bits[1:]
    row_bits = [1 << b for b in range(rows_n.bit_length() - 1)]
    relative = [0]
    for bit in reversed(feat_bits):
        relative = relative + [j + bit for j in relative]

    groups = [[(0, s) for s in range(lo_n)] + [(1, 0)]]
    for k in range(1, hi_n):
        groups.append([(k, s) for s in range(1, lo_n)] + ([(k + 1, 0)] if k + 1 < hi_n else []))
    slots = [slot for group in groups for slot in group]
    white_groups = [[(k, s) for s in range(lo_n)] for k in range(hi_n)]
    white_slots = [slot for group in white_groups for slot in group]

    def per_device(candidates, inv_factor, weights, strata):
        rows_dev, feat_block = candidates.shape
        row_block = inv_factor.shape[0]
        features = feat_block * feats_n
        half = rows_dev // 2
        row, feat = lax.axis_index("row"), lax.axis_index("feat")
        starts = (jnp.asarray(relative, jnp.int32) ^ feat) * (row_block // feats_n)
        def sources(chosen):
            table = [[source(r, *slot) for slot in chosen] for r in range(rows_n)]
            return jnp.asarray(table, jnp.int32)[row]

        places, white_places = sources(slots), sources(white_slots)
        block = (row % per_feat)[None]
        apart = feat ^ (row // per_feat)

        def pieces_of(chosen):
            return [p for slot in chosen for p in chunks[slot]]

        def column_far(mine):
            for bit in reversed(far_bits):
                got = send(mine, perm(
                    lambda r, f: (r, f ^ bit),
                    lambda r, f: (f ^ (r // per_feat)) % (2 * bit) == 0,
                ))
                if len(far_bits) > 1:
                    mine = got = jnp.where(apart % (2 * bit) == 0, mine, got)
            return got

        def to_far(near):
            keep, away = halve(starts, *near)
            for bit in far_bits[:-1]:
                keep, away = halve(starts, keep, swap(away, 0, bit))
            return keep, swap(away, 0, far_bits[-1])

        chunks = {(0, 0): [candidates]}
        small = jnp.stack([weights, strata.astype(jnp.float32)])
        small_all = jnp.where((jnp.arange(rows_n) == row)[:, None, None], small[None], 0.0)
        small_bits = list(row_bits)

        columns, far_columns, white, near, far = [], [], [], [], []
        for k in range(hi_n + 1):
            fresh, out = [], {}
            if k > 0:
                last = k == hi_n - 1
                picked = pick(block, pieces_of(groups[k - 1]), row_block, half if last else 0)
                columns.append(picked[0])
            if k < hi_n - 1:
                fresh.append((k + 1, 0))
                chunks[k + 1, 0] = [send(chunks[k, 0][0], hi_pairs)]
                held = chunks[k, 0][0]
                for s in range(1, lo_n):
                    fresh.append((k, s))
                    held = send(held, lo_pairs)
                    chunks[k, s] = [held]
            elif k < hi_n:
                held = picked[1]
                for s in range(1, lo_n):
                    fresh.append((k, s))
                    held = send(held, lo_pairs)
                    chunks[k, s] = [held, send(picked[1 + s], hi_pairs)]
            out["fresh"] = [chunks[slot] for slot in fresh]
            if small_bits:
                bit = small_bits.pop(0)
                out["small"] = small_all + swap(small_all, bit, 0)
            if k > 0:
                out["column"] = column_far(columns[-1])
                out["white"] = whiten(starts, inv_factor, pieces_of(white_groups[k - 1]))
            if k > 1:
                keep, away = white[k - 2]
                out["near"] = keep, swap(away, 0, 1)
            if k > 2:
                out["far"] = to_far(near[k - 3])
            out = fence(out)
            for slot, value in zip(fresh, out["fresh"]):
                chunks[slot] = value
            small_all = out.get("small", small_all)
            for name, kept in (("column", far_columns), ("white", white), ("near", near), ("far", far)):
                if name in out:
                    kept.append(out[name])
        while small_bits:
            small_all = small_all + swap(small_all, small_bits.pop(0), 0)

        keep, away = white[-1]
        packed = pack((apart == 0).astype(jnp.int32)[None], columns, far_columns)
        last, before, packed = fence(((keep, swap(away, 0, 1)), to_far(near[-1]), packed))
        far.append(before)
        last, beside = fence((to_far(last), swap(packed, 0, 1)))
        far.append(last)
        total = squares(white_places, far, [len(g) for g in white_groups], rows_dev)
        total = fence(total + swap(total, 0, 1))
        column_t = join((apart % 2 == 0).astype(jnp.int32)[None], packed, beside)
        bits = [(0, bit) for bit in far_bits] + [(bit, 0) for bit in row_bits]
        for i, bit in enumerate(bits):
            total = total + swap(total, *bit)
            if i == 0:
                total, column_t = fence((total, column_t))

        step_wide, new_weight, leverage = weight_step(
            row[None], total, small_all[:, 0], small_all[:, 1], features
        )
        piece_starts = []
        for i, slot in enumerate(slots):
            place = places[i] * rows_dev
            for piece in chunks[slot]:
                piece_starts.append(place)
                place = place + piece.shape[0]
        information = increment(jnp.stack(piece_starts), step_wide, column_t, pieces_of(slots))
        return (new_weight.reshape(rows_dev), leverage.reshape(rows_dev), information)

    return per_device


def solution(mesh):
    in_specs = (P("row", "feat"), P("row", "feat"), P("row"), P("row"))
    out_specs = (P("row"), P("row"), P("row", "feat"))
    return jax.shard_map(
        make(mesh), mesh=mesh, in_specs=in_specs, out_specs=out_specs, check_vma=False
    )
```

time: 157 us -> 150 us (0.955)
  Pallas kernels: 68.3 us -> 56 us
  local copies, waits for them, and re-layouts: 19.9 us -> 26.5 us
  starting transfers between devices: 38.7 us -> 36.5 us
    pallas_call x13 -> x17, Pallas kernels: 68.3 us -> 56 us  [call(): pl.pallas_call(kernel, in_specs=[pl.BlockSpec(memory_space=pltpu.SMEM)] +...]
    unnamed x70 -> x88, local copies, waits for them, and re-layouts: 14.8 us -> 25 us
    slice x10 -> x0, local copies, waits for them, and re-layouts: 3.68 us -> none  [the longest x8 3.64 us: halve(): return (part[:left], part[left:].astype(jnp.bfloat16))]
    ppermute x31 -> x29, starting transfers between devices: 38.7 us -> 36.5 us  [send(): return lax.ppermute(x, BOTH, pairs)]
    ppermute x31 -> x29, waiting for transfers between devices: 20.5 us -> 21 us  [send(): return lax.ppermute(x, BOTH, pairs)]
  transfers between devices with their start and end apart: 31 -> 29, of which waited for: 7 -> 7; matrix products, arithmetic and copies ran while one was open for 4% -> 2% of each run, Pallas kernels for 33% -> 26%
where the time goes in v3:
time: 150 us; the launch traced here: 148 us
  Pallas kernels  56 us (37%)
  starting transfers between devices  36.5 us (24%)
  local copies, waits for them, and re-layouts  26.5 us (18%)
  waiting for transfers between devices  21 us (14%)
  between operations  6.4 us (4%)
  other arithmetic  2.16 us (1%)
    pallas_call x17, Pallas kernels, call(): pl.pallas_call(kernel, in_specs=[pl.BlockSpec(memory_space=pltpu.SMEM)] +...  56 us
    ppermute x29, starting transfers between devices, send(): return lax.ppermute(x, BOTH, pairs)  36.5 us
    unnamed x88, local copies, waits for them, and re-layouts  25 us
    ppermute x29, waiting for transfers between devices, send(): return lax.ppermute(x, BOTH, pairs)  21 us
  transfers between devices with their start and end apart: 29, of which 7 were waited for; matrix products, arithmetic and copies ran while one was open for 2% of the time, Pallas kernels for 26%

profile of v3, /device:TPU:0, one launch (start us, length us, event | category | flops | bytes accessed | tf_op | source)
XLA Modules:
  0.0 148.5 jit_solution(16075727779750972939)
XLA Ops:
  0.6 3.0 %collective-permute-start.1 = (bf16[64,4096]{1,0:T(8,128)(2,1)}, bf16[64,4096]{1,0:T(8,128)(2,1)S(1)}, u32[]{:S(2)}, u32[]{:S(2)}) collective-permute-start(bf16[64,4096]{1,0:T(8,128)(2,1)} %refs_0_.5), channel_id=1, source_target_pairs={{0,4},{1,5},{2,6},{3,7},{4,0},{5,1},{6,2},{7,3},{8,12},{9,13},{10,... | collective-permute-start | bytes 1572872 | tf_op jit(solution)/shard_map/ppermute | solution.py:332
  3.6 2.6 %collective-permute-start = (bf16[64,4096]{1,0:T(8,128)(2,1)}, bf16[64,4096]{1,0:T(8,128)(2,1)S(1)}, u32[]{:S(2)}, u32[]{:S(2)}) collective-permute-start(bf16[64,4096]{1,0:T(8,128)(2,1)} %refs_0_.5), channel_id=1, source_target_pairs={{0,16},{1,17},{2,18},{3,19},{4,20},{5,21},{6,22},{7,23},{8,0},{9,1... | collective-permute-start | bytes 1572872 | tf_op jit(solution)/shard_map/ppermute | solution.py:332
  8.8 7.1 %collective-permute-done.2 = f32[8,2,64]{2,0,1:T(8,128)S(1)} collective-permute-done((f32[8,2,64]{2,0,1:T(8,128)S(1)}, f32[8,2,64]{2,0,1:T(8,128)S(1)}, u32[]{:S(2)}, u32[]{:S(2)}) %collective-permute-start.2) | collective-permute-done | bytes 4128 | tf_op jit(solution)/shard_map/ppermute | solution.py:332
  16.0 1.4 collective-permute-done.refs_2_.refs_0_
  18.0 3.3 %collective-permute-start.4 = (bf16[64,4096]{1,0:T(8,128)(2,1)S(1)}, bf16[64,4096]{1,0:T(8,128)(2,1)S(1)}, u32[]{:S(2)}, u32[]{:S(2)}) collective-permute-start(bf16[64,4096]{1,0:T(8,128)(2,1)S(1)} %collective-permute-done.refs_2_.refs_0_), channel_id=1, source_target_pairs={{0,16},{1,17},{2,18},{3,19},{4,20},{5,21},{6,22},{7,23},{8,0},{9,1... | collective-permute-start | bytes 1572872 | tf_op jit(solution)/shard_map/ppermute | solution.py:332
  21.3 1.0 copy-done.2
  22.4 3.6 %collective-permute-start.3 = (bf16[192,2048]{1,0:T(8,128)(2,1)S(1)}, bf16[192,2048]{1,0:T(8,128)(2,1)S(1)}, u32[]{:S(2)}, u32[]{:S(2)}) collective-permute-start(bf16[192,2048]{1,0:T(8,128)(2,1)S(1)} %pick.4.refs_0_), channel_id=1, source_target_pairs={{0,2},{4,6},{9,11},{13,15},{18,16},{22,20},{27,25},{31,29}} | collective-permute-start | bytes 2359304 | tf_op jit(solution)/shard_map/ppermute | solution.py:332
  26.0 8.2 %whiten.4 = (f32[1024,128]{1,0:T(8,128)S(1)}, bf16[1024,128]{1,0:T(8,128)(2,1)S(1)}) custom-call(s32[4]{0:T(128)S(1)} %xor_multiply_fusion.starts_ref._, bf16[2048,4096]{1,0:T(8,128)(2,1)} %f_ref.7, bf16[64,4096]{1,0:T(8,128)(2,1)S(1)} %copy-done.3, bf16[64,4096]{1,0:T(8,128)(2,1)S(1)} %collective-permute-done.1.refs_1_), custom_call_target="tpu_custom_call" | custom-call | flops 8589934592 | bytes 1000 | tf_op jit(solution)/shard_map/whiten/pallas_call | solution.py:31
  34.3 1.1 collective-permute-done.3.refs_4_
  36.3 1.5 %collective-permute-start.9 = (bf16[64,4096]{1,0:T(8,128)(2,1)S(1)}, bf16[64,4096]{1,0:T(8,128)(2,1)S(1)}, u32[]{:S(2)}, u32[]{:S(2)}) collective-permute-start(bf16[64,4096]{1,0:T(8,128)(2,1)S(1)} %collective-permute-done.4.refs_1_.refs_0_.refs_4_), channel_id=1, source_target_pairs={{0,4},{1,5},{2,6},{3,7},{4,0},{5,1},{6,2},{7,3},{8,12},{9,13},{10,... | collective-permute-start | bytes 1572872 | tf_op jit(solution)/shard_map/ppermute | solution.py:332
  37.8 2.9 %collective-permute-start.8 = (bf16[64,4096]{1,0:T(8,128)(2,1)S(1)}, bf16[64,4096]{1,0:T(8,128)(2,1)S(1)}, u32[]{:S(2)}, u32[]{:S(2)}) collective-permute-start(bf16[64,4096]{1,0:T(8,128)(2,1)S(1)} %collective-permute-done.4.refs_1_.refs_0_.refs_4_), channel_id=1, source_target_pairs={{0,16},{1,17},{2,18},{3,19},{4,20},{5,21},{6,22},{7,23},{8,0},{9,1... | collective-permute-start | bytes 1572872 | tf_op jit(solution)/shard_map/ppermute | solution.py:332
  40.8 1.5 %collective-permute-start.7 = (bf16[128,2048]{1,0:T(8,128)(2,1)S(1)}, bf16[128,2048]{1,0:T(8,128)(2,1)S(1)}, u32[]{:S(2)}, u32[]{:S(2)}) collective-permute-start(bf16[128,2048]{1,0:T(8,128)(2,1)S(1)} %pick.5.refs_1_), channel_id=1, source_target_pairs={{0,2},{4,6},{9,11},{13,15},{18,16},{22,20},{27,25},{31,29}} | collective-permute-start | bytes 1572872 | tf_op jit(solution)/shard_map/ppermute | solution.py:332
  42.3 8.2 %whiten.5 = (f32[1024,128]{1,0:T(8,128)S(1)}, bf16[1024,128]{1,0:T(8,128)(2,1)S(1)}) custom-call(s32[4]{0:T(128)S(1)} %xor_multiply_fusion.starts_ref._, bf16[2048,4096]{1,0:T(8,128)(2,1)} %f_ref.7, bf16[64,4096]{1,0:T(8,128)(2,1)S(1)} %collective-permute-done.refs_2_.refs_0_, bf16[64,4096]{1,0:T(8,128)(2,1)S(1)} %collective-permute-done.5.refs_0_.refs_1_.refs_3_), custom_call_target="tpu_custom_call" | custom-call | flops 8589934592 | bytes 1000 | tf_op jit(solution)/shard_map/whiten/pallas_call | solution.py:31
  52.8 4.5 %collective-permute-start.15 = (bf16[32,4096]{1,0:T(8,128)(2,1)S(1)}, bf16[32,4096]{1,0:T(8,128)(2,1)S(1)}, u32[]{:S(2)}, u32[]{:S(2)}) collective-permute-start(bf16[32,4096]{1,0:T(8,128)(2,1)S(1)} %get-tuple-element.88), channel_id=1, source_target_pairs={{0,16},{1,17},{2,18},{3,19},{4,20},{5,21},{6,22},{7,23},{8,0},{9,1... | collective-permute-start | bytes 786440 | tf_op jit(solution)/shard_map/ppermute | solution.py:332
  57.3 2.7 %collective-permute-start.12 = (bf16[128,2048]{1,0:T(8,128)(2,1)S(1)}, bf16[128,2048]{1,0:T(8,128)(2,1)S(1)}, u32[]{:S(2)}, u32[]{:S(2)}) collective-permute-start(bf16[128,2048]{1,0:T(8,128)(2,1)S(1)} %get-tuple-element.82.refs_2_), channel_id=1, source_target_pairs={{0,2},{4,6},{9,11},{13,15},{18,16},{22,20},{27,25},{31,29}} | collective-permute-start | bytes 1572872 | tf_op jit(solution)/shard_map/ppermute | solution.py:332
  60.1 8.2 %whiten.6 = (f32[1024,128]{1,0:T(8,128)S(1)}, bf16[1024,128]{1,0:T(8,128)(2,1)S(1)}) custom-call(s32[4]{0:T(128)S(1)} %xor_multiply_fusion.starts_ref._, bf16[2048,4096]{1,0:T(8,128)(2,1)} %f_ref.7, bf16[64,4096]{1,0:T(8,128)(2,1)S(1)} %collective-permute-done.4.refs_1_.refs_0_.refs_4_, bf16[64,4096]{1,0:T(8,128)(2,1)S(1)} %collective-permute-done.9.refs_0_.refs_1_.refs_5_), custom_call_target="tpu_custom_call" | custom-call | flops 8589934592 | bytes 1000 | tf_op jit(solution)/shard_map/whiten/pallas_call | solution.py:31
  68.5 2.7 %collective-permute-start.17 = (bf16[64,2048]{1,0:T(8,128)(2,1)S(1)}, bf16[64,2048]{1,0:T(8,128)(2,1)S(1)}, u32[]{:S(2)}, u32[]{:S(2)}) collective-permute-start(bf16[64,2048]{1,0:T(8,128)(2,1)S(1)} %pick.7.refs_3_), channel_id=1, source_target_pairs={{0,2},{4,6},{9,11},{13,15},{18,16},{22,20},{27,25},{31,29}} | collective-permute-start | bytes 786440 | tf_op jit(solution)/shard_map/ppermute | solution.py:332
  72.5 8.3 %whiten.7 = (f32[1024,128]{1,0:T(8,128)S(1)}, bf16[1024,128]{1,0:T(8,128)(2,1)}) custom-call(s32[4]{0:T(128)S(1)} %xor_multiply_fusion.starts_ref._, bf16[2048,4096]{1,0:T(8,128)(2,1)} %f_ref.7, bf16[64,4096]{1,0:T(8,128)(2,1)S(1)} %collective-permute-done.8.refs_1_.refs_0_.refs_6_, bf16[32,4096]{1,0:T(8,128)(2,1)S(1)} %collective-permute-done.14.refs_0_.refs_1_.refs_7_, ...), custom_call_target="tpu_custom_call" | custom-call | flops 8589934592 | bytes 1000 | tf_op jit(solution)/shard_map/whiten/pallas_call | solution.py:31
  82.2 1.2 halve.6
  84.2 1.7 %collective-permute-start.21 = (bf16[512,128]{1,0:T(8,128)(2,1)}, bf16[512,128]{1,0:T(8,128)(2,1)}, u32[]{:S(2)}, u32[]{:S(2)}) collective-permute-start(bf16[512,128]{1,0:T(8,128)(2,1)} %get-tuple-element.112), channel_id=1, source_target_pairs={{0,2},{1,3},{2,0},{3,1},{4,6},{5,7},{6,4},{7,5},{8,10},{9,11},{10,... | collective-permute-start | bytes 393224 | tf_op jit(solution)/shard_map/ppermute | solution.py:332
  86.0 1.0 copy-done.17
  87.0 0.9 copy-done.23
  88.0 1.1 copy-done.25
  89.1 1.0 copy-done.27
  90.1 1.0 copy-done.29
  91.2 1.0 copy-done.31
  92.2 0.9 copy-done.35
  94.2 1.0 halve.7
  96.3 4.4 %collective-permute-done.22.refs_7_ = bf16[512,128]{1,0:T(8,128)(2,1)S(1)} collective-permute-done((bf16[512,128]{1,0:T(8,128)(2,1)S(1)}, bf16[512,128]{1,0:T(8,128)(2,1)S(1)}, u32[]{:S(2)}, u32[]{:S(2)}) %collective-permute-start.22) | collective-permute-done | bytes 131104 | tf_op jit(solution)/shard_map/ppermute | solution.py:332
  100.7 0.9 copy-done.37
  101.7 0.9 copy-done.39
  102.6 0.9 copy-done.41
  104.5 1.2 squares.1
  105.7 1.2 collective-permute-done.24
  107.1 2.3 %join.1.col_ref = bf16[2048,512]{1,0:T(8,128)(2,1)S(1)} custom-call(s32[1]{0:T(128)} %bitcast.6.flag_ref, bf16[512,2048]{1,0:T(8,128)(2,1)S(1)} %pack.1.own_ref, bf16[512,2048]{1,0:T(8,128)(2,1)} %collective-permute-done.23.other_ref), custom_call_target="tpu_custom_call" | custom-call | flops 1000 | bytes 1000 | tf_op jit(solution)/shard_map/join/pallas_call | solution.py:31
  109.4 1.3 copy-done
  110.7 1.5 %collective-permute-start.26 = (f32[8,64]{1,0:T(8,128)S(1)}, f32[8,64]{1,0:T(8,128)S(1)}, u32[]{:S(2)}, u32[]{:S(2)}) collective-permute-start(f32[8,64]{1,0:T(8,128)S(1)} %add.46), channel_id=1, source_target_pairs={{0,4},{1,5},{2,6},{3,7},{4,0},{5,1},{6,2},{7,3},{8,12},{9,13},{10,... | collective-permute-start | bytes 6152 | tf_op jit(solution)/shard_map/ppermute | solution.py:332
  112.2 2.1 %collective-permute-done.26 = f32[8,64]{1,0:T(8,128)S(1)} collective-permute-done((f32[8,64]{1,0:T(8,128)S(1)}, f32[8,64]{1,0:T(8,128)S(1)}, u32[]{:S(2)}, u32[]{:S(2)}) %collective-permute-start.26) | collective-permute-done | bytes 2080 | tf_op jit(solution)/shard_map/ppermute | solution.py:332
  120.3 1.0 collective-permute-start.28
  121.3 3.6 %collective-permute-done.28 = f32[8,64]{1,0:T(8,128)S(1)} collective-permute-done((f32[8,64]{1,0:T(8,128)S(1)}, f32[8,64]{1,0:T(8,128)S(1)}, u32[]{:S(2)}, u32[]{:S(2)}) %collective-permute-start.28) | collective-permute-done | bytes 2080 | tf_op jit(solution)/shard_map/ppermute | solution.py:332
  125.6 1.6 %copy-done.1 = bf16[2048,512]{1,0:T(8,128)(2,1)S(1)} copy-done((bf16[2048,512]{1,0:T(8,128)(2,1)S(1)}, bf16[2048,512]{1,0:T(8,128)(2,1)}, u32[]{:S(2)}) %copy-start.1) | copy-done | bytes 2097176
  127.2 1.0 copy-done.7
  128.2 1.0 copy-done.9
  129.2 1.0 copy-done.11
  130.3 1.0 copy-done.13
  131.3 1.0 copy-done.15
  132.4 0.9 copy-done.21
  133.3 15.2 %increment.1 = f32[2048,4096]{1,0:T(8,128)} custom-call(s32[9]{0:T(128)S(1)} %stack.51.starts_ref, f32[512,128]{1,0:T(8,128)S(1)} %get-tuple-element.131.d_ref, bf16[2048,512]{1,0:T(8,128)(2,1)S(1)} %copy-done.1, bf16[64,4096]{1,0:T(8,128)(2,1)S(1)} %copy-done.3, bf16[64,4096]{1,0:T(8,128)(2,1)S(1)} %copy-done.5, bf16[64,4096]{1,0:T(8,128)(2,1)S(1)} %copy-done.7, ...), custom_call_target="tpu_custom_call" | custom-call | flops 1000 | bytes 1000 | tf_op jit(solution)/shard_map/increment/pallas_call | solution.py:31
  (132 shorter events, 14.7 us)
Async XLA Ops:
  0.6 15.4 %collective-permute-start.1 = (bf16[64,4096]{1,0:T(8,128)(2,1)}, bf16[64,4096]{1,0:T(8,128)(2,1)S(1)}, u32[]{:S(2)}, u32[]{:S(2)}) collective-permute-start(bf16[64,4096]{1,0:T(8,128)(2,1)} %refs_0_.5), channel_id=1, source_target_pairs={{0,4},{1,5},{2,6},{3,7},{4,0},{5,1},{6,2},{7,3},{8,12},{9,13},{10,... | collective-permute-start | bytes 1572872 | tf_op jit(solution)/shard_map/ppermute | solution.py:332
  3.6 13.8 %collective-permute-start = (bf16[64,4096]{1,0:T(8,128)(2,1)}, bf16[64,4096]{1,0:T(8,128)(2,1)S(1)}, u32[]{:S(2)}, u32[]{:S(2)}) collective-permute-start(bf16[64,4096]{1,0:T(8,128)(2,1)} %refs_0_.5), channel_id=1, source_target_pairs={{0,16},{1,17},{2,18},{3,19},{4,20},{5,21},{6,22},{7,23},{8,0},{9,1... | collective-permute-start | bytes 1572872 | tf_op jit(solution)/shard_map/ppermute | solution.py:332
  7.6 8.3 %collective-permute-start.2 = (f32[8,2,64]{2,0,1:T(8,128)S(1)}, f32[8,2,64]{2,0,1:T(8,128)S(1)}, u32[]{:S(2)}, u32[]{:S(2)}) collective-permute-start(f32[8,2,64]{2,0,1:T(8,128)S(1)} %broadcast_select_fusion), channel_id=1, source_target_pairs={{0,4},{1,5},{2,6},{3,7},{4,0},{5,1},{6,2},{7,3},{8,12},{9,13},{10,... | collective-permute-start | bytes 12296 | tf_op jit(solution)/shard_map/ppermute | solution.py:332
  16.0 18.2 %copy-start.4 = (bf16[64,4096]{1,0:T(8,128)(2,1)}, bf16[64,4096]{1,0:T(8,128)(2,1)S(1)}, u32[]{:S(2)}) copy-start(bf16[64,4096]{1,0:T(8,128)(2,1)S(1)} %collective-permute-done.1.refs_1_) | copy-start | bytes 1572868
  17.4 24.8 %copy-start.6 = (bf16[64,4096]{1,0:T(8,128)(2,1)}, bf16[64,4096]{1,0:T(8,128)(2,1)S(1)}, u32[]{:S(2)}) copy-start(bf16[64,4096]{1,0:T(8,128)(2,1)S(1)} %collective-permute-done.refs_2_.refs_0_) | copy-start | bytes 1572868
  17.4 16.8 %collective-permute-start.5 = (bf16[64,4096]{1,0:T(8,128)(2,1)S(1)}, bf16[64,4096]{1,0:T(8,128)(2,1)S(1)}, u32[]{:S(2)}, u32[]{:S(2)}) collective-permute-start(bf16[64,4096]{1,0:T(8,128)(2,1)S(1)} %collective-permute-done.refs_2_.refs_0_), channel_id=1, source_target_pairs={{0,4},{1,5},{2,6},{3,7},{4,0},{5,1},{6,2},{7,3},{8,12},{9,13},{10,... | collective-permute-start | bytes 1572872 | tf_op jit(solution)/shard_map/ppermute | solution.py:332
  18.0 16.3 %collective-permute-start.4 = (bf16[64,4096]{1,0:T(8,128)(2,1)S(1)}, bf16[64,4096]{1,0:T(8,128)(2,1)S(1)}, u32[]{:S(2)}, u32[]{:S(2)}) collective-permute-start(bf16[64,4096]{1,0:T(8,128)(2,1)S(1)} %collective-permute-done.refs_2_.refs_0_), channel_id=1, source_target_pairs={{0,16},{1,17},{2,18},{3,19},{4,20},{5,21},{6,22},{7,23},{8,0},{9,1... | collective-permute-start | bytes 1572872 | tf_op jit(solution)/shard_map/ppermute | solution.py:332
  21.3 13.0 %collective-permute-start.6 = (f32[8,2,64]{2,0,1:T(8,128)S(1)}, f32[8,2,64]{2,0,1:T(8,128)S(1)}, u32[]{:S(2)}, u32[]{:S(2)}) collective-permute-start(f32[8,2,64]{2,0,1:T(8,128)S(1)} %fusion), channel_id=1, source_target_pairs={{0,8},{1,9},{2,10},{3,11},{4,12},{5,13},{6,14},{7,15},{8,0},{9,1},... | collective-permute-start | bytes 12296 | tf_op jit(solution)/shard_map/ppermute | solution.py:332
  22.3 3.7 %copy-start.3 = (bf16[64,4096]{1,0:T(8,128)(2,1)S(1)}, bf16[64,4096]{1,0:T(8,128)(2,1)}, u32[]{:S(2)}) copy-start(bf16[64,4096]{1,0:T(8,128)(2,1)} %refs_0_.5) | copy-start | bytes 1572868
  22.4 13.1 %collective-permute-start.3 = (bf16[192,2048]{1,0:T(8,128)(2,1)S(1)}, bf16[192,2048]{1,0:T(8,128)(2,1)S(1)}, u32[]{:S(2)}, u32[]{:S(2)}) collective-permute-start(bf16[192,2048]{1,0:T(8,128)(2,1)S(1)} %pick.4.refs_0_), channel_id=1, source_target_pairs={{0,2},{4,6},{9,11},{13,15},{18,16},{22,20},{27,25},{31,29}} | collective-permute-start | bytes 2359304 | tf_op jit(solution)/shard_map/ppermute | solution.py:332
  34.3 16.3 %copy-start.8 = (bf16[64,4096]{1,0:T(8,128)(2,1)}, bf16[64,4096]{1,0:T(8,128)(2,1)S(1)}, u32[]{:S(2)}) copy-start(bf16[64,4096]{1,0:T(8,128)(2,1)S(1)} %collective-permute-done.5.refs_0_.refs_1_.refs_3_) | copy-start | bytes 1572868
  34.3 25.8 %copy-start.10 = (bf16[64,4096]{1,0:T(8,128)(2,1)}, bf16[64,4096]{1,0:T(8,128)(2,1)S(1)}, u32[]{:S(2)}) copy-start(bf16[64,4096]{1,0:T(8,128)(2,1)S(1)} %collective-permute-done.4.refs_1_.refs_0_.refs_4_) | copy-start | bytes 1572868
  36.3 14.3 %collective-permute-start.9 = (bf16[64,4096]{1,0:T(8,128)(2,1)S(1)}, bf16[64,4096]{1,0:T(8,128)(2,1)S(1)}, u32[]{:S(2)}, u32[]{:S(2)}) collective-permute-start(bf16[64,4096]{1,0:T(8,128)(2,1)S(1)} %collective-permute-done.4.refs_1_.refs_0_.refs_4_), channel_id=1, source_target_pairs={{0,4},{1,5},{2,6},{3,7},{4,0},{5,1},{6,2},{7,3},{8,12},{9,13},{10,... | collective-permute-start | bytes 1572872 | tf_op jit(solution)/shard_map/ppermute | solution.py:332
  37.8 12.8 %collective-permute-start.8 = (bf16[64,4096]{1,0:T(8,128)(2,1)S(1)}, bf16[64,4096]{1,0:T(8,128)(2,1)S(1)}, u32[]{:S(2)}, u32[]{:S(2)}) collective-permute-start(bf16[64,4096]{1,0:T(8,128)(2,1)S(1)} %collective-permute-done.4.refs_1_.refs_0_.refs_4_), channel_id=1, source_target_pairs={{0,16},{1,17},{2,18},{3,19},{4,20},{5,21},{6,22},{7,23},{8,0},{9,1... | collective-permute-start | bytes 1572872 | tf_op jit(solution)/shard_map/ppermute | solution.py:332
  40.7 9.9 %collective-permute-start.11 = (f32[8,2,64]{2,0,1:T(8,128)S(1)}, f32[8,2,64]{2,0,1:T(8,128)S(1)}, u32[]{:S(2)}, u32[]{:S(2)}) collective-permute-start(f32[8,2,64]{2,0,1:T(8,128)S(1)} %add.43), channel_id=1, source_target_pairs={{0,16},{1,17},{2,18},{3,19},{4,20},{5,21},{6,22},{7,23},{8,24},{9,... | collective-permute-start | bytes 12296 | tf_op jit(solution)/shard_map/ppermute | solution.py:332
  40.7 9.9 %collective-permute-start.10 = (bf16[1024,128]{1,0:T(8,128)(2,1)S(1)}, bf16[1024,128]{1,0:T(8,128)(2,1)S(1)}, u32[]{:S(2)}, u32[]{:S(2)}) collective-permute-start(bf16[1024,128]{1,0:T(8,128)(2,1)S(1)} %get-tuple-element.76), channel_id=1, source_target_pairs={{0,1},{1,0},{2,3},{3,2},{4,5},{5,4},{6,7},{7,6},{8,9},{9,8},{10,11... | collective-permute-start | bytes 786440 | tf_op jit(solution)/shard_map/ppermute | solution.py:332
  40.7 9.8 %copy-start.16 = (bf16[128,2048]{1,0:T(8,128)(2,1)}, bf16[128,2048]{1,0:T(8,128)(2,1)S(1)}, u32[]{:S(2)}) copy-start(bf16[128,2048]{1,0:T(8,128)(2,1)S(1)} %pick.5.refs_1_) | copy-start | bytes 1572868
  40.8 9.8 %collective-permute-start.7 = (bf16[128,2048]{1,0:T(8,128)(2,1)S(1)}, bf16[128,2048]{1,0:T(8,128)(2,1)S(1)}, u32[]{:S(2)}, u32[]{:S(2)}) collective-permute-start(bf16[128,2048]{1,0:T(8,128)(2,1)S(1)} %pick.5.refs_1_), channel_id=1, source_target_pairs={{0,2},{4,6},{9,11},{13,15},{18,16},{22,20},{27,25},{31,29}} | collective-permute-start | bytes 1572872 | tf_op jit(solution)/shard_map/ppermute | solution.py:332
  50.6 17.7 %copy-start.26 = (bf16[128,2048]{1,0:T(8,128)(2,1)}, bf16[128,2048]{1,0:T(8,128)(2,1)S(1)}, u32[]{:S(2)}) copy-start(bf16[128,2048]{1,0:T(8,128)(2,1)S(1)} %collective-permute-done.7.refs_5_) | copy-start | bytes 1572868
  50.6 17.7 %copy-start.12 = (bf16[64,4096]{1,0:T(8,128)(2,1)}, bf16[64,4096]{1,0:T(8,128)(2,1)S(1)}, u32[]{:S(2)}) copy-start(bf16[64,4096]{1,0:T(8,128)(2,1)S(1)} %collective-permute-done.9.refs_0_.refs_1_.refs_5_) | copy-start | bytes 1572868
  50.6 21.9 %copy-start.14 = (bf16[64,4096]{1,0:T(8,128)(2,1)}, bf16[64,4096]{1,0:T(8,128)(2,1)S(1)}, u32[]{:S(2)}) copy-start(bf16[64,4096]{1,0:T(8,128)(2,1)S(1)} %collective-permute-done.8.refs_1_.refs_0_.refs_6_) | copy-start | bytes 1572868
  51.2 6.1 %copy-start.36 = (f32[512,128]{1,0:T(8,128)}, f32[512,128]{1,0:T(8,128)S(1)}, u32[]{:S(2)}) copy-start(f32[512,128]{1,0:T(8,128)S(1)} %get-tuple-element.93.refs_0_) | copy-start | bytes 786436
  51.2 17.1 %collective-permute-start.13 = (bf16[512,128]{1,0:T(8,128)(2,1)S(1)}, bf16[512,128]{1,0:T(8,128)(2,1)S(1)}, u32[]{:S(2)}, u32[]{:S(2)}) collective-permute-start(bf16[512,128]{1,0:T(8,128)(2,1)S(1)} %get-tuple-element.86), channel_id=1, source_target_pairs={{0,2},{1,3},{2,0},{3,1},{4,6},{5,7},{6,4},{7,5},{8,10},{9,11},{10,... | collective-permute-start | bytes 393224 | tf_op jit(solution)/shard_map/ppermute | solution.py:332
  52.1 16.2 %collective-permute-start.16 = (bf16[1024,128]{1,0:T(8,128)(2,1)S(1)}, bf16[1024,128]{1,0:T(8,128)(2,1)S(1)}, u32[]{:S(2)}, u32[]{:S(2)}) collective-permute-start(bf16[1024,128]{1,0:T(8,128)(2,1)S(1)} %get-tuple-element.90), channel_id=1, source_target_pairs={{0,1},{1,0},{2,3},{3,2},{4,5},{5,4},{6,7},{7,6},{8,9},{9,8},{10,11... | collective-permute-start | bytes 786440 | tf_op jit(solution)/shard_map/ppermute | solution.py:332
  52.2 16.1 %copy-start.28 = (bf16[128,2048]{1,0:T(8,128)(2,1)}, bf16[128,2048]{1,0:T(8,128)(2,1)S(1)}, u32[]{:S(2)}) copy-start(bf16[128,2048]{1,0:T(8,128)(2,1)S(1)} %get-tuple-element.82.refs_2_) | copy-start | bytes 1572868
  52.2 16.2 %collective-permute-start.14 = (bf16[32,4096]{1,0:T(8,128)(2,1)S(1)}, bf16[32,4096]{1,0:T(8,128)(2,1)S(1)}, u32[]{:S(2)}, u32[]{:S(2)}) collective-permute-start(bf16[32,4096]{1,0:T(8,128)(2,1)S(1)} %get-tuple-element.87), channel_id=1, source_target_pairs={{0,4},{1,5},{2,6},{3,7},{4,0},{5,1},{6,2},{7,3},{8,12},{9,13},{10,... | collective-permute-start | bytes 786440 | tf_op jit(solution)/shard_map/ppermute | solution.py:332
  52.8 15.6 %collective-permute-start.15 = (bf16[32,4096]{1,0:T(8,128)(2,1)S(1)}, bf16[32,4096]{1,0:T(8,128)(2,1)S(1)}, u32[]{:S(2)}, u32[]{:S(2)}) collective-permute-start(bf16[32,4096]{1,0:T(8,128)(2,1)S(1)} %get-tuple-element.88), channel_id=1, source_target_pairs={{0,16},{1,17},{2,18},{3,19},{4,20},{5,21},{6,22},{7,23},{8,0},{9,1... | collective-permute-start | bytes 786440 | tf_op jit(solution)/shard_map/ppermute | solution.py:332
  57.3 11.1 %collective-permute-start.12 = (bf16[128,2048]{1,0:T(8,128)(2,1)S(1)}, bf16[128,2048]{1,0:T(8,128)(2,1)S(1)}, u32[]{:S(2)}, u32[]{:S(2)}) collective-permute-start(bf16[128,2048]{1,0:T(8,128)(2,1)S(1)} %get-tuple-element.82.refs_2_), channel_id=1, source_target_pairs={{0,2},{4,6},{9,11},{13,15},{18,16},{22,20},{27,25},{31,29}} | collective-permute-start | bytes 1572872 | tf_op jit(solution)/shard_map/ppermute | solution.py:332
  68.4 12.4 %copy-start.18 = (bf16[32,4096]{1,0:T(8,128)(2,1)}, bf16[32,4096]{1,0:T(8,128)(2,1)S(1)}, u32[]{:S(2)}) copy-start(bf16[32,4096]{1,0:T(8,128)(2,1)S(1)} %collective-permute-done.14.refs_0_.refs_1_.refs_7_) | copy-start | bytes 786436
  68.4 12.4 %copy-start.20 = (bf16[32,4096]{1,0:T(8,128)(2,1)}, bf16[32,4096]{1,0:T(8,128)(2,1)S(1)}, u32[]{:S(2)}) copy-start(bf16[32,4096]{1,0:T(8,128)(2,1)S(1)} %collective-permute-done.15.refs_1_.refs_2_.refs_8_) | copy-start | bytes 786436
  68.4 12.4 %copy-start.30 = (bf16[128,2048]{1,0:T(8,128)(2,1)}, bf16[128,2048]{1,0:T(8,128)(2,1)S(1)}, u32[]{:S(2)}) copy-start(bf16[128,2048]{1,0:T(8,128)(2,1)S(1)} %collective-permute-done.12.refs_6_) | copy-start | bytes 1572868
  68.5 12.4 %copy-start.22 = (bf16[64,2048]{1,0:T(8,128)(2,1)}, bf16[64,2048]{1,0:T(8,128)(2,1)S(1)}, u32[]{:S(2)}) copy-start(bf16[64,2048]{1,0:T(8,128)(2,1)S(1)} %pick.7.refs_3_) | copy-start | bytes 786436
  68.5 13.2 %collective-permute-start.17 = (bf16[64,2048]{1,0:T(8,128)(2,1)S(1)}, bf16[64,2048]{1,0:T(8,128)(2,1)S(1)}, u32[]{:S(2)}, u32[]{:S(2)}) collective-permute-start(bf16[64,2048]{1,0:T(8,128)(2,1)S(1)} %pick.7.refs_3_), channel_id=1, source_target_pairs={{0,2},{4,6},{9,11},{13,15},{18,16},{22,20},{27,25},{31,29}} | collective-permute-start | bytes 786440 | tf_op jit(solution)/shard_map/ppermute | solution.py:332
  71.2 10.5 %collective-permute-start.19 = (bf16[1024,128]{1,0:T(8,128)(2,1)S(1)}, bf16[1024,128]{1,0:T(8,128)(2,1)S(1)}, u32[]{:S(2)}, u32[]{:S(2)}) collective-permute-start(bf16[1024,128]{1,0:T(8,128)(2,1)S(1)} %get-tuple-element.102), channel_id=1, source_target_pairs={{0,1},{1,0},{2,3},{3,2},{4,5},{5,4},{6,7},{7,6},{8,9},{9,8},{10,11... | collective-permute-start | bytes 786440 | tf_op jit(solution)/shard_map/ppermute | solution.py:332
  72.5 9.1 %collective-permute-start.18 = (bf16[512,128]{1,0:T(8,128)(2,1)S(1)}, bf16[512,128]{1,0:T(8,128)(2,1)S(1)}, u32[]{:S(2)}, u32[]{:S(2)}) collective-permute-start(bf16[512,128]{1,0:T(8,128)(2,1)S(1)} %get-tuple-element.100), channel_id=1, source_target_pairs={{0,2},{1,3},{2,0},{3,1},{4,6},{5,7},{6,4},{7,5},{8,10},{9,11},{10,... | collective-permute-start | bytes 393224 | tf_op jit(solution)/shard_map/ppermute | solution.py:332
  81.7 2.6 %copy-start.42 = (bf16[512,128]{1,0:T(8,128)(2,1)}, bf16[512,128]{1,0:T(8,128)(2,1)S(1)}, u32[]{:S(2)}) copy-start(bf16[512,128]{1,0:T(8,128)(2,1)S(1)} %collective-permute-done.18.refs_3_) | copy-start | bytes 393220
  81.7 1.8 %copy-start.34 = (bf16[64,2048]{1,0:T(8,128)(2,1)}, bf16[64,2048]{1,0:T(8,128)(2,1)S(1)}, u32[]{:S(2)}) copy-start(bf16[64,2048]{1,0:T(8,128)(2,1)S(1)} %collective-permute-done.17.refs_7_) | copy-start | bytes 786436
  81.7 11.7 %collective-permute-start.20 = (bf16[1024,128]{1,0:T(8,128)(2,1)}, bf16[1024,128]{1,0:T(8,128)(2,1)}, u32[]{:S(2)}, u32[]{:S(2)}) collective-permute-start(bf16[1024,128]{1,0:T(8,128)(2,1)} %get-tuple-element.108), channel_id=1, source_target_pairs={{0,1},{1,0},{2,3},{3,2},{4,5},{5,4},{6,7},{7,6},{8,9},{9,8},{10,11... | collective-permute-start | bytes 786440 | tf_op jit(solution)/shard_map/ppermute | solution.py:332
  84.2 9.1 %collective-permute-start.21 = (bf16[512,128]{1,0:T(8,128)(2,1)}, bf16[512,128]{1,0:T(8,128)(2,1)}, u32[]{:S(2)}, u32[]{:S(2)}) collective-permute-start(bf16[512,128]{1,0:T(8,128)(2,1)} %get-tuple-element.112), channel_id=1, source_target_pairs={{0,2},{1,3},{2,0},{3,1},{4,6},{5,7},{6,4},{7,5},{8,10},{9,11},{10,... | collective-permute-start | bytes 393224 | tf_op jit(solution)/shard_map/ppermute | solution.py:332
  93.3 7.4 %collective-permute-start.23 = (bf16[512,2048]{1,0:T(8,128)(2,1)S(1)}, bf16[512,2048]{1,0:T(8,128)(2,1)}, u32[]{:S(2)}, u32[]{:S(2)}) collective-permute-start(bf16[512,2048]{1,0:T(8,128)(2,1)S(1)} %pack.1.own_ref), channel_id=1, source_target_pairs={{0,1},{1,0},{2,3},{3,2},{4,5},{5,4},{6,7},{7,6},{8,9},{9,8},{10,11... | collective-permute-start | bytes 6291464 | tf_op jit(solution)/shard_map/ppermute | solution.py:332
  95.2 5.5 %collective-permute-start.22 = (bf16[512,128]{1,0:T(8,128)(2,1)S(1)}, bf16[512,128]{1,0:T(8,128)(2,1)S(1)}, u32[]{:S(2)}, u32[]{:S(2)}) collective-permute-start(bf16[512,128]{1,0:T(8,128)(2,1)S(1)} %get-tuple-element.122), channel_id=1, source_target_pairs={{0,2},{1,3},{2,0},{3,1},{4,6},{5,7},{6,4},{7,5},{8,10},{9,11},{10,... | collective-permute-start | bytes 393224 | tf_op jit(solution)/shard_map/ppermute | solution.py:332
  105.6 1.2 collective-permute-start.24
  106.8 3.9 %collective-permute-start.25 = (f32[8,64]{1,0:T(8,128)S(1)}, f32[8,64]{1,0:T(8,128)S(1)}, u32[]{:S(2)}, u32[]{:S(2)}) collective-permute-start(f32[8,64]{1,0:T(8,128)S(1)} %add.45), channel_id=1, source_target_pairs={{0,2},{1,3},{2,0},{3,1},{4,6},{5,7},{6,4},{7,5},{8,10},{9,11},{10,... | collective-permute-start | bytes 6152 | tf_op jit(solution)/shard_map/ppermute | solution.py:332
  107.1 18.5 %copy-start.5 = (bf16[64,4096]{1,0:T(8,128)(2,1)S(1)}, bf16[64,4096]{1,0:T(8,128)(2,1)}, u32[]{:S(2)}) copy-start(bf16[64,4096]{1,0:T(8,128)(2,1)} %copy-done.4) | copy-start | bytes 1572868
  107.1 18.5 %copy-start.19 = (bf16[32,4096]{1,0:T(8,128)(2,1)S(1)}, bf16[32,4096]{1,0:T(8,128)(2,1)}, u32[]{:S(2)}) copy-start(bf16[32,4096]{1,0:T(8,128)(2,1)} %copy-done.18) | copy-start | bytes 786436
  110.7 3.6 %collective-permute-start.26 = (f32[8,64]{1,0:T(8,128)S(1)}, f32[8,64]{1,0:T(8,128)S(1)}, u32[]{:S(2)}, u32[]{:S(2)}) collective-permute-start(f32[8,64]{1,0:T(8,128)S(1)} %add.46), channel_id=1, source_target_pairs={{0,4},{1,5},{2,6},{3,7},{4,0},{5,1},{6,2},{7,3},{8,12},{9,13},{10,... | collective-permute-start | bytes 6152 | tf_op jit(solution)/shard_map/ppermute | solution.py:332
  114.3 6.0 %collective-permute-start.27 = (f32[8,64]{1,0:T(8,128)S(1)}, f32[8,64]{1,0:T(8,128)S(1)}, u32[]{:S(2)}, u32[]{:S(2)}) collective-permute-start(f32[8,64]{1,0:T(8,128)S(1)} %add.48), channel_id=1, source_target_pairs={{0,8},{1,9},{2,10},{3,11},{4,12},{5,13},{6,14},{7,15},{8,0},{9,1},... | collective-permute-start | bytes 6152 | tf_op jit(solution)/shard_map/ppermute | solution.py:332
  120.3 4.6 %collective-permute-start.28 = (f32[8,64]{1,0:T(8,128)S(1)}, f32[8,64]{1,0:T(8,128)S(1)}, u32[]{:S(2)}, u32[]{:S(2)}) collective-permute-start(f32[8,64]{1,0:T(8,128)S(1)} %add.49), channel_id=1, source_target_pairs={{0,16},{1,17},{2,18},{3,19},{4,20},{5,21},{6,22},{7,23},{8,24},{9,... | collective-permute-start | bytes 6152 | tf_op jit(solution)/shard_map/ppermute | solution.py:332
  (25 other events, 25.2 us)

commit v4 on v3

--- a/solution.py
+++ b/solution.py
@@ -40,23 +40,25 @@
     )(scalars, *held, *rest)
 
 
-def whiten_kernel(tile, starts_ref, f_ref, *refs):
-    pieces, (keep_ref, away_ref, x_ref, xt_ref, buf_ref, sems) = refs[:-6], refs[-6:]
-    slots = buf_ref.shape[0]
-    tiles = f_ref.shape[0] // tile
-    per_block = tiles // starts_ref.shape[0]
-    half = tiles // 2
-
-    def copy(t):
-        order = lax.rem(t + half, tiles)
-        start = starts_ref[order // per_block] + lax.rem(order, per_block) * tile
-        slot = lax.rem(t, slots)
-        return pltpu.make_async_copy(
-            f_ref.at[pl.ds(pl.multiple_of(start, tile), tile)], buf_ref.at[slot], sems.at[slot]
-        )
-
-    for t in range(min(slots, tiles)):
-        copy(jnp.int32(t)).start()
+def touch_kernel(starts_ref, f_ref, out_ref):
+    for i in range(starts_ref.shape[0]):
+        out_ref[i] = starts_ref[i]
+
+
+def touch(starts, inv_factor):
+    return pl.pallas_call(
+        touch_kernel,
+        in_specs=[pl.BlockSpec(memory_space=pltpu.SMEM), pl.BlockSpec(memory_space=pltpu.VMEM)],
+        out_specs=pl.BlockSpec(memory_space=pltpu.SMEM),
+        out_shape=jax.ShapeDtypeStruct(starts.shape, starts.dtype),
+        compiler_params=pltpu.CompilerParams(vmem_limit_bytes=16 * MIB),
+        cost_estimate=pl.CostEstimate(flops=1000, bytes_accessed=1000, transcendentals=0),
+        name="touch",
+    )(starts, inv_factor)
+
+
+def whiten_kernel(starts_ref, f_ref, *refs):
+    pieces, (keep_ref, away_ref, x_ref, xt_ref) = refs[:-4], refs[-4:]
     place = 0
     for piece in pieces:
         x_ref[pl.ds(place, piece.shape[0]), :] = piece[...]
@@ -64,48 +66,32 @@
     wide = min(512, x_ref.shape[1])
     for c in range(x_ref.shape[1] // wide):
         xt_ref[pl.ds(c * wide, wide), :] = x_ref[:, c * wide:(c + 1) * wide].T
+    blocks = starts_ref.shape[0]
+    tile = f_ref.shape[0] // blocks
 
     def product(t):
-        copy(t).wait()
-        part = jnp.dot(buf_ref[lax.rem(t, slots)], xt_ref[...], preferred_element_type=jnp.float32)
-
-        @pl.when(t + slots < tiles)
-        def _():
-            copy(t + slots).start()
-
-        return part
-
-    def away(t, carry):
-        away_ref[pl.ds(pl.multiple_of(t * tile, tile), tile), :] = product(t).astype(jnp.bfloat16)
+        start = pl.multiple_of(starts_ref[t], tile)
+        return jnp.dot(f_ref[pl.ds(start, tile), :], xt_ref[...], preferred_element_type=jnp.float32)
+
+    def step(t, carry):
+        place = pl.multiple_of(t * tile, tile)
+        away_ref[pl.ds(place, tile), :] = product(blocks // 2 + t).astype(jnp.bfloat16)
+        keep_ref[pl.ds(place, tile), :] = product(t)
         return carry
 
-    def keep(t, carry):
-        keep_ref[pl.ds(pl.multiple_of((t - half) * tile, tile), tile), :] = product(t)
-        return carry
-
-    lax.fori_loop(0, half, away, 0)
-    lax.fori_loop(half, tiles, keep, 0)
+    lax.fori_loop(0, blocks // 2, step, 0)
 
 
 def whiten(starts, inv_factor, pieces):
     row_block, feat_block = inv_factor.shape
     rows = sum(p.shape[0] for p in pieces)
-    tile = min(256, row_block // starts.shape[0])
-    slots = 3
     out = (row_block // 2, rows)
     return call(
-        functools.partial(whiten_kernel, tile),
+        whiten_kernel,
         "whiten",
         [jax.ShapeDtypeStruct(out, jnp.float32), jax.ShapeDtypeStruct(out, jnp.bfloat16)],
-        [
-            pltpu.VMEM((rows, feat_block), jnp.bfloat16),
-            pltpu.VMEM((feat_block, rows), jnp.bfloat16),
-            pltpu.VMEM((slots, tile, feat_block), jnp.bfloat16),
-            pltpu.SemaphoreType.DMA((slots,)),
-        ],
-        (starts, pieces),
-        (inv_factor,),
-        vmem=46,
+        [pltpu.VMEM((rows, feat_block), jnp.bfloat16), pltpu.VMEM((feat_block, rows), jnp.bfloat16)],
+        (starts, [inv_factor] + pieces),
         flops=8 * row_block * feat_block * rows,
     )
 
@@ -203,9 +189,11 @@
     )
 
 
-def square_kernel(sizes, places_ref, *refs):
+def square_kernel(sizes, places_ref, w_ref, strata_ref, *refs):
     out_ref = refs[-1]
     count = out_ref.shape[1]
+    slots = sum(sizes)
+    out_ref[...] = jnp.zeros_like(out_ref)
     slot = 0
     for g, size in enumerate(sizes):
         value = refs[2 * g][...] + refs[2 * g + 1][...].astype(jnp.float32)
@@ -214,19 +202,26 @@
             out_ref[pl.ds(places_ref[slot], 1), :] = line[:, i * count:(i + 1) * count]
             slot += 1
 
-
-def squares(places, pairs, sizes, count):
+    @pl.when(places_ref[slots + 1] == 0)
+    def _():
+        out_ref[pl.ds(slots + places_ref[slots], 1), :] = w_ref[...]
+        out_ref[pl.ds(2 * slots + places_ref[slots], 1), :] = strata_ref[...].astype(jnp.float32)
+
+
+def squares(places, weights, strata, pairs, sizes):
+    count = weights.shape[1]
     return call(
         functools.partial(square_kernel, sizes),
         "squares",
-        jax.ShapeDtypeStruct((sum(sizes), count), jnp.float32),
+        jax.ShapeDtypeStruct((3 * sum(sizes), count), jnp.float32),
         [],
-        (places, [x for pair in pairs for x in pair]),
-    )
-
-
-def weight_kernel(strata_n, features, row_ref, raw_ref, w_ref, strata_ref, wide_ref, new_ref, lev_ref, all_ref):
-    raw, weights, strata = raw_ref[...], w_ref[...], strata_ref[...]
+        (places, [weights, strata] + [x for pair in pairs for x in pair]),
+    )
+
+
+def weight_kernel(strata_n, features, row_ref, sums_ref, wide_ref, new_ref, lev_ref, all_ref):
+    groups = sums_ref.shape[0] // 3
+    raw, weights, strata = [sums_ref[pl.ds(i * groups, groups), :] for i in range(3)]
     products = weights * raw
     ratio = jnp.zeros_like(raw)
     for s in range(strata_n):
@@ -237,15 +232,15 @@
     new = products * ratio
     all_ref[...] = new
     new_ref[...] = all_ref[pl.ds(row_ref[0], 1), :]
-    lev_ref[...] = raw_ref[pl.ds(row_ref[0], 1), :] / features
+    lev_ref[...] = sums_ref[pl.ds(row_ref[0], 1), :] / features
     step = new - weights
-    groups, count = step.shape
+    count = step.shape[1]
     for g in range(groups):
         wide_ref[pl.ds(g * count, count), :] = jnp.broadcast_to(step[g:g + 1, :], (LANES, count)).T
 
 
-def weight_step(row, raw, weights, strata, features):
-    groups, count = raw.shape
+def weight_step(row, sums, features):
+    groups, count = sums.shape[0] // 3, sums.shape[1]
     return call(
         functools.partial(weight_kernel, 2 * groups, features),
         "weight_step",
@@ -255,7 +250,7 @@
             jax.ShapeDtypeStruct((1, count), jnp.float32),
         ],
         [pltpu.VMEM((groups, count), jnp.float32)],
-        (row, [raw, weights, strata]),
+        (row, [sums]),
     )
 
 
@@ -395,10 +390,6 @@
             return keep, swap(away, 0, far_bits[-1])
 
         chunks = {(0, 0): [candidates]}
-        small = jnp.stack([weights, strata.astype(jnp.float32)])
-        small_all = jnp.where((jnp.arange(rows_n) == row)[:, None, None], small[None], 0.0)
-        small_bits = list(row_bits)
-
         columns, far_columns, white, near, far = [], [], [], [], []
         for k in range(hi_n + 1):
             fresh, out = [], {}
@@ -421,9 +412,8 @@
                     held = send(held, lo_pairs)
                     chunks[k, s] = [held, send(picked[1 + s], hi_pairs)]
             out["fresh"] = [chunks[slot] for slot in fresh]
-            if small_bits:
-                bit = small_bits.pop(0)
-                out["small"] = small_all + swap(small_all, bit, 0)
+            if k == 0:
+                out["starts"] = touch(starts, inv_factor)
             if k > 0:
                 out["column"] = column_far(columns[-1])
                 out["white"] = whiten(starts, inv_factor, pieces_of(white_groups[k - 1]))
@@ -435,20 +425,23 @@
             out = fence(out)
             for slot, value in zip(fresh, out["fresh"]):
                 chunks[slot] = value
-            small_all = out.get("small", small_all)
+            starts = out.get("starts", starts)
             for name, kept in (("column", far_columns), ("white", white), ("near", near), ("far", far)):
                 if name in out:
                     kept.append(out[name])
-        while small_bits:
-            small_all = small_all + swap(small_all, small_bits.pop(0), 0)
-
         keep, away = white[-1]
         packed = pack((apart == 0).astype(jnp.int32)[None], columns, far_columns)
         last, before, packed = fence(((keep, swap(away, 0, 1)), to_far(near[-1]), packed))
         far.append(before)
         last, beside = fence((to_far(last), swap(packed, 0, 1)))
         far.append(last)
-        total = squares(white_places, far, [len(g) for g in white_groups], rows_dev)
+        total = squares(
+            jnp.concatenate([white_places, row[None], feat[None]]),
+            weights[None],
+            strata[None],
+            far,
+            [len(g) for g in white_groups],
+        )
         total = fence(total + swap(total, 0, 1))
         column_t = join((apart % 2 == 0).astype(jnp.int32)[None], packed, beside)
         bits = [(0, bit) for bit in far_bits] + [(bit, 0) for bit in row_bits]
@@ -457,9 +450,7 @@
             if i == 0:
                 total, column_t = fence((total, column_t))
 
-        step_wide, new_weight, leverage = weight_step(
-            row[None], total, small_all[:, 0], small_all[:, 1], features
-        )
+        step_wide, new_weight, leverage = weight_step(row[None], total, features)
         piece_starts = []
         for i, slot in enumerate(slots):
             place = places[i] * rows_dev

time: 150 us -> 145 us (0.967)
  local copies, waits for them, and re-layouts: 26.5 us -> 37.4 us
  Pallas kernels: 56 us -> 47 us
  waiting for transfers between devices: 21 us -> 18.3 us
  starting transfers between devices: 36.5 us -> 34.2 us
    unnamed x88 -> x96, local copies, waits for them, and re-layouts: 25 us -> 35.9 us
    pallas_call x17, Pallas kernels: 56 us -> 45.8 us  [call(): pl.pallas_call(kernel, in_specs=[pl.BlockSpec(memory_space=pltpu.SMEM)] +...]
    ppermute x29 -> x26, waiting for transfers between devices: 21 us -> 18.3 us  [send(): return lax.ppermute(x, BOTH, pairs)]
    ppermute x29 -> x26, starting transfers between devices: 36.5 us -> 34.2 us  [send(): return lax.ppermute(x, BOTH, pairs)]
  transfers between devices with their start and end apart: 29 -> 26, of which waited for: 7 -> 10; matrix products, arithmetic and copies ran while one was open for 2% -> 1% of each run, Pallas kernels for 26% -> 20%
where the time goes in v4:
time: 145 us; the launch traced here: 144 us
  Pallas kernels  47 us (32%)
  local copies, waits for them, and re-layouts  37.4 us (26%)
  starting transfers between devices  34.2 us (24%)
  waiting for transfers between devices  18.3 us (13%)
  between operations  6.35 us (4%)
    pallas_call x17, Pallas kernels, call(): pl.pallas_call(kernel, in_specs=[pl.BlockSpec(memory_space=pltpu.SMEM)] +...  45.8 us
    unnamed x96, local copies, waits for them, and re-layouts  35.9 us
    ppermute x26, starting transfers between devices, send(): return lax.ppermute(x, BOTH, pairs)  34.2 us
    ppermute x26, waiting for transfers between devices, send(): return lax.ppermute(x, BOTH, pairs)  18.3 us
  transfers between devices with their start and end apart: 26, of which 10 were waited for; matrix products, arithmetic and copies ran while one was open for 1% of the time, Pallas kernels for 20%

profile of v4, /device:TPU:0, one launch (start us, length us, event | category | flops | bytes accessed | tf_op | source)
XLA Modules:
  0.0 143.9 jit_solution(10053546768915745710)
XLA Ops:
  0.6 3.0 %collective-permute-start.1 = (bf16[64,4096]{1,0:T(8,128)(2,1)}, bf16[64,4096]{1,0:T(8,128)(2,1)S(1)}, u32[]{:S(2)}, u32[]{:S(2)}) collective-permute-start(bf16[64,4096]{1,0:T(8,128)(2,1)} %refs_0_.5), channel_id=1, source_target_pairs={{0,4},{1,5},{2,6},{3,7},{4,0},{5,1},{6,2},{7,3},{8,12},{9,13},{10,... | collective-permute-start | bytes 1572872 | tf_op jit(solution)/shard_map/ppermute | solution.py:327
  3.6 2.6 %collective-permute-start = (bf16[64,4096]{1,0:T(8,128)(2,1)}, bf16[64,4096]{1,0:T(8,128)(2,1)S(1)}, u32[]{:S(2)}, u32[]{:S(2)}) collective-permute-start(bf16[64,4096]{1,0:T(8,128)(2,1)} %refs_0_.5), channel_id=1, source_target_pairs={{0,16},{1,17},{2,18},{3,19},{4,20},{5,21},{6,22},{7,23},{8,0},{9,1... | collective-permute-start | bytes 1572872 | tf_op jit(solution)/shard_map/ppermute | solution.py:327
  6.9 5.8 %copy-done = bf16[2048,4096]{1,0:T(8,128)(2,1)S(1)} copy-done((bf16[2048,4096]{1,0:T(8,128)(2,1)S(1)}, bf16[2048,4096]{1,0:T(8,128)(2,1)}, u32[]{:S(2)}) %copy-start) | copy-done | bytes 16777240
  12.7 1.1 touch.1.starts_ref._
  13.8 2.0 %collective-permute-done.1.refs_1_ = bf16[64,4096]{1,0:T(8,128)(2,1)S(1)} collective-permute-done((bf16[64,4096]{1,0:T(8,128)(2,1)}, bf16[64,4096]{1,0:T(8,128)(2,1)S(1)}, u32[]{:S(2)}, u32[]{:S(2)}) %collective-permute-start.1) | collective-permute-done | bytes 524320 | tf_op jit(solution)/shard_map/ppermute | solution.py:327
  15.8 1.7 %collective-permute-done.refs_2_.refs_0_ = bf16[64,4096]{1,0:T(8,128)(2,1)S(1)} collective-permute-done((bf16[64,4096]{1,0:T(8,128)(2,1)}, bf16[64,4096]{1,0:T(8,128)(2,1)S(1)}, u32[]{:S(2)}, u32[]{:S(2)}) %collective-permute-start) | collective-permute-done | bytes 524320 | tf_op jit(solution)/shard_map/ppermute | solution.py:327
  18.0 3.3 %collective-permute-start.3 = (bf16[64,4096]{1,0:T(8,128)(2,1)S(1)}, bf16[64,4096]{1,0:T(8,128)(2,1)S(1)}, u32[]{:S(2)}, u32[]{:S(2)}) collective-permute-start(bf16[64,4096]{1,0:T(8,128)(2,1)S(1)} %collective-permute-done.refs_2_.refs_0_), channel_id=1, source_target_pairs={{0,16},{1,17},{2,18},{3,19},{4,20},{5,21},{6,22},{7,23},{8,0},{9,1... | collective-permute-start | bytes 1572872 | tf_op jit(solution)/shard_map/ppermute | solution.py:327
  21.3 3.5 %collective-permute-start.2 = (bf16[192,2048]{1,0:T(8,128)(2,1)S(1)}, bf16[192,2048]{1,0:T(8,128)(2,1)S(1)}, u32[]{:S(2)}, u32[]{:S(2)}) collective-permute-start(bf16[192,2048]{1,0:T(8,128)(2,1)S(1)} %pick.4.refs_0_), channel_id=1, source_target_pairs={{0,2},{4,6},{9,11},{13,15},{18,16},{22,20},{27,25},{31,29}} | collective-permute-start | bytes 2359304 | tf_op jit(solution)/shard_map/ppermute | solution.py:327
  24.8 5.8 %copy-done.1 = bf16[2048,4096]{1,0:T(8,128)(2,1)S(1)} copy-done((bf16[2048,4096]{1,0:T(8,128)(2,1)S(1)}, bf16[2048,4096]{1,0:T(8,128)(2,1)}, u32[]{:S(2)}) %copy-start.1) | copy-done | bytes 16777240
  30.6 5.5 %whiten.4 = (f32[1024,128]{1,0:T(8,128)S(1)}, bf16[1024,128]{1,0:T(8,128)(2,1)S(1)}) custom-call(s32[4]{0:T(128)S(1)} %touch.1.starts_ref._, bf16[2048,4096]{1,0:T(8,128)(2,1)S(1)} %copy-done.1, bf16[64,4096]{1,0:T(8,128)(2,1)S(1)} %copy-done.5, bf16[64,4096]{1,0:T(8,128)(2,1)S(1)} %collective-permute-done.1.refs_1_), custom_call_target="tpu_custom_call" | custom-call | flops 8589934592 | bytes 1000 | tf_op jit(solution)/shard_map/whiten/pallas_call | solution.py:31
  37.1 1.5 %collective-permute-start.7 = (bf16[64,4096]{1,0:T(8,128)(2,1)S(1)}, bf16[64,4096]{1,0:T(8,128)(2,1)S(1)}, u32[]{:S(2)}, u32[]{:S(2)}) collective-permute-start(bf16[64,4096]{1,0:T(8,128)(2,1)S(1)} %collective-permute-done.3.refs_1_.refs_0_.refs_4_), channel_id=1, source_target_pairs={{0,4},{1,5},{2,6},{3,7},{4,0},{5,1},{6,2},{7,3},{8,12},{9,13},{10,... | collective-permute-start | bytes 1572872 | tf_op jit(solution)/shard_map/ppermute | solution.py:327
  38.6 3.1 %collective-permute-start.5 = (bf16[128,2048]{1,0:T(8,128)(2,1)S(1)}, bf16[128,2048]{1,0:T(8,128)(2,1)S(1)}, u32[]{:S(2)}, u32[]{:S(2)}) collective-permute-start(bf16[128,2048]{1,0:T(8,128)(2,1)S(1)} %pick.5.refs_1_), channel_id=1, source_target_pairs={{0,2},{4,6},{9,11},{13,15},{18,16},{22,20},{27,25},{31,29}} | collective-permute-start | bytes 1572872 | tf_op jit(solution)/shard_map/ppermute | solution.py:327
  41.8 5.5 %whiten.5 = (f32[1024,128]{1,0:T(8,128)S(1)}, bf16[1024,128]{1,0:T(8,128)(2,1)S(1)}) custom-call(s32[4]{0:T(128)S(1)} %touch.1.starts_ref._, bf16[2048,4096]{1,0:T(8,128)(2,1)S(1)} %copy-done.2, bf16[64,4096]{1,0:T(8,128)(2,1)S(1)} %collective-permute-done.refs_2_.refs_0_, bf16[64,4096]{1,0:T(8,128)(2,1)S(1)} %collective-permute-done.4.refs_0_.refs_1_.refs_3_), custom_call_target="tpu_custom_call" | custom-call | flops 8589934592 | bytes 1000 | tf_op jit(solution)/shard_map/whiten/pallas_call | solution.py:31
  47.3 2.0 %collective-permute-done.5.refs_5_ = bf16[128,2048]{1,0:T(8,128)(2,1)S(1)} collective-permute-done((bf16[128,2048]{1,0:T(8,128)(2,1)S(1)}, bf16[128,2048]{1,0:T(8,128)(2,1)S(1)}, u32[]{:S(2)}, u32[]{:S(2)}) %collective-permute-start.5) | collective-permute-done | bytes 524320 | tf_op jit(solution)/shard_map/ppermute | solution.py:327
  49.9 2.5 %collective-permute-start.10 = (bf16[512,128]{1,0:T(8,128)(2,1)S(1)}, bf16[512,128]{1,0:T(8,128)(2,1)S(1)}, u32[]{:S(2)}, u32[]{:S(2)}) collective-permute-start(bf16[512,128]{1,0:T(8,128)(2,1)S(1)} %get-tuple-element.83), channel_id=1, source_target_pairs={{0,2},{1,3},{2,0},{3,1},{4,6},{5,7},{6,4},{7,5},{8,10},{9,11},{10,... | collective-permute-start | bytes 393224 | tf_op jit(solution)/shard_map/ppermute | solution.py:327
  53.2 2.0 %collective-permute-start.9 = (bf16[128,2048]{1,0:T(8,128)(2,1)S(1)}, bf16[128,2048]{1,0:T(8,128)(2,1)S(1)}, u32[]{:S(2)}, u32[]{:S(2)}) collective-permute-start(bf16[128,2048]{1,0:T(8,128)(2,1)S(1)} %get-tuple-element.79.refs_2_), channel_id=1, source_target_pairs={{0,2},{4,6},{9,11},{13,15},{18,16},{22,20},{27,25},{31,29}} | collective-permute-start | bytes 1572872 | tf_op jit(solution)/shard_map/ppermute | solution.py:327
  55.2 5.5 %whiten.6 = (f32[1024,128]{1,0:T(8,128)S(1)}, bf16[1024,128]{1,0:T(8,128)(2,1)S(1)}) custom-call(s32[4]{0:T(128)S(1)} %touch.1.starts_ref._, bf16[2048,4096]{1,0:T(8,128)(2,1)S(1)} %copy-done.2, bf16[64,4096]{1,0:T(8,128)(2,1)S(1)} %collective-permute-done.3.refs_1_.refs_0_.refs_4_, bf16[64,4096]{1,0:T(8,128)(2,1)S(1)} %collective-permute-done.7.refs_0_.refs_1_.refs_5_), custom_call_target="tpu_custom_call" | custom-call | flops 8589934592 | bytes 1000 | tf_op jit(solution)/shard_map/whiten/pallas_call | solution.py:31
  62.7 4.4 %collective-permute-start.14 = (bf16[64,2048]{1,0:T(8,128)(2,1)S(1)}, bf16[64,2048]{1,0:T(8,128)(2,1)S(1)}, u32[]{:S(2)}, u32[]{:S(2)}) collective-permute-start(bf16[64,2048]{1,0:T(8,128)(2,1)S(1)} %pick.7.refs_3_), channel_id=1, source_target_pairs={{0,2},{4,6},{9,11},{13,15},{18,16},{22,20},{27,25},{31,29}} | collective-permute-start | bytes 786440 | tf_op jit(solution)/shard_map/ppermute | solution.py:327
  67.9 6.3 %whiten.7 = (f32[1024,128]{1,0:T(8,128)S(1)}, bf16[1024,128]{1,0:T(8,128)(2,1)}) custom-call(s32[4]{0:T(128)S(1)} %touch.1.starts_ref._, bf16[2048,4096]{1,0:T(8,128)(2,1)S(1)} %copy-done.2, bf16[64,4096]{1,0:T(8,128)(2,1)S(1)} %collective-permute-done.6.refs_1_.refs_0_.refs_6_, bf16[32,4096]{1,0:T(8,128)(2,1)S(1)} %collective-permute-done.11.refs_0_.refs_1_.refs_7_, ...), custom_call_target="tpu_custom_call" | custom-call | flops 8589934592 | bytes 1000 | tf_op jit(solution)/shard_map/whiten/pallas_call | solution.py:31
  75.5 1.2 halve.6
  77.5 1.7 %collective-permute-start.18 = (bf16[512,128]{1,0:T(8,128)(2,1)}, bf16[512,128]{1,0:T(8,128)(2,1)}, u32[]{:S(2)}, u32[]{:S(2)}) collective-permute-start(bf16[512,128]{1,0:T(8,128)(2,1)} %get-tuple-element.109), channel_id=1, source_target_pairs={{0,2},{1,3},{2,0},{3,1},{4,6},{5,7},{6,4},{7,5},{8,10},{9,11},{10,... | collective-permute-start | bytes 393224 | tf_op jit(solution)/shard_map/ppermute | solution.py:327
  79.2 1.0 copy-done.19
  80.3 0.9 copy-done.25
  81.2 1.1 copy-done.27
  82.4 1.0 copy-done.29
  83.4 1.0 copy-done.31
  84.4 1.0 copy-done.33
  85.5 0.9 copy-done.43
  86.7 1.0 copy-done.35
  87.7 1.0 halve.7
  89.9 4.8 %collective-permute-done.19.refs_7_ = bf16[512,128]{1,0:T(8,128)(2,1)S(1)} collective-permute-done((bf16[512,128]{1,0:T(8,128)(2,1)S(1)}, bf16[512,128]{1,0:T(8,128)(2,1)S(1)}, u32[]{:S(2)}, u32[]{:S(2)}) %collective-permute-start.19) | collective-permute-done | bytes 131104 | tf_op jit(solution)/shard_map/ppermute | solution.py:327
  95.7 0.9 copy-done.39
  98.5 1.2 squares.1
  99.6 1.2 collective-permute-done.21
  101.1 2.3 %join.1.col_ref = bf16[2048,512]{1,0:T(8,128)(2,1)S(1)} custom-call(s32[1]{0:T(128)} %bitcast.7.flag_ref, bf16[512,2048]{1,0:T(8,128)(2,1)S(1)} %pack.1.own_ref, bf16[512,2048]{1,0:T(8,128)(2,1)} %collective-permute-done.20.other_ref), custom_call_target="tpu_custom_call" | custom-call | flops 1000 | bytes 1000 | tf_op jit(solution)/shard_map/join/pallas_call | solution.py:31
  103.4 1.3 copy-done.3
  104.7 1.5 %collective-permute-start.23 = (f32[24,64]{1,0:T(8,128)S(1)}, f32[24,64]{1,0:T(8,128)S(1)}, u32[]{:S(2)}, u32[]{:S(2)}) collective-permute-start(f32[24,64]{1,0:T(8,128)S(1)} %add.34), channel_id=1, source_target_pairs={{0,4},{1,5},{2,6},{3,7},{4,0},{5,1},{6,2},{7,3},{8,12},{9,13},{10,... | collective-permute-start | bytes 18440 | tf_op jit(solution)/shard_map/ppermute | solution.py:327
  106.2 2.2 %collective-permute-done.23 = f32[24,64]{1,0:T(8,128)S(1)} collective-permute-done((f32[24,64]{1,0:T(8,128)S(1)}, f32[24,64]{1,0:T(8,128)S(1)}, u32[]{:S(2)}, u32[]{:S(2)}) %collective-permute-start.23) | collective-permute-done | bytes 6176 | tf_op jit(solution)/shard_map/ppermute | solution.py:327
  108.7 3.4 %collective-permute-done.24 = f32[24,64]{1,0:T(8,128)S(1)} collective-permute-done((f32[24,64]{1,0:T(8,128)S(1)}, f32[24,64]{1,0:T(8,128)S(1)}, u32[]{:S(2)}, u32[]{:S(2)}) %collective-permute-start.24) | collective-permute-done | bytes 6176 | tf_op jit(solution)/shard_map/ppermute | solution.py:327
  112.1 2.2 %collective-permute-start.25 = (f32[24,64]{1,0:T(8,128)S(1)}, f32[24,64]{1,0:T(8,128)S(1)}, u32[]{:S(2)}, u32[]{:S(2)}) collective-permute-start(f32[24,64]{1,0:T(8,128)S(1)} %add.37), channel_id=1, source_target_pairs={{0,16},{1,17},{2,18},{3,19},{4,20},{5,21},{6,22},{7,23},{8,24},{9,... | collective-permute-start | bytes 18440 | tf_op jit(solution)/shard_map/ppermute | solution.py:327
  121.0 1.6 %copy-done.4 = bf16[2048,512]{1,0:T(8,128)(2,1)S(1)} copy-done((bf16[2048,512]{1,0:T(8,128)(2,1)S(1)}, bf16[2048,512]{1,0:T(8,128)(2,1)}, u32[]{:S(2)}) %copy-start.4) | copy-done | bytes 2097176
  122.6 1.0 copy-done.9
  123.7 1.0 copy-done.11
  124.7 1.0 copy-done.13
  125.7 1.0 copy-done.15
  126.8 1.0 copy-done.17
  127.8 0.9 copy-done.23
  128.8 15.2 %increment.1 = f32[2048,4096]{1,0:T(8,128)} custom-call(s32[9]{0:T(128)S(1)} %stack.39.starts_ref, f32[512,128]{1,0:T(8,128)S(1)} %get-tuple-element.127.d_ref, bf16[2048,512]{1,0:T(8,128)(2,1)S(1)} %copy-done.4, bf16[64,4096]{1,0:T(8,128)(2,1)S(1)} %copy-done.5, bf16[64,4096]{1,0:T(8,128)(2,1)S(1)} %copy-done.7, bf16[64,4096]{1,0:T(8,128)(2,1)S(1)} %copy-done.9, ...), custom_call_target="tpu_custom_call" | custom-call | flops 1000 | bytes 1000 | tf_op jit(solution)/shard_map/increment/pallas_call | solution.py:31
  (128 shorter events, 14.5 us)
Async XLA Ops:
  0.6 15.1 %collective-permute-start.1 = (bf16[64,4096]{1,0:T(8,128)(2,1)}, bf16[64,4096]{1,0:T(8,128)(2,1)S(1)}, u32[]{:S(2)}, u32[]{:S(2)}) collective-permute-start(bf16[64,4096]{1,0:T(8,128)(2,1)} %refs_0_.5), channel_id=1, source_target_pairs={{0,4},{1,5},{2,6},{3,7},{4,0},{5,1},{6,2},{7,3},{8,12},{9,13},{10,... | collective-permute-start | bytes 1572872 | tf_op jit(solution)/shard_map/ppermute | solution.py:327
  3.6 13.8 %collective-permute-start = (bf16[64,4096]{1,0:T(8,128)(2,1)}, bf16[64,4096]{1,0:T(8,128)(2,1)S(1)}, u32[]{:S(2)}, u32[]{:S(2)}) collective-permute-start(bf16[64,4096]{1,0:T(8,128)(2,1)} %refs_0_.5), channel_id=1, source_target_pairs={{0,16},{1,17},{2,18},{3,19},{4,20},{5,21},{6,22},{7,23},{8,0},{9,1... | collective-permute-start | bytes 1572872 | tf_op jit(solution)/shard_map/ppermute | solution.py:327
  6.9 5.8 %copy-start = (bf16[2048,4096]{1,0:T(8,128)(2,1)S(1)}, bf16[2048,4096]{1,0:T(8,128)(2,1)}, u32[]{:S(2)}) copy-start(bf16[2048,4096]{1,0:T(8,128)(2,1)} %f_ref.9) | copy-start | bytes 50331652
  12.7 8.6 %copy-start.5 = (bf16[64,4096]{1,0:T(8,128)(2,1)S(1)}, bf16[64,4096]{1,0:T(8,128)(2,1)}, u32[]{:S(2)}) copy-start(bf16[64,4096]{1,0:T(8,128)(2,1)} %refs_0_.5) | copy-start | bytes 1572868
  15.8 20.3 %copy-start.6 = (bf16[64,4096]{1,0:T(8,128)(2,1)}, bf16[64,4096]{1,0:T(8,128)(2,1)S(1)}, u32[]{:S(2)}) copy-start(bf16[64,4096]{1,0:T(8,128)(2,1)S(1)} %collective-permute-done.1.refs_1_) | copy-start | bytes 1572868
  17.4 24.3 %copy-start.8 = (bf16[64,4096]{1,0:T(8,128)(2,1)}, bf16[64,4096]{1,0:T(8,128)(2,1)S(1)}, u32[]{:S(2)}) copy-start(bf16[64,4096]{1,0:T(8,128)(2,1)S(1)} %collective-permute-done.refs_2_.refs_0_) | copy-start | bytes 1572868
  17.4 18.7 %collective-permute-start.4 = (bf16[64,4096]{1,0:T(8,128)(2,1)S(1)}, bf16[64,4096]{1,0:T(8,128)(2,1)S(1)}, u32[]{:S(2)}, u32[]{:S(2)}) collective-permute-start(bf16[64,4096]{1,0:T(8,128)(2,1)S(1)} %collective-permute-done.refs_2_.refs_0_), channel_id=1, source_target_pairs={{0,4},{1,5},{2,6},{3,7},{4,0},{5,1},{6,2},{7,3},{8,12},{9,13},{10,... | collective-permute-start | bytes 1572872 | tf_op jit(solution)/shard_map/ppermute | solution.py:327
  18.0 18.1 %collective-permute-start.3 = (bf16[64,4096]{1,0:T(8,128)(2,1)S(1)}, bf16[64,4096]{1,0:T(8,128)(2,1)S(1)}, u32[]{:S(2)}, u32[]{:S(2)}) collective-permute-start(bf16[64,4096]{1,0:T(8,128)(2,1)S(1)} %collective-permute-done.refs_2_.refs_0_), channel_id=1, source_target_pairs={{0,16},{1,17},{2,18},{3,19},{4,20},{5,21},{6,22},{7,23},{8,0},{9,1... | collective-permute-start | bytes 1572872 | tf_op jit(solution)/shard_map/ppermute | solution.py:327
  21.3 14.8 %collective-permute-start.2 = (bf16[192,2048]{1,0:T(8,128)(2,1)S(1)}, bf16[192,2048]{1,0:T(8,128)(2,1)S(1)}, u32[]{:S(2)}, u32[]{:S(2)}) collective-permute-start(bf16[192,2048]{1,0:T(8,128)(2,1)S(1)} %pick.4.refs_0_), channel_id=1, source_target_pairs={{0,2},{4,6},{9,11},{13,15},{18,16},{22,20},{27,25},{31,29}} | collective-permute-start | bytes 2359304 | tf_op jit(solution)/shard_map/ppermute | solution.py:327
  24.8 5.8 %copy-start.1 = (bf16[2048,4096]{1,0:T(8,128)(2,1)S(1)}, bf16[2048,4096]{1,0:T(8,128)(2,1)}, u32[]{:S(2)}) copy-start(bf16[2048,4096]{1,0:T(8,128)(2,1)} %f_ref.9) | copy-start | bytes 50331652
  30.6 11.2 %copy-start.2 = (bf16[2048,4096]{1,0:T(8,128)(2,1)S(1)}, bf16[2048,4096]{1,0:T(8,128)(2,1)}, u32[]{:S(2)}) copy-start(bf16[2048,4096]{1,0:T(8,128)(2,1)} %f_ref.9) | copy-start | bytes 50331652
  36.1 11.2 %copy-start.10 = (bf16[64,4096]{1,0:T(8,128)(2,1)}, bf16[64,4096]{1,0:T(8,128)(2,1)S(1)}, u32[]{:S(2)}) copy-start(bf16[64,4096]{1,0:T(8,128)(2,1)S(1)} %collective-permute-done.4.refs_0_.refs_1_.refs_3_) | copy-start | bytes 1572868
  36.1 19.1 %copy-start.12 = (bf16[64,4096]{1,0:T(8,128)(2,1)}, bf16[64,4096]{1,0:T(8,128)(2,1)S(1)}, u32[]{:S(2)}) copy-start(bf16[64,4096]{1,0:T(8,128)(2,1)S(1)} %collective-permute-done.3.refs_1_.refs_0_.refs_4_) | copy-start | bytes 1572868
  37.1 12.2 %collective-permute-start.7 = (bf16[64,4096]{1,0:T(8,128)(2,1)S(1)}, bf16[64,4096]{1,0:T(8,128)(2,1)S(1)}, u32[]{:S(2)}, u32[]{:S(2)}) collective-permute-start(bf16[64,4096]{1,0:T(8,128)(2,1)S(1)} %collective-permute-done.3.refs_1_.refs_0_.refs_4_), channel_id=1, source_target_pairs={{0,4},{1,5},{2,6},{3,7},{4,0},{5,1},{6,2},{7,3},{8,12},{9,13},{10,... | collective-permute-start | bytes 1572872 | tf_op jit(solution)/shard_map/ppermute | solution.py:327
  38.6 10.7 %collective-permute-start.6 = (bf16[64,4096]{1,0:T(8,128)(2,1)S(1)}, bf16[64,4096]{1,0:T(8,128)(2,1)S(1)}, u32[]{:S(2)}, u32[]{:S(2)}) collective-permute-start(bf16[64,4096]{1,0:T(8,128)(2,1)S(1)} %collective-permute-done.3.refs_1_.refs_0_.refs_4_), channel_id=1, source_target_pairs={{0,16},{1,17},{2,18},{3,19},{4,20},{5,21},{6,22},{7,23},{8,0},{9,1... | collective-permute-start | bytes 1572872 | tf_op jit(solution)/shard_map/ppermute | solution.py:327
  38.6 8.8 %collective-permute-start.8 = (bf16[1024,128]{1,0:T(8,128)(2,1)S(1)}, bf16[1024,128]{1,0:T(8,128)(2,1)S(1)}, u32[]{:S(2)}, u32[]{:S(2)}) collective-permute-start(bf16[1024,128]{1,0:T(8,128)(2,1)S(1)} %get-tuple-element.74), channel_id=1, source_target_pairs={{0,1},{1,0},{2,3},{3,2},{4,5},{5,4},{6,7},{7,6},{8,9},{9,8},{10,11... | collective-permute-start | bytes 786440 | tf_op jit(solution)/shard_map/ppermute | solution.py:327
  38.6 8.7 %copy-start.18 = (bf16[128,2048]{1,0:T(8,128)(2,1)}, bf16[128,2048]{1,0:T(8,128)(2,1)S(1)}, u32[]{:S(2)}) copy-start(bf16[128,2048]{1,0:T(8,128)(2,1)S(1)} %pick.5.refs_1_) | copy-start | bytes 1572868
  38.6 10.7 %collective-permute-start.5 = (bf16[128,2048]{1,0:T(8,128)(2,1)S(1)}, bf16[128,2048]{1,0:T(8,128)(2,1)S(1)}, u32[]{:S(2)}, u32[]{:S(2)}) collective-permute-start(bf16[128,2048]{1,0:T(8,128)(2,1)S(1)} %pick.5.refs_1_), channel_id=1, source_target_pairs={{0,2},{4,6},{9,11},{13,15},{18,16},{22,20},{27,25},{31,29}} | collective-permute-start | bytes 1572872 | tf_op jit(solution)/shard_map/ppermute | solution.py:327
  49.3 11.4 %copy-start.28 = (bf16[128,2048]{1,0:T(8,128)(2,1)}, bf16[128,2048]{1,0:T(8,128)(2,1)S(1)}, u32[]{:S(2)}) copy-start(bf16[128,2048]{1,0:T(8,128)(2,1)S(1)} %collective-permute-done.5.refs_5_) | copy-start | bytes 1572868
  49.3 11.4 %copy-start.14 = (bf16[64,4096]{1,0:T(8,128)(2,1)}, bf16[64,4096]{1,0:T(8,128)(2,1)S(1)}, u32[]{:S(2)}) copy-start(bf16[64,4096]{1,0:T(8,128)(2,1)S(1)} %collective-permute-done.7.refs_0_.refs_1_.refs_5_) | copy-start | bytes 1572868
  49.3 18.5 %copy-start.16 = (bf16[64,4096]{1,0:T(8,128)(2,1)}, bf16[64,4096]{1,0:T(8,128)(2,1)S(1)}, u32[]{:S(2)}) copy-start(bf16[64,4096]{1,0:T(8,128)(2,1)S(1)} %collective-permute-done.6.refs_1_.refs_0_.refs_6_) | copy-start | bytes 1572868
  49.9 10.8 %copy-start.36 = (f32[512,128]{1,0:T(8,128)}, f32[512,128]{1,0:T(8,128)S(1)}, u32[]{:S(2)}) copy-start(f32[512,128]{1,0:T(8,128)S(1)} %get-tuple-element.90.refs_0_) | copy-start | bytes 786436
  49.9 10.9 %collective-permute-start.10 = (bf16[512,128]{1,0:T(8,128)(2,1)S(1)}, bf16[512,128]{1,0:T(8,128)(2,1)S(1)}, u32[]{:S(2)}, u32[]{:S(2)}) collective-permute-start(bf16[512,128]{1,0:T(8,128)(2,1)S(1)} %get-tuple-element.83), channel_id=1, source_target_pairs={{0,2},{1,3},{2,0},{3,1},{4,6},{5,7},{6,4},{7,5},{8,10},{9,11},{10,... | collective-permute-start | bytes 393224 | tf_op jit(solution)/shard_map/ppermute | solution.py:327
  52.5 8.3 %collective-permute-start.13 = (bf16[1024,128]{1,0:T(8,128)(2,1)S(1)}, bf16[1024,128]{1,0:T(8,128)(2,1)S(1)}, u32[]{:S(2)}, u32[]{:S(2)}) collective-permute-start(bf16[1024,128]{1,0:T(8,128)(2,1)S(1)} %get-tuple-element.87), channel_id=1, source_target_pairs={{0,1},{1,0},{2,3},{3,2},{4,5},{5,4},{6,7},{7,6},{8,9},{9,8},{10,11... | collective-permute-start | bytes 786440 | tf_op jit(solution)/shard_map/ppermute | solution.py:327
  52.6 8.2 %copy-start.30 = (bf16[128,2048]{1,0:T(8,128)(2,1)}, bf16[128,2048]{1,0:T(8,128)(2,1)S(1)}, u32[]{:S(2)}) copy-start(bf16[128,2048]{1,0:T(8,128)(2,1)S(1)} %get-tuple-element.79.refs_2_) | copy-start | bytes 1572868
  52.6 8.8 %collective-permute-start.11 = (bf16[32,4096]{1,0:T(8,128)(2,1)S(1)}, bf16[32,4096]{1,0:T(8,128)(2,1)S(1)}, u32[]{:S(2)}, u32[]{:S(2)}) collective-permute-start(bf16[32,4096]{1,0:T(8,128)(2,1)S(1)} %get-tuple-element.84), channel_id=1, source_target_pairs={{0,4},{1,5},{2,6},{3,7},{4,0},{5,1},{6,2},{7,3},{8,12},{9,13},{10,... | collective-permute-start | bytes 786440 | tf_op jit(solution)/shard_map/ppermute | solution.py:327
  53.2 8.4 %collective-permute-start.12 = (bf16[32,4096]{1,0:T(8,128)(2,1)S(1)}, bf16[32,4096]{1,0:T(8,128)(2,1)S(1)}, u32[]{:S(2)}, u32[]{:S(2)}) collective-permute-start(bf16[32,4096]{1,0:T(8,128)(2,1)S(1)} %get-tuple-element.85), channel_id=1, source_target_pairs={{0,16},{1,17},{2,18},{3,19},{4,20},{5,21},{6,22},{7,23},{8,0},{9,1... | collective-permute-start | bytes 786440 | tf_op jit(solution)/shard_map/ppermute | solution.py:327
  53.2 8.7 %collective-permute-start.9 = (bf16[128,2048]{1,0:T(8,128)(2,1)S(1)}, bf16[128,2048]{1,0:T(8,128)(2,1)S(1)}, u32[]{:S(2)}, u32[]{:S(2)}) collective-permute-start(bf16[128,2048]{1,0:T(8,128)(2,1)S(1)} %get-tuple-element.79.refs_2_), channel_id=1, source_target_pairs={{0,2},{4,6},{9,11},{13,15},{18,16},{22,20},{27,25},{31,29}} | collective-permute-start | bytes 1572872 | tf_op jit(solution)/shard_map/ppermute | solution.py:327
  61.3 12.8 %copy-start.20 = (bf16[32,4096]{1,0:T(8,128)(2,1)}, bf16[32,4096]{1,0:T(8,128)(2,1)S(1)}, u32[]{:S(2)}) copy-start(bf16[32,4096]{1,0:T(8,128)(2,1)S(1)} %collective-permute-done.11.refs_0_.refs_1_.refs_7_) | copy-start | bytes 786436
  61.6 12.5 %copy-start.22 = (bf16[32,4096]{1,0:T(8,128)(2,1)}, bf16[32,4096]{1,0:T(8,128)(2,1)S(1)}, u32[]{:S(2)}) copy-start(bf16[32,4096]{1,0:T(8,128)(2,1)S(1)} %collective-permute-done.12.refs_1_.refs_2_.refs_8_) | copy-start | bytes 786436
  62.7 11.5 %copy-start.24 = (bf16[64,2048]{1,0:T(8,128)(2,1)}, bf16[64,2048]{1,0:T(8,128)(2,1)S(1)}, u32[]{:S(2)}) copy-start(bf16[64,2048]{1,0:T(8,128)(2,1)S(1)} %pick.7.refs_3_) | copy-start | bytes 786436
  62.7 12.3 %collective-permute-start.14 = (bf16[64,2048]{1,0:T(8,128)(2,1)S(1)}, bf16[64,2048]{1,0:T(8,128)(2,1)S(1)}, u32[]{:S(2)}, u32[]{:S(2)}) collective-permute-start(bf16[64,2048]{1,0:T(8,128)(2,1)S(1)} %pick.7.refs_3_), channel_id=1, source_target_pairs={{0,2},{4,6},{9,11},{13,15},{18,16},{22,20},{27,25},{31,29}} | collective-permute-start | bytes 786440 | tf_op jit(solution)/shard_map/ppermute | solution.py:327
  67.1 7.9 %collective-permute-start.16 = (bf16[1024,128]{1,0:T(8,128)(2,1)S(1)}, bf16[1024,128]{1,0:T(8,128)(2,1)S(1)}, u32[]{:S(2)}, u32[]{:S(2)}) collective-permute-start(bf16[1024,128]{1,0:T(8,128)(2,1)S(1)} %get-tuple-element.99), channel_id=1, source_target_pairs={{0,1},{1,0},{2,3},{3,2},{4,5},{5,4},{6,7},{7,6},{8,9},{9,8},{10,11... | collective-permute-start | bytes 786440 | tf_op jit(solution)/shard_map/ppermute | solution.py:327
  67.8 6.4 %copy-start.38 = (f32[512,128]{1,0:T(8,128)}, f32[512,128]{1,0:T(8,128)S(1)}, u32[]{:S(2)}) copy-start(f32[512,128]{1,0:T(8,128)S(1)} %get-tuple-element.102.refs_2_) | copy-start | bytes 786436
  67.8 7.2 %collective-permute-start.15 = (bf16[512,128]{1,0:T(8,128)(2,1)S(1)}, bf16[512,128]{1,0:T(8,128)(2,1)S(1)}, u32[]{:S(2)}, u32[]{:S(2)}) collective-permute-start(bf16[512,128]{1,0:T(8,128)(2,1)S(1)} %get-tuple-element.97), channel_id=1, source_target_pairs={{0,2},{1,3},{2,0},{3,1},{4,6},{5,7},{6,4},{7,5},{8,10},{9,11},{10,... | collective-permute-start | bytes 393224 | tf_op jit(solution)/shard_map/ppermute | solution.py:327
  75.0 11.6 %collective-permute-start.17 = (bf16[1024,128]{1,0:T(8,128)(2,1)}, bf16[1024,128]{1,0:T(8,128)(2,1)}, u32[]{:S(2)}, u32[]{:S(2)}) collective-permute-start(bf16[1024,128]{1,0:T(8,128)(2,1)} %get-tuple-element.105), channel_id=1, source_target_pairs={{0,1},{1,0},{2,3},{3,2},{4,5},{5,4},{6,7},{7,6},{8,9},{9,8},{10,11... | collective-permute-start | bytes 786440 | tf_op jit(solution)/shard_map/ppermute | solution.py:327
  77.5 9.1 %collective-permute-start.18 = (bf16[512,128]{1,0:T(8,128)(2,1)}, bf16[512,128]{1,0:T(8,128)(2,1)}, u32[]{:S(2)}, u32[]{:S(2)}) collective-permute-start(bf16[512,128]{1,0:T(8,128)(2,1)} %get-tuple-element.109), channel_id=1, source_target_pairs={{0,2},{1,3},{2,0},{3,1},{4,6},{5,7},{6,4},{7,5},{8,10},{9,11},{10,... | collective-permute-start | bytes 393224 | tf_op jit(solution)/shard_map/ppermute | solution.py:327
  86.4 8.3 %copy-start.46 = (f32[64]{0:T(128)S(1)}, f32[64]{0:T(128)}, u32[]{:S(2)}) copy-start(f32[64]{0:T(128)} %param.9) | copy-start | bytes 772
  86.4 8.3 %copy-start.47 = (s32[64]{0:T(128)S(1)}, s32[64]{0:T(128)}, u32[]{:S(2)}) copy-start(s32[64]{0:T(128)} %param.10) | copy-start | bytes 772
  86.6 8.1 %collective-permute-start.20 = (bf16[512,2048]{1,0:T(8,128)(2,1)S(1)}, bf16[512,2048]{1,0:T(8,128)(2,1)}, u32[]{:S(2)}, u32[]{:S(2)}) collective-permute-start(bf16[512,2048]{1,0:T(8,128)(2,1)S(1)} %pack.1.own_ref), channel_id=1, source_target_pairs={{0,1},{1,0},{2,3},{3,2},{4,5},{5,4},{6,7},{7,6},{8,9},{9,8},{10,11... | collective-permute-start | bytes 6291464 | tf_op jit(solution)/shard_map/ppermute | solution.py:327
  88.7 6.0 %collective-permute-start.19 = (bf16[512,128]{1,0:T(8,128)(2,1)S(1)}, bf16[512,128]{1,0:T(8,128)(2,1)S(1)}, u32[]{:S(2)}, u32[]{:S(2)}) collective-permute-start(bf16[512,128]{1,0:T(8,128)(2,1)S(1)} %get-tuple-element.119), channel_id=1, source_target_pairs={{0,2},{1,3},{2,0},{3,1},{4,6},{5,7},{6,4},{7,5},{8,10},{9,11},{10,... | collective-permute-start | bytes 393224 | tf_op jit(solution)/shard_map/ppermute | solution.py:327
  99.6 1.2 collective-permute-start.21
  100.8 3.9 %collective-permute-start.22 = (f32[24,64]{1,0:T(8,128)S(1)}, f32[24,64]{1,0:T(8,128)S(1)}, u32[]{:S(2)}, u32[]{:S(2)}) collective-permute-start(f32[24,64]{1,0:T(8,128)S(1)} %add.33), channel_id=1, source_target_pairs={{0,2},{1,3},{2,0},{3,1},{4,6},{5,7},{6,4},{7,5},{8,10},{9,11},{10,... | collective-permute-start | bytes 18440 | tf_op jit(solution)/shard_map/ppermute | solution.py:327
  101.1 19.9 %copy-start.7 = (bf16[64,4096]{1,0:T(8,128)(2,1)S(1)}, bf16[64,4096]{1,0:T(8,128)(2,1)}, u32[]{:S(2)}) copy-start(bf16[64,4096]{1,0:T(8,128)(2,1)} %copy-done.6) | copy-start | bytes 1572868
  101.1 19.9 %copy-start.21 = (bf16[32,4096]{1,0:T(8,128)(2,1)S(1)}, bf16[32,4096]{1,0:T(8,128)(2,1)}, u32[]{:S(2)}) copy-start(bf16[32,4096]{1,0:T(8,128)(2,1)} %copy-done.20) | copy-start | bytes 786436
  104.7 3.7 %collective-permute-start.23 = (f32[24,64]{1,0:T(8,128)S(1)}, f32[24,64]{1,0:T(8,128)S(1)}, u32[]{:S(2)}, u32[]{:S(2)}) collective-permute-start(f32[24,64]{1,0:T(8,128)S(1)} %add.34), channel_id=1, source_target_pairs={{0,4},{1,5},{2,6},{3,7},{4,0},{5,1},{6,2},{7,3},{8,12},{9,13},{10,... | collective-permute-start | bytes 18440 | tf_op jit(solution)/shard_map/ppermute | solution.py:327
  108.4 3.7 %collective-permute-start.24 = (f32[24,64]{1,0:T(8,128)S(1)}, f32[24,64]{1,0:T(8,128)S(1)}, u32[]{:S(2)}, u32[]{:S(2)}) collective-permute-start(f32[24,64]{1,0:T(8,128)S(1)} %add.36), channel_id=1, source_target_pairs={{0,8},{1,9},{2,10},{3,11},{4,12},{5,13},{6,14},{7,15},{8,0},{9,1},... | collective-permute-start | bytes 18440 | tf_op jit(solution)/shard_map/ppermute | solution.py:327
  112.1 8.1 %collective-permute-start.25 = (f32[24,64]{1,0:T(8,128)S(1)}, f32[24,64]{1,0:T(8,128)S(1)}, u32[]{:S(2)}, u32[]{:S(2)}) collective-permute-start(f32[24,64]{1,0:T(8,128)S(1)} %add.37), channel_id=1, source_target_pairs={{0,16},{1,17},{2,18},{3,19},{4,20},{5,21},{6,22},{7,23},{8,24},{9,... | collective-permute-start | bytes 18440 | tf_op jit(solution)/shard_map/ppermute | solution.py:327
  (26 other events, 28.7 us)

commit v5 on v4

v5 whole, which is shorter than its diff:
```python
import functools

import jax
import jax.numpy as jnp
from jax import lax
from jax.experimental import pallas as pl
from jax.experimental.pallas import tpu as pltpu
from jax.sharding import PartitionSpec as P

BOTH = ("row", "feat")
HI = 4
MIB = 1 << 20
LANES = 128
BIG = 56
BLOCK, NEAR, EVEN, ROW, FEAT, STARTS = range(6)


def ring_order(count):
    return list(range(0, count, 2)) + list(range(1, count, 2))[::-1]


def ring_next(count):
    order = ring_order(count)
    return {order[i]: order[(i + 1) % count] for i in range(count)}


def call(kernel, name, out_shape, scratch, args, fixed=(), vmem=16, flops=1000):
    on_vmem = pl.BlockSpec(memory_space=pltpu.VMEM)
    on_hbm = pl.BlockSpec(memory_space=pltpu.HBM)
    scalars, rest = args
    out_hbm = "out" in fixed
    held = [x for x in fixed if not isinstance(x, str)]
    return pl.pallas_call(
        kernel,
        in_specs=[pl.BlockSpec(memory_space=pltpu.SMEM)] + [on_hbm] * len(held) + [on_vmem] * len(rest),
        out_specs=jax.tree.map(lambda _: on_hbm if out_hbm else on_vmem, out_shape),
        out_shape=out_shape,
        scratch_shapes=scratch,
        compiler_params=pltpu.CompilerParams(vmem_limit_bytes=vmem * MIB),
        cost_estimate=pl.CostEstimate(flops=flops, bytes_accessed=1000, transcendentals=0),
        name=name,
    )(scalars, *held, *rest)


def touch_kernel(scalars_ref, f_ref, out_ref):
    for i in range(scalars_ref.shape[0]):
        out_ref[i] = scalars_ref[i]


def touch(scalars, inv_factor):
    return pl.pallas_call(
        touch_kernel,
        in_specs=[pl.BlockSpec(memory_space=pltpu.SMEM), pl.BlockSpec(memory_space=pltpu.VMEM)],
        out_specs=pl.BlockSpec(memory_space=pltpu.SMEM),
        out_shape=jax.ShapeDtypeStruct(scalars.shape, scalars.dtype),
        compiler_params=pltpu.CompilerParams(vmem_limit_bytes=16 * MIB),
        cost_estimate=pl.CostEstimate(flops=1000, bytes_accessed=1000, transcendentals=0),
        name="touch",
    )(scalars, inv_factor)


def whiten_kernel(blocks, scalars_ref, f_ref, *refs):
    pieces, (keep_ref, away_ref, x_ref, xt_ref) = refs[:-4], refs[-4:]
    place = 0
    for piece in pieces:
        x_ref[pl.ds(place, piece.shape[0]), :] = piece[...]
        place += piece.shape[0]
    wide = min(512, x_ref.shape[1])
    for c in range(x_ref.shape[1] // wide):
        xt_ref[pl.ds(c * wide, wide), :] = x_ref[:, c * wide:(c + 1) * wide].T
    tile = f_ref.shape[0] // blocks

    def product(t):
        start = pl.multiple_of(scalars_ref[STARTS + t], tile)
        return jnp.dot(f_ref[pl.ds(start, tile), :], xt_ref[...], preferred_element_type=jnp.float32)

    def step(t, carry):
        place = pl.multiple_of(t * tile, tile)
        away_ref[pl.ds(place, tile), :] = product(blocks // 2 + t).astype(jnp.bfloat16)
        keep_ref[pl.ds(place, tile), :] = product(t)
        return carry

    lax.fori_loop(0, blocks // 2, step, 0)


def whiten(scalars, blocks, inv_factor, pieces):
    row_block, feat_block = inv_factor.shape
    rows = sum(p.shape[0] for p in pieces)
    out = (row_block // 2, rows)
    return call(
        functools.partial(whiten_kernel, blocks),
        "whiten",
        [jax.ShapeDtypeStruct(out, jnp.float32), jax.ShapeDtypeStruct(out, jnp.bfloat16)],
        [pltpu.VMEM((rows, feat_block), jnp.bfloat16), pltpu.VMEM((feat_block, rows), jnp.bfloat16)],
        (scalars, [inv_factor] + pieces),
        flops=8 * row_block * feat_block * rows,
    )


def halve_kernel(_, part_ref, got_ref, keep_ref, away_ref):
    left = keep_ref.shape[0]
    keep_ref[...] = part_ref[:left, :] + got_ref[:left, :].astype(jnp.float32)
    away_ref[...] = (part_ref[left:, :] + got_ref[left:, :].astype(jnp.float32)).astype(jnp.bfloat16)


def halve(scalars, part, got):
    out = (part.shape[0] // 2, part.shape[1])
    return call(
        halve_kernel,
        "halve",
        [jax.ShapeDtypeStruct(out, jnp.float32), jax.ShapeDtypeStruct(out, jnp.bfloat16)],
        [],
        (scalars, [part, got]),
    )


def pick_kernel(count, half, scalars_ref, *refs):
    pieces, outs = refs[:count], refs[count:]
    width = outs[0].shape[1]
    start = pl.multiple_of(scalars_ref[BLOCK] * width, width)
    place = 0
    for piece in pieces:
        outs[0][pl.ds(place, piece.shape[0]), :] = piece[:, pl.ds(start, width)]
        place += piece.shape[0]
    if half:
        outs[1][...] = pieces[-1][:half, :]
        for out, piece in zip(outs[2:], pieces):
            out[...] = piece[half:, :]


def pick(scalars, pieces, width, half=0):
    rows = sum(p.shape[0] for p in pieces)
    out = [jax.ShapeDtypeStruct((rows, width), jnp.bfloat16)]
    if half:
        out += [jax.ShapeDtypeStruct((half, pieces[0].shape[1]), jnp.bfloat16)] * len(pieces)
    return call(
        functools.partial(pick_kernel, len(pieces), half), "pick", out, [], (scalars, pieces)
    )


def fetch(pairs, sems):
    copies = [pltpu.make_async_copy(a, b, sems.at[i]) for i, (a, b) in enumerate(pairs)]
    for copy in copies:
        copy.start()
    return copies


def pack_kernel(count, scalars_ref, *refs):
    out_ref, sems = refs[-2:]

    def copy(sources):
        place, pairs = 0, []
        for source in sources:
            pairs.append((source, out_ref.at[pl.ds(place, source.shape[0])]))
            place += source.shape[0]
        for one in fetch(pairs, sems):
            one.wait()

    @pl.when(scalars_ref[NEAR] == 1)
    def _():
        copy(refs[:count])

    @pl.when(scalars_ref[NEAR] == 0)
    def _():
        copy(refs[count:-2])


def pack(scalars, own, got):
    out = (sum(x.shape[0] for x in own), own[0].shape[1])
    return call(
        functools.partial(pack_kernel, len(own)),
        "pack",
        jax.ShapeDtypeStruct(out, jnp.bfloat16),
        [pltpu.SemaphoreType.DMA((len(own),))],
        (scalars, []),
        tuple(own + got),
        BIG,
    )


def join_kernel(scalars_ref, own_ref, other_ref, out_ref, x_ref, xt_ref, sems):
    @pl.when(scalars_ref[EVEN] == 1)
    def _():
        fetch([(own_ref, x_ref)], sems)[0].wait()

    @pl.when(scalars_ref[EVEN] == 0)
    def _():
        fetch([(other_ref, x_ref)], sems)[0].wait()

    wide = min(256, x_ref.shape[1])
    for c in range(x_ref.shape[1] // wide):
        xt_ref[pl.ds(c * wide, wide), :] = x_ref[:, c * wide:(c + 1) * wide].T
    fetch([(xt_ref, out_ref)], sems)[0].wait()


def join(scalars, own, other):
    rows, width = own.shape
    return call(
        join_kernel,
        "join",
        jax.ShapeDtypeStruct((width, rows), jnp.bfloat16),
        [
            pltpu.VMEM((rows, width), jnp.bfloat16),
            pltpu.VMEM((width, rows), jnp.bfloat16),
            pltpu.SemaphoreType.DMA((1,)),
        ],
        (scalars, []),
        (own, other, "out"),
        BIG,
    )


def square_kernel(sizes, first, scalars_ref, *refs):
    early = 2 * len(sizes) - 2
    held = refs[early + 5:-1]
    w_ref, strata_ref, keep_ref, got_ref, out_ref = refs[early:early + 5]
    copies = fetch(list(zip(refs[:early], held)), refs[-1])
    count = out_ref.shape[1]
    slots = sum(sizes)
    out_ref[...] = jnp.zeros_like(out_ref)

    @pl.when(scalars_ref[FEAT] == 0)
    def _():
        out_ref[pl.ds(slots + scalars_ref[ROW], 1), :] = w_ref[...]
        out_ref[pl.ds(2 * slots + scalars_ref[ROW], 1), :] = strata_ref[...].astype(jnp.float32)

    def put(g, part_ref, other_ref):
        slot = first + sum(sizes[:g])
        value = part_ref[...] + other_ref[...].astype(jnp.float32)
        line = jnp.sum(value * value, axis=0, keepdims=True)
        for i in range(sizes[g]):
            out_ref[pl.ds(scalars_ref[slot + i], 1), :] = line[:, i * count:(i + 1) * count]

    put(len(sizes) - 1, keep_ref, got_ref)
    for copy in copies:
        copy.wait()
    for g in range(len(sizes) - 1):
        put(g, held[2 * g], held[2 * g + 1])


def squares(scalars, first, weights, strata, pairs, sizes):
    count = weights.shape[1]
    early = [x for pair in pairs[:-1] for x in pair]
    return call(
        functools.partial(square_kernel, sizes, first),
        "squares",
        jax.ShapeDtypeStruct((3 * sum(sizes), count), jnp.float32),
        [pltpu.VMEM(x.shape, x.dtype) for x in early] + [pltpu.SemaphoreType.DMA((len(early),))],
        (scalars, [weights, strata] + list(pairs[-1])),
        tuple(early),
        BIG,
    )


def weight_step(strata_n, features, row, sums_ref, new_ref, lev_ref, all_ref, d_ref):
    groups = sums_ref.shape[0] // 3
    raw, weights, strata = [sums_ref[pl.ds(i * groups, groups), :] for i in range(3)]
    products = weights * raw
    ratio = jnp.zeros_like(raw)
    for s in range(strata_n):
        inside = strata == float(s)
        mass = jnp.sum(jnp.where(inside, weights, 0.0), keepdims=True)
        product = jnp.sum(jnp.where(inside, products, 0.0), keepdims=True)
        ratio = jnp.where(inside, mass / product, ratio)
    new = products * ratio
    all_ref[...] = new
    new_ref[...] = all_ref[pl.ds(row, 1), :]
    lev_ref[...] = sums_ref[pl.ds(row, 1), :] / features
    step = new - weights
    count = step.shape[1]
    for g in range(groups):
        d_ref[pl.ds(g * count, count), :] = jnp.broadcast_to(step[g:g + 1, :], (LANES, count)).T


def information_kernel(features, pieces_of, scalars_ref, col_hbm, *refs):
    n = len(pieces_of)
    pieces, sums_ref, out_ref, new_ref, lev_ref = refs[:n], refs[n], *refs[n + 1:n + 4]
    all_ref, d_ref, col_ref, p_ref, s_ref, buf_ref, col_sem, p_sems, sems = refs[n + 4:]
    width = s_ref.shape[1]
    steps = out_ref.shape[1] // width
    count = sums_ref.shape[1]
    sizes = [piece.shape[0] for piece in pieces]
    offsets = [sum(sizes[:i]) for i in range(n)]

    def bring(j, i):
        columns = pl.ds(pl.multiple_of(j * width, width), width)
        return pltpu.make_async_copy(
            pieces[i].at[:, columns], p_ref.at[pl.ds(offsets[i], sizes[i]), columns], p_sems.at[j, i]
        )

    def copy(j):
        slot = lax.rem(j, 2)
        return pltpu.make_async_copy(
            buf_ref.at[slot], out_ref.at[:, pl.ds(pl.multiple_of(j * width, width), width)], sems.at[slot]
        )

    column = pltpu.make_async_copy(col_hbm, col_ref, col_sem.at[0])
    for j in range(steps):
        for i in range(n):
            bring(j, i).start()
        if j == 0:
            column.start()
    weight_step(
        2 * (sums_ref.shape[0] // 3), features, scalars_ref[ROW], sums_ref, new_ref, lev_ref, all_ref, d_ref
    )
    column.wait()

    def step(j, carry):
        for i in range(n):
            bring(j, i).wait()
        for i, (slot, first) in enumerate(pieces_of):
            size = sizes[i]
            start = pl.multiple_of(scalars_ref[slot] * count + first, size)
            scale = d_ref[pl.ds(start, size), :]
            for c in range(width // LANES):
                start = pl.multiple_of(j * width + c * LANES, LANES)
                value = p_ref[pl.ds(offsets[i], size), pl.ds(start, LANES)].astype(jnp.float32)
                s_ref[pl.ds(offsets[i], size), c * LANES:(c + 1) * LANES] = (scale * value).astype(jnp.bfloat16)

        @pl.when(j > 1)
        def _():
            copy(j - 2).wait()

        buf_ref[lax.rem(j, 2)] = jnp.dot(col_ref[...], s_ref[...], preferred_element_type=jnp.float32)
        copy(j).start()
        return carry

    lax.fori_loop(0, steps, step, 0)
    for j in range(max(0, steps - 2), steps):
        copy(jnp.int32(j)).wait()


def increment(scalars, pieces_of, sums, column_t, pieces, features):
    row_block, rows = column_t.shape
    groups, count = sums.shape[0] // 3, sums.shape[1]
    feat_block = pieces[0].shape[1]
    width = min(512, feat_block)
    steps = feat_block // width
    on_vmem = pl.BlockSpec(memory_space=pltpu.VMEM)
    on_hbm = pl.BlockSpec(memory_space=pltpu.HBM)
    return pl.pallas_call(
        functools.partial(information_kernel, features, pieces_of),
        in_specs=[pl.BlockSpec(memory_space=pltpu.SMEM)] + [on_hbm] * (1 + len(pieces)) + [on_vmem],
        out_specs=[on_hbm, on_vmem, on_vmem],
        out_shape=[
            jax.ShapeDtypeStruct((row_block, feat_block), jnp.float32),
            jax.ShapeDtypeStruct((1, count), jnp.float32),
            jax.ShapeDtypeStruct((1, count), jnp.float32),
        ],
        scratch_shapes=[
            pltpu.VMEM((groups, count), jnp.float32),
            pltpu.VMEM((rows, LANES), jnp.float32),
            pltpu.VMEM((row_block, rows), jnp.bfloat16),
            pltpu.VMEM((rows, feat_block), jnp.bfloat16),
            pltpu.VMEM((rows, width), jnp.bfloat16),
            pltpu.VMEM((2, row_block, width), jnp.float32),
            pltpu.SemaphoreType.DMA((1,)),
            pltpu.SemaphoreType.DMA((steps, len(pieces))),
            pltpu.SemaphoreType.DMA((2,)),
        ],
        compiler_params=pltpu.CompilerParams(vmem_limit_bytes=BIG * MIB),
        cost_estimate=pl.CostEstimate(
            flops=2 * row_block * feat_block * rows, bytes_accessed=1000, transcendentals=0
        ),
        name="increment",
    )(scalars, column_t, *pieces, sums)


def make(mesh):
    rows_n, feats_n = mesh.shape["row"], mesh.shape["feat"]
    hi_n = HI
    lo_n = rows_n // hi_n
    per_feat = rows_n // feats_n
    everyone = [(r, f) for r in range(rows_n) for f in range(feats_n)]

    def perm(target, keep=lambda r, f: True):
        out = []
        for r, f in everyone:
            if keep(r, f):
                r2, f2 = target(r, f)
                out.append((r * feats_n + f, r2 * feats_n + f2))
        return out

    def send(x, pairs):
        return lax.ppermute(x, BOTH, pairs)

    def swap(x, r_bit, f_bit):
        return send(x, perm(lambda r, f: (r ^ r_bit, f ^ f_bit)))

    fence = lax.optimization_barrier
    hi_next, lo_next = ring_next(hi_n), ring_next(lo_n)
    hi_pairs = perm(lambda r, f: (hi_next[r // lo_n] * lo_n + r % lo_n, f))
    lo_pairs = perm(lambda r, f: (r // lo_n * lo_n + lo_next[r % lo_n], f))
    hi_order, lo_order = ring_order(hi_n), ring_order(lo_n)

    def source(r, k, s):
        h, l = r // lo_n, r % lo_n
        h2 = hi_order[(hi_order.index(h) - k) % hi_n]
        l2 = lo_order[(lo_order.index(l) - s) % lo_n]
        return h2 * lo_n + l2

    feat_bits = [1 << b for b in range(feats_n.bit_length() - 1)]
    far_bits = feat_bits[1:]
    row_bits = [1 << b for b in range(rows_n.bit_length() - 1)]
    relative = [0]
    for bit in reversed(feat_bits):
        relative = relative + [j + bit for j in relative]

    groups = [[(0, s) for s in range(lo_n)] + [(1, 0)]]
    for k in range(1, hi_n):
        groups.append([(k, s) for s in range(1, lo_n)] + ([(k + 1, 0)] if k + 1 < hi_n else []))
    slots = [slot for group in groups for slot in group]
    white_groups = [[(k, s) for s in range(lo_n)] for k in range(hi_n)]
    white_slots = [slot for group in white_groups for slot in group]

    def per_device(candidates, inv_factor, weights, strata):
        rows_dev, feat_block = candidates.shape
        row_block = inv_factor.shape[0]
        features = feat_block * feats_n
        half = rows_dev // 2
        row, feat = lax.axis_index("row"), lax.axis_index("feat")
        def sources(chosen):
            table = [[source(r, *slot) for slot in chosen] for r in range(rows_n)]
            return jnp.asarray(table, jnp.int32)[row]

        apart = feat ^ (row // per_feat)
        fixed = [row % per_feat, apart == 0, apart % 2 == 0, row, feat]
        scalars = jnp.concatenate([
            jnp.stack([jnp.asarray(x, jnp.int32) for x in fixed]),
            (jnp.asarray(relative, jnp.int32) ^ feat) * (row_block // feats_n),
            sources(slots),
            sources(white_slots),
        ])
        first_place = STARTS + feats_n
        first_white = first_place + rows_n

        def pieces_of(chosen):
            return [p for slot in chosen for p in chunks[slot]]

        def column_far(mine):
            for bit in reversed(far_bits):
                got = send(mine, perm(
                    lambda r, f: (r, f ^ bit),
                    lambda r, f: (f ^ (r // per_feat)) % (2 * bit) == 0,
                ))
                if len(far_bits) > 1:
                    mine = got = jnp.where(apart % (2 * bit) == 0, mine, got)
            return got

        def to_far(near):
            keep, away = halve(scalars, *near)
            for bit in far_bits[:-1]:
                keep, away = halve(scalars, keep, swap(away, 0, bit))
            return keep, swap(away, 0, far_bits[-1])

        chunks = {(0, 0): [candidates]}
        columns, far_columns, white, near, far = [], [], [], [], []
        for k in range(hi_n + 1):
            fresh, out = [], {}
            if k > 0:
                last = k == hi_n - 1
                picked = pick(scalars, pieces_of(groups[k - 1]), row_block, half if last else 0)
                columns.append(picked[0])
            if k < hi_n - 1:
                fresh.append((k + 1, 0))
                chunks[k + 1, 0] = [send(chunks[k, 0][0], hi_pairs)]
                held = chunks[k, 0][0]
                for s in range(1, lo_n):
                    fresh.append((k, s))
                    held = send(held, lo_pairs)
                    chunks[k, s] = [held]
            elif k < hi_n:
                held = picked[1]
                for s in range(1, lo_n):
                    fresh.append((k, s))
                    held = send(held, lo_pairs)
                    chunks[k, s] = [held, send(picked[1 + s], hi_pairs)]
            out["fresh"] = [chunks[slot] for slot in fresh]
            if k == 0:
                out["scalars"] = touch(scalars, inv_factor)
            if k > 0:
                out["column"] = column_far(columns[-1])
                out["white"] = whiten(scalars, feats_n, inv_factor, pieces_of(white_groups[k - 1]))
            if k > 1:
                keep, away = white[k - 2]
                out["near"] = keep, swap(away, 0, 1)
            if k > 2:
                out["far"] = to_far(near[k - 3])
            out = fence(out)
            for slot, value in zip(fresh, out["fresh"]):
                chunks[slot] = value
            scalars = out.get("scalars", scalars)
            for name, kept in (("column", far_columns), ("white", white), ("near", near), ("far", far)):
                if name in out:
                    kept.append(out[name])
        keep, away = white[-1]
        packed = pack(scalars, columns, far_columns)
        last, before, packed = fence(((keep, swap(away, 0, 1)), to_far(near[-1]), packed))
        far.append(before)
        last, beside = fence((to_far(last), swap(packed, 0, 1)))
        far.append(last)
        sizes = [len(g) for g in white_groups]
        total = squares(scalars, first_white, weights[None], strata[None], far, sizes)
        total = fence(total + swap(total, 0, 1))
        column_t = join(scalars, packed, beside)
        bits = [(0, bit) for bit in far_bits] + [(bit, 0) for bit in row_bits]
        for i, bit in enumerate(bits):
            total = total + swap(total, *bit)
            if i == 0:
                total, column_t = fence((total, column_t))

        origins = []
        for i, slot in enumerate(slots):
            first = 0
            for piece in chunks[slot]:
                origins.append((first_place + i, first))
                first += piece.shape[0]
        information, new_weight, leverage = increment(
            scalars, origins, total, column_t, pieces_of(slots), features
        )
        return (new_weight.reshape(rows_dev), leverage.reshape(rows_dev), information)

    return per_device


def solution(mesh):
    in_specs = (P("row", "feat"), P("row", "feat"), P("row"), P("row"))
    out_specs = (P("row"), P("row"), P("row", "feat"))
    return jax.shard_map(
        make(mesh), mesh=mesh, in_specs=in_specs, out_specs=out_specs, check_vma=False
    )
```

time: 145 us -> 136 us (0.938)
  local copies, waits for them, and re-layouts: 37.4 us -> 9.72 us
  Pallas kernels: 47 us -> 58.6 us
  waiting for transfers between devices: 18.3 us -> 26.6 us
  between operations: 6.35 us -> 1.37 us
  starting transfers between devices: 34.2 us -> 37.3 us
    unnamed x96 -> x60, local copies, waits for them, and re-layouts: 35.9 us -> 8.95 us
    pallas_call x0 -> x1, Pallas kernels: none -> 19.7 us  [increment(): pl.pallas_call(functools.partial(information_kernel, features, pieces_of)...]
    ppermute x26, waiting for transfers between devices: 18.3 us -> 26.6 us  [send(): return lax.ppermute(x, BOTH, pairs)]
    pallas_call x17 -> x15, Pallas kernels: 45.8 us -> 37.8 us  [call(): pl.pallas_call(kernel, in_specs=[pl.BlockSpec(memory_space=pltpu.SMEM)] +...]
    ppermute x26, starting transfers between devices: 34.2 us -> 37.3 us  [send(): return lax.ppermute(x, BOTH, pairs)]
  transfers between devices with their start and end apart: 26 -> 26, of which waited for: 10 -> 12; matrix products, arithmetic and copies ran while one was open for 1% -> 1% of each run, Pallas kernels for 20% -> 25%
where the time goes in v5:
time: 136 us
  Pallas kernels  58.6 us (43%)
  starting transfers between devices  37.3 us (27%)
  waiting for transfers between devices  26.6 us (20%)
  local copies, waits for them, and re-layouts  9.72 us (7%)
  other arithmetic  1.98 us (1%)
  between operations  1.37 us (1%)
    pallas_call x15, Pallas kernels, call(): pl.pallas_call(kernel, in_specs=[pl.BlockSpec(memory_space=pltpu.SMEM)] +...  37.8 us
    ppermute x26, starting transfers between devices, send(): return lax.ppermute(x, BOTH, pairs)  37.3 us
    ppermute x26, waiting for transfers between devices, send(): return lax.ppermute(x, BOTH, pairs)  26.6 us
    pallas_call x1, Pallas kernels, increment(): pl.pallas_call(functools.partial(information_kernel, features, pieces_of)...  19.7 us
    unnamed x60, local copies, waits for them, and re-layouts  8.95 us
  transfers between devices with their start and end apart: 26, of which 12 were waited for; matrix products, arithmetic and copies ran while one was open for 1% of the time, Pallas kernels for 25%

profile of v5, /device:TPU:0, one launch (start us, length us, event | category | flops | bytes accessed | tf_op | source)
XLA Modules:
  0.0 135.6 jit_solution(5054142420296671468)
XLA Ops:
  0.6 3.0 %collective-permute-start.1 = (bf16[64,4096]{1,0:T(8,128)(2,1)}, bf16[64,4096]{1,0:T(8,128)(2,1)S(1)}, u32[]{:S(2)}, u32[]{:S(2)}) collective-permute-start(bf16[64,4096]{1,0:T(8,128)(2,1)} %refs_0_.5), channel_id=1, source_target_pairs={{0,4},{1,5},{2,6},{3,7},{4,0},{5,1},{6,2},{7,3},{8,12},{9,13},{10,... | collective-permute-start | bytes 1572872 | tf_op jit(solution)/shard_map/ppermute | solution.py:385
  3.6 2.6 %collective-permute-start = (bf16[64,4096]{1,0:T(8,128)(2,1)}, bf16[64,4096]{1,0:T(8,128)(2,1)S(1)}, u32[]{:S(2)}, u32[]{:S(2)}) collective-permute-start(bf16[64,4096]{1,0:T(8,128)(2,1)} %refs_0_.5), channel_id=1, source_target_pairs={{0,16},{1,17},{2,18},{3,19},{4,20},{5,21},{6,22},{7,23},{8,0},{9,1... | collective-permute-start | bytes 1572872 | tf_op jit(solution)/shard_map/ppermute | solution.py:385
  6.2 0.7 dynamic-slice_bitcast_fusion
  6.9 0.7 xor_multiply_fusion
  7.7 5.8 %copy-done = bf16[2048,4096]{1,0:T(8,128)(2,1)S(1)} copy-done((bf16[2048,4096]{1,0:T(8,128)(2,1)S(1)}, bf16[2048,4096]{1,0:T(8,128)(2,1)}, u32[]{:S(2)}) %copy-start) | copy-done | bytes 16777240
  13.4 1.1 touch.1.scalars_ref._
  14.6 1.2 collective-permute-done.1.refs_1_
  15.8 1.7 %collective-permute-done.refs_2_.refs_0_ = bf16[64,4096]{1,0:T(8,128)(2,1)S(1)} collective-permute-done((bf16[64,4096]{1,0:T(8,128)(2,1)}, bf16[64,4096]{1,0:T(8,128)(2,1)S(1)}, u32[]{:S(2)}, u32[]{:S(2)}) %collective-permute-start) | collective-permute-done | bytes 524320 | tf_op jit(solution)/shard_map/ppermute | solution.py:385
  18.0 3.3 %collective-permute-start.3 = (bf16[64,4096]{1,0:T(8,128)(2,1)S(1)}, bf16[64,4096]{1,0:T(8,128)(2,1)S(1)}, u32[]{:S(2)}, u32[]{:S(2)}) collective-permute-start(bf16[64,4096]{1,0:T(8,128)(2,1)S(1)} %collective-permute-done.refs_2_.refs_0_), channel_id=1, source_target_pairs={{0,16},{1,17},{2,18},{3,19},{4,20},{5,21},{6,22},{7,23},{8,0},{9,1... | collective-permute-start | bytes 1572872 | tf_op jit(solution)/shard_map/ppermute | solution.py:385
  21.3 1.0 copy-done.5
  22.3 0.6 pick.4.refs_0_
  22.9 3.5 %collective-permute-start.2 = (bf16[192,2048]{1,0:T(8,128)(2,1)S(1)}, bf16[192,2048]{1,0:T(8,128)(2,1)S(1)}, u32[]{:S(2)}, u32[]{:S(2)}) collective-permute-start(bf16[192,2048]{1,0:T(8,128)(2,1)S(1)} %pick.4.refs_0_), channel_id=1, source_target_pairs={{0,2},{4,6},{9,11},{13,15},{18,16},{22,20},{27,25},{31,29}} | collective-permute-start | bytes 2359304 | tf_op jit(solution)/shard_map/ppermute | solution.py:385
  26.4 5.5 %whiten.4 = (f32[1024,128]{1,0:T(8,128)S(1)}, bf16[1024,128]{1,0:T(8,128)(2,1)S(1)}) custom-call(s32[25]{0:T(128)S(1)} %touch.1.scalars_ref._, bf16[2048,4096]{1,0:T(8,128)(2,1)S(1)} %copy-done.1, bf16[64,4096]{1,0:T(8,128)(2,1)S(1)} %copy-done.5, bf16[64,4096]{1,0:T(8,128)(2,1)S(1)} %collective-permute-done.1.refs_1_), custom_call_target="tpu_custom_call" | custom-call | flops 8589934592 | bytes 1000 | tf_op jit(solution)/shard_map/whiten/pallas_call | solution.py:33
  32.0 3.8 %collective-permute-done.2.refs_4_ = bf16[192,2048]{1,0:T(8,128)(2,1)S(1)} collective-permute-done((bf16[192,2048]{1,0:T(8,128)(2,1)S(1)}, bf16[192,2048]{1,0:T(8,128)(2,1)S(1)}, u32[]{:S(2)}, u32[]{:S(2)}) %collective-permute-start.2) | collective-permute-done | bytes 786464 | tf_op jit(solution)/shard_map/ppermute | solution.py:385
  35.8 1.5 %collective-permute-start.7 = (bf16[64,4096]{1,0:T(8,128)(2,1)S(1)}, bf16[64,4096]{1,0:T(8,128)(2,1)S(1)}, u32[]{:S(2)}, u32[]{:S(2)}) collective-permute-start(bf16[64,4096]{1,0:T(8,128)(2,1)S(1)} %collective-permute-done.3.refs_1_.refs_0_.refs_4_), channel_id=1, source_target_pairs={{0,4},{1,5},{2,6},{3,7},{4,0},{5,1},{6,2},{7,3},{8,12},{9,13},{10,... | collective-permute-start | bytes 1572872 | tf_op jit(solution)/shard_map/ppermute | solution.py:385
  37.3 1.6 %collective-permute-start.6 = (bf16[64,4096]{1,0:T(8,128)(2,1)S(1)}, bf16[64,4096]{1,0:T(8,128)(2,1)S(1)}, u32[]{:S(2)}, u32[]{:S(2)}) collective-permute-start(bf16[64,4096]{1,0:T(8,128)(2,1)S(1)} %collective-permute-done.3.refs_1_.refs_0_.refs_4_), channel_id=1, source_target_pairs={{0,16},{1,17},{2,18},{3,19},{4,20},{5,21},{6,22},{7,23},{8,0},{9,1... | collective-permute-start | bytes 1572872 | tf_op jit(solution)/shard_map/ppermute | solution.py:385
  39.6 2.8 %collective-permute-start.5 = (bf16[128,2048]{1,0:T(8,128)(2,1)S(1)}, bf16[128,2048]{1,0:T(8,128)(2,1)S(1)}, u32[]{:S(2)}, u32[]{:S(2)}) collective-permute-start(bf16[128,2048]{1,0:T(8,128)(2,1)S(1)} %pick.5.refs_1_), channel_id=1, source_target_pairs={{0,2},{4,6},{9,11},{13,15},{18,16},{22,20},{27,25},{31,29}} | collective-permute-start | bytes 1572872 | tf_op jit(solution)/shard_map/ppermute | solution.py:385
  42.4 5.5 %whiten.5 = (f32[1024,128]{1,0:T(8,128)S(1)}, bf16[1024,128]{1,0:T(8,128)(2,1)S(1)}) custom-call(s32[25]{0:T(128)S(1)} %touch.1.scalars_ref._, bf16[2048,4096]{1,0:T(8,128)(2,1)S(1)} %copy-done.1, bf16[64,4096]{1,0:T(8,128)(2,1)S(1)} %collective-permute-done.refs_2_.refs_0_, bf16[64,4096]{1,0:T(8,128)(2,1)S(1)} %collective-permute-done.4.refs_0_.refs_1_.refs_3_), custom_call_target="tpu_custom_call" | custom-call | flops 8589934592 | bytes 1000 | tf_op jit(solution)/shard_map/whiten/pallas_call | solution.py:33
  47.9 2.0 %collective-permute-done.5.refs_5_ = bf16[128,2048]{1,0:T(8,128)(2,1)S(1)} collective-permute-done((bf16[128,2048]{1,0:T(8,128)(2,1)S(1)}, bf16[128,2048]{1,0:T(8,128)(2,1)S(1)}, u32[]{:S(2)}, u32[]{:S(2)}) %collective-permute-start.5) | collective-permute-done | bytes 524320 | tf_op jit(solution)/shard_map/ppermute | solution.py:385
  49.9 0.6 halve.4
  50.5 2.5 %collective-permute-start.10 = (bf16[512,128]{1,0:T(8,128)(2,1)S(1)}, bf16[512,128]{1,0:T(8,128)(2,1)S(1)}, u32[]{:S(2)}, u32[]{:S(2)}) collective-permute-start(bf16[512,128]{1,0:T(8,128)(2,1)S(1)} %get-tuple-element.83), channel_id=1, source_target_pairs={{0,2},{1,3},{2,0},{3,1},{4,6},{5,7},{6,4},{7,5},{8,10},{9,11},{10,... | collective-permute-start | bytes 393224 | tf_op jit(solution)/shard_map/ppermute | solution.py:385
  53.1 0.6 pick.6
  53.7 0.6 collective-permute-start.11
  54.3 3.1 %collective-permute-start.9 = (bf16[128,2048]{1,0:T(8,128)(2,1)S(1)}, bf16[128,2048]{1,0:T(8,128)(2,1)S(1)}, u32[]{:S(2)}, u32[]{:S(2)}) collective-permute-start(bf16[128,2048]{1,0:T(8,128)(2,1)S(1)} %get-tuple-element.79.refs_2_), channel_id=1, source_target_pairs={{0,2},{4,6},{9,11},{13,15},{18,16},{22,20},{27,25},{31,29}} | collective-permute-start | bytes 1572872 | tf_op jit(solution)/shard_map/ppermute | solution.py:385
  57.4 5.5 %whiten.6 = (f32[1024,128]{1,0:T(8,128)S(1)}, bf16[1024,128]{1,0:T(8,128)(2,1)S(1)}) custom-call(s32[25]{0:T(128)S(1)} %touch.1.scalars_ref._, bf16[2048,4096]{1,0:T(8,128)(2,1)S(1)} %copy-done.1, bf16[64,4096]{1,0:T(8,128)(2,1)S(1)} %collective-permute-done.3.refs_1_.refs_0_.refs_4_, bf16[64,4096]{1,0:T(8,128)(2,1)S(1)} %collective-permute-done.7.refs_0_.refs_1_.refs_5_), custom_call_target="tpu_custom_call" | custom-call | flops 8589934592 | bytes 1000 | tf_op jit(solution)/shard_map/whiten/pallas_call | solution.py:33
  63.1 1.0 collective-permute-done.9.refs_6_
  64.6 4.4 %collective-permute-start.14 = (bf16[64,2048]{1,0:T(8,128)(2,1)S(1)}, bf16[64,2048]{1,0:T(8,128)(2,1)S(1)}, u32[]{:S(2)}, u32[]{:S(2)}) collective-permute-start(bf16[64,2048]{1,0:T(8,128)(2,1)S(1)} %pick.7.refs_3_), channel_id=1, source_target_pairs={{0,2},{4,6},{9,11},{13,15},{18,16},{22,20},{27,25},{31,29}} | collective-permute-start | bytes 786440 | tf_op jit(solution)/shard_map/ppermute | solution.py:385
  69.1 0.6 halve.5
  69.8 5.5 %whiten.7 = (f32[1024,128]{1,0:T(8,128)S(1)}, bf16[1024,128]{1,0:T(8,128)(2,1)S(1)}) custom-call(s32[25]{0:T(128)S(1)} %touch.1.scalars_ref._, bf16[2048,4096]{1,0:T(8,128)(2,1)S(1)} %copy-done.1, bf16[64,4096]{1,0:T(8,128)(2,1)S(1)} %collective-permute-done.6.refs_1_.refs_0_.refs_6_, bf16[32,4096]{1,0:T(8,128)(2,1)S(1)} %collective-permute-done.11.refs_0_.refs_1_.refs_7_, ...), custom_call_target="tpu_custom_call" | custom-call | flops 8589934592 | bytes 1000 | tf_op jit(solution)/shard_map/whiten/pallas_call | solution.py:33
  76.6 0.7 copy-done.15
  77.3 2.3 %collective-permute-start.18 = (bf16[512,128]{1,0:T(8,128)(2,1)S(1)}, bf16[512,128]{1,0:T(8,128)(2,1)S(1)}, u32[]{:S(2)}, u32[]{:S(2)}) collective-permute-start(bf16[512,128]{1,0:T(8,128)(2,1)S(1)} %get-tuple-element.109), channel_id=1, source_target_pairs={{0,2},{1,3},{2,0},{3,1},{4,6},{5,7},{6,4},{7,5},{8,10},{9,11},{10,... | collective-permute-start | bytes 393224 | tf_op jit(solution)/shard_map/ppermute | solution.py:385
  79.6 3.5 %pack.1.own_ref = bf16[512,2048]{1,0:T(8,128)(2,1)} custom-call(s32[25]{0:T(128)} %copy-done.19, bf16[192,2048]{1,0:T(8,128)(2,1)} %copy-done.2, bf16[128,2048]{1,0:T(8,128)(2,1)} %copy-done.3, bf16[128,2048]{1,0:T(8,128)(2,1)} %copy-done.8, bf16[64,2048]{1,0:T(8,128)(2,1)} %copy-done.4, bf16[192,2048]{1,0:T(8,128)(2,1)} %copy-done.22, ...), custom_call_target="tpu_custom_call" | custom-call | flops 1000 | bytes 1000 | tf_op jit(solution)/shard_map/pack/pallas_call | solution.py:33
  83.2 0.6 collective-permute-done.18.refs_5_
  84.4 0.7 copy-done.16
  85.1 1.7 %collective-permute-start.19 = (bf16[512,128]{1,0:T(8,128)(2,1)S(1)}, bf16[512,128]{1,0:T(8,128)(2,1)S(1)}, u32[]{:S(2)}, u32[]{:S(2)}) collective-permute-start(bf16[512,128]{1,0:T(8,128)(2,1)S(1)} %get-tuple-element.119), channel_id=1, source_target_pairs={{0,2},{1,3},{2,0},{3,1},{4,6},{5,7},{6,4},{7,5},{8,10},{9,11},{10,... | collective-permute-start | bytes 393224 | tf_op jit(solution)/shard_map/ppermute | solution.py:385
  86.8 4.2 %collective-permute-done.19.refs_9_ = bf16[512,128]{1,0:T(8,128)(2,1)S(1)} collective-permute-done((bf16[512,128]{1,0:T(8,128)(2,1)S(1)}, bf16[512,128]{1,0:T(8,128)(2,1)S(1)}, u32[]{:S(2)}, u32[]{:S(2)}) %collective-permute-start.19) | collective-permute-done | bytes 131104 | tf_op jit(solution)/shard_map/ppermute | solution.py:385
  91.0 0.6 copy-done.29
  91.6 3.2 %squares.1 = f32[24,64]{1,0:T(8,128)} custom-call(s32[25]{0:T(128)} %copy-done.19, f32[512,128]{1,0:T(8,128)} %copy-done.13, bf16[512,128]{1,0:T(8,128)(2,1)} %copy-done.26, f32[512,128]{1,0:T(8,128)} %copy-done.14, bf16[512,128]{1,0:T(8,128)(2,1)} %copy-done.27, f32[512,128]{1,0:T(8,128)} %copy-done.15, bf16[512,128]{1,0:T(8,128)(2,1)} %copy-done.28, ...), custom_call_target="tpu_custom_call" | custom-call | flops 1000 | bytes 1000 | tf_op jit(solution)/shard_map/squares/pallas_call | solution.py:33
  95.0 1.4 %collective-permute-done.21 = f32[24,64]{1,0:T(8,128)S(1)} collective-permute-done((f32[24,64]{1,0:T(8,128)}, f32[24,64]{1,0:T(8,128)S(1)}, u32[]{:S(2)}, u32[]{:S(2)}) %collective-permute-start.21) | collective-permute-done | bytes 6176 | tf_op jit(solution)/shard_map/ppermute | solution.py:385
  96.3 0.7 add.30
  97.0 1.7 %collective-permute-start.22 = (f32[24,64]{1,0:T(8,128)S(1)}, f32[24,64]{1,0:T(8,128)S(1)}, u32[]{:S(2)}, u32[]{:S(2)}) collective-permute-start(f32[24,64]{1,0:T(8,128)S(1)} %add.30), channel_id=1, source_target_pairs={{0,2},{1,3},{2,0},{3,1},{4,6},{5,7},{6,4},{7,5},{8,10},{9,11},{10,... | collective-permute-start | bytes 18440 | tf_op jit(solution)/shard_map/ppermute | solution.py:385
  98.8 4.2 %join.1.col_hbm = bf16[2048,512]{1,0:T(8,128)(2,1)} custom-call(s32[25]{0:T(128)} %copy-done.19, bf16[512,2048]{1,0:T(8,128)(2,1)} %pack.1.own_ref, bf16[512,2048]{1,0:T(8,128)(2,1)} %copy-done.21), custom_call_target="tpu_custom_call" | custom-call | flops 1000 | bytes 1000 | tf_op jit(solution)/shard_map/join/pallas_call | solution.py:33
  103.0 1.6 %collective-permute-start.23 = (f32[24,64]{1,0:T(8,128)S(1)}, f32[24,64]{1,0:T(8,128)S(1)}, u32[]{:S(2)}, u32[]{:S(2)}) collective-permute-start(f32[24,64]{1,0:T(8,128)S(1)} %add.31), channel_id=1, source_target_pairs={{0,4},{1,5},{2,6},{3,7},{4,0},{5,1},{6,2},{7,3},{8,12},{9,13},{10,... | collective-permute-start | bytes 18440 | tf_op jit(solution)/shard_map/ppermute | solution.py:385
  104.6 2.2 %collective-permute-done.23 = f32[24,64]{1,0:T(8,128)S(1)} collective-permute-done((f32[24,64]{1,0:T(8,128)S(1)}, f32[24,64]{1,0:T(8,128)S(1)}, u32[]{:S(2)}, u32[]{:S(2)}) %collective-permute-start.23) | collective-permute-done | bytes 6176 | tf_op jit(solution)/shard_map/ppermute | solution.py:385
  106.8 3.7 %collective-permute-done.24 = f32[24,64]{1,0:T(8,128)S(1)} collective-permute-done((f32[24,64]{1,0:T(8,128)S(1)}, f32[24,64]{1,0:T(8,128)S(1)}, u32[]{:S(2)}, u32[]{:S(2)}) %collective-permute-start.24) | collective-permute-done | bytes 6176 | tf_op jit(solution)/shard_map/ppermute | solution.py:385
  110.5 4.6 %collective-permute-done.25 = f32[24,64]{1,0:T(8,128)S(1)} collective-permute-done((f32[24,64]{1,0:T(8,128)S(1)}, f32[24,64]{1,0:T(8,128)S(1)}, u32[]{:S(2)}, u32[]{:S(2)}) %collective-permute-start.25) | collective-permute-done | bytes 6176 | tf_op jit(solution)/shard_map/ppermute | solution.py:385
  115.1 0.6 add.34.refs_9_
  115.7 19.7 %increment.1 = (f32[2048,4096]{1,0:T(8,128)}, f32[1,64]{1,0:T(1,128)}, f32[1,64]{1,0:T(1,128)}) custom-call(s32[25]{0:T(128)} %copy-done.19, bf16[2048,512]{1,0:T(8,128)(2,1)} %join.1.col_hbm, bf16[64,4096]{1,0:T(8,128)(2,1)} %refs_0_.5, bf16[64,4096]{1,0:T(8,128)(2,1)} %copy-done.6, bf16[64,4096]{1,0:T(8,128)(2,1)} %copy-done.7, ...), custom_call_target="tpu_custom_call" | custom-call | flops 8589934592 | bytes 1000 | tf_op jit(solution)/shard_map/increment/pallas_call | solution.py:341
  (89 shorter events, 3.9 us)
Async XLA Ops:
  0.6 15.1 %collective-permute-start.1 = (bf16[64,4096]{1,0:T(8,128)(2,1)}, bf16[64,4096]{1,0:T(8,128)(2,1)S(1)}, u32[]{:S(2)}, u32[]{:S(2)}) collective-permute-start(bf16[64,4096]{1,0:T(8,128)(2,1)} %refs_0_.5), channel_id=1, source_target_pairs={{0,4},{1,5},{2,6},{3,7},{4,0},{5,1},{6,2},{7,3},{8,12},{9,13},{10,... | collective-permute-start | bytes 1572872 | tf_op jit(solution)/shard_map/ppermute | solution.py:385
  3.6 13.8 %collective-permute-start = (bf16[64,4096]{1,0:T(8,128)(2,1)}, bf16[64,4096]{1,0:T(8,128)(2,1)S(1)}, u32[]{:S(2)}, u32[]{:S(2)}) collective-permute-start(bf16[64,4096]{1,0:T(8,128)(2,1)} %refs_0_.5), channel_id=1, source_target_pairs={{0,16},{1,17},{2,18},{3,19},{4,20},{5,21},{6,22},{7,23},{8,0},{9,1... | collective-permute-start | bytes 1572872 | tf_op jit(solution)/shard_map/ppermute | solution.py:385
  13.4 13.0 %copy-start.1 = (bf16[2048,4096]{1,0:T(8,128)(2,1)S(1)}, bf16[2048,4096]{1,0:T(8,128)(2,1)}, u32[]{:S(2)}) copy-start(bf16[2048,4096]{1,0:T(8,128)(2,1)} %f_ref.9) | copy-start | bytes 50331652
  14.6 61.4 %copy-start.19 = (s32[25]{0:T(128)}, s32[25]{0:T(128)S(1)}, u32[]{:S(2)}) copy-start(s32[25]{0:T(128)S(1)} %touch.1.scalars_ref._) | copy-start | bytes 304
  15.8 16.2 %copy-start.6 = (bf16[64,4096]{1,0:T(8,128)(2,1)}, bf16[64,4096]{1,0:T(8,128)(2,1)S(1)}, u32[]{:S(2)}) copy-start(bf16[64,4096]{1,0:T(8,128)(2,1)S(1)} %collective-permute-done.1.refs_1_) | copy-start | bytes 1572868
  17.4 24.9 %copy-start.7 = (bf16[64,4096]{1,0:T(8,128)(2,1)}, bf16[64,4096]{1,0:T(8,128)(2,1)S(1)}, u32[]{:S(2)}) copy-start(bf16[64,4096]{1,0:T(8,128)(2,1)S(1)} %collective-permute-done.refs_2_.refs_0_) | copy-start | bytes 1572868
  17.4 14.5 %collective-permute-start.4 = (bf16[64,4096]{1,0:T(8,128)(2,1)S(1)}, bf16[64,4096]{1,0:T(8,128)(2,1)S(1)}, u32[]{:S(2)}, u32[]{:S(2)}) collective-permute-start(bf16[64,4096]{1,0:T(8,128)(2,1)S(1)} %collective-permute-done.refs_2_.refs_0_), channel_id=1, source_target_pairs={{0,4},{1,5},{2,6},{3,7},{4,0},{5,1},{6,2},{7,3},{8,12},{9,13},{10,... | collective-permute-start | bytes 1572872 | tf_op jit(solution)/shard_map/ppermute | solution.py:385
  18.0 14.0 %collective-permute-start.3 = (bf16[64,4096]{1,0:T(8,128)(2,1)S(1)}, bf16[64,4096]{1,0:T(8,128)(2,1)S(1)}, u32[]{:S(2)}, u32[]{:S(2)}) collective-permute-start(bf16[64,4096]{1,0:T(8,128)(2,1)S(1)} %collective-permute-done.refs_2_.refs_0_), channel_id=1, source_target_pairs={{0,16},{1,17},{2,18},{3,19},{4,20},{5,21},{6,22},{7,23},{8,0},{9,1... | collective-permute-start | bytes 1572872 | tf_op jit(solution)/shard_map/ppermute | solution.py:385
  22.9 9.0 %copy-start.2 = (bf16[192,2048]{1,0:T(8,128)(2,1)}, bf16[192,2048]{1,0:T(8,128)(2,1)S(1)}, u32[]{:S(2)}) copy-start(bf16[192,2048]{1,0:T(8,128)(2,1)S(1)} %pick.4.refs_0_) | copy-start | bytes 2359300
  22.9 12.9 %collective-permute-start.2 = (bf16[192,2048]{1,0:T(8,128)(2,1)S(1)}, bf16[192,2048]{1,0:T(8,128)(2,1)S(1)}, u32[]{:S(2)}, u32[]{:S(2)}) collective-permute-start(bf16[192,2048]{1,0:T(8,128)(2,1)S(1)} %pick.4.refs_0_), channel_id=1, source_target_pairs={{0,2},{4,6},{9,11},{13,15},{18,16},{22,20},{27,25},{31,29}} | collective-permute-start | bytes 2359304 | tf_op jit(solution)/shard_map/ppermute | solution.py:385
  32.0 15.9 %copy-start.9 = (bf16[64,4096]{1,0:T(8,128)(2,1)}, bf16[64,4096]{1,0:T(8,128)(2,1)S(1)}, u32[]{:S(2)}) copy-start(bf16[64,4096]{1,0:T(8,128)(2,1)S(1)} %collective-permute-done.4.refs_0_.refs_1_.refs_3_) | copy-start | bytes 1572868
  32.0 25.4 %copy-start.10 = (bf16[64,4096]{1,0:T(8,128)(2,1)}, bf16[64,4096]{1,0:T(8,128)(2,1)S(1)}, u32[]{:S(2)}) copy-start(bf16[64,4096]{1,0:T(8,128)(2,1)S(1)} %collective-permute-done.3.refs_1_.refs_0_.refs_4_) | copy-start | bytes 1572868
  35.8 12.1 %copy-start.22 = (bf16[192,2048]{1,0:T(8,128)(2,1)}, bf16[192,2048]{1,0:T(8,128)(2,1)S(1)}, u32[]{:S(2)}) copy-start(bf16[192,2048]{1,0:T(8,128)(2,1)S(1)} %collective-permute-done.2.refs_4_) | copy-start | bytes 2359300
  35.8 14.1 %collective-permute-start.7 = (bf16[64,4096]{1,0:T(8,128)(2,1)S(1)}, bf16[64,4096]{1,0:T(8,128)(2,1)S(1)}, u32[]{:S(2)}, u32[]{:S(2)}) collective-permute-start(bf16[64,4096]{1,0:T(8,128)(2,1)S(1)} %collective-permute-done.3.refs_1_.refs_0_.refs_4_), channel_id=1, source_target_pairs={{0,4},{1,5},{2,6},{3,7},{4,0},{5,1},{6,2},{7,3},{8,12},{9,13},{10,... | collective-permute-start | bytes 1572872 | tf_op jit(solution)/shard_map/ppermute | solution.py:385
  37.3 12.6 %collective-permute-start.6 = (bf16[64,4096]{1,0:T(8,128)(2,1)S(1)}, bf16[64,4096]{1,0:T(8,128)(2,1)S(1)}, u32[]{:S(2)}, u32[]{:S(2)}) collective-permute-start(bf16[64,4096]{1,0:T(8,128)(2,1)S(1)} %collective-permute-done.3.refs_1_.refs_0_.refs_4_), channel_id=1, source_target_pairs={{0,16},{1,17},{2,18},{3,19},{4,20},{5,21},{6,22},{7,23},{8,0},{9,1... | collective-permute-start | bytes 1572872 | tf_op jit(solution)/shard_map/ppermute | solution.py:385
  39.0 9.0 %collective-permute-start.8 = (bf16[1024,128]{1,0:T(8,128)(2,1)S(1)}, bf16[1024,128]{1,0:T(8,128)(2,1)S(1)}, u32[]{:S(2)}, u32[]{:S(2)}) collective-permute-start(bf16[1024,128]{1,0:T(8,128)(2,1)S(1)} %get-tuple-element.74), channel_id=1, source_target_pairs={{0,1},{1,0},{2,3},{3,2},{4,5},{5,4},{6,7},{7,6},{8,9},{9,8},{10,11... | collective-permute-start | bytes 786440 | tf_op jit(solution)/shard_map/ppermute | solution.py:385
  39.6 8.4 %copy-start.3 = (bf16[128,2048]{1,0:T(8,128)(2,1)}, bf16[128,2048]{1,0:T(8,128)(2,1)S(1)}, u32[]{:S(2)}) copy-start(bf16[128,2048]{1,0:T(8,128)(2,1)S(1)} %pick.5.refs_1_) | copy-start | bytes 1572868
  39.6 10.3 %collective-permute-start.5 = (bf16[128,2048]{1,0:T(8,128)(2,1)S(1)}, bf16[128,2048]{1,0:T(8,128)(2,1)S(1)}, u32[]{:S(2)}, u32[]{:S(2)}) collective-permute-start(bf16[128,2048]{1,0:T(8,128)(2,1)S(1)} %pick.5.refs_1_), channel_id=1, source_target_pairs={{0,2},{4,6},{9,11},{13,15},{18,16},{22,20},{27,25},{31,29}} | collective-permute-start | bytes 1572872 | tf_op jit(solution)/shard_map/ppermute | solution.py:385
  49.9 13.1 %copy-start.23 = (bf16[128,2048]{1,0:T(8,128)(2,1)}, bf16[128,2048]{1,0:T(8,128)(2,1)S(1)}, u32[]{:S(2)}) copy-start(bf16[128,2048]{1,0:T(8,128)(2,1)S(1)} %collective-permute-done.5.refs_5_) | copy-start | bytes 1572868
  49.9 13.1 %copy-start.11 = (bf16[64,4096]{1,0:T(8,128)(2,1)}, bf16[64,4096]{1,0:T(8,128)(2,1)S(1)}, u32[]{:S(2)}) copy-start(bf16[64,4096]{1,0:T(8,128)(2,1)S(1)} %collective-permute-done.7.refs_0_.refs_1_.refs_5_) | copy-start | bytes 1572868
  49.9 19.9 %copy-start.12 = (bf16[64,4096]{1,0:T(8,128)(2,1)}, bf16[64,4096]{1,0:T(8,128)(2,1)S(1)}, u32[]{:S(2)}) copy-start(bf16[64,4096]{1,0:T(8,128)(2,1)S(1)} %collective-permute-done.6.refs_1_.refs_0_.refs_6_) | copy-start | bytes 1572868
  50.5 12.5 %copy-start.13 = (f32[512,128]{1,0:T(8,128)}, f32[512,128]{1,0:T(8,128)S(1)}, u32[]{:S(2)}) copy-start(f32[512,128]{1,0:T(8,128)S(1)} %get-tuple-element.90.refs_0_) | copy-start | bytes 786436
  50.5 12.5 %collective-permute-start.10 = (bf16[512,128]{1,0:T(8,128)(2,1)S(1)}, bf16[512,128]{1,0:T(8,128)(2,1)S(1)}, u32[]{:S(2)}, u32[]{:S(2)}) collective-permute-start(bf16[512,128]{1,0:T(8,128)(2,1)S(1)} %get-tuple-element.83), channel_id=1, source_target_pairs={{0,2},{1,3},{2,0},{3,1},{4,6},{5,7},{6,4},{7,5},{8,10},{9,11},{10,... | collective-permute-start | bytes 393224 | tf_op jit(solution)/shard_map/ppermute | solution.py:385
  53.1 9.9 %collective-permute-start.13 = (bf16[1024,128]{1,0:T(8,128)(2,1)S(1)}, bf16[1024,128]{1,0:T(8,128)(2,1)S(1)}, u32[]{:S(2)}, u32[]{:S(2)}) collective-permute-start(bf16[1024,128]{1,0:T(8,128)(2,1)S(1)} %get-tuple-element.87), channel_id=1, source_target_pairs={{0,1},{1,0},{2,3},{3,2},{4,5},{5,4},{6,7},{7,6},{8,9},{9,8},{10,11... | collective-permute-start | bytes 786440 | tf_op jit(solution)/shard_map/ppermute | solution.py:385
  53.7 9.3 %copy-start.8 = (bf16[128,2048]{1,0:T(8,128)(2,1)}, bf16[128,2048]{1,0:T(8,128)(2,1)S(1)}, u32[]{:S(2)}) copy-start(bf16[128,2048]{1,0:T(8,128)(2,1)S(1)} %get-tuple-element.79.refs_2_) | copy-start | bytes 1572868
  53.7 9.3 %collective-permute-start.11 = (bf16[32,4096]{1,0:T(8,128)(2,1)S(1)}, bf16[32,4096]{1,0:T(8,128)(2,1)S(1)}, u32[]{:S(2)}, u32[]{:S(2)}) collective-permute-start(bf16[32,4096]{1,0:T(8,128)(2,1)S(1)} %get-tuple-element.84), channel_id=1, source_target_pairs={{0,4},{1,5},{2,6},{3,7},{4,0},{5,1},{6,2},{7,3},{8,12},{9,13},{10,... | collective-permute-start | bytes 786440 | tf_op jit(solution)/shard_map/ppermute | solution.py:385
  54.3 8.7 %collective-permute-start.12 = (bf16[32,4096]{1,0:T(8,128)(2,1)S(1)}, bf16[32,4096]{1,0:T(8,128)(2,1)S(1)}, u32[]{:S(2)}, u32[]{:S(2)}) collective-permute-start(bf16[32,4096]{1,0:T(8,128)(2,1)S(1)} %get-tuple-element.85), channel_id=1, source_target_pairs={{0,16},{1,17},{2,18},{3,19},{4,20},{5,21},{6,22},{7,23},{8,0},{9,1... | collective-permute-start | bytes 786440 | tf_op jit(solution)/shard_map/ppermute | solution.py:385
  54.3 9.8 %collective-permute-start.9 = (bf16[128,2048]{1,0:T(8,128)(2,1)S(1)}, bf16[128,2048]{1,0:T(8,128)(2,1)S(1)}, u32[]{:S(2)}, u32[]{:S(2)}) collective-permute-start(bf16[128,2048]{1,0:T(8,128)(2,1)S(1)} %get-tuple-element.79.refs_2_), channel_id=1, source_target_pairs={{0,2},{4,6},{9,11},{13,15},{18,16},{22,20},{27,25},{31,29}} | collective-permute-start | bytes 1572872 | tf_op jit(solution)/shard_map/ppermute | solution.py:385
  63.0 12.4 %copy-start.26 = (bf16[512,128]{1,0:T(8,128)(2,1)}, bf16[512,128]{1,0:T(8,128)(2,1)S(1)}, u32[]{:S(2)}) copy-start(bf16[512,128]{1,0:T(8,128)(2,1)S(1)} %collective-permute-done.10.refs_1_) | copy-start | bytes 393220
  63.0 12.3 %copy-start.17 = (bf16[32,4096]{1,0:T(8,128)(2,1)}, bf16[32,4096]{1,0:T(8,128)(2,1)S(1)}, u32[]{:S(2)}) copy-start(bf16[32,4096]{1,0:T(8,128)(2,1)S(1)} %collective-permute-done.11.refs_0_.refs_1_.refs_7_) | copy-start | bytes 786436
  63.1 12.3 %copy-start.18 = (bf16[32,4096]{1,0:T(8,128)(2,1)}, bf16[32,4096]{1,0:T(8,128)(2,1)S(1)}, u32[]{:S(2)}) copy-start(bf16[32,4096]{1,0:T(8,128)(2,1)S(1)} %collective-permute-done.12.refs_1_.refs_2_.refs_8_) | copy-start | bytes 786436
  64.1 11.3 %copy-start.24 = (bf16[128,2048]{1,0:T(8,128)(2,1)}, bf16[128,2048]{1,0:T(8,128)(2,1)S(1)}, u32[]{:S(2)}) copy-start(bf16[128,2048]{1,0:T(8,128)(2,1)S(1)} %collective-permute-done.9.refs_6_) | copy-start | bytes 1572868
  64.6 10.8 %copy-start.4 = (bf16[64,2048]{1,0:T(8,128)(2,1)}, bf16[64,2048]{1,0:T(8,128)(2,1)S(1)}, u32[]{:S(2)}) copy-start(bf16[64,2048]{1,0:T(8,128)(2,1)S(1)} %pick.7.refs_3_) | copy-start | bytes 786436
  64.6 11.1 %collective-permute-start.14 = (bf16[64,2048]{1,0:T(8,128)(2,1)S(1)}, bf16[64,2048]{1,0:T(8,128)(2,1)S(1)}, u32[]{:S(2)}, u32[]{:S(2)}) collective-permute-start(bf16[64,2048]{1,0:T(8,128)(2,1)S(1)} %pick.7.refs_3_), channel_id=1, source_target_pairs={{0,2},{4,6},{9,11},{13,15},{18,16},{22,20},{27,25},{31,29}} | collective-permute-start | bytes 786440 | tf_op jit(solution)/shard_map/ppermute | solution.py:385
  69.1 6.7 %collective-permute-start.16 = (bf16[1024,128]{1,0:T(8,128)(2,1)S(1)}, bf16[1024,128]{1,0:T(8,128)(2,1)S(1)}, u32[]{:S(2)}, u32[]{:S(2)}) collective-permute-start(bf16[1024,128]{1,0:T(8,128)(2,1)S(1)} %get-tuple-element.99), channel_id=1, source_target_pairs={{0,1},{1,0},{2,3},{3,2},{4,5},{5,4},{6,7},{7,6},{8,9},{9,8},{10,11... | collective-permute-start | bytes 786440 | tf_op jit(solution)/shard_map/ppermute | solution.py:385
  69.7 6.0 %collective-permute-start.15 = (bf16[512,128]{1,0:T(8,128)(2,1)S(1)}, bf16[512,128]{1,0:T(8,128)(2,1)S(1)}, u32[]{:S(2)}, u32[]{:S(2)}) collective-permute-start(bf16[512,128]{1,0:T(8,128)(2,1)S(1)} %get-tuple-element.97), channel_id=1, source_target_pairs={{0,2},{1,3},{2,0},{3,1},{4,6},{5,7},{6,4},{7,5},{8,10},{9,11},{10,... | collective-permute-start | bytes 393224 | tf_op jit(solution)/shard_map/ppermute | solution.py:385
  75.7 7.4 %copy-start.27 = (bf16[512,128]{1,0:T(8,128)(2,1)}, bf16[512,128]{1,0:T(8,128)(2,1)S(1)}, u32[]{:S(2)}) copy-start(bf16[512,128]{1,0:T(8,128)(2,1)S(1)} %collective-permute-done.15.refs_3_) | copy-start | bytes 393220
  75.7 8.0 %collective-permute-start.17 = (bf16[1024,128]{1,0:T(8,128)(2,1)S(1)}, bf16[1024,128]{1,0:T(8,128)(2,1)S(1)}, u32[]{:S(2)}, u32[]{:S(2)}) collective-permute-start(bf16[1024,128]{1,0:T(8,128)(2,1)S(1)} %get-tuple-element.105), channel_id=1, source_target_pairs={{0,1},{1,0},{2,3},{3,2},{4,5},{5,4},{6,7},{7,6},{8,9},{9,8},{10,11... | collective-permute-start | bytes 786440 | tf_op jit(solution)/shard_map/ppermute | solution.py:385
  77.3 6.4 %collective-permute-start.18 = (bf16[512,128]{1,0:T(8,128)(2,1)S(1)}, bf16[512,128]{1,0:T(8,128)(2,1)S(1)}, u32[]{:S(2)}, u32[]{:S(2)}) collective-permute-start(bf16[512,128]{1,0:T(8,128)(2,1)S(1)} %get-tuple-element.109), channel_id=1, source_target_pairs={{0,2},{1,3},{2,0},{3,1},{4,6},{5,7},{6,4},{7,5},{8,10},{9,11},{10,... | collective-permute-start | bytes 393224 | tf_op jit(solution)/shard_map/ppermute | solution.py:385
  83.8 7.2 %copy-start.28 = (bf16[512,128]{1,0:T(8,128)(2,1)}, bf16[512,128]{1,0:T(8,128)(2,1)S(1)}, u32[]{:S(2)}) copy-start(bf16[512,128]{1,0:T(8,128)(2,1)S(1)} %collective-permute-done.18.refs_5_) | copy-start | bytes 393220
  83.8 7.2 %collective-permute-start.20 = (bf16[512,2048]{1,0:T(8,128)(2,1)}, bf16[512,2048]{1,0:T(8,128)(2,1)S(1)}, u32[]{:S(2)}, u32[]{:S(2)}) collective-permute-start(bf16[512,2048]{1,0:T(8,128)(2,1)} %pack.1.own_ref), channel_id=1, source_target_pairs={{0,1},{1,0},{2,3},{3,2},{4,5},{5,4},{6,7},{7,6},{8,9},{9,8},{10,11... | collective-permute-start | bytes 6291464 | tf_op jit(solution)/shard_map/ppermute | solution.py:385
  85.1 5.9 %collective-permute-start.19 = (bf16[512,128]{1,0:T(8,128)(2,1)S(1)}, bf16[512,128]{1,0:T(8,128)(2,1)S(1)}, u32[]{:S(2)}, u32[]{:S(2)}) collective-permute-start(bf16[512,128]{1,0:T(8,128)(2,1)S(1)} %get-tuple-element.119), channel_id=1, source_target_pairs={{0,2},{1,3},{2,0},{3,1},{4,6},{5,7},{6,4},{7,5},{8,10},{9,11},{10,... | collective-permute-start | bytes 393224 | tf_op jit(solution)/shard_map/ppermute | solution.py:385
  91.0 7.8 %copy-start.21 = (bf16[512,2048]{1,0:T(8,128)(2,1)}, bf16[512,2048]{1,0:T(8,128)(2,1)S(1)}, u32[]{:S(2)}) copy-start(bf16[512,2048]{1,0:T(8,128)(2,1)S(1)} %collective-permute-done.20.other_ref) | copy-start | bytes 6291460
  94.9 1.5 %collective-permute-start.21 = (f32[24,64]{1,0:T(8,128)}, f32[24,64]{1,0:T(8,128)S(1)}, u32[]{:S(2)}, u32[]{:S(2)}) collective-permute-start(f32[24,64]{1,0:T(8,128)} %squares.1), channel_id=1, source_target_pairs={{0,1},{1,0},{2,3},{3,2},{4,5},{5,4},{6,7},{7,6},{8,9},{9,8},{10,11... | collective-permute-start | bytes 18440 | tf_op jit(solution)/shard_map/ppermute | solution.py:385
  97.0 6.0 %collective-permute-start.22 = (f32[24,64]{1,0:T(8,128)S(1)}, f32[24,64]{1,0:T(8,128)S(1)}, u32[]{:S(2)}, u32[]{:S(2)}) collective-permute-start(f32[24,64]{1,0:T(8,128)S(1)} %add.30), channel_id=1, source_target_pairs={{0,2},{1,3},{2,0},{3,1},{4,6},{5,7},{6,4},{7,5},{8,10},{9,11},{10,... | collective-permute-start | bytes 18440 | tf_op jit(solution)/shard_map/ppermute | solution.py:385
  103.0 3.8 %collective-permute-start.23 = (f32[24,64]{1,0:T(8,128)S(1)}, f32[24,64]{1,0:T(8,128)S(1)}, u32[]{:S(2)}, u32[]{:S(2)}) collective-permute-start(f32[24,64]{1,0:T(8,128)S(1)} %add.31), channel_id=1, source_target_pairs={{0,4},{1,5},{2,6},{3,7},{4,0},{5,1},{6,2},{7,3},{8,12},{9,13},{10,... | collective-permute-start | bytes 18440 | tf_op jit(solution)/shard_map/ppermute | solution.py:385
  106.8 3.7 %collective-permute-start.24 = (f32[24,64]{1,0:T(8,128)S(1)}, f32[24,64]{1,0:T(8,128)S(1)}, u32[]{:S(2)}, u32[]{:S(2)}) collective-permute-start(f32[24,64]{1,0:T(8,128)S(1)} %add.32), channel_id=1, source_target_pairs={{0,8},{1,9},{2,10},{3,11},{4,12},{5,13},{6,14},{7,15},{8,0},{9,1},... | collective-permute-start | bytes 18440 | tf_op jit(solution)/shard_map/ppermute | solution.py:385
  110.5 4.6 %collective-permute-start.25 = (f32[24,64]{1,0:T(8,128)S(1)}, f32[24,64]{1,0:T(8,128)S(1)}, u32[]{:S(2)}, u32[]{:S(2)}) collective-permute-start(f32[24,64]{1,0:T(8,128)S(1)} %add.33), channel_id=1, source_target_pairs={{0,16},{1,17},{2,18},{3,19},{4,20},{5,21},{6,22},{7,23},{8,24},{9,... | collective-permute-start | bytes 18440 | tf_op jit(solution)/shard_map/ppermute | solution.py:385
  (8 other events, 24.9 us)

commit v6 on v5

--- a/solution.py
+++ b/solution.py
@@ -59,8 +59,8 @@
     )(scalars, inv_factor)
 
 
-def whiten_kernel(blocks, scalars_ref, f_ref, *refs):
-    pieces, (keep_ref, away_ref, x_ref, xt_ref) = refs[:-4], refs[-4:]
+def whiten_kernel(blocks, before, scalars_ref, f_ref, *refs):
+    earlier, pieces, (keep_ref, away_ref, x_ref, xt_ref) = refs[:before], refs[before:-4], refs[-4:]
     place = 0
     for piece in pieces:
         x_ref[pl.ds(place, piece.shape[0]), :] = piece[...]
@@ -69,6 +69,11 @@
     for c in range(x_ref.shape[1] // wide):
         xt_ref[pl.ds(c * wide, wide), :] = x_ref[:, c * wide:(c + 1) * wide].T
     tile = f_ref.shape[0] // blocks
+    done = 0
+    if before:
+        done = earlier[0].shape[1]
+        keep_ref[:, :done] = earlier[0][...]
+        away_ref[:, :done] = earlier[1][...]
 
     def product(t):
         start = pl.multiple_of(scalars_ref[STARTS + t], tile)
@@ -76,23 +81,23 @@
 
     def step(t, carry):
         place = pl.multiple_of(t * tile, tile)
-        away_ref[pl.ds(place, tile), :] = product(blocks // 2 + t).astype(jnp.bfloat16)
-        keep_ref[pl.ds(place, tile), :] = product(t)
+        away_ref[pl.ds(place, tile), done:] = product(blocks // 2 + t).astype(jnp.bfloat16)
+        keep_ref[pl.ds(place, tile), done:] = product(t)
         return carry
 
     lax.fori_loop(0, blocks // 2, step, 0)
 
 
-def whiten(scalars, blocks, inv_factor, pieces):
+def whiten(scalars, blocks, inv_factor, pieces, earlier=()):
     row_block, feat_block = inv_factor.shape
     rows = sum(p.shape[0] for p in pieces)
-    out = (row_block // 2, rows)
-    return call(
-        functools.partial(whiten_kernel, blocks),
+    out = (row_block // 2, rows + (earlier[0].shape[1] if earlier else 0))
+    return call(
+        functools.partial(whiten_kernel, blocks, len(earlier)),
         "whiten",
         [jax.ShapeDtypeStruct(out, jnp.float32), jax.ShapeDtypeStruct(out, jnp.bfloat16)],
         [pltpu.VMEM((rows, feat_block), jnp.bfloat16), pltpu.VMEM((feat_block, rows), jnp.bfloat16)],
-        (scalars, [inv_factor] + pieces),
+        (scalars, [inv_factor] + list(earlier) + pieces),
         flops=8 * row_block * feat_block * rows,
     )
 
@@ -178,14 +183,16 @@
     )
 
 
-def join_kernel(scalars_ref, own_ref, other_ref, out_ref, x_ref, xt_ref, sems):
+def join_kernel(first, scalars_ref, own_ref, other_ref, out_ref, x_ref, xt_ref, sems):
+    columns = pl.ds(first, x_ref.shape[1])
+
     @pl.when(scalars_ref[EVEN] == 1)
     def _():
-        fetch([(own_ref, x_ref)], sems)[0].wait()
+        fetch([(own_ref.at[:, columns], x_ref)], sems)[0].wait()
 
     @pl.when(scalars_ref[EVEN] == 0)
     def _():
-        fetch([(other_ref, x_ref)], sems)[0].wait()
+        fetch([(other_ref.at[:, columns], x_ref)], sems)[0].wait()
 
     wide = min(256, x_ref.shape[1])
     for c in range(x_ref.shape[1] // wide):
@@ -193,10 +200,10 @@
     fetch([(xt_ref, out_ref)], sems)[0].wait()
 
 
-def join(scalars, own, other):
-    rows, width = own.shape
-    return call(
-        join_kernel,
+def join(scalars, own, other, half):
+    rows, width = own.shape[0], own.shape[1] // 2
+    return call(
+        functools.partial(join_kernel, half * width),
         "join",
         jax.ShapeDtypeStruct((width, rows), jnp.bfloat16),
         [
@@ -210,13 +217,19 @@
     )
 
 
-def square_kernel(sizes, first, scalars_ref, *refs):
-    early = 2 * len(sizes) - 2
+def put_squares(out_ref, scalars_ref, slot, part_ref, other_ref):
+    count = out_ref.shape[1]
+    value = part_ref[...] + other_ref[...].astype(jnp.float32)
+    line = jnp.sum(value * value, axis=0, keepdims=True)
+    for i in range(line.shape[1] // count):
+        out_ref[pl.ds(scalars_ref[slot + i], 1), :] = line[:, i * count:(i + 1) * count]
+
+
+def early_kernel(slots, firsts, scalars_ref, *refs):
+    early = 2 * len(firsts) - 2
     held = refs[early + 5:-1]
     w_ref, strata_ref, keep_ref, got_ref, out_ref = refs[early:early + 5]
     copies = fetch(list(zip(refs[:early], held)), refs[-1])
-    count = out_ref.shape[1]
-    slots = sum(sizes)
     out_ref[...] = jnp.zeros_like(out_ref)
 
     @pl.when(scalars_ref[FEAT] == 0)
@@ -224,31 +237,38 @@
         out_ref[pl.ds(slots + scalars_ref[ROW], 1), :] = w_ref[...]
         out_ref[pl.ds(2 * slots + scalars_ref[ROW], 1), :] = strata_ref[...].astype(jnp.float32)
 
-    def put(g, part_ref, other_ref):
-        slot = first + sum(sizes[:g])
-        value = part_ref[...] + other_ref[...].astype(jnp.float32)
-        line = jnp.sum(value * value, axis=0, keepdims=True)
-        for i in range(sizes[g]):
-            out_ref[pl.ds(scalars_ref[slot + i], 1), :] = line[:, i * count:(i + 1) * count]
-
-    put(len(sizes) - 1, keep_ref, got_ref)
+    put_squares(out_ref, scalars_ref, firsts[-1], keep_ref, got_ref)
     for copy in copies:
         copy.wait()
-    for g in range(len(sizes) - 1):
-        put(g, held[2 * g], held[2 * g + 1])
-
-
-def squares(scalars, first, weights, strata, pairs, sizes):
-    count = weights.shape[1]
+    for g, first in enumerate(firsts[:-1]):
+        put_squares(out_ref, scalars_ref, first, held[2 * g], held[2 * g + 1])
+
+
+def early_squares(scalars, firsts, slots, weights, strata, pairs):
     early = [x for pair in pairs[:-1] for x in pair]
     return call(
-        functools.partial(square_kernel, sizes, first),
-        "squares",
-        jax.ShapeDtypeStruct((3 * sum(sizes), count), jnp.float32),
+        functools.partial(early_kernel, slots, firsts),
+        "early_squares",
+        jax.ShapeDtypeStruct((3 * slots, weights.shape[1]), jnp.float32),
         [pltpu.VMEM(x.shape, x.dtype) for x in early] + [pltpu.SemaphoreType.DMA((len(early),))],
         (scalars, [weights, strata] + list(pairs[-1])),
         tuple(early),
         BIG,
+    )
+
+
+def last_kernel(first, scalars_ref, sums_ref, keep_ref, got_ref, out_ref):
+    out_ref[...] = sums_ref[...]
+    put_squares(out_ref, scalars_ref, first, keep_ref, got_ref)
+
+
+def last_squares(scalars, first, sums, pair):
+    return call(
+        functools.partial(last_kernel, first),
+        "last_squares",
+        jax.ShapeDtypeStruct(sums.shape, jnp.float32),
+        [],
+        (scalars, [sums] + list(pair)),
     )
 
 
@@ -272,21 +292,22 @@
         d_ref[pl.ds(g * count, count), :] = jnp.broadcast_to(step[g:g + 1, :], (LANES, count)).T
 
 
-def information_kernel(features, pieces_of, scalars_ref, col_hbm, *refs):
+def information_kernel(features, pieces_of, scalars_ref, low_hbm, high_hbm, *refs):
     n = len(pieces_of)
-    pieces, sums_ref, out_ref, new_ref, lev_ref = refs[:n], refs[n], *refs[n + 1:n + 4]
-    all_ref, d_ref, col_ref, p_ref, s_ref, buf_ref, col_sem, p_sems, sems = refs[n + 4:]
+    pieces, (sums_ref, got_ref, out_ref, new_ref, lev_ref) = refs[:n], refs[n:n + 5]
+    all_ref, total_ref, d_ref, col_ref, p_ref, s_ref, buf_ref, col_sems, first_sems, rest_sems, sems = refs[n + 5:]
     width = s_ref.shape[1]
     steps = out_ref.shape[1] // width
     count = sums_ref.shape[1]
     sizes = [piece.shape[0] for piece in pieces]
     offsets = [sum(sizes[:i]) for i in range(n)]
 
-    def bring(j, i):
-        columns = pl.ds(pl.multiple_of(j * width, width), width)
-        return pltpu.make_async_copy(
-            pieces[i].at[:, columns], p_ref.at[pl.ds(offsets[i], sizes[i]), columns], p_sems.at[j, i]
-        )
+    def bring(start, size):
+        columns = pl.ds(start, size)
+        return [
+            (piece.at[:, columns], p_ref.at[pl.ds(offset, rows), columns])
+            for piece, offset, rows in zip(pieces, offsets, sizes)
+        ]
 
     def copy(j):
         slot = lax.rem(j, 2)
@@ -294,20 +315,23 @@
             buf_ref.at[slot], out_ref.at[:, pl.ds(pl.multiple_of(j * width, width), width)], sems.at[slot]
         )
 
-    column = pltpu.make_async_copy(col_hbm, col_ref, col_sem.at[0])
-    for j in range(steps):
-        for i in range(n):
-            bring(j, i).start()
-        if j == 0:
-            column.start()
+    half = col_ref.shape[0] // 2
+    first = fetch(bring(0, width), first_sems)
+    first += fetch([(low_hbm, col_ref.at[:half]), (high_hbm, col_ref.at[half:])], col_sems)
+    rest = fetch(bring(width, (steps - 1) * width), rest_sems) if steps > 1 else []
+    total_ref[...] = sums_ref[...] + got_ref[...]
     weight_step(
-        2 * (sums_ref.shape[0] // 3), features, scalars_ref[ROW], sums_ref, new_ref, lev_ref, all_ref, d_ref
-    )
-    column.wait()
+        2 * (sums_ref.shape[0] // 3), features, scalars_ref[ROW], total_ref, new_ref, lev_ref, all_ref, d_ref
+    )
+    for one in first:
+        one.wait()
 
     def step(j, carry):
-        for i in range(n):
-            bring(j, i).wait()
+        @pl.when(j == 1)
+        def _():
+            for one in rest:
+                one.wait()
+
         for i, (slot, first) in enumerate(pieces_of):
             size = sizes[i]
             start = pl.multiple_of(scalars_ref[slot] * count + first, size)
@@ -330,8 +354,8 @@
         copy(jnp.int32(j)).wait()
 
 
-def increment(scalars, pieces_of, sums, column_t, pieces, features):
-    row_block, rows = column_t.shape
+def increment(scalars, pieces_of, sums, got, columns_t, pieces, features):
+    row_block, rows = 2 * columns_t[0].shape[0], columns_t[0].shape[1]
     groups, count = sums.shape[0] // 3, sums.shape[1]
     feat_block = pieces[0].shape[1]
     width = min(512, feat_block)
@@ -340,7 +364,7 @@
     on_hbm = pl.BlockSpec(memory_space=pltpu.HBM)
     return pl.pallas_call(
         functools.partial(information_kernel, features, pieces_of),
-        in_specs=[pl.BlockSpec(memory_space=pltpu.SMEM)] + [on_hbm] * (1 + len(pieces)) + [on_vmem],
+        in_specs=[pl.BlockSpec(memory_space=pltpu.SMEM)] + [on_hbm] * (2 + len(pieces)) + [on_vmem] * 2,
         out_specs=[on_hbm, on_vmem, on_vmem],
         out_shape=[
             jax.ShapeDtypeStruct((row_block, feat_block), jnp.float32),
@@ -349,13 +373,15 @@
         ],
         scratch_shapes=[
             pltpu.VMEM((groups, count), jnp.float32),
+            pltpu.VMEM((3 * groups, count), jnp.float32),
             pltpu.VMEM((rows, LANES), jnp.float32),
             pltpu.VMEM((row_block, rows), jnp.bfloat16),
             pltpu.VMEM((rows, feat_block), jnp.bfloat16),
             pltpu.VMEM((rows, width), jnp.bfloat16),
             pltpu.VMEM((2, row_block, width), jnp.float32),
-            pltpu.SemaphoreType.DMA((1,)),
-            pltpu.SemaphoreType.DMA((steps, len(pieces))),
+            pltpu.SemaphoreType.DMA((2,)),
+            pltpu.SemaphoreType.DMA((len(pieces),)),
+            pltpu.SemaphoreType.DMA((len(pieces),)),
             pltpu.SemaphoreType.DMA((2,)),
         ],
         compiler_params=pltpu.CompilerParams(vmem_limit_bytes=BIG * MIB),
@@ -363,7 +389,7 @@
             flops=2 * row_block * feat_block * rows, bytes_accessed=1000, transcendentals=0
         ),
         name="increment",
-    )(scalars, column_t, *pieces, sums)
+    )(scalars, *columns_t, *pieces, sums, got)
 
 
 def make(mesh):
@@ -410,7 +436,7 @@
     for k in range(1, hi_n):
         groups.append([(k, s) for s in range(1, lo_n)] + ([(k + 1, 0)] if k + 1 < hi_n else []))
     slots = [slot for group in groups for slot in group]
-    white_groups = [[(k, s) for s in range(lo_n)] for k in range(hi_n)]
+    white_groups = [[(k, s) for k in ks for s in range(lo_n)] for ks in [[0, 1]] + [[k] for k in range(2, hi_n)]]
     white_slots = [slot for group in white_groups for slot in group]
 
     def per_device(candidates, inv_factor, weights, strata):
@@ -480,12 +506,14 @@
                 out["scalars"] = touch(scalars, inv_factor)
             if k > 0:
                 out["column"] = column_far(columns[-1])
-                out["white"] = whiten(scalars, feats_n, inv_factor, pieces_of(white_groups[k - 1]))
-            if k > 1:
-                keep, away = white[k - 2]
+                white_pieces = pieces_of([(k - 1, s) for s in range(lo_n)])
+                earlier = white.pop() if k == 2 else ()
+                out["white"] = whiten(scalars, feats_n, inv_factor, white_pieces, earlier)
+            if k > 2:
+                keep, away = white[k - 3]
                 out["near"] = keep, swap(away, 0, 1)
-            if k > 2:
-                out["far"] = to_far(near[k - 3])
+            if k > 3:
+                out["far"] = to_far(near[k - 4])
             out = fence(out)
             for slot, value in zip(fresh, out["fresh"]):
                 chunks[slot] = value
@@ -497,18 +525,20 @@
         packed = pack(scalars, columns, far_columns)
         last, before, packed = fence(((keep, swap(away, 0, 1)), to_far(near[-1]), packed))
         far.append(before)
-        last, beside = fence((to_far(last), swap(packed, 0, 1)))
-        far.append(last)
-        sizes = [len(g) for g in white_groups]
-        total = squares(scalars, first_white, weights[None], strata[None], far, sizes)
+        slots_n = len(white_slots)
+        firsts = [first_white + sum(len(x) for x in white_groups[:g]) for g in range(len(white_groups))]
+        sums = early_squares(scalars, firsts[:-1], slots_n, weights[None], strata[None], far)
+        last, beside, sums = fence((to_far(last), swap(packed, 0, 1), sums))
+        total = last_squares(scalars, firsts[-1], sums, last)
         total = fence(total + swap(total, 0, 1))
-        column_t = join(scalars, packed, beside)
+        columns_t = []
         bits = [(0, bit) for bit in far_bits] + [(bit, 0) for bit in row_bits]
-        for i, bit in enumerate(bits):
+        for bit in bits[:-1]:
             total = total + swap(total, *bit)
-            if i == 0:
-                total, column_t = fence((total, column_t))
-
+            if len(columns_t) < 2:
+                columns_t.append(join(scalars, packed, beside, len(columns_t)))
+                total, columns_t = fence((total, columns_t))
+        got = swap(total, *bits[-1])
         origins = []
         for i, slot in enumerate(slots):
             first = 0
@@ -516,7 +546,7 @@
                 origins.append((first_place + i, first))
                 first += piece.shape[0]
         information, new_weight, leverage = increment(
-            scalars, origins, total, column_t, pieces_of(slots), features
+            scalars, origins, total, got, columns_t, pieces_of(slots), features
         )
         return (new_weight.reshape(rows_dev), leverage.reshape(rows_dev), information)
 

time: 136 us -> 130 us (0.956)
  waiting for transfers between devices: 26.6 us -> 20.8 us
  starting transfers between devices: 37.3 us -> 35.6 us
  Pallas kernels: 58.6 us -> 60.2 us
    ppermute x26 -> x24, waiting for transfers between devices: 26.6 us -> 20.8 us  [send(): return lax.ppermute(x, BOTH, pairs)]
    pallas_call x15 -> x16, Pallas kernels: 37.8 us -> 39.8 us  [call(): pl.pallas_call(kernel, in_specs=[pl.BlockSpec(memory_space=pltpu.SMEM)] +...]
    ppermute x26 -> x24, starting transfers between devices: 37.3 us -> 35.6 us  [send(): return lax.ppermute(x, BOTH, pairs)]
  transfers between devices with their start and end apart: 26 -> 24, of which waited for: 12 -> 11; matrix products, arithmetic and copies ran while one was open for 1% -> 1% of each run, Pallas kernels for 25% -> 31%
where the time goes in v6:
time: 130 us
  Pallas kernels  60.2 us (46%)
  starting transfers between devices  35.6 us (27%)
  waiting for transfers between devices  20.8 us (16%)
  local copies, waits for them, and re-layouts  11 us (8%)
  between operations  1.34 us (1%)
    pallas_call x16, Pallas kernels, call(): pl.pallas_call(kernel, in_specs=[pl.BlockSpec(memory_space=pltpu.SMEM)] +...  39.8 us
    ppermute x24, starting transfers between devices, send(): return lax.ppermute(x, BOTH, pairs)  35.6 us
    ppermute x24, waiting for transfers between devices, send(): return lax.ppermute(x, BOTH, pairs)  20.8 us
    pallas_call x1, Pallas kernels, increment(): pl.pallas_call(functools.partial(information_kernel, features, pieces_of)...  19.2 us
    unnamed x60, local copies, waits for them, and re-layouts  10.2 us
  transfers between devices with their start and end apart: 24, of which 11 were waited for; matrix products, arithmetic and copies ran while one was open for 1% of the time, Pallas kernels for 31%

profile of v6, /device:TPU:0, one launch (start us, length us, event | category | flops | bytes accessed | tf_op | source)
XLA Modules:
  0.0 129.7 jit_solution(12797165042505773324)
XLA Ops:
  0.6 3.0 %collective-permute-start.1 = (bf16[64,4096]{1,0:T(8,128)(2,1)}, bf16[64,4096]{1,0:T(8,128)(2,1)S(1)}, u32[]{:S(2)}, u32[]{:S(2)}) collective-permute-start(bf16[64,4096]{1,0:T(8,128)(2,1)} %refs_0_.5), channel_id=1, source_target_pairs={{0,4},{1,5},{2,6},{3,7},{4,0},{5,1},{6,2},{7,3},{8,12},{9,13},{10,... | collective-permute-start | bytes 1572872 | tf_op jit(solution)/shard_map/ppermute | solution.py:411
  3.6 2.6 %collective-permute-start = (bf16[64,4096]{1,0:T(8,128)(2,1)}, bf16[64,4096]{1,0:T(8,128)(2,1)S(1)}, u32[]{:S(2)}, u32[]{:S(2)}) collective-permute-start(bf16[64,4096]{1,0:T(8,128)(2,1)} %refs_0_.5), channel_id=1, source_target_pairs={{0,16},{1,17},{2,18},{3,19},{4,20},{5,21},{6,22},{7,23},{8,0},{9,1... | collective-permute-start | bytes 1572872 | tf_op jit(solution)/shard_map/ppermute | solution.py:411
  6.2 0.7 dynamic-slice_bitcast_fusion
  6.9 0.7 xor_multiply_fusion
  7.7 5.8 %copy-done = bf16[2048,4096]{1,0:T(8,128)(2,1)S(1)} copy-done((bf16[2048,4096]{1,0:T(8,128)(2,1)S(1)}, bf16[2048,4096]{1,0:T(8,128)(2,1)}, u32[]{:S(2)}) %copy-start) | copy-done | bytes 16777240
  13.4 1.1 touch.1.scalars_ref._
  14.6 1.2 collective-permute-done.1.refs_1_
  15.8 1.7 %collective-permute-done.refs_2_ = bf16[64,4096]{1,0:T(8,128)(2,1)S(1)} collective-permute-done((bf16[64,4096]{1,0:T(8,128)(2,1)}, bf16[64,4096]{1,0:T(8,128)(2,1)S(1)}, u32[]{:S(2)}, u32[]{:S(2)}) %collective-permute-start) | collective-permute-done | bytes 524320 | tf_op jit(solution)/shard_map/ppermute | solution.py:411
  18.0 3.3 %collective-permute-start.3 = (bf16[64,4096]{1,0:T(8,128)(2,1)S(1)}, bf16[64,4096]{1,0:T(8,128)(2,1)S(1)}, u32[]{:S(2)}, u32[]{:S(2)}) collective-permute-start(bf16[64,4096]{1,0:T(8,128)(2,1)S(1)} %collective-permute-done.refs_2_), channel_id=1, source_target_pairs={{0,16},{1,17},{2,18},{3,19},{4,20},{5,21},{6,22},{7,23},{8,0},{9,1... | collective-permute-start | bytes 1572872 | tf_op jit(solution)/shard_map/ppermute | solution.py:411
  21.3 1.0 copy-done.5
  22.9 3.5 %collective-permute-start.2 = (bf16[192,2048]{1,0:T(8,128)(2,1)S(1)}, bf16[192,2048]{1,0:T(8,128)(2,1)S(1)}, u32[]{:S(2)}, u32[]{:S(2)}) collective-permute-start(bf16[192,2048]{1,0:T(8,128)(2,1)S(1)} %pick.4.refs_0_), channel_id=1, source_target_pairs={{0,2},{4,6},{9,11},{13,15},{18,16},{22,20},{27,25},{31,29}} | collective-permute-start | bytes 2359304 | tf_op jit(solution)/shard_map/ppermute | solution.py:411
  26.4 5.5 %whiten.4 = (f32[1024,128]{1,0:T(8,128)S(1)}, bf16[1024,128]{1,0:T(8,128)(2,1)S(1)}) custom-call(s32[25]{0:T(128)S(1)} %touch.1.scalars_ref._, bf16[2048,4096]{1,0:T(8,128)(2,1)S(1)} %copy-done.1, bf16[64,4096]{1,0:T(8,128)(2,1)S(1)} %copy-done.5, bf16[64,4096]{1,0:T(8,128)(2,1)S(1)} %collective-permute-done.1.refs_1_), custom_call_target="tpu_custom_call" | custom-call | flops 8589934592 | bytes 1000 | tf_op jit(solution)/shard_map/whiten/pallas_call | solution.py:33
  32.0 3.9 %collective-permute-done.2.refs_4_ = bf16[192,2048]{1,0:T(8,128)(2,1)S(1)} collective-permute-done((bf16[192,2048]{1,0:T(8,128)(2,1)S(1)}, bf16[192,2048]{1,0:T(8,128)(2,1)S(1)}, u32[]{:S(2)}, u32[]{:S(2)}) %collective-permute-start.2) | collective-permute-done | bytes 786464 | tf_op jit(solution)/shard_map/ppermute | solution.py:411
  35.8 1.5 %collective-permute-start.7 = (bf16[64,4096]{1,0:T(8,128)(2,1)S(1)}, bf16[64,4096]{1,0:T(8,128)(2,1)S(1)}, u32[]{:S(2)}, u32[]{:S(2)}) collective-permute-start(bf16[64,4096]{1,0:T(8,128)(2,1)S(1)} %collective-permute-done.3.refs_1_.refs_0_.refs_4_), channel_id=1, source_target_pairs={{0,4},{1,5},{2,6},{3,7},{4,0},{5,1},{6,2},{7,3},{8,12},{9,13},{10,... | collective-permute-start | bytes 1572872 | tf_op jit(solution)/shard_map/ppermute | solution.py:411
  37.3 1.6 %collective-permute-start.6 = (bf16[64,4096]{1,0:T(8,128)(2,1)S(1)}, bf16[64,4096]{1,0:T(8,128)(2,1)S(1)}, u32[]{:S(2)}, u32[]{:S(2)}) collective-permute-start(bf16[64,4096]{1,0:T(8,128)(2,1)S(1)} %collective-permute-done.3.refs_1_.refs_0_.refs_4_), channel_id=1, source_target_pairs={{0,16},{1,17},{2,18},{3,19},{4,20},{5,21},{6,22},{7,23},{8,0},{9,1... | collective-permute-start | bytes 1572872 | tf_op jit(solution)/shard_map/ppermute | solution.py:411
  39.6 2.8 %collective-permute-start.5 = (bf16[128,2048]{1,0:T(8,128)(2,1)S(1)}, bf16[128,2048]{1,0:T(8,128)(2,1)S(1)}, u32[]{:S(2)}, u32[]{:S(2)}) collective-permute-start(bf16[128,2048]{1,0:T(8,128)(2,1)S(1)} %pick.5.refs_1_), channel_id=1, source_target_pairs={{0,2},{4,6},{9,11},{13,15},{18,16},{22,20},{27,25},{31,29}} | collective-permute-start | bytes 1572872 | tf_op jit(solution)/shard_map/ppermute | solution.py:411
  42.4 5.6 %whiten.5 = (f32[1024,256]{1,0:T(8,128)S(1)}, bf16[1024,256]{1,0:T(8,128)(2,1)S(1)}) custom-call(s32[25]{0:T(128)S(1)} %touch.1.scalars_ref._, bf16[2048,4096]{1,0:T(8,128)(2,1)S(1)} %copy-done.1, f32[1024,128]{1,0:T(8,128)S(1)} %get-tuple-element.71.refs_0_, bf16[1024,128]{1,0:T(8,128)(2,1)S(1)} %get-tuple-element.72.refs_1_, ...), custom_call_target="tpu_custom_call" | custom-call | flops 8589934592 | bytes 1000 | tf_op jit(solution)/shard_map/whiten/pallas_call | solution.py:33
  47.9 1.1 collective-permute-done.5.refs_5_
  49.1 0.6 pick.6
  49.8 0.6 collective-permute-start.9
  50.4 1.6 %collective-permute-start.10 = (bf16[32,4096]{1,0:T(8,128)(2,1)S(1)}, bf16[32,4096]{1,0:T(8,128)(2,1)S(1)}, u32[]{:S(2)}, u32[]{:S(2)}) collective-permute-start(bf16[32,4096]{1,0:T(8,128)(2,1)S(1)} %get-tuple-element.79), channel_id=1, source_target_pairs={{0,16},{1,17},{2,18},{3,19},{4,20},{5,21},{6,22},{7,23},{8,0},{9,1... | collective-permute-start | bytes 786440 | tf_op jit(solution)/shard_map/ppermute | solution.py:411
  52.0 2.8 %collective-permute-start.8 = (bf16[128,2048]{1,0:T(8,128)(2,1)S(1)}, bf16[128,2048]{1,0:T(8,128)(2,1)S(1)}, u32[]{:S(2)}, u32[]{:S(2)}) collective-permute-start(bf16[128,2048]{1,0:T(8,128)(2,1)S(1)} %get-tuple-element.77.refs_2_), channel_id=1, source_target_pairs={{0,2},{4,6},{9,11},{13,15},{18,16},{22,20},{27,25},{31,29}} | collective-permute-start | bytes 1572872 | tf_op jit(solution)/shard_map/ppermute | solution.py:411
  54.8 5.5 %whiten.6 = (f32[1024,128]{1,0:T(8,128)S(1)}, bf16[1024,128]{1,0:T(8,128)(2,1)S(1)}) custom-call(s32[25]{0:T(128)S(1)} %touch.1.scalars_ref._, bf16[2048,4096]{1,0:T(8,128)(2,1)S(1)} %copy-done.1, bf16[64,4096]{1,0:T(8,128)(2,1)S(1)} %collective-permute-done.3.refs_1_.refs_0_.refs_4_, bf16[64,4096]{1,0:T(8,128)(2,1)S(1)} %collective-permute-done.7.refs_0_.refs_1_.refs_5_), custom_call_target="tpu_custom_call" | custom-call | flops 8589934592 | bytes 1000 | tf_op jit(solution)/shard_map/whiten/pallas_call | solution.py:33
  60.4 1.0 collective-permute-done.8.refs_6_
  62.0 4.4 %collective-permute-start.12 = (bf16[64,2048]{1,0:T(8,128)(2,1)S(1)}, bf16[64,2048]{1,0:T(8,128)(2,1)S(1)}, u32[]{:S(2)}, u32[]{:S(2)}) collective-permute-start(bf16[64,2048]{1,0:T(8,128)(2,1)S(1)} %pick.7.refs_3_), channel_id=1, source_target_pairs={{0,2},{4,6},{9,11},{13,15},{18,16},{22,20},{27,25},{31,29}} | collective-permute-start | bytes 786440 | tf_op jit(solution)/shard_map/ppermute | solution.py:411
  66.4 0.6 halve.3
  67.3 5.5 %whiten.7 = (f32[1024,128]{1,0:T(8,128)S(1)}, bf16[1024,128]{1,0:T(8,128)(2,1)S(1)}) custom-call(s32[25]{0:T(128)S(1)} %touch.1.scalars_ref._, bf16[2048,4096]{1,0:T(8,128)(2,1)S(1)} %copy-done.1, bf16[64,4096]{1,0:T(8,128)(2,1)S(1)} %collective-permute-done.6.refs_1_.refs_0_.refs_6_, bf16[32,4096]{1,0:T(8,128)(2,1)S(1)} %collective-permute-done.9.refs_0_.refs_1_.refs_7_, ...), custom_call_target="tpu_custom_call" | custom-call | flops 8589934592 | bytes 1000 | tf_op jit(solution)/shard_map/whiten/pallas_call | solution.py:33
  72.8 0.7 collective-permute-done.13.refs_1_
  73.5 0.6 halve.4
  74.2 0.7 copy-done.14
  74.9 2.1 %collective-permute-start.16 = (bf16[512,128]{1,0:T(8,128)(2,1)S(1)}, bf16[512,128]{1,0:T(8,128)(2,1)S(1)}, u32[]{:S(2)}, u32[]{:S(2)}) collective-permute-start(bf16[512,128]{1,0:T(8,128)(2,1)S(1)} %get-tuple-element.99), channel_id=1, source_target_pairs={{0,2},{1,3},{2,0},{3,1},{4,6},{5,7},{6,4},{7,5},{8,10},{9,11},{10,... | collective-permute-start | bytes 393224 | tf_op jit(solution)/shard_map/ppermute | solution.py:411
  77.0 3.5 %pack.1.own_ref = bf16[512,2048]{1,0:T(8,128)(2,1)} custom-call(s32[25]{0:T(128)} %copy-done.17, bf16[192,2048]{1,0:T(8,128)(2,1)} %copy-done.2, bf16[128,2048]{1,0:T(8,128)(2,1)} %copy-done.3, bf16[128,2048]{1,0:T(8,128)(2,1)} %copy-done.8, bf16[64,2048]{1,0:T(8,128)(2,1)} %copy-done.4, bf16[192,2048]{1,0:T(8,128)(2,1)} %copy-done.22, ...), custom_call_target="tpu_custom_call" | custom-call | flops 1000 | bytes 1000 | tf_op jit(solution)/shard_map/pack/pallas_call | solution.py:33
  80.5 0.6 collective-permute-done.16.refs_5_
  81.1 0.6 copy-done.18
  82.4 1.8 %collective-permute-start.17 = (bf16[512,128]{1,0:T(8,128)(2,1)S(1)}, bf16[512,128]{1,0:T(8,128)(2,1)S(1)}, u32[]{:S(2)}, u32[]{:S(2)}) collective-permute-start(bf16[512,128]{1,0:T(8,128)(2,1)S(1)} %get-tuple-element.107), channel_id=1, source_target_pairs={{0,2},{1,3},{2,0},{3,1},{4,6},{5,7},{6,4},{7,5},{8,10},{9,11},{10,... | collective-permute-start | bytes 393224 | tf_op jit(solution)/shard_map/ppermute | solution.py:411
  84.2 2.9 %early_squares.1.sums_ref = f32[24,64]{1,0:T(8,128)} custom-call(s32[25]{0:T(128)} %copy-done.17, f32[512,256]{1,0:T(8,128)} %copy-done.9, bf16[512,256]{1,0:T(8,128)(2,1)} %copy-done.25, f32[1,64]{1,0:T(1,128)} %bitcast.11, s32[1,64]{1,0:T(1,128)} %bitcast.12, f32[512,128]{1,0:T(8,128)} %copy-done.14, bf16[512,128]{1,0:T(8,128)(2,1)} %copy-done.27), custom_call_target="tpu_custom_call" | custom-call | flops 1000 | bytes 1000 | tf_op jit(solution)/shard_map/early_squares/pallas_call | solution.py:33
  87.1 1.2 collective-permute-done.17.got_ref
  88.3 0.6 copy-done.19
  89.0 0.7 copy-done.20
  89.7 0.7 last_squares.1
  90.4 1.2 collective-permute-done.19
  91.6 1.7 %collective-permute-start.20 = (f32[24,64]{1,0:T(8,128)S(1)}, f32[24,64]{1,0:T(8,128)S(1)}, u32[]{:S(2)}, u32[]{:S(2)}) collective-permute-start(f32[24,64]{1,0:T(8,128)S(1)} %add.27), channel_id=1, source_target_pairs={{0,2},{1,3},{2,0},{3,1},{4,6},{5,7},{6,4},{7,5},{8,10},{9,11},{10,... | collective-permute-start | bytes 18440 | tf_op jit(solution)/shard_map/ppermute | solution.py:411
  93.3 3.2 %join.2.low_hbm = bf16[1024,512]{1,0:T(8,128)(2,1)} custom-call(s32[25]{0:T(128)} %copy-done.17, bf16[512,2048]{1,0:T(8,128)(2,1)} %pack.1.own_ref, bf16[512,2048]{1,0:T(8,128)(2,1)} %copy-done.21), custom_call_target="tpu_custom_call" | custom-call | flops 1000 | bytes 1000 | tf_op jit(solution)/shard_map/join/pallas_call | solution.py:33
  96.6 1.6 %collective-permute-start.21 = (f32[24,64]{1,0:T(8,128)S(1)}, f32[24,64]{1,0:T(8,128)S(1)}, u32[]{:S(2)}, u32[]{:S(2)}) collective-permute-start(f32[24,64]{1,0:T(8,128)S(1)} %add.28), channel_id=1, source_target_pairs={{0,4},{1,5},{2,6},{3,7},{4,0},{5,1},{6,2},{7,3},{8,12},{9,13},{10,... | collective-permute-start | bytes 18440 | tf_op jit(solution)/shard_map/ppermute | solution.py:411
  98.1 3.2 %join.3.high_hbm = bf16[1024,512]{1,0:T(8,128)(2,1)} custom-call(s32[25]{0:T(128)} %copy-done.17, bf16[512,2048]{1,0:T(8,128)(2,1)} %pack.1.own_ref, bf16[512,2048]{1,0:T(8,128)(2,1)} %copy-done.21), custom_call_target="tpu_custom_call" | custom-call | flops 1000 | bytes 1000 | tf_op jit(solution)/shard_map/join/pallas_call | solution.py:33
  101.4 3.7 %collective-permute-done.22 = f32[24,64]{1,0:T(8,128)S(1)} collective-permute-done((f32[24,64]{1,0:T(8,128)S(1)}, f32[24,64]{1,0:T(8,128)S(1)}, u32[]{:S(2)}, u32[]{:S(2)}) %collective-permute-start.22) | collective-permute-done | bytes 6176 | tf_op jit(solution)/shard_map/ppermute | solution.py:411
  105.1 4.6 %collective-permute-done.23.refs_10_ = f32[24,64]{1,0:T(8,128)S(1)} collective-permute-done((f32[24,64]{1,0:T(8,128)S(1)}, f32[24,64]{1,0:T(8,128)S(1)}, u32[]{:S(2)}, u32[]{:S(2)}) %collective-permute-start.23) | collective-permute-done | bytes 6176 | tf_op jit(solution)/shard_map/ppermute | solution.py:411
  110.3 19.2 %increment.1 = (f32[2048,4096]{1,0:T(8,128)}, f32[1,64]{1,0:T(1,128)}, f32[1,64]{1,0:T(1,128)}) custom-call(s32[25]{0:T(128)} %copy-done.17, bf16[1024,512]{1,0:T(8,128)(2,1)} %join.2.low_hbm, bf16[1024,512]{1,0:T(8,128)(2,1)} %join.3.high_hbm, bf16[64,4096]{1,0:T(8,128)(2,1)} %refs_0_.5, bf16[64,4096]{1,0:T(8,128)(2,1)} %copy-done.6, ...), custom_call_target="tpu_custom_call" | custom-call | flops 8589934592 | bytes 1000 | tf_op jit(solution)/shard_map/increment/pallas_call | solution.py:365
  (85 shorter events, 4.0 us)
Async XLA Ops:
  0.6 15.1 %collective-permute-start.1 = (bf16[64,4096]{1,0:T(8,128)(2,1)}, bf16[64,4096]{1,0:T(8,128)(2,1)S(1)}, u32[]{:S(2)}, u32[]{:S(2)}) collective-permute-start(bf16[64,4096]{1,0:T(8,128)(2,1)} %refs_0_.5), channel_id=1, source_target_pairs={{0,4},{1,5},{2,6},{3,7},{4,0},{5,1},{6,2},{7,3},{8,12},{9,13},{10,... | collective-permute-start | bytes 1572872 | tf_op jit(solution)/shard_map/ppermute | solution.py:411
  3.6 13.8 %collective-permute-start = (bf16[64,4096]{1,0:T(8,128)(2,1)}, bf16[64,4096]{1,0:T(8,128)(2,1)S(1)}, u32[]{:S(2)}, u32[]{:S(2)}) collective-permute-start(bf16[64,4096]{1,0:T(8,128)(2,1)} %refs_0_.5), channel_id=1, source_target_pairs={{0,16},{1,17},{2,18},{3,19},{4,20},{5,21},{6,22},{7,23},{8,0},{9,1... | collective-permute-start | bytes 1572872 | tf_op jit(solution)/shard_map/ppermute | solution.py:411
  7.7 5.8 %copy-start = (bf16[2048,4096]{1,0:T(8,128)(2,1)S(1)}, bf16[2048,4096]{1,0:T(8,128)(2,1)}, u32[]{:S(2)}) copy-start(bf16[2048,4096]{1,0:T(8,128)(2,1)} %f_ref.9) | copy-start | bytes 50331652
  13.4 13.0 %copy-start.1 = (bf16[2048,4096]{1,0:T(8,128)(2,1)S(1)}, bf16[2048,4096]{1,0:T(8,128)(2,1)}, u32[]{:S(2)}) copy-start(bf16[2048,4096]{1,0:T(8,128)(2,1)} %f_ref.9) | copy-start | bytes 50331652
  14.6 58.9 %copy-start.17 = (s32[25]{0:T(128)}, s32[25]{0:T(128)S(1)}, u32[]{:S(2)}) copy-start(s32[25]{0:T(128)S(1)} %touch.1.scalars_ref._) | copy-start | bytes 304
  15.8 16.2 %copy-start.6 = (bf16[64,4096]{1,0:T(8,128)(2,1)}, bf16[64,4096]{1,0:T(8,128)(2,1)S(1)}, u32[]{:S(2)}) copy-start(bf16[64,4096]{1,0:T(8,128)(2,1)S(1)} %collective-permute-done.1.refs_1_) | copy-start | bytes 1572868
  17.4 24.9 %copy-start.7 = (bf16[64,4096]{1,0:T(8,128)(2,1)}, bf16[64,4096]{1,0:T(8,128)(2,1)S(1)}, u32[]{:S(2)}) copy-start(bf16[64,4096]{1,0:T(8,128)(2,1)S(1)} %collective-permute-done.refs_2_) | copy-start | bytes 1572868
  17.4 14.5 %collective-permute-start.4 = (bf16[64,4096]{1,0:T(8,128)(2,1)S(1)}, bf16[64,4096]{1,0:T(8,128)(2,1)S(1)}, u32[]{:S(2)}, u32[]{:S(2)}) collective-permute-start(bf16[64,4096]{1,0:T(8,128)(2,1)S(1)} %collective-permute-done.refs_2_), channel_id=1, source_target_pairs={{0,4},{1,5},{2,6},{3,7},{4,0},{5,1},{6,2},{7,3},{8,12},{9,13},{10,... | collective-permute-start | bytes 1572872 | tf_op jit(solution)/shard_map/ppermute | solution.py:411
  18.0 14.0 %collective-permute-start.3 = (bf16[64,4096]{1,0:T(8,128)(2,1)S(1)}, bf16[64,4096]{1,0:T(8,128)(2,1)S(1)}, u32[]{:S(2)}, u32[]{:S(2)}) collective-permute-start(bf16[64,4096]{1,0:T(8,128)(2,1)S(1)} %collective-permute-done.refs_2_), channel_id=1, source_target_pairs={{0,16},{1,17},{2,18},{3,19},{4,20},{5,21},{6,22},{7,23},{8,0},{9,1... | collective-permute-start | bytes 1572872 | tf_op jit(solution)/shard_map/ppermute | solution.py:411
  22.9 25.0 %copy-start.2 = (bf16[192,2048]{1,0:T(8,128)(2,1)}, bf16[192,2048]{1,0:T(8,128)(2,1)S(1)}, u32[]{:S(2)}) copy-start(bf16[192,2048]{1,0:T(8,128)(2,1)S(1)} %pick.4.refs_0_) | copy-start | bytes 2359300
  22.9 12.9 %collective-permute-start.2 = (bf16[192,2048]{1,0:T(8,128)(2,1)S(1)}, bf16[192,2048]{1,0:T(8,128)(2,1)S(1)}, u32[]{:S(2)}, u32[]{:S(2)}) collective-permute-start(bf16[192,2048]{1,0:T(8,128)(2,1)S(1)} %pick.4.refs_0_), channel_id=1, source_target_pairs={{0,2},{4,6},{9,11},{13,15},{18,16},{22,20},{27,25},{31,29}} | collective-permute-start | bytes 2359304 | tf_op jit(solution)/shard_map/ppermute | solution.py:411
  32.0 17.8 %copy-start.10 = (bf16[64,4096]{1,0:T(8,128)(2,1)}, bf16[64,4096]{1,0:T(8,128)(2,1)S(1)}, u32[]{:S(2)}) copy-start(bf16[64,4096]{1,0:T(8,128)(2,1)S(1)} %collective-permute-done.4.refs_0_.refs_3_) | copy-start | bytes 1572868
  32.0 22.8 %copy-start.11 = (bf16[64,4096]{1,0:T(8,128)(2,1)}, bf16[64,4096]{1,0:T(8,128)(2,1)S(1)}, u32[]{:S(2)}) copy-start(bf16[64,4096]{1,0:T(8,128)(2,1)S(1)} %collective-permute-done.3.refs_1_.refs_0_.refs_4_) | copy-start | bytes 1572868
  35.8 13.9 %copy-start.22 = (bf16[192,2048]{1,0:T(8,128)(2,1)}, bf16[192,2048]{1,0:T(8,128)(2,1)S(1)}, u32[]{:S(2)}) copy-start(bf16[192,2048]{1,0:T(8,128)(2,1)S(1)} %collective-permute-done.2.refs_4_) | copy-start | bytes 2359300
  35.8 13.2 %collective-permute-start.7 = (bf16[64,4096]{1,0:T(8,128)(2,1)S(1)}, bf16[64,4096]{1,0:T(8,128)(2,1)S(1)}, u32[]{:S(2)}, u32[]{:S(2)}) collective-permute-start(bf16[64,4096]{1,0:T(8,128)(2,1)S(1)} %collective-permute-done.3.refs_1_.refs_0_.refs_4_), channel_id=1, source_target_pairs={{0,4},{1,5},{2,6},{3,7},{4,0},{5,1},{6,2},{7,3},{8,12},{9,13},{10,... | collective-permute-start | bytes 1572872 | tf_op jit(solution)/shard_map/ppermute | solution.py:411
  37.3 11.7 %collective-permute-start.6 = (bf16[64,4096]{1,0:T(8,128)(2,1)S(1)}, bf16[64,4096]{1,0:T(8,128)(2,1)S(1)}, u32[]{:S(2)}, u32[]{:S(2)}) collective-permute-start(bf16[64,4096]{1,0:T(8,128)(2,1)S(1)} %collective-permute-done.3.refs_1_.refs_0_.refs_4_), channel_id=1, source_target_pairs={{0,16},{1,17},{2,18},{3,19},{4,20},{5,21},{6,22},{7,23},{8,0},{9,1... | collective-permute-start | bytes 1572872 | tf_op jit(solution)/shard_map/ppermute | solution.py:411
  39.6 20.8 %copy-start.3 = (bf16[128,2048]{1,0:T(8,128)(2,1)}, bf16[128,2048]{1,0:T(8,128)(2,1)S(1)}, u32[]{:S(2)}) copy-start(bf16[128,2048]{1,0:T(8,128)(2,1)S(1)} %pick.5.refs_1_) | copy-start | bytes 1572868
  39.6 9.4 %collective-permute-start.5 = (bf16[128,2048]{1,0:T(8,128)(2,1)S(1)}, bf16[128,2048]{1,0:T(8,128)(2,1)S(1)}, u32[]{:S(2)}, u32[]{:S(2)}) collective-permute-start(bf16[128,2048]{1,0:T(8,128)(2,1)S(1)} %pick.5.refs_1_), channel_id=1, source_target_pairs={{0,2},{4,6},{9,11},{13,15},{18,16},{22,20},{27,25},{31,29}} | collective-permute-start | bytes 1572872 | tf_op jit(solution)/shard_map/ppermute | solution.py:411
  49.0 13.0 %copy-start.23 = (bf16[128,2048]{1,0:T(8,128)(2,1)}, bf16[128,2048]{1,0:T(8,128)(2,1)S(1)}, u32[]{:S(2)}) copy-start(bf16[128,2048]{1,0:T(8,128)(2,1)S(1)} %collective-permute-done.5.refs_5_) | copy-start | bytes 1572868
  49.0 13.0 %copy-start.12 = (bf16[64,4096]{1,0:T(8,128)(2,1)}, bf16[64,4096]{1,0:T(8,128)(2,1)S(1)}, u32[]{:S(2)}) copy-start(bf16[64,4096]{1,0:T(8,128)(2,1)S(1)} %collective-permute-done.7.refs_0_.refs_1_.refs_5_) | copy-start | bytes 1572868
  49.0 18.2 %copy-start.13 = (bf16[64,4096]{1,0:T(8,128)(2,1)}, bf16[64,4096]{1,0:T(8,128)(2,1)S(1)}, u32[]{:S(2)}) copy-start(bf16[64,4096]{1,0:T(8,128)(2,1)S(1)} %collective-permute-done.6.refs_1_.refs_0_.refs_6_) | copy-start | bytes 1572868
  49.0 11.3 %collective-permute-start.11 = (bf16[1024,256]{1,0:T(8,128)(2,1)S(1)}, bf16[1024,256]{1,0:T(8,128)(2,1)S(1)}, u32[]{:S(2)}, u32[]{:S(2)}) collective-permute-start(bf16[1024,256]{1,0:T(8,128)(2,1)S(1)} %get-tuple-element.81), channel_id=1, source_target_pairs={{0,1},{1,0},{2,3},{3,2},{4,5},{5,4},{6,7},{7,6},{8,9},{9,8},{10,11... | collective-permute-start | bytes 1572872 | tf_op jit(solution)/shard_map/ppermute | solution.py:411
  49.7 17.3 %copy-start.8 = (bf16[128,2048]{1,0:T(8,128)(2,1)}, bf16[128,2048]{1,0:T(8,128)(2,1)S(1)}, u32[]{:S(2)}) copy-start(bf16[128,2048]{1,0:T(8,128)(2,1)S(1)} %get-tuple-element.77.refs_2_) | copy-start | bytes 1572868
  49.8 10.6 %collective-permute-start.9 = (bf16[32,4096]{1,0:T(8,128)(2,1)S(1)}, bf16[32,4096]{1,0:T(8,128)(2,1)S(1)}, u32[]{:S(2)}, u32[]{:S(2)}) collective-permute-start(bf16[32,4096]{1,0:T(8,128)(2,1)S(1)} %get-tuple-element.78), channel_id=1, source_target_pairs={{0,4},{1,5},{2,6},{3,7},{4,0},{5,1},{6,2},{7,3},{8,12},{9,13},{10,... | collective-permute-start | bytes 786440 | tf_op jit(solution)/shard_map/ppermute | solution.py:411
  50.4 10.0 %collective-permute-start.10 = (bf16[32,4096]{1,0:T(8,128)(2,1)S(1)}, bf16[32,4096]{1,0:T(8,128)(2,1)S(1)}, u32[]{:S(2)}, u32[]{:S(2)}) collective-permute-start(bf16[32,4096]{1,0:T(8,128)(2,1)S(1)} %get-tuple-element.79), channel_id=1, source_target_pairs={{0,16},{1,17},{2,18},{3,19},{4,20},{5,21},{6,22},{7,23},{8,0},{9,1... | collective-permute-start | bytes 786440 | tf_op jit(solution)/shard_map/ppermute | solution.py:411
  52.0 9.4 %collective-permute-start.8 = (bf16[128,2048]{1,0:T(8,128)(2,1)S(1)}, bf16[128,2048]{1,0:T(8,128)(2,1)S(1)}, u32[]{:S(2)}, u32[]{:S(2)}) collective-permute-start(bf16[128,2048]{1,0:T(8,128)(2,1)S(1)} %get-tuple-element.77.refs_2_), channel_id=1, source_target_pairs={{0,2},{4,6},{9,11},{13,15},{18,16},{22,20},{27,25},{31,29}} | collective-permute-start | bytes 1572872 | tf_op jit(solution)/shard_map/ppermute | solution.py:411
  60.3 12.5 %copy-start.15 = (bf16[32,4096]{1,0:T(8,128)(2,1)}, bf16[32,4096]{1,0:T(8,128)(2,1)S(1)}, u32[]{:S(2)}) copy-start(bf16[32,4096]{1,0:T(8,128)(2,1)S(1)} %collective-permute-done.9.refs_0_.refs_1_.refs_7_) | copy-start | bytes 786436
  60.4 12.4 %copy-start.16 = (bf16[32,4096]{1,0:T(8,128)(2,1)}, bf16[32,4096]{1,0:T(8,128)(2,1)S(1)}, u32[]{:S(2)}) copy-start(bf16[32,4096]{1,0:T(8,128)(2,1)S(1)} %collective-permute-done.10.refs_1_.refs_2_.refs_8_) | copy-start | bytes 786436
  61.4 11.4 %copy-start.24 = (bf16[128,2048]{1,0:T(8,128)(2,1)}, bf16[128,2048]{1,0:T(8,128)(2,1)S(1)}, u32[]{:S(2)}) copy-start(bf16[128,2048]{1,0:T(8,128)(2,1)S(1)} %collective-permute-done.8.refs_6_) | copy-start | bytes 1572868
  62.0 12.1 %copy-start.4 = (bf16[64,2048]{1,0:T(8,128)(2,1)}, bf16[64,2048]{1,0:T(8,128)(2,1)S(1)}, u32[]{:S(2)}) copy-start(bf16[64,2048]{1,0:T(8,128)(2,1)S(1)} %pick.7.refs_3_) | copy-start | bytes 786436
  62.0 10.8 %collective-permute-start.12 = (bf16[64,2048]{1,0:T(8,128)(2,1)S(1)}, bf16[64,2048]{1,0:T(8,128)(2,1)S(1)}, u32[]{:S(2)}, u32[]{:S(2)}) collective-permute-start(bf16[64,2048]{1,0:T(8,128)(2,1)S(1)} %pick.7.refs_3_), channel_id=1, source_target_pairs={{0,2},{4,6},{9,11},{13,15},{18,16},{22,20},{27,25},{31,29}} | collective-permute-start | bytes 786440 | tf_op jit(solution)/shard_map/ppermute | solution.py:411
  67.1 7.8 %copy-start.9 = (f32[512,256]{1,0:T(8,128)}, f32[512,256]{1,0:T(8,128)S(1)}, u32[]{:S(2)}) copy-start(f32[512,256]{1,0:T(8,128)S(1)} %get-tuple-element.109.refs_0_) | copy-start | bytes 1572868
  67.1 6.4 %collective-permute-start.13 = (bf16[512,256]{1,0:T(8,128)(2,1)S(1)}, bf16[512,256]{1,0:T(8,128)(2,1)S(1)}, u32[]{:S(2)}, u32[]{:S(2)}) collective-permute-start(bf16[512,256]{1,0:T(8,128)(2,1)S(1)} %get-tuple-element.89), channel_id=1, source_target_pairs={{0,2},{1,3},{2,0},{3,1},{4,6},{5,7},{6,4},{7,5},{8,10},{9,11},{10,... | collective-permute-start | bytes 786440 | tf_op jit(solution)/shard_map/ppermute | solution.py:411
  67.2 6.4 %collective-permute-start.14 = (bf16[1024,128]{1,0:T(8,128)(2,1)S(1)}, bf16[1024,128]{1,0:T(8,128)(2,1)S(1)}, u32[]{:S(2)}, u32[]{:S(2)}) collective-permute-start(bf16[1024,128]{1,0:T(8,128)(2,1)S(1)} %get-tuple-element.91), channel_id=1, source_target_pairs={{0,1},{1,0},{2,3},{3,2},{4,5},{5,4},{6,7},{7,6},{8,9},{9,8},{10,11... | collective-permute-start | bytes 786440 | tf_op jit(solution)/shard_map/ppermute | solution.py:411
  72.8 4.1 %copy-start.26 = (bf16[64,2048]{1,0:T(8,128)(2,1)}, bf16[64,2048]{1,0:T(8,128)(2,1)S(1)}, u32[]{:S(2)}) copy-start(bf16[64,2048]{1,0:T(8,128)(2,1)S(1)} %collective-permute-done.12.refs_7_) | copy-start | bytes 786436
  73.5 10.6 %copy-start.25 = (bf16[512,256]{1,0:T(8,128)(2,1)}, bf16[512,256]{1,0:T(8,128)(2,1)S(1)}, u32[]{:S(2)}) copy-start(bf16[512,256]{1,0:T(8,128)(2,1)S(1)} %collective-permute-done.13.refs_1_) | copy-start | bytes 786436
  73.5 7.6 %collective-permute-start.15 = (bf16[1024,128]{1,0:T(8,128)(2,1)S(1)}, bf16[1024,128]{1,0:T(8,128)(2,1)S(1)}, u32[]{:S(2)}, u32[]{:S(2)}) collective-permute-start(bf16[1024,128]{1,0:T(8,128)(2,1)S(1)} %get-tuple-element.95), channel_id=1, source_target_pairs={{0,1},{1,0},{2,3},{3,2},{4,5},{5,4},{6,7},{7,6},{8,9},{9,8},{10,11... | collective-permute-start | bytes 786440 | tf_op jit(solution)/shard_map/ppermute | solution.py:411
  74.9 6.2 %collective-permute-start.16 = (bf16[512,128]{1,0:T(8,128)(2,1)S(1)}, bf16[512,128]{1,0:T(8,128)(2,1)S(1)}, u32[]{:S(2)}, u32[]{:S(2)}) collective-permute-start(bf16[512,128]{1,0:T(8,128)(2,1)S(1)} %get-tuple-element.99), channel_id=1, source_target_pairs={{0,2},{1,3},{2,0},{3,1},{4,6},{5,7},{6,4},{7,5},{8,10},{9,11},{10,... | collective-permute-start | bytes 393224 | tf_op jit(solution)/shard_map/ppermute | solution.py:411
  81.1 3.1 %copy-start.27 = (bf16[512,128]{1,0:T(8,128)(2,1)}, bf16[512,128]{1,0:T(8,128)(2,1)S(1)}, u32[]{:S(2)}) copy-start(bf16[512,128]{1,0:T(8,128)(2,1)S(1)} %collective-permute-done.16.refs_5_) | copy-start | bytes 393220
  81.1 7.2 %collective-permute-start.18 = (bf16[512,2048]{1,0:T(8,128)(2,1)}, bf16[512,2048]{1,0:T(8,128)(2,1)S(1)}, u32[]{:S(2)}, u32[]{:S(2)}) collective-permute-start(bf16[512,2048]{1,0:T(8,128)(2,1)} %pack.1.own_ref), channel_id=1, source_target_pairs={{0,1},{1,0},{2,3},{3,2},{4,5},{5,4},{6,7},{7,6},{8,9},{9,8},{10,11... | collective-permute-start | bytes 6291464 | tf_op jit(solution)/shard_map/ppermute | solution.py:411
  82.4 6.0 %collective-permute-start.17 = (bf16[512,128]{1,0:T(8,128)(2,1)S(1)}, bf16[512,128]{1,0:T(8,128)(2,1)S(1)}, u32[]{:S(2)}, u32[]{:S(2)}) collective-permute-start(bf16[512,128]{1,0:T(8,128)(2,1)S(1)} %get-tuple-element.107), channel_id=1, source_target_pairs={{0,2},{1,3},{2,0},{3,1},{4,6},{5,7},{6,4},{7,5},{8,10},{9,11},{10,... | collective-permute-start | bytes 393224 | tf_op jit(solution)/shard_map/ppermute | solution.py:411
  88.3 5.0 %copy-start.21 = (bf16[512,2048]{1,0:T(8,128)(2,1)}, bf16[512,2048]{1,0:T(8,128)(2,1)S(1)}, u32[]{:S(2)}) copy-start(bf16[512,2048]{1,0:T(8,128)(2,1)S(1)} %collective-permute-done.18.other_ref) | copy-start | bytes 6291460
  90.4 1.2 collective-permute-start.19
  91.6 5.0 %collective-permute-start.20 = (f32[24,64]{1,0:T(8,128)S(1)}, f32[24,64]{1,0:T(8,128)S(1)}, u32[]{:S(2)}, u32[]{:S(2)}) collective-permute-start(f32[24,64]{1,0:T(8,128)S(1)} %add.27), channel_id=1, source_target_pairs={{0,2},{1,3},{2,0},{3,1},{4,6},{5,7},{6,4},{7,5},{8,10},{9,11},{10,... | collective-permute-start | bytes 18440 | tf_op jit(solution)/shard_map/ppermute | solution.py:411
  96.6 4.8 %collective-permute-start.21 = (f32[24,64]{1,0:T(8,128)S(1)}, f32[24,64]{1,0:T(8,128)S(1)}, u32[]{:S(2)}, u32[]{:S(2)}) collective-permute-start(f32[24,64]{1,0:T(8,128)S(1)} %add.28), channel_id=1, source_target_pairs={{0,4},{1,5},{2,6},{3,7},{4,0},{5,1},{6,2},{7,3},{8,12},{9,13},{10,... | collective-permute-start | bytes 18440 | tf_op jit(solution)/shard_map/ppermute | solution.py:411
  101.3 3.8 %collective-permute-start.22 = (f32[24,64]{1,0:T(8,128)S(1)}, f32[24,64]{1,0:T(8,128)S(1)}, u32[]{:S(2)}, u32[]{:S(2)}) collective-permute-start(f32[24,64]{1,0:T(8,128)S(1)} %add.29), channel_id=1, source_target_pairs={{0,8},{1,9},{2,10},{3,11},{4,12},{5,13},{6,14},{7,15},{8,0},{9,1},... | collective-permute-start | bytes 18440 | tf_op jit(solution)/shard_map/ppermute | solution.py:411
  105.1 4.6 %copy-start.28 = (f32[24,64]{1,0:T(8,128)}, f32[24,64]{1,0:T(8,128)S(1)}, u32[]{:S(2)}) copy-start(f32[24,64]{1,0:T(8,128)S(1)} %add.30.refs_9_) | copy-start | bytes 18436
  105.1 4.6 %collective-permute-start.23 = (f32[24,64]{1,0:T(8,128)S(1)}, f32[24,64]{1,0:T(8,128)S(1)}, u32[]{:S(2)}, u32[]{:S(2)}) collective-permute-start(f32[24,64]{1,0:T(8,128)S(1)} %add.30.refs_9_), channel_id=1, source_target_pairs={{0,16},{1,17},{2,18},{3,19},{4,20},{5,21},{6,22},{7,23},{8,24},{9,... | collective-permute-start | bytes 18440 | tf_op jit(solution)/shard_map/ppermute | solution.py:411
  (6 other events, 4.4 us)

commit v7 on v6

--- a/solution.py
+++ b/solution.py
@@ -183,21 +183,30 @@
     )
 
 
-def join_kernel(first, scalars_ref, own_ref, other_ref, out_ref, x_ref, xt_ref, sems):
-    columns = pl.ds(first, x_ref.shape[1])
+def join_kernel(first, scalars_ref, own_ref, other_ref, out_ref, x_ref, xt_ref, in_sems, out_sems):
+    wide = min(256, x_ref.shape[1])
+    parts = [pl.ds(c * wide, wide) for c in range(x_ref.shape[1] // wide)]
+
+    def turn(source):
+        arriving = fetch(
+            [(source.at[:, pl.ds(first + c * wide, wide)], x_ref.at[:, part]) for c, part in enumerate(parts)],
+            in_sems,
+        )
+        leaving = []
+        for c, part in enumerate(parts):
+            arriving[c].wait()
+            xt_ref[part, :] = x_ref[:, part].T
+            leaving += fetch([(xt_ref.at[part], out_ref.at[part])], out_sems.at[pl.ds(c, 1)])
+        for one in leaving:
+            one.wait()
 
     @pl.when(scalars_ref[EVEN] == 1)
     def _():
-        fetch([(own_ref.at[:, columns], x_ref)], sems)[0].wait()
+        turn(own_ref)
 
     @pl.when(scalars_ref[EVEN] == 0)
     def _():
-        fetch([(other_ref.at[:, columns], x_ref)], sems)[0].wait()
-
-    wide = min(256, x_ref.shape[1])
-    for c in range(x_ref.shape[1] // wide):
-        xt_ref[pl.ds(c * wide, wide), :] = x_ref[:, c * wide:(c + 1) * wide].T
-    fetch([(xt_ref, out_ref)], sems)[0].wait()
+        turn(other_ref)
 
 
 def join(scalars, own, other, half):
@@ -209,7 +218,8 @@
         [
             pltpu.VMEM((rows, width), jnp.bfloat16),
             pltpu.VMEM((width, rows), jnp.bfloat16),
-            pltpu.SemaphoreType.DMA((1,)),
+            pltpu.SemaphoreType.DMA((max(1, width // 256),)),
+            pltpu.SemaphoreType.DMA((max(1, width // 256),)),
         ],
         (scalars, []),
         (own, other, "out"),
@@ -225,11 +235,8 @@
         out_ref[pl.ds(scalars_ref[slot + i], 1), :] = line[:, i * count:(i + 1) * count]
 
 
-def early_kernel(slots, firsts, scalars_ref, *refs):
-    early = 2 * len(firsts) - 2
-    held = refs[early + 5:-1]
-    w_ref, strata_ref, keep_ref, got_ref, out_ref = refs[early:early + 5]
-    copies = fetch(list(zip(refs[:early], held)), refs[-1])
+def early_kernel(slots, firsts, scalars_ref, w_ref, strata_ref, *refs):
+    out_ref = refs[-1]
     out_ref[...] = jnp.zeros_like(out_ref)
 
     @pl.when(scalars_ref[FEAT] == 0)
@@ -237,23 +244,17 @@
         out_ref[pl.ds(slots + scalars_ref[ROW], 1), :] = w_ref[...]
         out_ref[pl.ds(2 * slots + scalars_ref[ROW], 1), :] = strata_ref[...].astype(jnp.float32)
 
-    put_squares(out_ref, scalars_ref, firsts[-1], keep_ref, got_ref)
-    for copy in copies:
-        copy.wait()
-    for g, first in enumerate(firsts[:-1]):
-        put_squares(out_ref, scalars_ref, first, held[2 * g], held[2 * g + 1])
+    for g, first in enumerate(firsts):
+        put_squares(out_ref, scalars_ref, first, refs[2 * g], refs[2 * g + 1])
 
 
 def early_squares(scalars, firsts, slots, weights, strata, pairs):
-    early = [x for pair in pairs[:-1] for x in pair]
     return call(
         functools.partial(early_kernel, slots, firsts),
         "early_squares",
         jax.ShapeDtypeStruct((3 * slots, weights.shape[1]), jnp.float32),
-        [pltpu.VMEM(x.shape, x.dtype) for x in early] + [pltpu.SemaphoreType.DMA((len(early),))],
-        (scalars, [weights, strata] + list(pairs[-1])),
-        tuple(early),
-        BIG,
+        [],
+        (scalars, [weights, strata] + [x for pair in pairs for x in pair]),
     )
 
 
@@ -318,13 +319,13 @@
     half = col_ref.shape[0] // 2
     first = fetch(bring(0, width), first_sems)
     first += fetch([(low_hbm, col_ref.at[:half]), (high_hbm, col_ref.at[half:])], col_sems)
-    rest = fetch(bring(width, (steps - 1) * width), rest_sems) if steps > 1 else []
     total_ref[...] = sums_ref[...] + got_ref[...]
     weight_step(
         2 * (sums_ref.shape[0] // 3), features, scalars_ref[ROW], total_ref, new_ref, lev_ref, all_ref, d_ref
     )
     for one in first:
         one.wait()
+    rest = fetch(bring(width, (steps - 1) * width), rest_sems) if steps > 1 else []
 
     def step(j, carry):
         @pl.when(j == 1)

time: 130 us -> 127 us (0.977)
  Pallas kernels: 60.2 us -> 56.7 us
  waiting for transfers between devices: 20.8 us -> 23 us
  local copies, waits for them, and re-layouts: 11 us -> 8.97 us
    pallas_call x16, Pallas kernels: 39.8 us -> 37 us  [call(): pl.pallas_call(kernel, in_specs=[pl.BlockSpec(memory_space=pltpu.SMEM)] +...]
    ppermute x24, waiting for transfers between devices: 20.8 us -> 23 us  [send(): return lax.ppermute(x, BOTH, pairs)]
    unnamed x60 -> x52, local copies, waits for them, and re-layouts: 10.2 us -> 8.19 us
  transfers between devices with their start and end apart: 24 -> 24, of which waited for: 11 -> 11; matrix products, arithmetic and copies ran while one was open for 1% -> 1% of each run, Pallas kernels for 31% -> 29%
where the time goes in v7:
time: 127 us; the launch traced here: 126 us
  Pallas kernels  56.7 us (45%)
  starting transfers between devices  35.7 us (28%)
  waiting for transfers between devices  23 us (18%)
  local copies, waits for them, and re-layouts  8.97 us (7%)
    pallas_call x16, Pallas kernels, call(): pl.pallas_call(kernel, in_specs=[pl.BlockSpec(memory_space=pltpu.SMEM)] +...  37 us
    ppermute x24, starting transfers between devices, send(): return lax.ppermute(x, BOTH, pairs)  35.7 us
    ppermute x24, waiting for transfers between devices, send(): return lax.ppermute(x, BOTH, pairs)  23 us
    pallas_call x1, Pallas kernels, increment(): pl.pallas_call(functools.partial(information_kernel, features, pieces_of)...  18.6 us
    unnamed x52, local copies, waits for them, and re-layouts  8.19 us
  transfers between devices with their start and end apart: 24, of which 11 were waited for; matrix products, arithmetic and copies ran while one was open for 1% of the time, Pallas kernels for 29%

profile of v7, /device:TPU:0, one launch (start us, length us, event | category | flops | bytes accessed | tf_op | source)
XLA Modules:
  0.0 126.2 jit_solution(7745260869484491725)
XLA Ops:
  0.6 3.0 %collective-permute-start.1 = (bf16[64,4096]{1,0:T(8,128)(2,1)}, bf16[64,4096]{1,0:T(8,128)(2,1)S(1)}, u32[]{:S(2)}, u32[]{:S(2)}) collective-permute-start(bf16[64,4096]{1,0:T(8,128)(2,1)} %refs_0_.5), channel_id=1, source_target_pairs={{0,4},{1,5},{2,6},{3,7},{4,0},{5,1},{6,2},{7,3},{8,12},{9,13},{10,... | collective-permute-start | bytes 1572872 | tf_op jit(solution)/shard_map/ppermute | solution.py:412
  3.6 2.6 %collective-permute-start = (bf16[64,4096]{1,0:T(8,128)(2,1)}, bf16[64,4096]{1,0:T(8,128)(2,1)S(1)}, u32[]{:S(2)}, u32[]{:S(2)}) collective-permute-start(bf16[64,4096]{1,0:T(8,128)(2,1)} %refs_0_.5), channel_id=1, source_target_pairs={{0,16},{1,17},{2,18},{3,19},{4,20},{5,21},{6,22},{7,23},{8,0},{9,1... | collective-permute-start | bytes 1572872 | tf_op jit(solution)/shard_map/ppermute | solution.py:412
  6.2 0.7 dynamic-slice_bitcast_fusion
  6.9 0.7 xor_multiply_fusion
  7.7 5.8 %copy-done = bf16[2048,4096]{1,0:T(8,128)(2,1)S(1)} copy-done((bf16[2048,4096]{1,0:T(8,128)(2,1)S(1)}, bf16[2048,4096]{1,0:T(8,128)(2,1)}, u32[]{:S(2)}) %copy-start) | copy-done | bytes 16777240
  13.4 1.1 touch.1.scalars_ref._
  14.6 1.2 collective-permute-done.1.refs_1_
  15.8 1.7 %collective-permute-done.refs_2_ = bf16[64,4096]{1,0:T(8,128)(2,1)S(1)} collective-permute-done((bf16[64,4096]{1,0:T(8,128)(2,1)}, bf16[64,4096]{1,0:T(8,128)(2,1)S(1)}, u32[]{:S(2)}, u32[]{:S(2)}) %collective-permute-start) | collective-permute-done | bytes 524320 | tf_op jit(solution)/shard_map/ppermute | solution.py:412
  18.0 3.3 %collective-permute-start.3 = (bf16[64,4096]{1,0:T(8,128)(2,1)S(1)}, bf16[64,4096]{1,0:T(8,128)(2,1)S(1)}, u32[]{:S(2)}, u32[]{:S(2)}) collective-permute-start(bf16[64,4096]{1,0:T(8,128)(2,1)S(1)} %collective-permute-done.refs_2_), channel_id=1, source_target_pairs={{0,16},{1,17},{2,18},{3,19},{4,20},{5,21},{6,22},{7,23},{8,0},{9,1... | collective-permute-start | bytes 1572872 | tf_op jit(solution)/shard_map/ppermute | solution.py:412
  21.3 1.0 copy-done.5
  22.3 0.6 pick.4.refs_0_
  22.9 3.5 %collective-permute-start.2 = (bf16[192,2048]{1,0:T(8,128)(2,1)S(1)}, bf16[192,2048]{1,0:T(8,128)(2,1)S(1)}, u32[]{:S(2)}, u32[]{:S(2)}) collective-permute-start(bf16[192,2048]{1,0:T(8,128)(2,1)S(1)} %pick.4.refs_0_), channel_id=1, source_target_pairs={{0,2},{4,6},{9,11},{13,15},{18,16},{22,20},{27,25},{31,29}} | collective-permute-start | bytes 2359304 | tf_op jit(solution)/shard_map/ppermute | solution.py:412
  26.4 5.5 %whiten.4 = (f32[1024,128]{1,0:T(8,128)S(1)}, bf16[1024,128]{1,0:T(8,128)(2,1)S(1)}) custom-call(s32[25]{0:T(128)S(1)} %touch.1.scalars_ref._, bf16[2048,4096]{1,0:T(8,128)(2,1)S(1)} %copy-done.1, bf16[64,4096]{1,0:T(8,128)(2,1)S(1)} %copy-done.5, bf16[64,4096]{1,0:T(8,128)(2,1)S(1)} %collective-permute-done.1.refs_1_), custom_call_target="tpu_custom_call" | custom-call | flops 8589934592 | bytes 1000 | tf_op jit(solution)/shard_map/whiten/pallas_call | solution.py:33
  32.0 3.9 %collective-permute-done.2.refs_4_ = bf16[192,2048]{1,0:T(8,128)(2,1)S(1)} collective-permute-done((bf16[192,2048]{1,0:T(8,128)(2,1)S(1)}, bf16[192,2048]{1,0:T(8,128)(2,1)S(1)}, u32[]{:S(2)}, u32[]{:S(2)}) %collective-permute-start.2) | collective-permute-done | bytes 786464 | tf_op jit(solution)/shard_map/ppermute | solution.py:412
  35.8 1.5 %collective-permute-start.7 = (bf16[64,4096]{1,0:T(8,128)(2,1)S(1)}, bf16[64,4096]{1,0:T(8,128)(2,1)S(1)}, u32[]{:S(2)}, u32[]{:S(2)}) collective-permute-start(bf16[64,4096]{1,0:T(8,128)(2,1)S(1)} %collective-permute-done.3.refs_1_.refs_0_.refs_4_), channel_id=1, source_target_pairs={{0,4},{1,5},{2,6},{3,7},{4,0},{5,1},{6,2},{7,3},{8,12},{9,13},{10,... | collective-permute-start | bytes 1572872 | tf_op jit(solution)/shard_map/ppermute | solution.py:412
  37.3 1.6 %collective-permute-start.6 = (bf16[64,4096]{1,0:T(8,128)(2,1)S(1)}, bf16[64,4096]{1,0:T(8,128)(2,1)S(1)}, u32[]{:S(2)}, u32[]{:S(2)}) collective-permute-start(bf16[64,4096]{1,0:T(8,128)(2,1)S(1)} %collective-permute-done.3.refs_1_.refs_0_.refs_4_), channel_id=1, source_target_pairs={{0,16},{1,17},{2,18},{3,19},{4,20},{5,21},{6,22},{7,23},{8,0},{9,1... | collective-permute-start | bytes 1572872 | tf_op jit(solution)/shard_map/ppermute | solution.py:412
  39.6 2.8 %collective-permute-start.5 = (bf16[128,2048]{1,0:T(8,128)(2,1)S(1)}, bf16[128,2048]{1,0:T(8,128)(2,1)S(1)}, u32[]{:S(2)}, u32[]{:S(2)}) collective-permute-start(bf16[128,2048]{1,0:T(8,128)(2,1)S(1)} %pick.5.refs_1_), channel_id=1, source_target_pairs={{0,2},{4,6},{9,11},{13,15},{18,16},{22,20},{27,25},{31,29}} | collective-permute-start | bytes 1572872 | tf_op jit(solution)/shard_map/ppermute | solution.py:412
  42.4 5.6 %whiten.5 = (f32[1024,256]{1,0:T(8,128)S(1)}, bf16[1024,256]{1,0:T(8,128)(2,1)S(1)}) custom-call(s32[25]{0:T(128)S(1)} %touch.1.scalars_ref._, bf16[2048,4096]{1,0:T(8,128)(2,1)S(1)} %copy-done.1, f32[1024,128]{1,0:T(8,128)S(1)} %get-tuple-element.71.refs_0_, bf16[1024,128]{1,0:T(8,128)(2,1)S(1)} %get-tuple-element.72.refs_1_, ...), custom_call_target="tpu_custom_call" | custom-call | flops 8589934592 | bytes 1000 | tf_op jit(solution)/shard_map/whiten/pallas_call | solution.py:33
  47.9 1.1 collective-permute-done.5.refs_5_
  49.1 0.6 pick.6
  49.8 0.6 collective-permute-start.9
  50.4 1.6 %collective-permute-start.10 = (bf16[32,4096]{1,0:T(8,128)(2,1)S(1)}, bf16[32,4096]{1,0:T(8,128)(2,1)S(1)}, u32[]{:S(2)}, u32[]{:S(2)}) collective-permute-start(bf16[32,4096]{1,0:T(8,128)(2,1)S(1)} %get-tuple-element.79), channel_id=1, source_target_pairs={{0,16},{1,17},{2,18},{3,19},{4,20},{5,21},{6,22},{7,23},{8,0},{9,1... | collective-permute-start | bytes 786440 | tf_op jit(solution)/shard_map/ppermute | solution.py:412
  52.0 2.8 %collective-permute-start.8 = (bf16[128,2048]{1,0:T(8,128)(2,1)S(1)}, bf16[128,2048]{1,0:T(8,128)(2,1)S(1)}, u32[]{:S(2)}, u32[]{:S(2)}) collective-permute-start(bf16[128,2048]{1,0:T(8,128)(2,1)S(1)} %get-tuple-element.77.refs_2_), channel_id=1, source_target_pairs={{0,2},{4,6},{9,11},{13,15},{18,16},{22,20},{27,25},{31,29}} | collective-permute-start | bytes 1572872 | tf_op jit(solution)/shard_map/ppermute | solution.py:412
  54.8 5.5 %whiten.6 = (f32[1024,128]{1,0:T(8,128)S(1)}, bf16[1024,128]{1,0:T(8,128)(2,1)S(1)}) custom-call(s32[25]{0:T(128)S(1)} %touch.1.scalars_ref._, bf16[2048,4096]{1,0:T(8,128)(2,1)S(1)} %copy-done.1, bf16[64,4096]{1,0:T(8,128)(2,1)S(1)} %collective-permute-done.3.refs_1_.refs_0_.refs_4_, bf16[64,4096]{1,0:T(8,128)(2,1)S(1)} %collective-permute-done.7.refs_0_.refs_1_.refs_5_), custom_call_target="tpu_custom_call" | custom-call | flops 8589934592 | bytes 1000 | tf_op jit(solution)/shard_map/whiten/pallas_call | solution.py:33
  60.4 1.0 collective-permute-done.8.refs_6_
  62.0 4.4 %collective-permute-start.12 = (bf16[64,2048]{1,0:T(8,128)(2,1)S(1)}, bf16[64,2048]{1,0:T(8,128)(2,1)S(1)}, u32[]{:S(2)}, u32[]{:S(2)}) collective-permute-start(bf16[64,2048]{1,0:T(8,128)(2,1)S(1)} %pick.7.refs_3_), channel_id=1, source_target_pairs={{0,2},{4,6},{9,11},{13,15},{18,16},{22,20},{27,25},{31,29}} | collective-permute-start | bytes 786440 | tf_op jit(solution)/shard_map/ppermute | solution.py:412
  66.4 0.6 halve.3
  67.3 5.5 %whiten.7 = (f32[1024,128]{1,0:T(8,128)S(1)}, bf16[1024,128]{1,0:T(8,128)(2,1)S(1)}) custom-call(s32[25]{0:T(128)S(1)} %touch.1.scalars_ref._, bf16[2048,4096]{1,0:T(8,128)(2,1)S(1)} %copy-done.1, bf16[64,4096]{1,0:T(8,128)(2,1)S(1)} %collective-permute-done.6.refs_1_.refs_0_.refs_6_, bf16[32,4096]{1,0:T(8,128)(2,1)S(1)} %collective-permute-done.9.refs_0_.refs_1_.refs_7_, ...), custom_call_target="tpu_custom_call" | custom-call | flops 8589934592 | bytes 1000 | tf_op jit(solution)/shard_map/whiten/pallas_call | solution.py:33
  72.9 0.7 collective-permute-done.13.refs_1_
  73.6 0.6 halve.4
  74.2 2.1 %collective-permute-start.16 = (bf16[512,128]{1,0:T(8,128)(2,1)S(1)}, bf16[512,128]{1,0:T(8,128)(2,1)S(1)}, u32[]{:S(2)}, u32[]{:S(2)}) collective-permute-start(bf16[512,128]{1,0:T(8,128)(2,1)S(1)} %get-tuple-element.99), channel_id=1, source_target_pairs={{0,2},{1,3},{2,0},{3,1},{4,6},{5,7},{6,4},{7,5},{8,10},{9,11},{10,... | collective-permute-start | bytes 393224 | tf_op jit(solution)/shard_map/ppermute | solution.py:412
  76.3 3.5 %pack.1.own_ref = bf16[512,2048]{1,0:T(8,128)(2,1)} custom-call(s32[25]{0:T(128)} %copy-done.15, bf16[192,2048]{1,0:T(8,128)(2,1)} %copy-done.2, bf16[128,2048]{1,0:T(8,128)(2,1)} %copy-done.3, bf16[128,2048]{1,0:T(8,128)(2,1)} %copy-done.8, bf16[64,2048]{1,0:T(8,128)(2,1)} %copy-done.4, bf16[192,2048]{1,0:T(8,128)(2,1)} %copy-done.20, ...), custom_call_target="tpu_custom_call" | custom-call | flops 1000 | bytes 1000 | tf_op jit(solution)/shard_map/pack/pallas_call | solution.py:33
  79.8 0.6 collective-permute-done.16.refs_3_
  80.4 0.7 copy-done.16
  81.1 0.6 halve.5
  81.7 1.8 %collective-permute-start.17 = (bf16[512,128]{1,0:T(8,128)(2,1)S(1)}, bf16[512,128]{1,0:T(8,128)(2,1)S(1)}, u32[]{:S(2)}, u32[]{:S(2)}) collective-permute-start(bf16[512,128]{1,0:T(8,128)(2,1)S(1)} %get-tuple-element.107), channel_id=1, source_target_pairs={{0,2},{1,3},{2,0},{3,1},{4,6},{5,7},{6,4},{7,5},{8,10},{9,11},{10,... | collective-permute-start | bytes 393224 | tf_op jit(solution)/shard_map/ppermute | solution.py:412
  83.5 0.8 early_squares.1.sums_ref
  84.3 3.4 %collective-permute-done.17.got_ref = bf16[512,128]{1,0:T(8,128)(2,1)S(1)} collective-permute-done((bf16[512,128]{1,0:T(8,128)(2,1)S(1)}, bf16[512,128]{1,0:T(8,128)(2,1)S(1)}, u32[]{:S(2)}, u32[]{:S(2)}) %collective-permute-start.17) | collective-permute-done | bytes 131104 | tf_op jit(solution)/shard_map/ppermute | solution.py:412
  87.7 0.7 last_squares.1
  88.4 1.2 collective-permute-done.19
  89.6 1.7 %collective-permute-start.20 = (f32[24,64]{1,0:T(8,128)S(1)}, f32[24,64]{1,0:T(8,128)S(1)}, u32[]{:S(2)}, u32[]{:S(2)}) collective-permute-start(f32[24,64]{1,0:T(8,128)S(1)} %add.27), channel_id=1, source_target_pairs={{0,2},{1,3},{2,0},{3,1},{4,6},{5,7},{6,4},{7,5},{8,10},{9,11},{10,... | collective-permute-start | bytes 18440 | tf_op jit(solution)/shard_map/ppermute | solution.py:412
  91.3 2.9 %join.2.low_hbm = bf16[1024,512]{1,0:T(8,128)(2,1)} custom-call(s32[25]{0:T(128)} %copy-done.15, bf16[512,2048]{1,0:T(8,128)(2,1)} %pack.1.own_ref, bf16[512,2048]{1,0:T(8,128)(2,1)} %copy-done.19), custom_call_target="tpu_custom_call" | custom-call | flops 1000 | bytes 1000 | tf_op jit(solution)/shard_map/join/pallas_call | solution.py:33
  94.2 1.6 %collective-permute-start.21 = (f32[24,64]{1,0:T(8,128)S(1)}, f32[24,64]{1,0:T(8,128)S(1)}, u32[]{:S(2)}, u32[]{:S(2)}) collective-permute-start(f32[24,64]{1,0:T(8,128)S(1)} %add.28), channel_id=1, source_target_pairs={{0,4},{1,5},{2,6},{3,7},{4,0},{5,1},{6,2},{7,3},{8,12},{9,13},{10,... | collective-permute-start | bytes 18440 | tf_op jit(solution)/shard_map/ppermute | solution.py:412
  95.8 2.9 %join.3.high_hbm = bf16[1024,512]{1,0:T(8,128)(2,1)} custom-call(s32[25]{0:T(128)} %copy-done.15, bf16[512,2048]{1,0:T(8,128)(2,1)} %pack.1.own_ref, bf16[512,2048]{1,0:T(8,128)(2,1)} %copy-done.19), custom_call_target="tpu_custom_call" | custom-call | flops 1000 | bytes 1000 | tf_op jit(solution)/shard_map/join/pallas_call | solution.py:33
  98.8 3.7 %collective-permute-done.22 = f32[24,64]{1,0:T(8,128)S(1)} collective-permute-done((f32[24,64]{1,0:T(8,128)S(1)}, f32[24,64]{1,0:T(8,128)S(1)}, u32[]{:S(2)}, u32[]{:S(2)}) %collective-permute-start.22) | collective-permute-done | bytes 6176 | tf_op jit(solution)/shard_map/ppermute | solution.py:412
  102.5 4.6 %collective-permute-done.23.refs_10_ = f32[24,64]{1,0:T(8,128)S(1)} collective-permute-done((f32[24,64]{1,0:T(8,128)S(1)}, f32[24,64]{1,0:T(8,128)S(1)}, u32[]{:S(2)}, u32[]{:S(2)}) %collective-permute-start.23) | collective-permute-done | bytes 6176 | tf_op jit(solution)/shard_map/ppermute | solution.py:412
  107.1 0.6 copy-done.25
  107.7 18.6 %increment.1 = (f32[2048,4096]{1,0:T(8,128)}, f32[1,64]{1,0:T(1,128)}, f32[1,64]{1,0:T(1,128)}) custom-call(s32[25]{0:T(128)} %copy-done.15, bf16[1024,512]{1,0:T(8,128)(2,1)} %join.2.low_hbm, bf16[1024,512]{1,0:T(8,128)(2,1)} %join.3.high_hbm, bf16[64,4096]{1,0:T(8,128)(2,1)} %refs_0_.5, bf16[64,4096]{1,0:T(8,128)(2,1)} %copy-done.6, ...), custom_call_target="tpu_custom_call" | custom-call | flops 8589934592 | bytes 1000 | tf_op jit(solution)/shard_map/increment/pallas_call | solution.py:366
  (77 shorter events, 2.2 us)
Async XLA Ops:
  0.6 15.1 %collective-permute-start.1 = (bf16[64,4096]{1,0:T(8,128)(2,1)}, bf16[64,4096]{1,0:T(8,128)(2,1)S(1)}, u32[]{:S(2)}, u32[]{:S(2)}) collective-permute-start(bf16[64,4096]{1,0:T(8,128)(2,1)} %refs_0_.5), channel_id=1, source_target_pairs={{0,4},{1,5},{2,6},{3,7},{4,0},{5,1},{6,2},{7,3},{8,12},{9,13},{10,... | collective-permute-start | bytes 1572872 | tf_op jit(solution)/shard_map/ppermute | solution.py:412
  3.6 13.8 %collective-permute-start = (bf16[64,4096]{1,0:T(8,128)(2,1)}, bf16[64,4096]{1,0:T(8,128)(2,1)S(1)}, u32[]{:S(2)}, u32[]{:S(2)}) collective-permute-start(bf16[64,4096]{1,0:T(8,128)(2,1)} %refs_0_.5), channel_id=1, source_target_pairs={{0,16},{1,17},{2,18},{3,19},{4,20},{5,21},{6,22},{7,23},{8,0},{9,1... | collective-permute-start | bytes 1572872 | tf_op jit(solution)/shard_map/ppermute | solution.py:412
  7.7 5.8 %copy-start = (bf16[2048,4096]{1,0:T(8,128)(2,1)S(1)}, bf16[2048,4096]{1,0:T(8,128)(2,1)}, u32[]{:S(2)}) copy-start(bf16[2048,4096]{1,0:T(8,128)(2,1)} %f_ref.9) | copy-start | bytes 50331652
  13.4 13.0 %copy-start.1 = (bf16[2048,4096]{1,0:T(8,128)(2,1)S(1)}, bf16[2048,4096]{1,0:T(8,128)(2,1)}, u32[]{:S(2)}) copy-start(bf16[2048,4096]{1,0:T(8,128)(2,1)} %f_ref.9) | copy-start | bytes 50331652
  14.6 59.0 %copy-start.15 = (s32[25]{0:T(128)}, s32[25]{0:T(128)S(1)}, u32[]{:S(2)}) copy-start(s32[25]{0:T(128)S(1)} %touch.1.scalars_ref._) | copy-start | bytes 304
  15.8 16.2 %copy-start.6 = (bf16[64,4096]{1,0:T(8,128)(2,1)}, bf16[64,4096]{1,0:T(8,128)(2,1)S(1)}, u32[]{:S(2)}) copy-start(bf16[64,4096]{1,0:T(8,128)(2,1)S(1)} %collective-permute-done.1.refs_1_) | copy-start | bytes 1572868
  17.4 24.9 %copy-start.7 = (bf16[64,4096]{1,0:T(8,128)(2,1)}, bf16[64,4096]{1,0:T(8,128)(2,1)S(1)}, u32[]{:S(2)}) copy-start(bf16[64,4096]{1,0:T(8,128)(2,1)S(1)} %collective-permute-done.refs_2_) | copy-start | bytes 1572868
  17.4 14.5 %collective-permute-start.4 = (bf16[64,4096]{1,0:T(8,128)(2,1)S(1)}, bf16[64,4096]{1,0:T(8,128)(2,1)S(1)}, u32[]{:S(2)}, u32[]{:S(2)}) collective-permute-start(bf16[64,4096]{1,0:T(8,128)(2,1)S(1)} %collective-permute-done.refs_2_), channel_id=1, source_target_pairs={{0,4},{1,5},{2,6},{3,7},{4,0},{5,1},{6,2},{7,3},{8,12},{9,13},{10,... | collective-permute-start | bytes 1572872 | tf_op jit(solution)/shard_map/ppermute | solution.py:412
  18.0 14.0 %collective-permute-start.3 = (bf16[64,4096]{1,0:T(8,128)(2,1)S(1)}, bf16[64,4096]{1,0:T(8,128)(2,1)S(1)}, u32[]{:S(2)}, u32[]{:S(2)}) collective-permute-start(bf16[64,4096]{1,0:T(8,128)(2,1)S(1)} %collective-permute-done.refs_2_), channel_id=1, source_target_pairs={{0,16},{1,17},{2,18},{3,19},{4,20},{5,21},{6,22},{7,23},{8,0},{9,1... | collective-permute-start | bytes 1572872 | tf_op jit(solution)/shard_map/ppermute | solution.py:412
  21.3 1.0 copy-start.5
  22.9 25.0 %copy-start.2 = (bf16[192,2048]{1,0:T(8,128)(2,1)}, bf16[192,2048]{1,0:T(8,128)(2,1)S(1)}, u32[]{:S(2)}) copy-start(bf16[192,2048]{1,0:T(8,128)(2,1)S(1)} %pick.4.refs_0_) | copy-start | bytes 2359300
  22.9 12.9 %collective-permute-start.2 = (bf16[192,2048]{1,0:T(8,128)(2,1)S(1)}, bf16[192,2048]{1,0:T(8,128)(2,1)S(1)}, u32[]{:S(2)}, u32[]{:S(2)}) collective-permute-start(bf16[192,2048]{1,0:T(8,128)(2,1)S(1)} %pick.4.refs_0_), channel_id=1, source_target_pairs={{0,2},{4,6},{9,11},{13,15},{18,16},{22,20},{27,25},{31,29}} | collective-permute-start | bytes 2359304 | tf_op jit(solution)/shard_map/ppermute | solution.py:412
  31.9 17.8 %copy-start.9 = (bf16[64,4096]{1,0:T(8,128)(2,1)}, bf16[64,4096]{1,0:T(8,128)(2,1)S(1)}, u32[]{:S(2)}) copy-start(bf16[64,4096]{1,0:T(8,128)(2,1)S(1)} %collective-permute-done.4.refs_0_.refs_3_) | copy-start | bytes 1572868
  32.0 22.8 %copy-start.10 = (bf16[64,4096]{1,0:T(8,128)(2,1)}, bf16[64,4096]{1,0:T(8,128)(2,1)S(1)}, u32[]{:S(2)}) copy-start(bf16[64,4096]{1,0:T(8,128)(2,1)S(1)} %collective-permute-done.3.refs_1_.refs_0_.refs_4_) | copy-start | bytes 1572868
  35.8 13.9 %copy-start.20 = (bf16[192,2048]{1,0:T(8,128)(2,1)}, bf16[192,2048]{1,0:T(8,128)(2,1)S(1)}, u32[]{:S(2)}) copy-start(bf16[192,2048]{1,0:T(8,128)(2,1)S(1)} %collective-permute-done.2.refs_4_) | copy-start | bytes 2359300
  35.8 13.2 %collective-permute-start.7 = (bf16[64,4096]{1,0:T(8,128)(2,1)S(1)}, bf16[64,4096]{1,0:T(8,128)(2,1)S(1)}, u32[]{:S(2)}, u32[]{:S(2)}) collective-permute-start(bf16[64,4096]{1,0:T(8,128)(2,1)S(1)} %collective-permute-done.3.refs_1_.refs_0_.refs_4_), channel_id=1, source_target_pairs={{0,4},{1,5},{2,6},{3,7},{4,0},{5,1},{6,2},{7,3},{8,12},{9,13},{10,... | collective-permute-start | bytes 1572872 | tf_op jit(solution)/shard_map/ppermute | solution.py:412
  37.3 11.7 %collective-permute-start.6 = (bf16[64,4096]{1,0:T(8,128)(2,1)S(1)}, bf16[64,4096]{1,0:T(8,128)(2,1)S(1)}, u32[]{:S(2)}, u32[]{:S(2)}) collective-permute-start(bf16[64,4096]{1,0:T(8,128)(2,1)S(1)} %collective-permute-done.3.refs_1_.refs_0_.refs_4_), channel_id=1, source_target_pairs={{0,16},{1,17},{2,18},{3,19},{4,20},{5,21},{6,22},{7,23},{8,0},{9,1... | collective-permute-start | bytes 1572872 | tf_op jit(solution)/shard_map/ppermute | solution.py:412
  39.6 20.8 %copy-start.3 = (bf16[128,2048]{1,0:T(8,128)(2,1)}, bf16[128,2048]{1,0:T(8,128)(2,1)S(1)}, u32[]{:S(2)}) copy-start(bf16[128,2048]{1,0:T(8,128)(2,1)S(1)} %pick.5.refs_1_) | copy-start | bytes 1572868
  39.6 9.4 %collective-permute-start.5 = (bf16[128,2048]{1,0:T(8,128)(2,1)S(1)}, bf16[128,2048]{1,0:T(8,128)(2,1)S(1)}, u32[]{:S(2)}, u32[]{:S(2)}) collective-permute-start(bf16[128,2048]{1,0:T(8,128)(2,1)S(1)} %pick.5.refs_1_), channel_id=1, source_target_pairs={{0,2},{4,6},{9,11},{13,15},{18,16},{22,20},{27,25},{31,29}} | collective-permute-start | bytes 1572872 | tf_op jit(solution)/shard_map/ppermute | solution.py:412
  49.0 13.0 %copy-start.21 = (bf16[128,2048]{1,0:T(8,128)(2,1)}, bf16[128,2048]{1,0:T(8,128)(2,1)S(1)}, u32[]{:S(2)}) copy-start(bf16[128,2048]{1,0:T(8,128)(2,1)S(1)} %collective-permute-done.5.refs_5_) | copy-start | bytes 1572868
  49.0 13.0 %copy-start.11 = (bf16[64,4096]{1,0:T(8,128)(2,1)}, bf16[64,4096]{1,0:T(8,128)(2,1)S(1)}, u32[]{:S(2)}) copy-start(bf16[64,4096]{1,0:T(8,128)(2,1)S(1)} %collective-permute-done.7.refs_0_.refs_1_.refs_5_) | copy-start | bytes 1572868
  49.0 18.2 %copy-start.12 = (bf16[64,4096]{1,0:T(8,128)(2,1)}, bf16[64,4096]{1,0:T(8,128)(2,1)S(1)}, u32[]{:S(2)}) copy-start(bf16[64,4096]{1,0:T(8,128)(2,1)S(1)} %collective-permute-done.6.refs_1_.refs_0_.refs_6_) | copy-start | bytes 1572868
  49.0 11.3 %collective-permute-start.11 = (bf16[1024,256]{1,0:T(8,128)(2,1)S(1)}, bf16[1024,256]{1,0:T(8,128)(2,1)S(1)}, u32[]{:S(2)}, u32[]{:S(2)}) collective-permute-start(bf16[1024,256]{1,0:T(8,128)(2,1)S(1)} %get-tuple-element.81), channel_id=1, source_target_pairs={{0,1},{1,0},{2,3},{3,2},{4,5},{5,4},{6,7},{7,6},{8,9},{9,8},{10,11... | collective-permute-start | bytes 1572872 | tf_op jit(solution)/shard_map/ppermute | solution.py:412
  49.7 17.3 %copy-start.8 = (bf16[128,2048]{1,0:T(8,128)(2,1)}, bf16[128,2048]{1,0:T(8,128)(2,1)S(1)}, u32[]{:S(2)}) copy-start(bf16[128,2048]{1,0:T(8,128)(2,1)S(1)} %get-tuple-element.77.refs_2_) | copy-start | bytes 1572868
  49.8 10.6 %collective-permute-start.9 = (bf16[32,4096]{1,0:T(8,128)(2,1)S(1)}, bf16[32,4096]{1,0:T(8,128)(2,1)S(1)}, u32[]{:S(2)}, u32[]{:S(2)}) collective-permute-start(bf16[32,4096]{1,0:T(8,128)(2,1)S(1)} %get-tuple-element.78), channel_id=1, source_target_pairs={{0,4},{1,5},{2,6},{3,7},{4,0},{5,1},{6,2},{7,3},{8,12},{9,13},{10,... | collective-permute-start | bytes 786440 | tf_op jit(solution)/shard_map/ppermute | solution.py:412
  50.4 10.0 %collective-permute-start.10 = (bf16[32,4096]{1,0:T(8,128)(2,1)S(1)}, bf16[32,4096]{1,0:T(8,128)(2,1)S(1)}, u32[]{:S(2)}, u32[]{:S(2)}) collective-permute-start(bf16[32,4096]{1,0:T(8,128)(2,1)S(1)} %get-tuple-element.79), channel_id=1, source_target_pairs={{0,16},{1,17},{2,18},{3,19},{4,20},{5,21},{6,22},{7,23},{8,0},{9,1... | collective-permute-start | bytes 786440 | tf_op jit(solution)/shard_map/ppermute | solution.py:412
  52.0 9.4 %collective-permute-start.8 = (bf16[128,2048]{1,0:T(8,128)(2,1)S(1)}, bf16[128,2048]{1,0:T(8,128)(2,1)S(1)}, u32[]{:S(2)}, u32[]{:S(2)}) collective-permute-start(bf16[128,2048]{1,0:T(8,128)(2,1)S(1)} %get-tuple-element.77.refs_2_), channel_id=1, source_target_pairs={{0,2},{4,6},{9,11},{13,15},{18,16},{22,20},{27,25},{31,29}} | collective-permute-start | bytes 1572872 | tf_op jit(solution)/shard_map/ppermute | solution.py:412
  60.3 12.5 %copy-start.13 = (bf16[32,4096]{1,0:T(8,128)(2,1)}, bf16[32,4096]{1,0:T(8,128)(2,1)S(1)}, u32[]{:S(2)}) copy-start(bf16[32,4096]{1,0:T(8,128)(2,1)S(1)} %collective-permute-done.9.refs_0_.refs_1_.refs_7_) | copy-start | bytes 786436
  60.4 12.5 %copy-start.14 = (bf16[32,4096]{1,0:T(8,128)(2,1)}, bf16[32,4096]{1,0:T(8,128)(2,1)S(1)}, u32[]{:S(2)}) copy-start(bf16[32,4096]{1,0:T(8,128)(2,1)S(1)} %collective-permute-done.10.refs_1_.refs_2_.refs_8_) | copy-start | bytes 786436
  61.4 11.4 %copy-start.22 = (bf16[128,2048]{1,0:T(8,128)(2,1)}, bf16[128,2048]{1,0:T(8,128)(2,1)S(1)}, u32[]{:S(2)}) copy-start(bf16[128,2048]{1,0:T(8,128)(2,1)S(1)} %collective-permute-done.8.refs_6_) | copy-start | bytes 1572868
  62.0 12.1 %copy-start.4 = (bf16[64,2048]{1,0:T(8,128)(2,1)}, bf16[64,2048]{1,0:T(8,128)(2,1)S(1)}, u32[]{:S(2)}) copy-start(bf16[64,2048]{1,0:T(8,128)(2,1)S(1)} %pick.7.refs_3_) | copy-start | bytes 786436
  62.0 10.8 %collective-permute-start.12 = (bf16[64,2048]{1,0:T(8,128)(2,1)S(1)}, bf16[64,2048]{1,0:T(8,128)(2,1)S(1)}, u32[]{:S(2)}, u32[]{:S(2)}) collective-permute-start(bf16[64,2048]{1,0:T(8,128)(2,1)S(1)} %pick.7.refs_3_), channel_id=1, source_target_pairs={{0,2},{4,6},{9,11},{13,15},{18,16},{22,20},{27,25},{31,29}} | collective-permute-start | bytes 786440 | tf_op jit(solution)/shard_map/ppermute | solution.py:412
  67.1 16.4 %copy-start.17 = (f32[64]{0:T(128)S(1)}, f32[64]{0:T(128)}, u32[]{:S(2)}) copy-start(f32[64]{0:T(128)} %param.9) | copy-start | bytes 772
  67.1 16.4 %copy-start.18 = (s32[64]{0:T(128)S(1)}, s32[64]{0:T(128)}, u32[]{:S(2)}) copy-start(s32[64]{0:T(128)} %param.10) | copy-start | bytes 772
  67.1 6.4 %collective-permute-start.13 = (bf16[512,256]{1,0:T(8,128)(2,1)S(1)}, bf16[512,256]{1,0:T(8,128)(2,1)S(1)}, u32[]{:S(2)}, u32[]{:S(2)}) collective-permute-start(bf16[512,256]{1,0:T(8,128)(2,1)S(1)} %get-tuple-element.89), channel_id=1, source_target_pairs={{0,2},{1,3},{2,0},{3,1},{4,6},{5,7},{6,4},{7,5},{8,10},{9,11},{10,... | collective-permute-start | bytes 786440 | tf_op jit(solution)/shard_map/ppermute | solution.py:412
  67.2 6.4 %collective-permute-start.14 = (bf16[1024,128]{1,0:T(8,128)(2,1)S(1)}, bf16[1024,128]{1,0:T(8,128)(2,1)S(1)}, u32[]{:S(2)}, u32[]{:S(2)}) collective-permute-start(bf16[1024,128]{1,0:T(8,128)(2,1)S(1)} %get-tuple-element.91), channel_id=1, source_target_pairs={{0,1},{1,0},{2,3},{3,2},{4,5},{5,4},{6,7},{7,6},{8,9},{9,8},{10,11... | collective-permute-start | bytes 786440 | tf_op jit(solution)/shard_map/ppermute | solution.py:412
  72.8 3.4 %copy-start.23 = (bf16[64,2048]{1,0:T(8,128)(2,1)}, bf16[64,2048]{1,0:T(8,128)(2,1)S(1)}, u32[]{:S(2)}) copy-start(bf16[64,2048]{1,0:T(8,128)(2,1)S(1)} %collective-permute-done.12.refs_7_) | copy-start | bytes 786436
  73.5 6.9 %collective-permute-start.15 = (bf16[1024,128]{1,0:T(8,128)(2,1)S(1)}, bf16[1024,128]{1,0:T(8,128)(2,1)S(1)}, u32[]{:S(2)}, u32[]{:S(2)}) collective-permute-start(bf16[1024,128]{1,0:T(8,128)(2,1)S(1)} %get-tuple-element.95), channel_id=1, source_target_pairs={{0,1},{1,0},{2,3},{3,2},{4,5},{5,4},{6,7},{7,6},{8,9},{9,8},{10,11... | collective-permute-start | bytes 786440 | tf_op jit(solution)/shard_map/ppermute | solution.py:412
  74.2 6.3 %collective-permute-start.16 = (bf16[512,128]{1,0:T(8,128)(2,1)S(1)}, bf16[512,128]{1,0:T(8,128)(2,1)S(1)}, u32[]{:S(2)}, u32[]{:S(2)}) collective-permute-start(bf16[512,128]{1,0:T(8,128)(2,1)S(1)} %get-tuple-element.99), channel_id=1, source_target_pairs={{0,2},{1,3},{2,0},{3,1},{4,6},{5,7},{6,4},{7,5},{8,10},{9,11},{10,... | collective-permute-start | bytes 393224 | tf_op jit(solution)/shard_map/ppermute | solution.py:412
  80.4 7.3 %collective-permute-start.18 = (bf16[512,2048]{1,0:T(8,128)(2,1)}, bf16[512,2048]{1,0:T(8,128)(2,1)S(1)}, u32[]{:S(2)}, u32[]{:S(2)}) collective-permute-start(bf16[512,2048]{1,0:T(8,128)(2,1)} %pack.1.own_ref), channel_id=1, source_target_pairs={{0,1},{1,0},{2,3},{3,2},{4,5},{5,4},{6,7},{7,6},{8,9},{9,8},{10,11... | collective-permute-start | bytes 6291464 | tf_op jit(solution)/shard_map/ppermute | solution.py:412
  81.7 6.0 %collective-permute-start.17 = (bf16[512,128]{1,0:T(8,128)(2,1)S(1)}, bf16[512,128]{1,0:T(8,128)(2,1)S(1)}, u32[]{:S(2)}, u32[]{:S(2)}) collective-permute-start(bf16[512,128]{1,0:T(8,128)(2,1)S(1)} %get-tuple-element.107), channel_id=1, source_target_pairs={{0,2},{1,3},{2,0},{3,1},{4,6},{5,7},{6,4},{7,5},{8,10},{9,11},{10,... | collective-permute-start | bytes 393224 | tf_op jit(solution)/shard_map/ppermute | solution.py:412
  87.7 3.6 %copy-start.19 = (bf16[512,2048]{1,0:T(8,128)(2,1)}, bf16[512,2048]{1,0:T(8,128)(2,1)S(1)}, u32[]{:S(2)}) copy-start(bf16[512,2048]{1,0:T(8,128)(2,1)S(1)} %collective-permute-done.18.other_ref) | copy-start | bytes 6291460
  88.4 1.2 collective-permute-start.19
  89.6 4.7 %collective-permute-start.20 = (f32[24,64]{1,0:T(8,128)S(1)}, f32[24,64]{1,0:T(8,128)S(1)}, u32[]{:S(2)}, u32[]{:S(2)}) collective-permute-start(f32[24,64]{1,0:T(8,128)S(1)} %add.27), channel_id=1, source_target_pairs={{0,2},{1,3},{2,0},{3,1},{4,6},{5,7},{6,4},{7,5},{8,10},{9,11},{10,... | collective-permute-start | bytes 18440 | tf_op jit(solution)/shard_map/ppermute | solution.py:412
  94.2 4.5 %collective-permute-start.21 = (f32[24,64]{1,0:T(8,128)S(1)}, f32[24,64]{1,0:T(8,128)S(1)}, u32[]{:S(2)}, u32[]{:S(2)}) collective-permute-start(f32[24,64]{1,0:T(8,128)S(1)} %add.28), channel_id=1, source_target_pairs={{0,4},{1,5},{2,6},{3,7},{4,0},{5,1},{6,2},{7,3},{8,12},{9,13},{10,... | collective-permute-start | bytes 18440 | tf_op jit(solution)/shard_map/ppermute | solution.py:412
  98.7 3.8 %collective-permute-start.22 = (f32[24,64]{1,0:T(8,128)S(1)}, f32[24,64]{1,0:T(8,128)S(1)}, u32[]{:S(2)}, u32[]{:S(2)}) collective-permute-start(f32[24,64]{1,0:T(8,128)S(1)} %add.29), channel_id=1, source_target_pairs={{0,8},{1,9},{2,10},{3,11},{4,12},{5,13},{6,14},{7,15},{8,0},{9,1},... | collective-permute-start | bytes 18440 | tf_op jit(solution)/shard_map/ppermute | solution.py:412
  102.5 4.6 %copy-start.24 = (f32[24,64]{1,0:T(8,128)}, f32[24,64]{1,0:T(8,128)S(1)}, u32[]{:S(2)}) copy-start(f32[24,64]{1,0:T(8,128)S(1)} %add.30.refs_9_) | copy-start | bytes 18436
  102.5 4.6 %collective-permute-start.23 = (f32[24,64]{1,0:T(8,128)S(1)}, f32[24,64]{1,0:T(8,128)S(1)}, u32[]{:S(2)}, u32[]{:S(2)}) collective-permute-start(f32[24,64]{1,0:T(8,128)S(1)} %add.30.refs_9_), channel_id=1, source_target_pairs={{0,16},{1,17},{2,18},{3,19},{4,20},{5,21},{6,22},{7,23},{8,24},{9,... | collective-permute-start | bytes 18440 | tf_op jit(solution)/shard_map/ppermute | solution.py:412
  (2 other events, 1.3 us)

commit v8 on v7

--- a/solution.py
+++ b/solution.py
@@ -359,7 +359,7 @@
     row_block, rows = 2 * columns_t[0].shape[0], columns_t[0].shape[1]
     groups, count = sums.shape[0] // 3, sums.shape[1]
     feat_block = pieces[0].shape[1]
-    width = min(512, feat_block)
+    width = min(256, feat_block)
     steps = feat_block // width
     on_vmem = pl.BlockSpec(memory_space=pltpu.VMEM)
     on_hbm = pl.BlockSpec(memory_space=pltpu.HBM)

time: 127 us -> 131 us (1.031)
  Pallas kernels: 56.7 us -> 60.6 us
    pallas_call x1, Pallas kernels: 18.6 us -> 22.4 us  [increment(): pl.pallas_call(functools.partial(information_kernel, features, pieces_of)...]
  transfers between devices with their start and end apart: 24 -> 24, of which waited for: 11 -> 11; matrix products, arithmetic and copies ran while one was open for 1% -> 1% of each run, Pallas kernels for 29% -> 28%
where the time goes in v8:
time: 131 us; the launch traced here: 130 us
  Pallas kernels  60.6 us (46%)
  starting transfers between devices  35.7 us (27%)
  waiting for transfers between devices  23 us (18%)
  local copies, waits for them, and re-layouts  8.97 us (7%)
    pallas_call x16, Pallas kernels, call(): pl.pallas_call(kernel, in_specs=[pl.BlockSpec(memory_space=pltpu.SMEM)] +...  37 us
    ppermute x24, starting transfers between devices, send(): return lax.ppermute(x, BOTH, pairs)  35.7 us
    ppermute x24, waiting for transfers between devices, send(): return lax.ppermute(x, BOTH, pairs)  23 us
    pallas_call x1, Pallas kernels, increment(): pl.pallas_call(functools.partial(information_kernel, features, pieces_of)...  22.4 us
    unnamed x52, local copies, waits for them, and re-layouts  8.19 us
  transfers between devices with their start and end apart: 24, of which 11 were waited for; matrix products, arithmetic and copies ran while one was open for 1% of the time, Pallas kernels for 28%

profile of v8, /device:TPU:0, one launch (start us, length us, event | category | flops | bytes accessed | tf_op | source)
XLA Modules:
  0.0 130.1 jit_solution(1834200281513776184)
XLA Ops:
  0.6 3.0 %collective-permute-start.1 = (bf16[64,4096]{1,0:T(8,128)(2,1)}, bf16[64,4096]{1,0:T(8,128)(2,1)S(1)}, u32[]{:S(2)}, u32[]{:S(2)}) collective-permute-start(bf16[64,4096]{1,0:T(8,128)(2,1)} %refs_0_.5), channel_id=1, source_target_pairs={{0,4},{1,5},{2,6},{3,7},{4,0},{5,1},{6,2},{7,3},{8,12},{9,13},{10,... | collective-permute-start | bytes 1572872 | tf_op jit(solution)/shard_map/ppermute | solution.py:412
  3.6 2.6 %collective-permute-start = (bf16[64,4096]{1,0:T(8,128)(2,1)}, bf16[64,4096]{1,0:T(8,128)(2,1)S(1)}, u32[]{:S(2)}, u32[]{:S(2)}) collective-permute-start(bf16[64,4096]{1,0:T(8,128)(2,1)} %refs_0_.5), channel_id=1, source_target_pairs={{0,16},{1,17},{2,18},{3,19},{4,20},{5,21},{6,22},{7,23},{8,0},{9,1... | collective-permute-start | bytes 1572872 | tf_op jit(solution)/shard_map/ppermute | solution.py:412
  6.2 0.7 dynamic-slice_bitcast_fusion
  6.9 0.7 xor_multiply_fusion
  7.7 5.8 %copy-done = bf16[2048,4096]{1,0:T(8,128)(2,1)S(1)} copy-done((bf16[2048,4096]{1,0:T(8,128)(2,1)S(1)}, bf16[2048,4096]{1,0:T(8,128)(2,1)}, u32[]{:S(2)}) %copy-start) | copy-done | bytes 16777240
  13.4 1.1 touch.1.scalars_ref._
  14.6 1.2 collective-permute-done.1.refs_1_
  15.8 1.7 %collective-permute-done.refs_2_ = bf16[64,4096]{1,0:T(8,128)(2,1)S(1)} collective-permute-done((bf16[64,4096]{1,0:T(8,128)(2,1)}, bf16[64,4096]{1,0:T(8,128)(2,1)S(1)}, u32[]{:S(2)}, u32[]{:S(2)}) %collective-permute-start) | collective-permute-done | bytes 524320 | tf_op jit(solution)/shard_map/ppermute | solution.py:412
  18.0 3.3 %collective-permute-start.3 = (bf16[64,4096]{1,0:T(8,128)(2,1)S(1)}, bf16[64,4096]{1,0:T(8,128)(2,1)S(1)}, u32[]{:S(2)}, u32[]{:S(2)}) collective-permute-start(bf16[64,4096]{1,0:T(8,128)(2,1)S(1)} %collective-permute-done.refs_2_), channel_id=1, source_target_pairs={{0,16},{1,17},{2,18},{3,19},{4,20},{5,21},{6,22},{7,23},{8,0},{9,1... | collective-permute-start | bytes 1572872 | tf_op jit(solution)/shard_map/ppermute | solution.py:412
  21.3 1.0 copy-done.5
  22.3 0.6 pick.4.refs_0_
  22.9 3.5 %collective-permute-start.2 = (bf16[192,2048]{1,0:T(8,128)(2,1)S(1)}, bf16[192,2048]{1,0:T(8,128)(2,1)S(1)}, u32[]{:S(2)}, u32[]{:S(2)}) collective-permute-start(bf16[192,2048]{1,0:T(8,128)(2,1)S(1)} %pick.4.refs_0_), channel_id=1, source_target_pairs={{0,2},{4,6},{9,11},{13,15},{18,16},{22,20},{27,25},{31,29}} | collective-permute-start | bytes 2359304 | tf_op jit(solution)/shard_map/ppermute | solution.py:412
  26.4 5.5 %whiten.4 = (f32[1024,128]{1,0:T(8,128)S(1)}, bf16[1024,128]{1,0:T(8,128)(2,1)S(1)}) custom-call(s32[25]{0:T(128)S(1)} %touch.1.scalars_ref._, bf16[2048,4096]{1,0:T(8,128)(2,1)S(1)} %copy-done.1, bf16[64,4096]{1,0:T(8,128)(2,1)S(1)} %copy-done.5, bf16[64,4096]{1,0:T(8,128)(2,1)S(1)} %collective-permute-done.1.refs_1_), custom_call_target="tpu_custom_call" | custom-call | flops 8589934592 | bytes 1000 | tf_op jit(solution)/shard_map/whiten/pallas_call | solution.py:33
  32.0 3.9 %collective-permute-done.2.refs_4_ = bf16[192,2048]{1,0:T(8,128)(2,1)S(1)} collective-permute-done((bf16[192,2048]{1,0:T(8,128)(2,1)S(1)}, bf16[192,2048]{1,0:T(8,128)(2,1)S(1)}, u32[]{:S(2)}, u32[]{:S(2)}) %collective-permute-start.2) | collective-permute-done | bytes 786464 | tf_op jit(solution)/shard_map/ppermute | solution.py:412
  35.8 1.5 %collective-permute-start.7 = (bf16[64,4096]{1,0:T(8,128)(2,1)S(1)}, bf16[64,4096]{1,0:T(8,128)(2,1)S(1)}, u32[]{:S(2)}, u32[]{:S(2)}) collective-permute-start(bf16[64,4096]{1,0:T(8,128)(2,1)S(1)} %collective-permute-done.3.refs_1_.refs_0_.refs_4_), channel_id=1, source_target_pairs={{0,4},{1,5},{2,6},{3,7},{4,0},{5,1},{6,2},{7,3},{8,12},{9,13},{10,... | collective-permute-start | bytes 1572872 | tf_op jit(solution)/shard_map/ppermute | solution.py:412
  37.3 1.6 %collective-permute-start.6 = (bf16[64,4096]{1,0:T(8,128)(2,1)S(1)}, bf16[64,4096]{1,0:T(8,128)(2,1)S(1)}, u32[]{:S(2)}, u32[]{:S(2)}) collective-permute-start(bf16[64,4096]{1,0:T(8,128)(2,1)S(1)} %collective-permute-done.3.refs_1_.refs_0_.refs_4_), channel_id=1, source_target_pairs={{0,16},{1,17},{2,18},{3,19},{4,20},{5,21},{6,22},{7,23},{8,0},{9,1... | collective-permute-start | bytes 1572872 | tf_op jit(solution)/shard_map/ppermute | solution.py:412
  39.6 2.8 %collective-permute-start.5 = (bf16[128,2048]{1,0:T(8,128)(2,1)S(1)}, bf16[128,2048]{1,0:T(8,128)(2,1)S(1)}, u32[]{:S(2)}, u32[]{:S(2)}) collective-permute-start(bf16[128,2048]{1,0:T(8,128)(2,1)S(1)} %pick.5.refs_1_), channel_id=1, source_target_pairs={{0,2},{4,6},{9,11},{13,15},{18,16},{22,20},{27,25},{31,29}} | collective-permute-start | bytes 1572872 | tf_op jit(solution)/shard_map/ppermute | solution.py:412
  42.4 5.6 %whiten.5 = (f32[1024,256]{1,0:T(8,128)S(1)}, bf16[1024,256]{1,0:T(8,128)(2,1)S(1)}) custom-call(s32[25]{0:T(128)S(1)} %touch.1.scalars_ref._, bf16[2048,4096]{1,0:T(8,128)(2,1)S(1)} %copy-done.1, f32[1024,128]{1,0:T(8,128)S(1)} %get-tuple-element.71.refs_0_, bf16[1024,128]{1,0:T(8,128)(2,1)S(1)} %get-tuple-element.72.refs_1_, ...), custom_call_target="tpu_custom_call" | custom-call | flops 8589934592 | bytes 1000 | tf_op jit(solution)/shard_map/whiten/pallas_call | solution.py:33
  47.9 1.1 collective-permute-done.5.refs_5_
  49.1 0.6 pick.6
  49.8 0.6 collective-permute-start.9
  50.4 1.6 %collective-permute-start.10 = (bf16[32,4096]{1,0:T(8,128)(2,1)S(1)}, bf16[32,4096]{1,0:T(8,128)(2,1)S(1)}, u32[]{:S(2)}, u32[]{:S(2)}) collective-permute-start(bf16[32,4096]{1,0:T(8,128)(2,1)S(1)} %get-tuple-element.79), channel_id=1, source_target_pairs={{0,16},{1,17},{2,18},{3,19},{4,20},{5,21},{6,22},{7,23},{8,0},{9,1... | collective-permute-start | bytes 786440 | tf_op jit(solution)/shard_map/ppermute | solution.py:412
  52.0 2.8 %collective-permute-start.8 = (bf16[128,2048]{1,0:T(8,128)(2,1)S(1)}, bf16[128,2048]{1,0:T(8,128)(2,1)S(1)}, u32[]{:S(2)}, u32[]{:S(2)}) collective-permute-start(bf16[128,2048]{1,0:T(8,128)(2,1)S(1)} %get-tuple-element.77.refs_2_), channel_id=1, source_target_pairs={{0,2},{4,6},{9,11},{13,15},{18,16},{22,20},{27,25},{31,29}} | collective-permute-start | bytes 1572872 | tf_op jit(solution)/shard_map/ppermute | solution.py:412
  54.8 5.5 %whiten.6 = (f32[1024,128]{1,0:T(8,128)S(1)}, bf16[1024,128]{1,0:T(8,128)(2,1)S(1)}) custom-call(s32[25]{0:T(128)S(1)} %touch.1.scalars_ref._, bf16[2048,4096]{1,0:T(8,128)(2,1)S(1)} %copy-done.1, bf16[64,4096]{1,0:T(8,128)(2,1)S(1)} %collective-permute-done.3.refs_1_.refs_0_.refs_4_, bf16[64,4096]{1,0:T(8,128)(2,1)S(1)} %collective-permute-done.7.refs_0_.refs_1_.refs_5_), custom_call_target="tpu_custom_call" | custom-call | flops 8589934592 | bytes 1000 | tf_op jit(solution)/shard_map/whiten/pallas_call | solution.py:33
  60.4 1.0 collective-permute-done.8.refs_6_
  62.0 4.4 %collective-permute-start.12 = (bf16[64,2048]{1,0:T(8,128)(2,1)S(1)}, bf16[64,2048]{1,0:T(8,128)(2,1)S(1)}, u32[]{:S(2)}, u32[]{:S(2)}) collective-permute-start(bf16[64,2048]{1,0:T(8,128)(2,1)S(1)} %pick.7.refs_3_), channel_id=1, source_target_pairs={{0,2},{4,6},{9,11},{13,15},{18,16},{22,20},{27,25},{31,29}} | collective-permute-start | bytes 786440 | tf_op jit(solution)/shard_map/ppermute | solution.py:412
  66.4 0.6 halve.3
  67.3 5.5 %whiten.7 = (f32[1024,128]{1,0:T(8,128)S(1)}, bf16[1024,128]{1,0:T(8,128)(2,1)S(1)}) custom-call(s32[25]{0:T(128)S(1)} %touch.1.scalars_ref._, bf16[2048,4096]{1,0:T(8,128)(2,1)S(1)} %copy-done.1, bf16[64,4096]{1,0:T(8,128)(2,1)S(1)} %collective-permute-done.6.refs_1_.refs_0_.refs_6_, bf16[32,4096]{1,0:T(8,128)(2,1)S(1)} %collective-permute-done.9.refs_0_.refs_1_.refs_7_, ...), custom_call_target="tpu_custom_call" | custom-call | flops 8589934592 | bytes 1000 | tf_op jit(solution)/shard_map/whiten/pallas_call | solution.py:33
  72.9 0.7 collective-permute-done.13.refs_1_
  73.6 0.6 halve.4
  74.2 2.1 %collective-permute-start.16 = (bf16[512,128]{1,0:T(8,128)(2,1)S(1)}, bf16[512,128]{1,0:T(8,128)(2,1)S(1)}, u32[]{:S(2)}, u32[]{:S(2)}) collective-permute-start(bf16[512,128]{1,0:T(8,128)(2,1)S(1)} %get-tuple-element.99), channel_id=1, source_target_pairs={{0,2},{1,3},{2,0},{3,1},{4,6},{5,7},{6,4},{7,5},{8,10},{9,11},{10,... | collective-permute-start | bytes 393224 | tf_op jit(solution)/shard_map/ppermute | solution.py:412
  76.3 3.5 %pack.1.own_ref = bf16[512,2048]{1,0:T(8,128)(2,1)} custom-call(s32[25]{0:T(128)} %copy-done.15, bf16[192,2048]{1,0:T(8,128)(2,1)} %copy-done.2, bf16[128,2048]{1,0:T(8,128)(2,1)} %copy-done.3, bf16[128,2048]{1,0:T(8,128)(2,1)} %copy-done.8, bf16[64,2048]{1,0:T(8,128)(2,1)} %copy-done.4, bf16[192,2048]{1,0:T(8,128)(2,1)} %copy-done.20, ...), custom_call_target="tpu_custom_call" | custom-call | flops 1000 | bytes 1000 | tf_op jit(solution)/shard_map/pack/pallas_call | solution.py:33
  79.8 0.6 collective-permute-done.16.refs_3_
  80.4 0.7 copy-done.16
  81.1 0.6 halve.5
  81.7 1.8 %collective-permute-start.17 = (bf16[512,128]{1,0:T(8,128)(2,1)S(1)}, bf16[512,128]{1,0:T(8,128)(2,1)S(1)}, u32[]{:S(2)}, u32[]{:S(2)}) collective-permute-start(bf16[512,128]{1,0:T(8,128)(2,1)S(1)} %get-tuple-element.107), channel_id=1, source_target_pairs={{0,2},{1,3},{2,0},{3,1},{4,6},{5,7},{6,4},{7,5},{8,10},{9,11},{10,... | collective-permute-start | bytes 393224 | tf_op jit(solution)/shard_map/ppermute | solution.py:412
  83.5 0.8 early_squares.1.sums_ref
  84.3 3.4 %collective-permute-done.17.got_ref = bf16[512,128]{1,0:T(8,128)(2,1)S(1)} collective-permute-done((bf16[512,128]{1,0:T(8,128)(2,1)S(1)}, bf16[512,128]{1,0:T(8,128)(2,1)S(1)}, u32[]{:S(2)}, u32[]{:S(2)}) %collective-permute-start.17) | collective-permute-done | bytes 131104 | tf_op jit(solution)/shard_map/ppermute | solution.py:412
  87.7 0.7 last_squares.1
  88.4 1.2 collective-permute-done.19
  89.6 1.7 %collective-permute-start.20 = (f32[24,64]{1,0:T(8,128)S(1)}, f32[24,64]{1,0:T(8,128)S(1)}, u32[]{:S(2)}, u32[]{:S(2)}) collective-permute-start(f32[24,64]{1,0:T(8,128)S(1)} %add.27), channel_id=1, source_target_pairs={{0,2},{1,3},{2,0},{3,1},{4,6},{5,7},{6,4},{7,5},{8,10},{9,11},{10,... | collective-permute-start | bytes 18440 | tf_op jit(solution)/shard_map/ppermute | solution.py:412
  91.3 2.9 %join.2.low_hbm = bf16[1024,512]{1,0:T(8,128)(2,1)} custom-call(s32[25]{0:T(128)} %copy-done.15, bf16[512,2048]{1,0:T(8,128)(2,1)} %pack.1.own_ref, bf16[512,2048]{1,0:T(8,128)(2,1)} %copy-done.19), custom_call_target="tpu_custom_call" | custom-call | flops 1000 | bytes 1000 | tf_op jit(solution)/shard_map/join/pallas_call | solution.py:33
  94.2 1.6 %collective-permute-start.21 = (f32[24,64]{1,0:T(8,128)S(1)}, f32[24,64]{1,0:T(8,128)S(1)}, u32[]{:S(2)}, u32[]{:S(2)}) collective-permute-start(f32[24,64]{1,0:T(8,128)S(1)} %add.28), channel_id=1, source_target_pairs={{0,4},{1,5},{2,6},{3,7},{4,0},{5,1},{6,2},{7,3},{8,12},{9,13},{10,... | collective-permute-start | bytes 18440 | tf_op jit(solution)/shard_map/ppermute | solution.py:412
  95.8 2.9 %join.3.high_hbm = bf16[1024,512]{1,0:T(8,128)(2,1)} custom-call(s32[25]{0:T(128)} %copy-done.15, bf16[512,2048]{1,0:T(8,128)(2,1)} %pack.1.own_ref, bf16[512,2048]{1,0:T(8,128)(2,1)} %copy-done.19), custom_call_target="tpu_custom_call" | custom-call | flops 1000 | bytes 1000 | tf_op jit(solution)/shard_map/join/pallas_call | solution.py:33
  98.8 3.7 %collective-permute-done.22 = f32[24,64]{1,0:T(8,128)S(1)} collective-permute-done((f32[24,64]{1,0:T(8,128)S(1)}, f32[24,64]{1,0:T(8,128)S(1)}, u32[]{:S(2)}, u32[]{:S(2)}) %collective-permute-start.22) | collective-permute-done | bytes 6176 | tf_op jit(solution)/shard_map/ppermute | solution.py:412
  102.5 4.6 %collective-permute-done.23.refs_10_ = f32[24,64]{1,0:T(8,128)S(1)} collective-permute-done((f32[24,64]{1,0:T(8,128)S(1)}, f32[24,64]{1,0:T(8,128)S(1)}, u32[]{:S(2)}, u32[]{:S(2)}) %collective-permute-start.23) | collective-permute-done | bytes 6176 | tf_op jit(solution)/shard_map/ppermute | solution.py:412
  107.1 0.6 copy-done.25
  107.7 22.4 %increment.1 = (f32[2048,4096]{1,0:T(8,128)}, f32[1,64]{1,0:T(1,128)}, f32[1,64]{1,0:T(1,128)}) custom-call(s32[25]{0:T(128)} %copy-done.15, bf16[1024,512]{1,0:T(8,128)(2,1)} %join.2.low_hbm, bf16[1024,512]{1,0:T(8,128)(2,1)} %join.3.high_hbm, bf16[64,4096]{1,0:T(8,128)(2,1)} %refs_0_.5, bf16[64,4096]{1,0:T(8,128)(2,1)} %copy-done.6, ...), custom_call_target="tpu_custom_call" | custom-call | flops 8589934592 | bytes 1000 | tf_op jit(solution)/shard_map/increment/pallas_call | solution.py:366
  (77 shorter events, 2.2 us)
Async XLA Ops:
  0.6 15.1 %collective-permute-start.1 = (bf16[64,4096]{1,0:T(8,128)(2,1)}, bf16[64,4096]{1,0:T(8,128)(2,1)S(1)}, u32[]{:S(2)}, u32[]{:S(2)}) collective-permute-start(bf16[64,4096]{1,0:T(8,128)(2,1)} %refs_0_.5), channel_id=1, source_target_pairs={{0,4},{1,5},{2,6},{3,7},{4,0},{5,1},{6,2},{7,3},{8,12},{9,13},{10,... | collective-permute-start | bytes 1572872 | tf_op jit(solution)/shard_map/ppermute | solution.py:412
  3.6 13.8 %collective-permute-start = (bf16[64,4096]{1,0:T(8,128)(2,1)}, bf16[64,4096]{1,0:T(8,128)(2,1)S(1)}, u32[]{:S(2)}, u32[]{:S(2)}) collective-permute-start(bf16[64,4096]{1,0:T(8,128)(2,1)} %refs_0_.5), channel_id=1, source_target_pairs={{0,16},{1,17},{2,18},{3,19},{4,20},{5,21},{6,22},{7,23},{8,0},{9,1... | collective-permute-start | bytes 1572872 | tf_op jit(solution)/shard_map/ppermute | solution.py:412
  7.7 5.8 %copy-start = (bf16[2048,4096]{1,0:T(8,128)(2,1)S(1)}, bf16[2048,4096]{1,0:T(8,128)(2,1)}, u32[]{:S(2)}) copy-start(bf16[2048,4096]{1,0:T(8,128)(2,1)} %f_ref.9) | copy-start | bytes 50331652
  13.4 13.0 %copy-start.1 = (bf16[2048,4096]{1,0:T(8,128)(2,1)S(1)}, bf16[2048,4096]{1,0:T(8,128)(2,1)}, u32[]{:S(2)}) copy-start(bf16[2048,4096]{1,0:T(8,128)(2,1)} %f_ref.9) | copy-start | bytes 50331652
  14.6 59.0 %copy-start.15 = (s32[25]{0:T(128)}, s32[25]{0:T(128)S(1)}, u32[]{:S(2)}) copy-start(s32[25]{0:T(128)S(1)} %touch.1.scalars_ref._) | copy-start | bytes 304
  15.8 16.2 %copy-start.6 = (bf16[64,4096]{1,0:T(8,128)(2,1)}, bf16[64,4096]{1,0:T(8,128)(2,1)S(1)}, u32[]{:S(2)}) copy-start(bf16[64,4096]{1,0:T(8,128)(2,1)S(1)} %collective-permute-done.1.refs_1_) | copy-start | bytes 1572868
  17.4 24.9 %copy-start.7 = (bf16[64,4096]{1,0:T(8,128)(2,1)}, bf16[64,4096]{1,0:T(8,128)(2,1)S(1)}, u32[]{:S(2)}) copy-start(bf16[64,4096]{1,0:T(8,128)(2,1)S(1)} %collective-permute-done.refs_2_) | copy-start | bytes 1572868
  17.4 14.5 %collective-permute-start.4 = (bf16[64,4096]{1,0:T(8,128)(2,1)S(1)}, bf16[64,4096]{1,0:T(8,128)(2,1)S(1)}, u32[]{:S(2)}, u32[]{:S(2)}) collective-permute-start(bf16[64,4096]{1,0:T(8,128)(2,1)S(1)} %collective-permute-done.refs_2_), channel_id=1, source_target_pairs={{0,4},{1,5},{2,6},{3,7},{4,0},{5,1},{6,2},{7,3},{8,12},{9,13},{10,... | collective-permute-start | bytes 1572872 | tf_op jit(solution)/shard_map/ppermute | solution.py:412
  18.0 14.0 %collective-permute-start.3 = (bf16[64,4096]{1,0:T(8,128)(2,1)S(1)}, bf16[64,4096]{1,0:T(8,128)(2,1)S(1)}, u32[]{:S(2)}, u32[]{:S(2)}) collective-permute-start(bf16[64,4096]{1,0:T(8,128)(2,1)S(1)} %collective-permute-done.refs_2_), channel_id=1, source_target_pairs={{0,16},{1,17},{2,18},{3,19},{4,20},{5,21},{6,22},{7,23},{8,0},{9,1... | collective-permute-start | bytes 1572872 | tf_op jit(solution)/shard_map/ppermute | solution.py:412
  21.3 1.0 copy-start.5
  22.9 25.0 %copy-start.2 = (bf16[192,2048]{1,0:T(8,128)(2,1)}, bf16[192,2048]{1,0:T(8,128)(2,1)S(1)}, u32[]{:S(2)}) copy-start(bf16[192,2048]{1,0:T(8,128)(2,1)S(1)} %pick.4.refs_0_) | copy-start | bytes 2359300
  22.9 12.9 %collective-permute-start.2 = (bf16[192,2048]{1,0:T(8,128)(2,1)S(1)}, bf16[192,2048]{1,0:T(8,128)(2,1)S(1)}, u32[]{:S(2)}, u32[]{:S(2)}) collective-permute-start(bf16[192,2048]{1,0:T(8,128)(2,1)S(1)} %pick.4.refs_0_), channel_id=1, source_target_pairs={{0,2},{4,6},{9,11},{13,15},{18,16},{22,20},{27,25},{31,29}} | collective-permute-start | bytes 2359304 | tf_op jit(solution)/shard_map/ppermute | solution.py:412
  31.9 17.8 %copy-start.9 = (bf16[64,4096]{1,0:T(8,128)(2,1)}, bf16[64,4096]{1,0:T(8,128)(2,1)S(1)}, u32[]{:S(2)}) copy-start(bf16[64,4096]{1,0:T(8,128)(2,1)S(1)} %collective-permute-done.4.refs_0_.refs_3_) | copy-start | bytes 1572868
  32.0 22.8 %copy-start.10 = (bf16[64,4096]{1,0:T(8,128)(2,1)}, bf16[64,4096]{1,0:T(8,128)(2,1)S(1)}, u32[]{:S(2)}) copy-start(bf16[64,4096]{1,0:T(8,128)(2,1)S(1)} %collective-permute-done.3.refs_1_.refs_0_.refs_4_) | copy-start | bytes 1572868
  35.8 13.9 %copy-start.20 = (bf16[192,2048]{1,0:T(8,128)(2,1)}, bf16[192,2048]{1,0:T(8,128)(2,1)S(1)}, u32[]{:S(2)}) copy-start(bf16[192,2048]{1,0:T(8,128)(2,1)S(1)} %collective-permute-done.2.refs_4_) | copy-start | bytes 2359300
  35.8 13.2 %collective-permute-start.7 = (bf16[64,4096]{1,0:T(8,128)(2,1)S(1)}, bf16[64,4096]{1,0:T(8,128)(2,1)S(1)}, u32[]{:S(2)}, u32[]{:S(2)}) collective-permute-start(bf16[64,4096]{1,0:T(8,128)(2,1)S(1)} %collective-permute-done.3.refs_1_.refs_0_.refs_4_), channel_id=1, source_target_pairs={{0,4},{1,5},{2,6},{3,7},{4,0},{5,1},{6,2},{7,3},{8,12},{9,13},{10,... | collective-permute-start | bytes 1572872 | tf_op jit(solution)/shard_map/ppermute | solution.py:412
  37.3 11.7 %collective-permute-start.6 = (bf16[64,4096]{1,0:T(8,128)(2,1)S(1)}, bf16[64,4096]{1,0:T(8,128)(2,1)S(1)}, u32[]{:S(2)}, u32[]{:S(2)}) collective-permute-start(bf16[64,4096]{1,0:T(8,128)(2,1)S(1)} %collective-permute-done.3.refs_1_.refs_0_.refs_4_), channel_id=1, source_target_pairs={{0,16},{1,17},{2,18},{3,19},{4,20},{5,21},{6,22},{7,23},{8,0},{9,1... | collective-permute-start | bytes 1572872 | tf_op jit(solution)/shard_map/ppermute | solution.py:412
  39.6 20.8 %copy-start.3 = (bf16[128,2048]{1,0:T(8,128)(2,1)}, bf16[128,2048]{1,0:T(8,128)(2,1)S(1)}, u32[]{:S(2)}) copy-start(bf16[128,2048]{1,0:T(8,128)(2,1)S(1)} %pick.5.refs_1_) | copy-start | bytes 1572868
  39.6 9.4 %collective-permute-start.5 = (bf16[128,2048]{1,0:T(8,128)(2,1)S(1)}, bf16[128,2048]{1,0:T(8,128)(2,1)S(1)}, u32[]{:S(2)}, u32[]{:S(2)}) collective-permute-start(bf16[128,2048]{1,0:T(8,128)(2,1)S(1)} %pick.5.refs_1_), channel_id=1, source_target_pairs={{0,2},{4,6},{9,11},{13,15},{18,16},{22,20},{27,25},{31,29}} | collective-permute-start | bytes 1572872 | tf_op jit(solution)/shard_map/ppermute | solution.py:412
  49.0 13.0 %copy-start.21 = (bf16[128,2048]{1,0:T(8,128)(2,1)}, bf16[128,2048]{1,0:T(8,128)(2,1)S(1)}, u32[]{:S(2)}) copy-start(bf16[128,2048]{1,0:T(8,128)(2,1)S(1)} %collective-permute-done.5.refs_5_) | copy-start | bytes 1572868
  49.0 13.0 %copy-start.11 = (bf16[64,4096]{1,0:T(8,128)(2,1)}, bf16[64,4096]{1,0:T(8,128)(2,1)S(1)}, u32[]{:S(2)}) copy-start(bf16[64,4096]{1,0:T(8,128)(2,1)S(1)} %collective-permute-done.7.refs_0_.refs_1_.refs_5_) | copy-start | bytes 1572868
  49.0 18.2 %copy-start.12 = (bf16[64,4096]{1,0:T(8,128)(2,1)}, bf16[64,4096]{1,0:T(8,128)(2,1)S(1)}, u32[]{:S(2)}) copy-start(bf16[64,4096]{1,0:T(8,128)(2,1)S(1)} %collective-permute-done.6.refs_1_.refs_0_.refs_6_) | copy-start | bytes 1572868
  49.0 11.3 %collective-permute-start.11 = (bf16[1024,256]{1,0:T(8,128)(2,1)S(1)}, bf16[1024,256]{1,0:T(8,128)(2,1)S(1)}, u32[]{:S(2)}, u32[]{:S(2)}) collective-permute-start(bf16[1024,256]{1,0:T(8,128)(2,1)S(1)} %get-tuple-element.81), channel_id=1, source_target_pairs={{0,1},{1,0},{2,3},{3,2},{4,5},{5,4},{6,7},{7,6},{8,9},{9,8},{10,11... | collective-permute-start | bytes 1572872 | tf_op jit(solution)/shard_map/ppermute | solution.py:412
  49.7 17.3 %copy-start.8 = (bf16[128,2048]{1,0:T(8,128)(2,1)}, bf16[128,2048]{1,0:T(8,128)(2,1)S(1)}, u32[]{:S(2)}) copy-start(bf16[128,2048]{1,0:T(8,128)(2,1)S(1)} %get-tuple-element.77.refs_2_) | copy-start | bytes 1572868
  49.8 10.6 %collective-permute-start.9 = (bf16[32,4096]{1,0:T(8,128)(2,1)S(1)}, bf16[32,4096]{1,0:T(8,128)(2,1)S(1)}, u32[]{:S(2)}, u32[]{:S(2)}) collective-permute-start(bf16[32,4096]{1,0:T(8,128)(2,1)S(1)} %get-tuple-element.78), channel_id=1, source_target_pairs={{0,4},{1,5},{2,6},{3,7},{4,0},{5,1},{6,2},{7,3},{8,12},{9,13},{10,... | collective-permute-start | bytes 786440 | tf_op jit(solution)/shard_map/ppermute | solution.py:412
  50.4 10.0 %collective-permute-start.10 = (bf16[32,4096]{1,0:T(8,128)(2,1)S(1)}, bf16[32,4096]{1,0:T(8,128)(2,1)S(1)}, u32[]{:S(2)}, u32[]{:S(2)}) collective-permute-start(bf16[32,4096]{1,0:T(8,128)(2,1)S(1)} %get-tuple-element.79), channel_id=1, source_target_pairs={{0,16},{1,17},{2,18},{3,19},{4,20},{5,21},{6,22},{7,23},{8,0},{9,1... | collective-permute-start | bytes 786440 | tf_op jit(solution)/shard_map/ppermute | solution.py:412
  52.0 9.4 %collective-permute-start.8 = (bf16[128,2048]{1,0:T(8,128)(2,1)S(1)}, bf16[128,2048]{1,0:T(8,128)(2,1)S(1)}, u32[]{:S(2)}, u32[]{:S(2)}) collective-permute-start(bf16[128,2048]{1,0:T(8,128)(2,1)S(1)} %get-tuple-element.77.refs_2_), channel_id=1, source_target_pairs={{0,2},{4,6},{9,11},{13,15},{18,16},{22,20},{27,25},{31,29}} | collective-permute-start | bytes 1572872 | tf_op jit(solution)/shard_map/ppermute | solution.py:412
  60.3 12.5 %copy-start.13 = (bf16[32,4096]{1,0:T(8,128)(2,1)}, bf16[32,4096]{1,0:T(8,128)(2,1)S(1)}, u32[]{:S(2)}) copy-start(bf16[32,4096]{1,0:T(8,128)(2,1)S(1)} %collective-permute-done.9.refs_0_.refs_1_.refs_7_) | copy-start | bytes 786436
  60.4 12.5 %copy-start.14 = (bf16[32,4096]{1,0:T(8,128)(2,1)}, bf16[32,4096]{1,0:T(8,128)(2,1)S(1)}, u32[]{:S(2)}) copy-start(bf16[32,4096]{1,0:T(8,128)(2,1)S(1)} %collective-permute-done.10.refs_1_.refs_2_.refs_8_) | copy-start | bytes 786436
  61.4 11.4 %copy-start.22 = (bf16[128,2048]{1,0:T(8,128)(2,1)}, bf16[128,2048]{1,0:T(8,128)(2,1)S(1)}, u32[]{:S(2)}) copy-start(bf16[128,2048]{1,0:T(8,128)(2,1)S(1)} %collective-permute-done.8.refs_6_) | copy-start | bytes 1572868
  62.0 12.1 %copy-start.4 = (bf16[64,2048]{1,0:T(8,128)(2,1)}, bf16[64,2048]{1,0:T(8,128)(2,1)S(1)}, u32[]{:S(2)}) copy-start(bf16[64,2048]{1,0:T(8,128)(2,1)S(1)} %pick.7.refs_3_) | copy-start | bytes 786436
  62.0 10.8 %collective-permute-start.12 = (bf16[64,2048]{1,0:T(8,128)(2,1)S(1)}, bf16[64,2048]{1,0:T(8,128)(2,1)S(1)}, u32[]{:S(2)}, u32[]{:S(2)}) collective-permute-start(bf16[64,2048]{1,0:T(8,128)(2,1)S(1)} %pick.7.refs_3_), channel_id=1, source_target_pairs={{0,2},{4,6},{9,11},{13,15},{18,16},{22,20},{27,25},{31,29}} | collective-permute-start | bytes 786440 | tf_op jit(solution)/shard_map/ppermute | solution.py:412
  67.1 16.4 %copy-start.17 = (f32[64]{0:T(128)S(1)}, f32[64]{0:T(128)}, u32[]{:S(2)}) copy-start(f32[64]{0:T(128)} %param.9) | copy-start | bytes 772
  67.1 16.4 %copy-start.18 = (s32[64]{0:T(128)S(1)}, s32[64]{0:T(128)}, u32[]{:S(2)}) copy-start(s32[64]{0:T(128)} %param.10) | copy-start | bytes 772
  67.1 6.4 %collective-permute-start.13 = (bf16[512,256]{1,0:T(8,128)(2,1)S(1)}, bf16[512,256]{1,0:T(8,128)(2,1)S(1)}, u32[]{:S(2)}, u32[]{:S(2)}) collective-permute-start(bf16[512,256]{1,0:T(8,128)(2,1)S(1)} %get-tuple-element.89), channel_id=1, source_target_pairs={{0,2},{1,3},{2,0},{3,1},{4,6},{5,7},{6,4},{7,5},{8,10},{9,11},{10,... | collective-permute-start | bytes 786440 | tf_op jit(solution)/shard_map/ppermute | solution.py:412
  67.2 6.4 %collective-permute-start.14 = (bf16[1024,128]{1,0:T(8,128)(2,1)S(1)}, bf16[1024,128]{1,0:T(8,128)(2,1)S(1)}, u32[]{:S(2)}, u32[]{:S(2)}) collective-permute-start(bf16[1024,128]{1,0:T(8,128)(2,1)S(1)} %get-tuple-element.91), channel_id=1, source_target_pairs={{0,1},{1,0},{2,3},{3,2},{4,5},{5,4},{6,7},{7,6},{8,9},{9,8},{10,11... | collective-permute-start | bytes 786440 | tf_op jit(solution)/shard_map/ppermute | solution.py:412
  72.8 3.4 %copy-start.23 = (bf16[64,2048]{1,0:T(8,128)(2,1)}, bf16[64,2048]{1,0:T(8,128)(2,1)S(1)}, u32[]{:S(2)}) copy-start(bf16[64,2048]{1,0:T(8,128)(2,1)S(1)} %collective-permute-done.12.refs_7_) | copy-start | bytes 786436
  73.5 6.9 %collective-permute-start.15 = (bf16[1024,128]{1,0:T(8,128)(2,1)S(1)}, bf16[1024,128]{1,0:T(8,128)(2,1)S(1)}, u32[]{:S(2)}, u32[]{:S(2)}) collective-permute-start(bf16[1024,128]{1,0:T(8,128)(2,1)S(1)} %get-tuple-element.95), channel_id=1, source_target_pairs={{0,1},{1,0},{2,3},{3,2},{4,5},{5,4},{6,7},{7,6},{8,9},{9,8},{10,11... | collective-permute-start | bytes 786440 | tf_op jit(solution)/shard_map/ppermute | solution.py:412
  74.2 6.3 %collective-permute-start.16 = (bf16[512,128]{1,0:T(8,128)(2,1)S(1)}, bf16[512,128]{1,0:T(8,128)(2,1)S(1)}, u32[]{:S(2)}, u32[]{:S(2)}) collective-permute-start(bf16[512,128]{1,0:T(8,128)(2,1)S(1)} %get-tuple-element.99), channel_id=1, source_target_pairs={{0,2},{1,3},{2,0},{3,1},{4,6},{5,7},{6,4},{7,5},{8,10},{9,11},{10,... | collective-permute-start | bytes 393224 | tf_op jit(solution)/shard_map/ppermute | solution.py:412
  80.4 7.3 %collective-permute-start.18 = (bf16[512,2048]{1,0:T(8,128)(2,1)}, bf16[512,2048]{1,0:T(8,128)(2,1)S(1)}, u32[]{:S(2)}, u32[]{:S(2)}) collective-permute-start(bf16[512,2048]{1,0:T(8,128)(2,1)} %pack.1.own_ref), channel_id=1, source_target_pairs={{0,1},{1,0},{2,3},{3,2},{4,5},{5,4},{6,7},{7,6},{8,9},{9,8},{10,11... | collective-permute-start | bytes 6291464 | tf_op jit(solution)/shard_map/ppermute | solution.py:412
  81.7 6.0 %collective-permute-start.17 = (bf16[512,128]{1,0:T(8,128)(2,1)S(1)}, bf16[512,128]{1,0:T(8,128)(2,1)S(1)}, u32[]{:S(2)}, u32[]{:S(2)}) collective-permute-start(bf16[512,128]{1,0:T(8,128)(2,1)S(1)} %get-tuple-element.107), channel_id=1, source_target_pairs={{0,2},{1,3},{2,0},{3,1},{4,6},{5,7},{6,4},{7,5},{8,10},{9,11},{10,... | collective-permute-start | bytes 393224 | tf_op jit(solution)/shard_map/ppermute | solution.py:412
  87.7 3.6 %copy-start.19 = (bf16[512,2048]{1,0:T(8,128)(2,1)}, bf16[512,2048]{1,0:T(8,128)(2,1)S(1)}, u32[]{:S(2)}) copy-start(bf16[512,2048]{1,0:T(8,128)(2,1)S(1)} %collective-permute-done.18.other_ref) | copy-start | bytes 6291460
  88.4 1.2 collective-permute-start.19
  89.6 4.7 %collective-permute-start.20 = (f32[24,64]{1,0:T(8,128)S(1)}, f32[24,64]{1,0:T(8,128)S(1)}, u32[]{:S(2)}, u32[]{:S(2)}) collective-permute-start(f32[24,64]{1,0:T(8,128)S(1)} %add.27), channel_id=1, source_target_pairs={{0,2},{1,3},{2,0},{3,1},{4,6},{5,7},{6,4},{7,5},{8,10},{9,11},{10,... | collective-permute-start | bytes 18440 | tf_op jit(solution)/shard_map/ppermute | solution.py:412
  94.2 4.5 %collective-permute-start.21 = (f32[24,64]{1,0:T(8,128)S(1)}, f32[24,64]{1,0:T(8,128)S(1)}, u32[]{:S(2)}, u32[]{:S(2)}) collective-permute-start(f32[24,64]{1,0:T(8,128)S(1)} %add.28), channel_id=1, source_target_pairs={{0,4},{1,5},{2,6},{3,7},{4,0},{5,1},{6,2},{7,3},{8,12},{9,13},{10,... | collective-permute-start | bytes 18440 | tf_op jit(solution)/shard_map/ppermute | solution.py:412
  98.7 3.8 %collective-permute-start.22 = (f32[24,64]{1,0:T(8,128)S(1)}, f32[24,64]{1,0:T(8,128)S(1)}, u32[]{:S(2)}, u32[]{:S(2)}) collective-permute-start(f32[24,64]{1,0:T(8,128)S(1)} %add.29), channel_id=1, source_target_pairs={{0,8},{1,9},{2,10},{3,11},{4,12},{5,13},{6,14},{7,15},{8,0},{9,1},... | collective-permute-start | bytes 18440 | tf_op jit(solution)/shard_map/ppermute | solution.py:412
  102.5 4.6 %copy-start.24 = (f32[24,64]{1,0:T(8,128)}, f32[24,64]{1,0:T(8,128)S(1)}, u32[]{:S(2)}) copy-start(f32[24,64]{1,0:T(8,128)S(1)} %add.30.refs_9_) | copy-start | bytes 18436
  102.5 4.6 %collective-permute-start.23 = (f32[24,64]{1,0:T(8,128)S(1)}, f32[24,64]{1,0:T(8,128)S(1)}, u32[]{:S(2)}, u32[]{:S(2)}) collective-permute-start(f32[24,64]{1,0:T(8,128)S(1)} %add.30.refs_9_), channel_id=1, source_target_pairs={{0,16},{1,17},{2,18},{3,19},{4,20},{5,21},{6,22},{7,23},{8,24},{9,... | collective-permute-start | bytes 18440 | tf_op jit(solution)/shard_map/ppermute | solution.py:412
  (2 other events, 1.3 us)
